TPU v7x, 32 devices: a whole 2x2x4 slice. The times are simulated.
32 devices in a mesh: groups: 2 (over x), rows: 8 (over z, y), tensor: 2 (over core).
Axes of the slice: x: 2, y: 2, z: 4, core: 2. Of those that a mesh axis runs over, the one named last changes fastest.
Arguments:
- passages: bfloat16 [10240, 8192], P(('groups', 'rows'), 'tensor'), parts along dimension 0, may hold values from -6 to 6
- kv_weight: bfloat16 [8192, 2, 1024], P('rows', None, 'tensor'), may hold values from -0.0625 to 0.0625
- new_hidden: bfloat16 [128, 3, 8192], P(('groups', 'rows'), None, 'tensor'), parts along dimension 0, may hold values from -6 to 6
- queries: bfloat16 [128, 3, 8192], P(('groups', 'rows'), None, 'tensor'), parts along dimension 0, may hold values from -64 to 64
- lengths: int32 [16, 8], P('groups'), parts along dimension 0, may hold values from 1 to 160, 640 in all within a row
- destinations: int32 [16, 8], P('groups'), parts along dimension 0, may hold values from 0 to 7, as said below
Outputs:
- attended: bfloat16 [128, 3, 8192], P(('groups', 'rows'), None, 'tensor'), parts along dimension 0
There are 2 independent parts, one for each index of `groups`. A program takes and returns all parts, laid end to end along the dimension named above; an argument that names none is the same for every part. Nothing has to cross between parts.
Inputs may be any that keep to these rules, and one draw needn't show every extreme that they name: `destinations`: row p names a different decode row for each of its 8 requests, and each decode row receives exactly one request from every prefill replica. `lengths`: each row sums to 640.
All inputs are finite; a program needn't handle non-finite values.
Results may differ from a plain program's by a relative error of at most 0.012.
The roundings to bfloat16 on the way count: a program that leaves them out, or rounds other values in their place, can miss the bound.
Values may be sent and summed in bfloat16 or wider, within the bound.
No kernel may reach another device: no remote copies, remote signals or barrier semaphores. Data moves between devices by JAX's collectives and lax.ppermute only.
A program may use at most 128 MiB of HBM per device.

v0:
```python
import math

import jax
import jax.numpy as jnp
from jax import lax
from jax.sharding import PartitionSpec as P

HD = 128


def rotate(vectors, positions):
    half_size = HD // 2
    index_float = jnp.arange(half_size, dtype=jnp.float32)
    inverse = jnp.exp(index_float * (-2.0 * math.log(1000000.0) / HD))
    angles = positions.astype(jnp.float32)[..., None] * inverse
    cosine = jnp.cos(angles)
    sine = jnp.sin(angles)
    first = vectors[..., :half_size]
    second = vectors[..., half_size:]
    return jnp.concatenate([first * cosine - second * sine, second * cosine + first * sine], -1)


def token_positions(starts_row, count):
    token_index = jnp.arange(count, dtype=jnp.int32)
    began = jnp.where(starts_row[None, :] <= token_index[:, None], starts_row[None, :], 0)
    return token_index - jnp.max(began, axis=1)


def attend(query, cache, new_pairs, request_length, longest):
    requests, steps = (query.shape[0], query.shape[1])
    local_heads = cache.shape[3]
    group_size = query.shape[2] // (local_heads * HD)
    keys_all = jnp.concatenate([cache[:, :, 0], new_pairs[:, :, 0]], 1)
    values_all = jnp.concatenate([cache[:, :, 1], new_pairs[:, :, 1]], 1)
    query_heads = query.reshape(requests, steps, local_heads, group_size, HD)
    scores = jnp.einsum(
        "rtkgd,rmkd->rtkgm", query_heads, keys_all, preferred_element_type=jnp.float32
    )
    scores = scores * (1.0 / math.sqrt(HD))
    slot_index = jnp.arange(longest + steps, dtype=jnp.int32)
    step_index = jnp.arange(steps, dtype=jnp.int32)
    in_cache = (slot_index[None, None, :] < request_length[:, None, None]) & (
        slot_index[None, None, :] < longest
    )
    in_new = (slot_index[None, None, :] >= longest) & (
        slot_index[None, None, :] - longest <= step_index[None, :, None]
    )
    allowed = (in_cache | in_new)[:, :, None, None, :]
    scores = jnp.where(allowed, scores, jnp.float32(-1e30))
    largest = jnp.max(scores, axis=-1, keepdims=True)
    raised = jnp.where(allowed, jnp.exp(scores - largest), jnp.float32(0.0))
    total = jnp.sum(raised, axis=-1, keepdims=True)
    weights = (raised / total).astype(jnp.bfloat16)
    output = jnp.einsum(
        "rtkgm,rmkd->rtkgd", weights, values_all, preferred_element_type=jnp.float32
    )
    return output.astype(jnp.bfloat16).reshape(requests, steps, -1)


def body(passages, kv_weight, new_hidden, queries, lengths, destinations):
    tok_rows = passages.shape[0]
    row_count = lax.axis_size("rows")
    row_index = lax.axis_index("rows")
    longest = 2 * tok_rows // row_count
    local_heads = kv_weight.shape[2] // HD
    columns = 2 * kv_weight.shape[2]
    steps = new_hidden.shape[1]
    full_tokens, full_new = (
        lax.all_gather(passages, "tensor", axis=1, tiled=True),
        lax.all_gather(new_hidden, "tensor", axis=2, tiled=True),
    )
    new_flat = full_new.reshape(-1, full_new.shape[2])
    piece = lax.all_gather(kv_weight, "rows", axis=0, tiled=True)
    count = piece.shape[0]
    weight_piece = piece.reshape(count, columns)
    projected = jnp.dot(full_tokens, weight_piece, preferred_element_type=jnp.float32)
    new_projected = jnp.dot(new_flat, weight_piece, preferred_element_type=jnp.float32)
    projected = projected.reshape(tok_rows, 2, local_heads, HD)
    new_projected = new_projected.reshape(-1, 2, local_heads, HD)
    starts = jnp.cumsum(lengths, axis=1) - lengths
    my_starts = lax.dynamic_index_in_dim(starts, row_index, 0, keepdims=False)
    my_lengths = lax.dynamic_index_in_dim(lengths, row_index, 0, keepdims=False)
    my_targets = lax.dynamic_index_in_dim(destinations, row_index, 0, keepdims=False)
    positions = token_positions(my_starts, tok_rows)
    cache_keys = rotate(projected[:, 0], positions[:, None]).astype(jnp.bfloat16)
    cache_values = projected[:, 1].astype(jnp.bfloat16)
    pairs = jnp.stack((cache_keys, cache_values), 1)
    pairs = jnp.concatenate([pairs, jnp.zeros((longest, 2, local_heads, HD), jnp.bfloat16)], 0)
    row_ids = jnp.arange(row_count, dtype=jnp.int32)
    sending = my_targets[None, :] == row_ids[:, None]
    send_start = jnp.sum(jnp.where(sending, my_starts[None, :], 0), axis=1)
    send_length = jnp.sum(jnp.where(sending, my_lengths[None, :], 0), axis=1)
    windows = jax.vmap(lambda start_row: lax.dynamic_slice_in_dim(pairs, start_row, longest, 0))(
        send_start
    )
    inside = jnp.arange(longest, dtype=jnp.int32)[None, :] < send_length[:, None]
    windows = jnp.where(inside[:, :, None, None, None], windows, jnp.zeros((), jnp.bfloat16))
    receiving = destinations == row_index
    recv_length = jnp.sum(jnp.where(receiving, lengths, 0), axis=1)
    new_projected = new_projected.reshape(row_count, steps, 2, local_heads, HD)
    new_positions = recv_length[:, None] + jnp.arange(steps, dtype=jnp.int32)[None, :]
    new_keys = rotate(new_projected[:, :, 0], new_positions[:, :, None]).astype(jnp.bfloat16)
    new_values = new_projected[:, :, 1].astype(jnp.bfloat16)
    new_pairs = jnp.stack((new_keys, new_values), 2)
    cache = lax.all_to_all(windows, "rows", split_axis=0, concat_axis=0, tiled=True)
    attended = attend(queries, cache, new_pairs, recv_length, longest)
    return attended


def solution(mesh):
    placed = (
        P(("groups", "rows"), "tensor"),
        P("rows", None, "tensor"),
        P(("groups", "rows"), None, "tensor"),
        P(("groups", "rows"), None, "tensor"),
        P("groups", None),
        P("groups", None),
    )
    return jax.shard_map(
        body,
        mesh=mesh,
        in_specs=placed,
        out_specs=P(("groups", "rows"), None, "tensor"),
        check_vma=False,
    )
```

profile of v0, /device:TPU:0, one launch (start us, length us, event | category | flops | bytes accessed | tf_op | source)
XLA Modules:
  0.0 389.3 jit_solution(17427849816406722964)
XLA Ops:
  6.5 0.7 all-gather.5.cloned.1.call-update
  7.3 0.7 all-gather.3.cloned.1.call-update
  8.0 0.2 reduce_window_sum.11
  8.4 0.1 select_reduce_fusion.3
  8.7 0.6 multiply_cosine_fusion
  9.3 230.5 %all-gather.5.cloned.1.call-done = bf16[8192,2,512]{2,1,0:T(2,128)(2,1)} async-done(((bf16[1024,2,512]{2,1,0:T(2,128)(2,1)}), bf16[8192,2,512]{2,1,0:T(2,128)(2,1)}) %all-gather.5.cloned.1.call-update) | async-done | bytes 16777232 | tf_op jit(solution)/shard_map/all_gather | solution.py:73
  239.8 41.6 %copy.42 = bf16[8192,2,512]{0,2,1:T(8,128)(2,1)} copy(bf16[8192,2,512]{2,1,0:T(2,128)(2,1)} %all-gather.5.cloned.1.call-done) | data formatting | bytes 33554432 | tf_op jit(solution)/shard_map/reshape | solution.py:75
  281.4 17.9 %fusion.1 = f32[640,2,4,128]{0,3,2,1:T(8,128)S(1)} fusion(bf16[2,4,128,8192]{3,2,1,0:T(8,128)(2,1)} %bitcast.91, bf16[640,8192]{1,0:T(8,128)(2,1)} %all-gather.3.cloned.1.call-done), kind=kOutput, calls=%fused_computation.2 | convolution fusion | flops 10737418240 | bytes 29884416 | tf_op jit(solution)/shard_map/dot_general | solution.py:76
  299.6 0.2 fusion.20
  299.7 0.1 pad_maximum_fusion
  299.9 1.7 copy.45
  301.5 0.6 concatenate.34.clone
  302.1 4.2 %gather_fusion = bf16[8,160,2,4,128]{4,3,2,1,0:T(4,128)(2,1)} fusion(bf16[800,2,4,128]{3,2,1,0:T(4,128)(2,1)S(1)} %concatenate.34.clone, s32[8]{0:T(128)S(1)} %fusion.33), kind=kCustom, calls=%fused_computation | custom fusion | bytes 5243008 | tf_op jit(solution)/shard_map/vmap()/gather | solution.py:93
  306.3 5.5 %broadcast_select_fusion = bf16[8,160,2,4,128]{4,3,2,1,0:T(4,128)(2,1)S(1)} fusion(bf16[8,160,2,4,128]{4,3,2,1,0:T(4,128)(2,1)} %gather_fusion, pred[8,160]{1,0:T(8,128)(4,1)S(1)} %iota_compare_fusion.2), kind=kLoop, calls=%fused_computation.4 | loop fusion | flops 1310720 | bytes 5244160 | tf_op jit(solution)/shard_map/jit(_where)/select_n | solution.py:97
  311.8 2.1 copy.31
  313.9 3.8 all-to-all-start
  317.6 2.3 all_gather.11
  320.0 0.1 multiply_cosine_fusion.1
  320.2 8.0 %fusion.17 = f32[8,3,2,4,128]{4,0,3,2,1:T(8,128)S(1)} fusion(bf16[2,4,128,8192,1]{3,2,1,0,4:T(8,128)(2,1)} %bitcast.92, bf16[8,3,8192]{2,0,1:T(8,128)(2,1)S(1)} %all_gather.11), kind=kOutput, calls=%fused_computation.29 | convolution fusion | flops 402653184 | bytes 17268736 | tf_op jit(solution)/shard_map/dot_general | solution.py:77
  328.5 48.4 %all-to-all-done = bf16[8,160,2,4,128]{4,1,3,2,0:T(8,128)(2,1)S(1)} async-done(((bf16[8,160,2,4,128]{4,1,3,2,0:T(8,128)(2,1)}), bf16[8,160,2,4,128]{4,1,3,2,0:T(8,128)(2,1)S(1)}, u32[]{:S(2)}, u32[]{:S(2)}) %all-to-all-start) | async-done | bytes 2621472 | tf_op jit(solution)/shard_map/all_to_all | solution.py:105
  376.9 1.7 slice_bitcast_fusion
  378.7 2.4 fusion.43
  381.1 0.5 fusion.16
  381.7 0.8 reshape.296
  (37 shorter events, 0.9 us)
Async XLA Ops:
  6.5 372.1 %copy-start = (bf16[8,3,4096]{2,0,1:T(8,128)(2,1)S(1)}, bf16[8,3,4096]{2,0,1:T(8,128)(2,1)}, u32[]{:S(2)}) copy-start(bf16[8,3,4096]{2,0,1:T(8,128)(2,1)} %param.9) | copy-start | bytes 589828
  6.5 233.3 %all-gather.5.cloned.1.call-start = ((), (), s32[]{:S(2)}) async-start(), calls=%async_computation.2 | async-start | bytes 18874368 | tf_op jit(solution)/shard_map/all_gather | solution.py:73
  7.3 0.8 copy-start.3
  7.3 0.9 copy-start.4
  7.3 274.2 %all-gather.3.cloned.1.call-start = ((), (), s32[]{:S(2)}) async-start(), calls=%async_computation.1 | async-start | bytes 15728640 | tf_op jit(solution)/shard_map/all_gather | solution.py:69
  313.9 3.8 copy-start.2
  313.9 63.1 %all-to-all-start = ((bf16[8,160,2,4,128]{4,1,3,2,0:T(8,128)(2,1)}), bf16[8,160,2,4,128]{4,1,3,2,0:T(8,128)(2,1)S(1)}, u32[]{:S(2)}, u32[]{:S(2)}) async-start(bf16[8,160,2,4,128]{4,1,3,2,0:T(8,128)(2,1)} %copy.31), calls=%async_computation | async-start | bytes 5242880 | tf_op jit(solution)/shard_map/all_to_all | solution.py:105
  378.7 2.4 copy-start.1
Sparse Core Ops, SparseCore 0:
  9.5 230.2 all-gather.4
  241.4 21.0 all-gather.2
where the time goes:
time: 391 us; the launch traced here: 389 us
  waiting for transfers between devices  280 us (72%)
  local copies, waits for them, and re-layouts  52.9 us (14%)
  matrix products  28.9 us (7%)
  between operations  13.6 us (3%)
  other arithmetic  7.43 us (2%)
    all_gather x1, waiting for transfers between devices, body(): piece = lax.all_gather(kv_weight, 'rows', axis=0, tiled=True)  230 us
    all_to_all x1, waiting for transfers between devices, body(): lax.all_to_all(windows, 'rows', split_axis=0, concat_axis=0, tiled=True)  48.4 us
    reshape x1, local copies, waits for them, and re-layouts, body(): weight_piece = piece.reshape(count, columns)  41.6 us
    dot_general x1, matrix products, body(): jnp.dot(full_tokens, weight_piece, preferred_element_type=jnp.float32)  17.9 us
    dot_general x1, matrix products, body(): jnp.dot(new_flat, weight_piece, preferred_element_type=jnp.float32)  8.05 us
  transfers between devices with their start and end apart: 3, of which 2 were waited for; matrix products, arithmetic and copies ran while one was open for 13% of the time, Pallas kernels for 0%

commit v1 on v0

v1 whole, which is shorter than its diff:
```python
import functools
import math

import jax
import jax.numpy as jnp
from jax import lax
from jax.experimental import pallas as pl
from jax.experimental.pallas import tpu as pltpu
from jax.sharding import PartitionSpec as P

HD = 128
HALF = HD // 2


def angle_tables(positions):
    index_float = jnp.arange(HALF, dtype=jnp.float32)
    inverse = jnp.exp(index_float * (-2.0 * math.log(1000000.0) / HD))
    angles = positions.astype(jnp.float32)[:, None] * inverse
    return jnp.cos(angles), jnp.sin(angles)


def token_tables(lengths, destinations, row_index, tokens, requests, steps, padded):
    my_lengths = lax.dynamic_index_in_dim(lengths, row_index, 0, keepdims=False)
    my_targets = lax.dynamic_index_in_dim(destinations, row_index, 0, keepdims=False)
    ends = jnp.cumsum(my_lengths)
    starts = ends - my_lengths
    token = jnp.arange(tokens, dtype=jnp.int32)[:, None]
    inside = (starts[None, :] <= token) & (token < ends[None, :])
    token_position = token[:, 0] - jnp.sum(jnp.where(inside, starts[None, :], 0), axis=1)
    token_target = jnp.sum(jnp.where(inside, my_targets[None, :], 0), axis=1)
    row_ids = jnp.arange(requests, dtype=jnp.int32)
    sending = my_targets[None, :] == row_ids[:, None]
    target_length = jnp.sum(jnp.where(sending, my_lengths[None, :], 0), axis=1)
    step = jnp.repeat(jnp.arange(steps, dtype=jnp.int32), requests)
    new_target = jnp.tile(row_ids, steps)
    new_position = jnp.tile(target_length, steps) + step
    spare = jnp.zeros((padded - tokens - requests * steps,), jnp.int32)
    position = jnp.concatenate([token_position, new_position, spare])
    target = jnp.concatenate([token_target, new_target, spare - 1])
    seen_from = jnp.concatenate([jnp.zeros_like(token_target), step, spare])
    query_info = jnp.stack([new_target, step], 1)
    return position, jnp.stack([target, seen_from], 0), query_info


def finish_kernel(heads, group, proj_ref, cos_ref, sin_ref, keys_ref, rows_ref, query_ref, out_ref):
    cosine, sine = cos_ref[...], sin_ref[...]
    allowed = (keys_ref[0:1, :] == rows_ref[:, 0:1]) & (keys_ref[1:2, :] <= rows_ref[:, 1:2])
    allowed = jnp.concatenate([allowed.astype(jnp.float32)] * group, 0) > 0.5
    queries = query_ref[...].astype(jnp.float32)
    count = queries.shape[0]
    width = heads * HD
    for h in range(heads):
        first = proj_ref[:, h * HD : h * HD + HALF]
        second = proj_ref[:, h * HD + HALF : (h + 1) * HD]
        keys = jnp.concatenate(
            [first * cosine - second * sine, second * cosine + first * sine], -1
        ).astype(jnp.bfloat16)
        values = proj_ref[:, width + h * HD : width + (h + 1) * HD].astype(jnp.bfloat16)
        at = h * group * HD
        query = jnp.concatenate(
            [queries[:, at + g * HD : at + (g + 1) * HD] for g in range(group)], 0
        ).astype(jnp.bfloat16)
        scores = lax.dot_general(
            query, keys, (((1,), (1,)), ((), ())), preferred_element_type=jnp.float32
        )
        scores = jnp.where(allowed, scores * (1.0 / math.sqrt(HD)), jnp.float32(-1e30))
        raised = jnp.exp(scores - jnp.max(scores, axis=-1, keepdims=True))
        total = jnp.sum(raised, axis=-1, keepdims=True)
        weights = (raised / total).astype(jnp.bfloat16)
        output = jnp.dot(weights, values, preferred_element_type=jnp.float32)
        for g in range(group):
            out_ref[:, at + g * HD : at + (g + 1) * HD] = output[
                g * count : (g + 1) * count
            ].astype(jnp.bfloat16)


def finish(projected, cosine, sine, key_info, query_info, queries):
    rows, width = projected.shape
    heads = width // (2 * HD)
    group = queries.shape[1] // (heads * HD)
    count = queries.shape[0]
    whole = pl.BlockSpec(memory_space=pltpu.VMEM)
    return pl.pallas_call(
        functools.partial(finish_kernel, heads, group),
        out_shape=jax.ShapeDtypeStruct(queries.shape, jnp.bfloat16),
        in_specs=[whole] * 6,
        out_specs=whole,
        compiler_params=pltpu.CompilerParams(vmem_limit_bytes=48 << 20),
        cost_estimate=pl.CostEstimate(
            flops=4 * heads * group * count * rows * HD,
            bytes_accessed=projected.size * 4 + 4 * queries.size,
            transcendentals=heads * group * count * rows,
        ),
        name="rotate_attend",
    )(projected, cosine, sine, key_info, query_info, queries)


def body(passages, kv_weight, new_hidden, queries, lengths, destinations):
    tokens = passages.shape[0]
    requests, steps, half_model = new_hidden.shape
    row_index = lax.axis_index("rows")
    count = requests * steps
    padded = -(-(tokens + count) // 16) * 16

    weight = kv_weight.reshape(kv_weight.shape[0], -1)
    weight = lax.all_gather(weight, "rows", axis=0, tiled=True)

    moved = jnp.concatenate([new_hidden, queries], 1)
    moved = lax.all_to_all(moved, "rows", split_axis=0, concat_axis=0, tiled=True)
    moved = jnp.swapaxes(moved, 0, 1)
    new_rows = moved[:steps].reshape(count, half_model)
    query_rows = moved[steps:].reshape(count, -1)

    hidden = jnp.concatenate(
        [passages, new_rows, jnp.zeros((padded - tokens - count, half_model), passages.dtype)], 0
    )
    hidden = lax.all_gather(hidden, "tensor", axis=1, tiled=True)

    position, key_info, query_info = token_tables(
        lengths, destinations, row_index, tokens, requests, steps, padded
    )
    cosine, sine = angle_tables(position)
    projected = jnp.dot(hidden, weight, preferred_element_type=jnp.float32)
    attended = finish(projected, cosine, sine, key_info, query_info, query_rows)
    attended = jnp.swapaxes(attended.reshape(steps, requests, -1), 0, 1)
    return lax.all_to_all(attended, "rows", split_axis=0, concat_axis=0, tiled=True)


def solution(mesh):
    placed = (
        P(("groups", "rows"), "tensor"),
        P("rows", None, "tensor"),
        P(("groups", "rows"), None, "tensor"),
        P(("groups", "rows"), None, "tensor"),
        P("groups", None),
        P("groups", None),
    )
    return jax.shard_map(
        body,
        mesh=mesh,
        in_specs=placed,
        out_specs=P(("groups", "rows"), None, "tensor"),
        check_vma=False,
    )
```

time: 391 us -> 332 us (0.85)
  local copies, waits for them, and re-layouts: 52.9 us -> 6.79 us
  waiting for transfers between devices: 280 us -> 262 us
  matrix products: 28.9 us -> 16.7 us
  blocking collectives: 2.27 us -> 11.6 us
    reshape x2 -> x4, local copies, waits for them, and re-layouts: 42.4 us -> 0.97 us  [the longest x1 41.6 us: body(): weight_piece = piece.reshape(count, columns)]
    all_to_all x1, waiting for transfers between devices: 48.4 us -> 14.4 us  [body(): lax.all_to_all(moved, 'rows', split_axis=0, concat_axis=0, tiled=True)]
    all_gather x2, waiting for transfers between devices: 230 us -> 248 us  [the longest x1 231 us: body(): weight = lax.all_gather(weight, 'rows', axis=0, tiled=True)]
    all_to_all x0 -> x1, blocking collectives: none -> 11.6 us  [body(): lax.all_to_all(attended, 'rows', split_axis=0, concat_axis=0, tiled=True)]
    dot_general x3 -> x1, matrix products: 26.5 us -> 16.7 us  [body(): projected = jnp.dot(hidden, weight, preferred_element_type=jnp.float32)]
    concatenate x3 -> x4, other arithmetic: 0.26 us -> 8.26 us  [the longest x1 7.05 us: body(): jnp.concatenate([passages, new_rows, jnp.zeros((padded - tokens - count,...]
    select_n x1 -> x0, other arithmetic: 5.49 us -> none  [body(): jnp.where(inside[:, :, None, None, None], windows, jnp.zeros((), jnp.bflo...]
    gather x1 -> x0, local copies, waits for them, and re-layouts: 4.17 us -> none  [body(): lax.dynamic_slice_in_dim(pairs, start_row, longest, 0)]
  transfers between devices with their start and end apart: 3 -> 3, of which waited for: 2 -> 3; matrix products, arithmetic and copies ran while one was open for 13% -> 2% of each run, Pallas kernels for 0% -> 0%
where the time goes in v1:
time: 332 us
  waiting for transfers between devices  262 us (79%)
  matrix products  16.7 us (5%)
  between operations  13.5 us (4%)
  blocking collectives  11.6 us (3%)
  other arithmetic  10.7 us (3%)
  starting transfers between devices  7.36 us (2%)
  local copies, waits for them, and re-layouts  6.79 us (2%)
    all_gather x1, waiting for transfers between devices, body(): weight = lax.all_gather(weight, 'rows', axis=0, tiled=True)  231 us
    all_gather x1, waiting for transfers between devices, body(): hidden = lax.all_gather(hidden, 'tensor', axis=1, tiled=True)  16.8 us
    dot_general x1, matrix products, body(): projected = jnp.dot(hidden, weight, preferred_element_type=jnp.float32)  16.7 us
    all_to_all x1, waiting for transfers between devices, body(): lax.all_to_all(moved, 'rows', split_axis=0, concat_axis=0, tiled=True)  14.4 us
    all_to_all x1, blocking collectives, body(): lax.all_to_all(attended, 'rows', split_axis=0, concat_axis=0, tiled=True)  11.6 us
    all_to_all x1, starting transfers between devices, body(): lax.all_to_all(moved, 'rows', split_axis=0, concat_axis=0, tiled=True)  7.28 us
    concatenate x1, other arithmetic, body(): jnp.concatenate([passages, new_rows, jnp.zeros((padded - tokens - count,...  7.05 us
  transfers between devices with their start and end apart: 3, of which 3 were waited for; matrix products, arithmetic and copies ran while one was open for 2% of the time, Pallas kernels for 0%

profile of v1, /device:TPU:0, one launch (start us, length us, event | category | flops | bytes accessed | tf_op | source)
XLA Modules:
  0.0 331.8 jit_solution(1694757919125094498)
XLA Ops:
  6.5 1.2 copy.22
  7.8 1.1 copy.21
  8.9 1.1 pad_maximum_fusion
  9.9 7.3 %all-to-all-start = ((bf16[8,6,4096]{2,1,0:T(8,128)(2,1)}), bf16[8,6,4096]{2,1,0:T(8,128)(2,1)S(1)}, u32[]{:S(2)}, u32[]{:S(2)}) async-start(bf16[8,6,4096]{2,1,0:T(8,128)(2,1)} %pad_maximum_fusion), calls=%async_computation | async-start | bytes 1048576 | tf_op jit(solution)/shard_map/all_to_all | solution.py:109
  17.4 14.4 %all-to-all-done = bf16[8,6,4096]{2,1,0:T(8,128)(2,1)S(1)} async-done(((bf16[8,6,4096]{2,1,0:T(8,128)(2,1)}), bf16[8,6,4096]{2,1,0:T(8,128)(2,1)S(1)}, u32[]{:S(2)}, u32[]{:S(2)}) %all-to-all-start) | async-done | bytes 393248 | tf_op jit(solution)/shard_map/all_to_all | solution.py:109
  31.7 0.2 copy.30
  32.0 7.1 %maximum_maximum_fusion = bf16[672,4096]{1,0:T(8,128)(2,1)} fusion(bf16[24,4096]{1,0:T(8,128)(2,1)S(1)} %get-tuple-element.8, bf16[640,4096]{1,0:T(8,128)(2,1)} %param.6, bf16[672]{0:T(1024)(128)(2,1)S(1)} %pad.15.clone), kind=kLoop, calls=%fused_computation | loop fusion | flops 16515072 | bytes 10945856 | tf_op jit(solution)/shard_map/concatenate | solution.py:114
  39.1 1.9 copy.27
  41.1 0.7 fusion.4
  41.8 0.2 reduce-window.4
  42.0 0.7 fusion.2
  42.7 0.1 select_reduce_fusion.2
  42.8 0.1 tile.21
  42.9 0.1 select_reduce_fusion
  43.1 0.1 tile.23
  43.5 0.1 copy.24.rows_ref
  43.6 1.3 multiply_sine_fusion
  44.9 16.8 %all-gather.3.cloned.1.call-done = bf16[672,8192]{1,0:T(8,128)(2,1)} async-done(((bf16[672,4096]{1,0:T(8,128)(2,1)}), bf16[672,8192]{1,0:T(8,128)(2,1)}) %all-gather.3.cloned.1.call-update) | async-done | bytes 11010064 | tf_op jit(solution)/shard_map/all_gather | solution.py:117
  61.7 230.9 %all-gather.5.cloned.1.call-done = bf16[8192,1024]{1,0:T(8,128)(2,1)} async-done(((bf16[1024,1024]{1,0:T(8,128)(2,1)}), bf16[8192,1024]{1,0:T(8,128)(2,1)}) %all-gather.5.cloned.1.call-update) | async-done | bytes 16777232 | tf_op jit(solution)/shard_map/all_gather | solution.py:106
  292.6 16.7 %fusion.5.proj_ref = f32[672,1024]{1,0:T(8,128)S(1)} fusion(bf16[672,8192]{1,0:T(8,128)(2,1)} %all-gather.3.cloned.1.call-done, bf16[8192,1024]{1,0:T(8,128)(2,1)} %all-gather.5.cloned.1.call-done), kind=kOutput, calls=%fused_computation.29 | convolution fusion | flops 11274289152 | bytes 30539776 | tf_op jit(solution)/shard_map/dot_general | solution.py:123
  309.3 3.0 rotate_attend.1
  312.4 0.2 copy.31
  312.6 11.6 %all_to_all.10 = bf16[8,3,4096]{2,1,0:T(4,128)(2,1)S(1)} all-to-all(bf16[8,3,4096]{2,1,0:T(4,128)(2,1)S(1)} %bitcast.32), channel_id=1, replica_groups=mesh['groups'=2,'rows'=8,'tensor'=2] {'rows'}, dimensions={0} | all-to-all | bytes 393216 | tf_op jit(solution)/shard_map/all_to_all | solution.py:126
  324.2 0.8 copy.26
  (29 shorter events, 0.7 us)
Async XLA Ops:
  6.5 32.6 %copy-start = (bf16[1024,2,512]{2,1,0:T(2,128)(2,1)S(1)}, bf16[1024,2,512]{2,1,0:T(2,128)(2,1)}, u32[]{:S(2)}) copy-start(bf16[1024,2,512]{2,1,0:T(2,128)(2,1)} %param.7) | copy-start | bytes 6291460
  9.9 21.8 %all-to-all-start = ((bf16[8,6,4096]{2,1,0:T(8,128)(2,1)}), bf16[8,6,4096]{2,1,0:T(8,128)(2,1)S(1)}, u32[]{:S(2)}, u32[]{:S(2)}) async-start(bf16[8,6,4096]{2,1,0:T(8,128)(2,1)} %pad_maximum_fusion), calls=%async_computation | async-start | bytes 1048576 | tf_op jit(solution)/shard_map/all_to_all | solution.py:109
  17.2 44.4 %all-gather.3.cloned.1.call-start = ((), (), s32[]{:S(2)}) async-start(), calls=%async_computation.2 | async-start | bytes 16515072 | tf_op jit(solution)/shard_map/all_gather | solution.py:117
  39.0 253.6 %all-gather.5.cloned.1.call-start = ((), (), s32[]{:S(2)}) async-start(), calls=%async_computation.3 | async-start | bytes 18874368 | tf_op jit(solution)/shard_map/all_gather | solution.py:106
Sparse Core Ops, SparseCore 0:
  39.2 22.4 all-gather.2
  63.8 228.7 all-gather.4

commit v2 on v1

--- a/solution.py
+++ b/solution.py
@@ -95,6 +95,54 @@
     )(projected, cosine, sine, key_info, query_info, queries)
 
 
+def add_kernel(pieces, has_total, *refs):
+    at_ref, refs = refs[0], refs[1:]
+    hidden, weight = refs[:pieces], refs[pieces : 2 * pieces]
+    total = refs[2 * pieces][...] if has_total else None
+    for columns, piece in zip(hidden, weight):
+        term = jnp.dot(columns[...], piece[...], preferred_element_type=jnp.float32)
+        total = term if total is None else total + term
+    refs[-1][...] = total
+
+
+def add_products(total, hidden, weights, blocks):
+    rows = hidden.shape[0]
+    depth, width = weights[0].shape
+    tile = min(width, 256)
+    pieces = len(weights)
+    out_block = pl.BlockSpec((rows, tile), lambda n, at: (0, n))
+    in_specs = [
+        pl.BlockSpec((rows, depth), functools.partial(lambda p, n, at: (0, at[p]), p))
+        for p in range(pieces)
+    ]
+    in_specs += [pl.BlockSpec((depth, tile), lambda n, at: (0, n))] * pieces
+    operands = [jnp.stack(blocks), *[hidden] * pieces, *weights]
+    if total is not None:
+        in_specs.append(out_block)
+        operands.append(total)
+    return pl.pallas_call(
+        functools.partial(add_kernel, pieces, total is not None),
+        out_shape=jax.ShapeDtypeStruct((rows, width), jnp.float32),
+        grid_spec=pltpu.PrefetchScalarGridSpec(
+            num_scalar_prefetch=1, grid=(width // tile,), in_specs=in_specs, out_specs=out_block
+        ),
+        input_output_aliases={} if total is None else {len(operands) - 1: 0},
+        compiler_params=pltpu.CompilerParams(vmem_limit_bytes=32 << 20),
+        cost_estimate=pl.CostEstimate(
+            flops=2 * rows * depth * width * pieces,
+            bytes_accessed=pieces * 2 * (rows * depth + depth * width) + 8 * rows * width,
+            transcendentals=0,
+        ),
+        name="add_products",
+    )(*operands)
+
+
+def ring_order(row_count):
+    evens = list(range(0, row_count, 2))
+    odds = list(range(1, row_count, 2))
+    return evens + odds[::-1]
+
+
 def body(passages, kv_weight, new_hidden, queries, lengths, destinations):
     tokens = passages.shape[0]
     requests, steps, half_model = new_hidden.shape
@@ -102,8 +150,29 @@
     count = requests * steps
     padded = -(-(tokens + count) // 16) * 16
 
-    weight = kv_weight.reshape(kv_weight.shape[0], -1)
-    weight = lax.all_gather(weight, "rows", axis=0, tiled=True)
+    row_count = lax.axis_size("rows")
+    depth = kv_weight.shape[0]
+    half = depth // 2
+    weight = kv_weight.reshape(depth, -1)
+    order = ring_order(row_count)
+    onward = [(order[i], order[(i + 1) % row_count]) for i in range(row_count)]
+    back = [(b, a) for a, b in onward]
+    place = {row: i for i, row in enumerate(order)}
+    owners = jnp.array(
+        [
+            [
+                [order[(place[r] - k) % row_count] for k in range(row_count)],
+                [order[(place[r] + k) % row_count] for k in range(row_count)],
+            ]
+            for r in range(row_count)
+        ],
+        jnp.int32,
+    )
+    owners = lax.dynamic_index_in_dim(owners, row_index, 0, keepdims=False)
+    pieces = [(weight[:half], weight[half:])]
+    for _ in range(row_count - 1):
+        first, second = pieces[-1]
+        pieces.append((lax.ppermute(first, "rows", onward), lax.ppermute(second, "rows", back)))
 
     moved = jnp.concatenate([new_hidden, queries], 1)
     moved = lax.all_to_all(moved, "rows", split_axis=0, concat_axis=0, tiled=True)
@@ -120,7 +189,10 @@
         lengths, destinations, row_index, tokens, requests, steps, padded
     )
     cosine, sine = angle_tables(position)
-    projected = jnp.dot(hidden, weight, preferred_element_type=jnp.float32)
+    projected = None
+    for k in range(row_count):
+        blocks = [2 * owners[side, k] + side for side in range(2)]
+        projected = add_products(projected, hidden, pieces[k], blocks)
     attended = finish(projected, cosine, sine, key_info, query_info, query_rows)
     attended = jnp.swapaxes(attended.reshape(steps, requests, -1), 0, 1)
     return lax.all_to_all(attended, "rows", split_axis=0, concat_axis=0, tiled=True)

time: 332 us -> 250 us (0.75)
  waiting for transfers between devices: 262 us -> 119 us
  Pallas kernels: 3.04 us -> 35.7 us
  starting transfers between devices: 7.36 us -> 24.6 us
  matrix products: 16.7 us -> 0 us
  local copies, waits for them, and re-layouts: 6.79 us -> 20.5 us
  between operations: 13.5 us -> 23.5 us
  blocking collectives: 11.6 us -> 15 us
    all_gather x1 -> x0, waiting for transfers between devices: 231 us -> none  [body(): weight = lax.all_gather(weight, 'rows', axis=0, tiled=True)]
    ppermute x0 -> x14, waiting for transfers between devices: none -> 104 us  [the longest x7 103 us: body(): lax.ppermute(second, 'rows', back)]
    pallas_call x0 -> x8, Pallas kernels: none -> 32.6 us  [add_products(): pl.pallas_call(functools.partial(add_kernel, pieces, total is not None),...]
    ppermute x0 -> x14, starting transfers between devices: none -> 17.3 us  [the longest x7 16 us: body(): lax.ppermute(second, 'rows', back)]
    all_gather x1, waiting for transfers between devices: 16.8 us -> 0.02 us  [body(): hidden = lax.all_gather(hidden, 'tensor', axis=1, tiled=True)]
    dot_general x1 -> x0, matrix products: 16.7 us -> none  [body(): projected = jnp.dot(hidden, weight, preferred_element_type=jnp.float32)]
    unnamed x5 -> x30, local copies, waits for them, and re-layouts: 4.23 us -> 14.8 us
    all_to_all x1, blocking collectives: 11.6 us -> 15 us  [body(): lax.all_to_all(attended, 'rows', split_axis=0, concat_axis=0, tiled=True)]
  transfers between devices with their start and end apart: 3 -> 16, of which waited for: 3 -> 10; matrix products, arithmetic and copies ran while one was open for 2% -> 3% of each run, Pallas kernels for 0% -> 11%
where the time goes in v2:
time: 250 us; the launch traced here: 249 us
  waiting for transfers between devices  119 us (48%)
  Pallas kernels  35.7 us (14%)
  starting transfers between devices  24.6 us (10%)
  between operations  23.5 us (9%)
  local copies, waits for them, and re-layouts  20.5 us (8%)
  blocking collectives  15 us (6%)
  other arithmetic  11.3 us (5%)
    ppermute x7, waiting for transfers between devices, body(): lax.ppermute(second, 'rows', back)  103 us
    pallas_call x8, Pallas kernels, add_products(): pl.pallas_call(functools.partial(add_kernel, pieces, total is not None),...  32.6 us
    ppermute x7, starting transfers between devices, body(): lax.ppermute(second, 'rows', back)  16 us
    all_to_all x1, blocking collectives, body(): lax.all_to_all(attended, 'rows', split_axis=0, concat_axis=0, tiled=True)  15 us
    unnamed x30, local copies, waits for them, and re-layouts  14.8 us
    all_to_all x1, waiting for transfers between devices, body(): lax.all_to_all(moved, 'rows', split_axis=0, concat_axis=0, tiled=True)  14.4 us
    all_to_all x1, starting transfers between devices, body(): lax.all_to_all(moved, 'rows', split_axis=0, concat_axis=0, tiled=True)  7.28 us
    concatenate x1, other arithmetic, body(): jnp.concatenate([passages, new_rows, jnp.zeros((padded - tokens - count,...  7.04 us
  transfers between devices with their start and end apart: 16, of which 10 were waited for; matrix products, arithmetic and copies ran while one was open for 3% of the time, Pallas kernels for 11%

profile of v2, /device:TPU:0, one launch (start us, length us, event | category | flops | bytes accessed | tf_op | source)
XLA Modules:
  0.0 249.3 jit_solution(4045892256614726159)
XLA Ops:
  9.8 7.3 %all-to-all-start = ((bf16[8,6,4096]{2,1,0:T(8,128)(2,1)}), bf16[8,6,4096]{2,1,0:T(8,128)(2,1)S(1)}, u32[]{:S(2)}, u32[]{:S(2)}) async-start(bf16[8,6,4096]{2,1,0:T(8,128)(2,1)} %pad_maximum_fusion), calls=%async_computation | async-start | bytes 1048576 | tf_op jit(solution)/shard_map/all_to_all | solution.py:178
  17.2 14.4 %all-to-all-done = bf16[8,6,4096]{2,1,0:T(8,128)(2,1)S(1)} async-done(((bf16[8,6,4096]{2,1,0:T(8,128)(2,1)}), bf16[8,6,4096]{2,1,0:T(8,128)(2,1)S(1)}, u32[]{:S(2)}, u32[]{:S(2)}) %all-to-all-start) | async-done | bytes 393248 | tf_op jit(solution)/shard_map/all_to_all | solution.py:178
  32.0 7.0 %maximum_maximum_fusion = bf16[672,4096]{1,0:T(8,128)(2,1)} fusion(bf16[24,4096]{1,0:T(8,128)(2,1)S(1)} %bitcast.56, bf16[640,4096]{1,0:T(8,128)(2,1)} %param.7, bf16[672]{0:T(1024)(128)(2,1)S(1)} %pad.29.clone), kind=kLoop, calls=%fused_computation | loop fusion | flops 16515072 | bytes 10945856 | tf_op jit(solution)/shard_map/concatenate | solution.py:183
  44.7 21.2 %collective-permute-done.7.refs_4_ = bf16[512,1024]{1,0:T(8,128)(2,1)S(1)} collective-permute-done((bf16[512,1024]{1,0:T(8,128)(2,1)S(1)}, bf16[512,1024]{1,0:T(8,128)(2,1)S(1)}, u32[]{:S(2)}, u32[]{:S(2)}) %collective-permute-start.7) | collective-permute-done | bytes 1048608 | tf_op jit(solution)/shard_map/ppermute | solution.py:175
  69.9 18.9 %collective-permute-done.8.refs_4_ = bf16[512,1024]{1,0:T(8,128)(2,1)S(1)} collective-permute-done((bf16[512,1024]{1,0:T(8,128)(2,1)S(1)}, bf16[512,1024]{1,0:T(8,128)(2,1)S(1)}, u32[]{:S(2)}, u32[]{:S(2)}) %collective-permute-start.8) | collective-permute-done | bytes 1048608 | tf_op jit(solution)/shard_map/ppermute | solution.py:175
  93.3 18.7 %collective-permute-done.9.refs_4_ = bf16[512,1024]{1,0:T(8,128)(2,1)S(1)} collective-permute-done((bf16[512,1024]{1,0:T(8,128)(2,1)S(1)}, bf16[512,1024]{1,0:T(8,128)(2,1)S(1)}, u32[]{:S(2)}, u32[]{:S(2)}) %collective-permute-start.9) | collective-permute-done | bytes 1048608 | tf_op jit(solution)/shard_map/ppermute | solution.py:175
  112.0 2.5 collective-permute-start.10
  116.9 18.1 %collective-permute-done.10.refs_4_ = bf16[512,1024]{1,0:T(8,128)(2,1)} collective-permute-done((bf16[512,1024]{1,0:T(8,128)(2,1)S(1)}, bf16[512,1024]{1,0:T(8,128)(2,1)}, u32[]{:S(2)}, u32[]{:S(2)}) %collective-permute-start.10) | collective-permute-done | bytes 1048608 | tf_op jit(solution)/shard_map/ppermute | solution.py:175
  135.0 2.6 %collective-permute-start.11 = (bf16[512,1024]{1,0:T(8,128)(2,1)}, bf16[512,1024]{1,0:T(8,128)(2,1)}, u32[]{:S(2)}, u32[]{:S(2)}) collective-permute-start(bf16[512,1024]{1,0:T(8,128)(2,1)} %collective-permute-done.10.refs_4_), channel_id=1, source_target_pairs={{4,0},{8,4},{12,8},{14,12},{10,14},{6,10},{2,6},{0,2},{5,1},{9,5},... | collective-permute-start | bytes 3145736 | tf_op jit(solution)/shard_map/ppermute | solution.py:175
  148.0 10.4 %collective-permute-done.11.refs_4_ = bf16[512,1024]{1,0:T(8,128)(2,1)} collective-permute-done((bf16[512,1024]{1,0:T(8,128)(2,1)}, bf16[512,1024]{1,0:T(8,128)(2,1)}, u32[]{:S(2)}, u32[]{:S(2)}) %collective-permute-start.11) | collective-permute-done | bytes 1048608 | tf_op jit(solution)/shard_map/ppermute | solution.py:175
  158.5 2.5 collective-permute-start.12
  166.0 15.8 %collective-permute-done.12.refs_4_ = bf16[512,1024]{1,0:T(8,128)(2,1)} collective-permute-done((bf16[512,1024]{1,0:T(8,128)(2,1)}, bf16[512,1024]{1,0:T(8,128)(2,1)}, u32[]{:S(2)}, u32[]{:S(2)}) %collective-permute-start.12) | collective-permute-done | bytes 1048608 | tf_op jit(solution)/shard_map/ppermute | solution.py:175
  181.8 2.5 collective-permute-start.13
  185.0 4.1 %copy-done = bf16[672,8192]{1,0:T(8,128)(2,1)S(1)} copy-done((bf16[672,8192]{1,0:T(8,128)(2,1)S(1)}, bf16[672,8192]{1,0:T(8,128)(2,1)}, u32[]{:S(2)}) %copy-start) | copy-done | bytes 11010072
  189.1 3.3 %add_products.8.refs_5_ = f32[672,1024]{1,0:T(8,128)S(1)} custom-call(s32[2]{0:T(128)S(1)} %pad_add_fusion.12.refs_0_, bf16[672,8192]{1,0:T(8,128)(2,1)S(1)} %copy-done, bf16[672,8192]{1,0:T(8,128)(2,1)S(1)} %copy-done, bf16[512,1024]{1,0:T(8,128)(2,1)S(1)} %bitcast.49, bf16[512,1024]{1,0:T(8,128)(2,1)S(1)} %bitcast.47), custom_call_target="tpu_custom_call" | custom-call | flops 1409286144 | bytes 8978432 | tf_op jit(solution)/shard_map/add_products/pallas_call | solution.py:123
  193.9 3.5 %add_products.9.refs_5_ = f32[672,1024]{1,0:T(8,128)S(1)} custom-call(s32[2]{0:T(128)S(1)} %pad_add_fusion.11.refs_0_, bf16[672,8192]{1,0:T(8,128)(2,1)S(1)} %copy-done.1, bf16[672,8192]{1,0:T(8,128)(2,1)S(1)} %copy-done.1, bf16[512,1024]{1,0:T(8,128)(2,1)S(1)} %copy-done.5, bf16[512,1024]{1,0:T(8,128)(2,1)S(1)} %copy-done.3, ...), custom_call_target="tpu_custom_call", output_to_operand_aliasing={{}: (5, {})} | custom-call | flops 1409286144 | bytes 8978432 | tf_op jit(solution)/shard_map/add_products/pallas_call | solution.py:123
  197.5 3.5 %add_products.10.refs_5_ = f32[672,1024]{1,0:T(8,128)S(1)} custom-call(s32[2]{0:T(128)S(1)} %pad_add_fusion.10.refs_0_, bf16[672,8192]{1,0:T(8,128)(2,1)S(1)} %copy-done.1, bf16[672,8192]{1,0:T(8,128)(2,1)S(1)} %copy-done.1, bf16[512,1024]{1,0:T(8,128)(2,1)S(1)} %copy-done.9, bf16[512,1024]{1,0:T(8,128)(2,1)S(1)} %copy-done.7, ...), custom_call_target="tpu_custom_call", output_to_operand_aliasing={{}: (5, {})} | custom-call | flops 1409286144 | bytes 8978432 | tf_op jit(solution)/shard_map/add_products/pallas_call | solution.py:123
  201.0 4.3 %add_products.11.refs_5_ = f32[672,1024]{1,0:T(8,128)S(1)} custom-call(s32[2]{0:T(128)S(1)} %pad_add_fusion.9.refs_0_, bf16[672,8192]{1,0:T(8,128)(2,1)S(1)} %copy-done.1, bf16[672,8192]{1,0:T(8,128)(2,1)S(1)} %copy-done.1, bf16[512,1024]{1,0:T(8,128)(2,1)} %collective-permute-done.2.refs_3_, ...), custom_call_target="tpu_custom_call", output_to_operand_aliasing={{}: (5, {})} | custom-call | flops 1409286144 | bytes 8978432 | tf_op jit(solution)/shard_map/add_products/pallas_call | solution.py:123
  205.4 4.5 %add_products.12.refs_5_ = f32[672,1024]{1,0:T(8,128)S(1)} custom-call(s32[2]{0:T(128)S(1)} %pad_add_fusion.8.refs_0_, bf16[672,8192]{1,0:T(8,128)(2,1)S(1)} %copy-done.1, bf16[672,8192]{1,0:T(8,128)(2,1)S(1)} %copy-done.1, bf16[512,1024]{1,0:T(8,128)(2,1)} %collective-permute-done.3.refs_3_, ...), custom_call_target="tpu_custom_call", output_to_operand_aliasing={{}: (5, {})} | custom-call | flops 1409286144 | bytes 8978432 | tf_op jit(solution)/shard_map/add_products/pallas_call | solution.py:123
  209.8 4.5 %add_products.13.refs_5_ = f32[672,1024]{1,0:T(8,128)S(1)} custom-call(s32[2]{0:T(128)S(1)} %pad_add_fusion.7.refs_0_, bf16[672,8192]{1,0:T(8,128)(2,1)S(1)} %copy-done.1, bf16[672,8192]{1,0:T(8,128)(2,1)S(1)} %copy-done.1, bf16[512,1024]{1,0:T(8,128)(2,1)} %collective-permute-done.4.refs_3_, ...), custom_call_target="tpu_custom_call", output_to_operand_aliasing={{}: (5, {})} | custom-call | flops 1409286144 | bytes 8978432 | tf_op jit(solution)/shard_map/add_products/pallas_call | solution.py:123
  214.3 4.5 %add_products.14.refs_5_ = f32[672,1024]{1,0:T(8,128)S(1)} custom-call(s32[2]{0:T(128)S(1)} %pad_add_fusion.6.refs_0_, bf16[672,8192]{1,0:T(8,128)(2,1)S(1)} %copy-done.1, bf16[672,8192]{1,0:T(8,128)(2,1)S(1)} %copy-done.1, bf16[512,1024]{1,0:T(8,128)(2,1)} %collective-permute-done.5.refs_3_, ...), custom_call_target="tpu_custom_call", output_to_operand_aliasing={{}: (5, {})} | custom-call | flops 1409286144 | bytes 8978432 | tf_op jit(solution)/shard_map/add_products/pallas_call | solution.py:123
  218.9 4.5 %add_products.15.proj_ref = f32[672,1024]{1,0:T(8,128)S(1)} custom-call(s32[2]{0:T(128)S(1)} %pad_add_fusion.5.refs_0_, bf16[672,8192]{1,0:T(8,128)(2,1)S(1)} %copy-done.1, bf16[672,8192]{1,0:T(8,128)(2,1)S(1)} %copy-done.1, bf16[512,1024]{1,0:T(8,128)(2,1)} %collective-permute-done.6.refs_3_, ...), custom_call_target="tpu_custom_call", output_to_operand_aliasing={{}: (5, {})} | custom-call | flops 1409286144 | bytes 8978432 | tf_op jit(solution)/shard_map/add_products/pallas_call | solution.py:123
  223.3 3.1 %rotate_attend.1 = bf16[24,4096]{1,0:T(8,128)(2,1)S(1)} custom-call(f32[672,1024]{1,0:T(8,128)S(1)} %add_products.15.proj_ref, f32[672,64]{1,0:T(8,128)S(1)} %get-tuple-element.12.cos_ref, f32[672,64]{1,0:T(8,128)S(1)} %get-tuple-element.11.sin_ref, s32[2,672]{1,0:T(2,128)S(1)} %pad_add_fusion.keys_ref, s32[24,2]{1,0:T(8,128)S(1)} %copy.28.rows_ref, ...), custom_call_target="tpu_custom_call" | custom-call | flops 264241152 | bytes 3145728 | tf_op jit(solution)/shard_map/rotate_attend/pallas_call | solution.py:83
  226.6 15.0 %all_to_all.10 = bf16[8,3,4096]{2,1,0:T(4,128)(2,1)S(1)} all-to-all(bf16[8,3,4096]{2,1,0:T(4,128)(2,1)S(1)} %bitcast.55), channel_id=1, replica_groups=mesh['groups'=2,'rows'=8,'tensor'=2] {'rows'}, dimensions={0} | all-to-all | bytes 393216 | tf_op jit(solution)/shard_map/all_to_all | solution.py:198
  (98 shorter events, 29.0 us)
Async XLA Ops:
  9.8 21.8 %all-to-all-start = ((bf16[8,6,4096]{2,1,0:T(8,128)(2,1)}), bf16[8,6,4096]{2,1,0:T(8,128)(2,1)S(1)}, u32[]{:S(2)}, u32[]{:S(2)}) async-start(bf16[8,6,4096]{2,1,0:T(8,128)(2,1)} %pad_maximum_fusion), calls=%async_computation | async-start | bytes 1048576 | tf_op jit(solution)/shard_map/all_to_all | solution.py:178
  17.1 167.9 %all-gather.2.cloned.1.call-start = ((), (), s32[]{:S(2)}) async-start(), calls=%async_computation.2 | async-start | bytes 16515072 | tf_op jit(solution)/shard_map/all_gather | solution.py:186
  39.0 1.6 copy-start.12
  42.3 23.6 %collective-permute-start.7 = (bf16[512,1024]{1,0:T(8,128)(2,1)S(1)}, bf16[512,1024]{1,0:T(8,128)(2,1)S(1)}, u32[]{:S(2)}, u32[]{:S(2)}) collective-permute-start(bf16[512,1024]{1,0:T(8,128)(2,1)S(1)} %bitcast.46), channel_id=1, source_target_pairs={{4,0},{8,4},{12,8},{14,12},{10,14},{6,10},{2,6},{0,2},{5,1},{9,5},... | collective-permute-start | bytes 3145736 | tf_op jit(solution)/shard_map/ppermute | solution.py:175
  44.1 24.9 %collective-permute-start = (bf16[512,1024]{1,0:T(8,128)(2,1)S(1)}, bf16[512,1024]{1,0:T(8,128)(2,1)S(1)}, u32[]{:S(2)}, u32[]{:S(2)}) collective-permute-start(bf16[512,1024]{1,0:T(8,128)(2,1)S(1)} %bitcast.48), channel_id=1, source_target_pairs={{0,4},{4,8},{8,12},{12,14},{14,10},{10,6},{6,2},{2,0},{1,5},{5,9},... | collective-permute-start | bytes 3145736 | tf_op jit(solution)/shard_map/ppermute | solution.py:175
  65.9 22.9 %collective-permute-start.8 = (bf16[512,1024]{1,0:T(8,128)(2,1)S(1)}, bf16[512,1024]{1,0:T(8,128)(2,1)S(1)}, u32[]{:S(2)}, u32[]{:S(2)}) collective-permute-start(bf16[512,1024]{1,0:T(8,128)(2,1)S(1)} %collective-permute-done.7.refs_4_), channel_id=1, source_target_pairs={{4,0},{8,4},{12,8},{14,12},{10,14},{6,10},{2,6},{0,2},{5,1},{9,5},... | collective-permute-start | bytes 3145736 | tf_op jit(solution)/shard_map/ppermute | solution.py:175
  69.0 23.3 %collective-permute-start.1 = (bf16[512,1024]{1,0:T(8,128)(2,1)S(1)}, bf16[512,1024]{1,0:T(8,128)(2,1)S(1)}, u32[]{:S(2)}, u32[]{:S(2)}) collective-permute-start(bf16[512,1024]{1,0:T(8,128)(2,1)S(1)} %collective-permute-done.refs_3_), channel_id=1, source_target_pairs={{0,4},{4,8},{8,12},{12,14},{14,10},{10,6},{6,2},{2,0},{1,5},{5,9},... | collective-permute-start | bytes 3145736 | tf_op jit(solution)/shard_map/ppermute | solution.py:175
  88.8 23.2 %collective-permute-start.9 = (bf16[512,1024]{1,0:T(8,128)(2,1)S(1)}, bf16[512,1024]{1,0:T(8,128)(2,1)S(1)}, u32[]{:S(2)}, u32[]{:S(2)}) collective-permute-start(bf16[512,1024]{1,0:T(8,128)(2,1)S(1)} %collective-permute-done.8.refs_4_), channel_id=1, source_target_pairs={{4,0},{8,4},{12,8},{14,12},{10,14},{6,10},{2,6},{0,2},{5,1},{9,5},... | collective-permute-start | bytes 3145736 | tf_op jit(solution)/shard_map/ppermute | solution.py:175
  92.3 23.2 %collective-permute-start.2 = (bf16[512,1024]{1,0:T(8,128)(2,1)S(1)}, bf16[512,1024]{1,0:T(8,128)(2,1)}, u32[]{:S(2)}, u32[]{:S(2)}) collective-permute-start(bf16[512,1024]{1,0:T(8,128)(2,1)S(1)} %collective-permute-done.1.refs_3_), channel_id=1, source_target_pairs={{0,4},{4,8},{8,12},{12,14},{14,10},{10,6},{6,2},{2,0},{1,5},{5,9},... | collective-permute-start | bytes 3145736 | tf_op jit(solution)/shard_map/ppermute | solution.py:175
  112.0 23.0 %collective-permute-start.10 = (bf16[512,1024]{1,0:T(8,128)(2,1)S(1)}, bf16[512,1024]{1,0:T(8,128)(2,1)}, u32[]{:S(2)}, u32[]{:S(2)}) collective-permute-start(bf16[512,1024]{1,0:T(8,128)(2,1)S(1)} %collective-permute-done.9.refs_4_), channel_id=1, source_target_pairs={{4,0},{8,4},{12,8},{14,12},{10,14},{6,10},{2,6},{0,2},{5,1},{9,5},... | collective-permute-start | bytes 3145736 | tf_op jit(solution)/shard_map/ppermute | solution.py:175
  115.5 22.5 %collective-permute-start.3 = (bf16[512,1024]{1,0:T(8,128)(2,1)}, bf16[512,1024]{1,0:T(8,128)(2,1)}, u32[]{:S(2)}, u32[]{:S(2)}) collective-permute-start(bf16[512,1024]{1,0:T(8,128)(2,1)} %collective-permute-done.2.refs_3_), channel_id=1, source_target_pairs={{0,4},{4,8},{8,12},{12,14},{14,10},{10,6},{6,2},{2,0},{1,5},{5,9},... | collective-permute-start | bytes 3145736 | tf_op jit(solution)/shard_map/ppermute | solution.py:175
  135.0 23.4 %collective-permute-start.11 = (bf16[512,1024]{1,0:T(8,128)(2,1)}, bf16[512,1024]{1,0:T(8,128)(2,1)}, u32[]{:S(2)}, u32[]{:S(2)}) collective-permute-start(bf16[512,1024]{1,0:T(8,128)(2,1)} %collective-permute-done.10.refs_4_), channel_id=1, source_target_pairs={{4,0},{8,4},{12,8},{14,12},{10,14},{6,10},{2,6},{0,2},{5,1},{9,5},... | collective-permute-start | bytes 3145736 | tf_op jit(solution)/shard_map/ppermute | solution.py:175
  138.0 23.3 %collective-permute-start.4 = (bf16[512,1024]{1,0:T(8,128)(2,1)}, bf16[512,1024]{1,0:T(8,128)(2,1)}, u32[]{:S(2)}, u32[]{:S(2)}) collective-permute-start(bf16[512,1024]{1,0:T(8,128)(2,1)} %collective-permute-done.3.refs_3_), channel_id=1, source_target_pairs={{0,4},{4,8},{8,12},{12,14},{14,10},{10,6},{6,2},{2,0},{1,5},{5,9},... | collective-permute-start | bytes 3145736 | tf_op jit(solution)/shard_map/ppermute | solution.py:175
  158.5 23.3 %collective-permute-start.12 = (bf16[512,1024]{1,0:T(8,128)(2,1)}, bf16[512,1024]{1,0:T(8,128)(2,1)}, u32[]{:S(2)}, u32[]{:S(2)}) collective-permute-start(bf16[512,1024]{1,0:T(8,128)(2,1)} %collective-permute-done.11.refs_4_), channel_id=1, source_target_pairs={{4,0},{8,4},{12,8},{14,12},{10,14},{6,10},{2,6},{0,2},{5,1},{9,5},... | collective-permute-start | bytes 3145736 | tf_op jit(solution)/shard_map/ppermute | solution.py:175
  161.3 23.3 %collective-permute-start.5 = (bf16[512,1024]{1,0:T(8,128)(2,1)}, bf16[512,1024]{1,0:T(8,128)(2,1)}, u32[]{:S(2)}, u32[]{:S(2)}) collective-permute-start(bf16[512,1024]{1,0:T(8,128)(2,1)} %collective-permute-done.4.refs_3_), channel_id=1, source_target_pairs={{0,4},{4,8},{8,12},{12,14},{14,10},{10,6},{6,2},{2,0},{1,5},{5,9},... | collective-permute-start | bytes 3145736 | tf_op jit(solution)/shard_map/ppermute | solution.py:175
  181.8 37.0 %collective-permute-start.13 = (bf16[512,1024]{1,0:T(8,128)(2,1)}, bf16[512,1024]{1,0:T(8,128)(2,1)}, u32[]{:S(2)}, u32[]{:S(2)}) collective-permute-start(bf16[512,1024]{1,0:T(8,128)(2,1)} %collective-permute-done.12.refs_4_), channel_id=1, source_target_pairs={{4,0},{8,4},{12,8},{14,12},{10,14},{6,10},{2,6},{0,2},{5,1},{9,5},... | collective-permute-start | bytes 3145736 | tf_op jit(solution)/shard_map/ppermute | solution.py:175
  184.6 34.2 %collective-permute-start.6 = (bf16[512,1024]{1,0:T(8,128)(2,1)}, bf16[512,1024]{1,0:T(8,128)(2,1)}, u32[]{:S(2)}, u32[]{:S(2)}) collective-permute-start(bf16[512,1024]{1,0:T(8,128)(2,1)} %collective-permute-done.5.refs_3_), channel_id=1, source_target_pairs={{0,4},{4,8},{8,12},{12,14},{14,10},{10,6},{6,2},{2,0},{1,5},{5,9},... | collective-permute-start | bytes 3145736 | tf_op jit(solution)/shard_map/ppermute | solution.py:175
  185.0 4.1 %copy-start = (bf16[672,8192]{1,0:T(8,128)(2,1)S(1)}, bf16[672,8192]{1,0:T(8,128)(2,1)}, u32[]{:S(2)}) copy-start(bf16[672,8192]{1,0:T(8,128)(2,1)} %all-gather.2.cloned.1.call-done.refs_1_.refs_2_) | copy-start | bytes 33030148
  189.1 4.1 %copy-start.1 = (bf16[672,8192]{1,0:T(8,128)(2,1)S(1)}, bf16[672,8192]{1,0:T(8,128)(2,1)}, u32[]{:S(2)}) copy-start(bf16[672,8192]{1,0:T(8,128)(2,1)} %all-gather.2.cloned.1.call-done.refs_1_.refs_2_) | copy-start | bytes 33030148
  189.1 4.4 %copy-start.3 = (bf16[512,1024]{1,0:T(8,128)(2,1)S(1)}, bf16[512,1024]{1,0:T(8,128)(2,1)}, u32[]{:S(2)}) copy-start(bf16[512,1024]{1,0:T(8,128)(2,1)} %copy-done.2) | copy-start | bytes 3145732
  189.1 4.8 %copy-start.5 = (bf16[512,1024]{1,0:T(8,128)(2,1)S(1)}, bf16[512,1024]{1,0:T(8,128)(2,1)}, u32[]{:S(2)}) copy-start(bf16[512,1024]{1,0:T(8,128)(2,1)} %copy-done.4) | copy-start | bytes 3145732
  193.9 3.5 %copy-start.7 = (bf16[512,1024]{1,0:T(8,128)(2,1)S(1)}, bf16[512,1024]{1,0:T(8,128)(2,1)}, u32[]{:S(2)}) copy-start(bf16[512,1024]{1,0:T(8,128)(2,1)} %copy-done.6) | copy-start | bytes 3145732
  193.9 3.5 %copy-start.9 = (bf16[512,1024]{1,0:T(8,128)(2,1)S(1)}, bf16[512,1024]{1,0:T(8,128)(2,1)}, u32[]{:S(2)}) copy-start(bf16[512,1024]{1,0:T(8,128)(2,1)} %copy-done.8) | copy-start | bytes 3145732
  197.5 3.5 %copy-start.11 = (bf16[512,1024]{1,0:T(8,128)(2,1)S(1)}, bf16[512,1024]{1,0:T(8,128)(2,1)}, u32[]{:S(2)}) copy-start(bf16[512,1024]{1,0:T(8,128)(2,1)} %copy-done.10) | copy-start | bytes 3145732
  (5 other events, 5.0 us)
Sparse Core Ops, SparseCore 0:
  39.2 22.4 all-gather.1

commit v3 on v1

--- a/solution.py
+++ b/solution.py
@@ -10,6 +10,11 @@
 
 HD = 128
 HALF = HD // 2
+CHUNKS = 2
+LAG = 3
+MOST_SHARDS = 8
+MERGED = 4
+RAISE = 16.0
 
 
 def angle_tables(positions):
@@ -42,7 +47,7 @@
     return position, jnp.stack([target, seen_from], 0), query_info
 
 
-def finish_kernel(heads, group, proj_ref, cos_ref, sin_ref, keys_ref, rows_ref, query_ref, out_ref):
+def finish_kernel(heads, group, held_ref, back_ref, cos_ref, sin_ref, keys_ref, rows_ref, query_ref, out_ref):
     cosine, sine = cos_ref[...], sin_ref[...]
     allowed = (keys_ref[0:1, :] == rows_ref[:, 0:1]) & (keys_ref[1:2, :] <= rows_ref[:, 1:2])
     allowed = jnp.concatenate([allowed.astype(jnp.float32)] * group, 0) > 0.5
@@ -50,12 +55,14 @@
     count = queries.shape[0]
     width = heads * HD
     for h in range(heads):
-        first = proj_ref[:, h * HD : h * HD + HALF]
-        second = proj_ref[:, h * HD + HALF : (h + 1) * HD]
+        key_at, value_at = slice(h * HD, (h + 1) * HD), slice(width + h * HD, width + (h + 1) * HD)
+        both = held_ref[:, key_at] + back_ref[:, key_at]
+        first, second = both[:, :HALF], both[:, HALF:]
         keys = jnp.concatenate(
             [first * cosine - second * sine, second * cosine + first * sine], -1
         ).astype(jnp.bfloat16)
-        values = proj_ref[:, width + h * HD : width + (h + 1) * HD].astype(jnp.bfloat16)
+        values = held_ref[:, value_at] + back_ref[:, value_at]
+        values = values.astype(jnp.bfloat16)
         at = h * group * HD
         query = jnp.concatenate(
             [queries[:, at + g * HD : at + (g + 1) * HD] for g in range(group)], 0
@@ -74,7 +81,7 @@
             ].astype(jnp.bfloat16)
 
 
-def finish(projected, cosine, sine, key_info, query_info, queries):
+def finish(projected, back, cosine, sine, key_info, query_info, queries):
     rows, width = projected.shape
     heads = width // (2 * HD)
     group = queries.shape[1] // (heads * HD)
@@ -83,45 +90,244 @@
     return pl.pallas_call(
         functools.partial(finish_kernel, heads, group),
         out_shape=jax.ShapeDtypeStruct(queries.shape, jnp.bfloat16),
-        in_specs=[whole] * 6,
+        in_specs=[whole] * 7,
         out_specs=whole,
         compiler_params=pltpu.CompilerParams(vmem_limit_bytes=48 << 20),
         cost_estimate=pl.CostEstimate(
             flops=4 * heads * group * count * rows * HD,
-            bytes_accessed=projected.size * 4 + 4 * queries.size,
+            bytes_accessed=projected.size * 8 + 4 * queries.size,
             transcendentals=heads * group * count * rows,
         ),
         name="rotate_attend",
-    )(projected, cosine, sine, key_info, query_info, queries)
+    )(projected, back, cosine, sine, key_info, query_info, queries)
+
+
+def pick_kernel(side_ref, source_ref, out_ref):
+    out_ref[...] = source_ref[...]
+
+
+def pick_columns(source, side, half, first, count):
+    rows = source.shape[0]
+    return pl.pallas_call(
+        pick_kernel,
+        out_shape=jax.ShapeDtypeStruct((rows, count * half), source.dtype),
+        grid_spec=pltpu.PrefetchScalarGridSpec(
+            num_scalar_prefetch=1,
+            grid=(count,),
+            in_specs=[pl.BlockSpec((rows, half), lambda j, s: (0, 2 * (first + j) + s[0]))],
+            out_specs=pl.BlockSpec((rows, half), lambda j, s: (0, j)),
+        ),
+        compiler_params=pltpu.CompilerParams(vmem_limit_bytes=24 << 20),
+        cost_estimate=pl.CostEstimate(
+            flops=0, bytes_accessed=4 * rows * count * half, transcendentals=0
+        ),
+        name="pick_columns",
+    )(side.reshape(1), source)
+
+
+def product_kernel(shards, split, layout, has_total, *refs):
+    place_ref, refs = refs[0], refs[1:]
+    hidden, refs = refs[: len(layout)], refs[len(layout) :]
+    weights, refs = refs[: shards * split], refs[shards * split :]
+    out_ref, held, sems = refs[-3:]
+    half = held.shape[1] // shards
+    spans = sorted({(part, at, rows) for part, at, rows, _, _, _ in layout})
+    for p in range(shards):
+        for (part, at, rows, row, first, blocks), source in zip(layout, hidden):
+            block = place_ref[p] - first
+
+            @pl.when((block >= 0) & (block < blocks))
+            def _():
+                columns = pl.ds(pl.multiple_of(block * half, half), half)
+                pltpu.make_async_copy(
+                    source.at[row : row + rows, columns],
+                    held.at[at : at + rows, p * half : (p + 1) * half],
+                    sems.at[p, part],
+                ).start()
+
+    total = refs[0][...] if has_total else None
+    for begin in range(0, shards, MERGED):
+        end = min(begin + MERGED, shards)
+        for p in range(begin, end):
+            for part, at, rows in spans:
+                target = held.at[at : at + rows, p * half : (p + 1) * half]
+                pltpu.make_async_copy(target, target, sems.at[p, part]).wait()
+        piece = jnp.concatenate([w[...] for w in weights[begin * split : end * split]], 0)
+        term = jnp.dot(
+            held[:, begin * half : end * half], piece, preferred_element_type=jnp.float32
+        )
+        total = term if total is None else total + term
+    out_ref[...] = total
+
+
+def products(total, hidden, weights, places, half):
+    split, shards = len(weights[0]), len(weights)
+    width = weights[0][0].shape[1]
+    operands, layout, at = [places], [], 0
+    for part, (row, rows, pieces) in enumerate(hidden):
+        first = 0
+        for piece in pieces:
+            operands.append(piece)
+            layout.append((part, at, rows, row, first, piece.shape[1] // half))
+            first += piece.shape[1] // half
+        at += rows
+    flat = [w for shard in weights for w in shard]
+    operands += flat
+    vmem = pl.BlockSpec(memory_space=pltpu.VMEM)
+    in_specs = [pl.BlockSpec(memory_space=pltpu.SMEM)]
+    in_specs += [pl.BlockSpec(memory_space=pl.ANY)] * len(layout) + [vmem] * len(flat)
+    if total is not None:
+        operands.append(total)
+        in_specs.append(vmem)
+    return pl.pallas_call(
+        functools.partial(product_kernel, shards, split, tuple(layout), total is not None),
+        out_shape=jax.ShapeDtypeStruct((at, width), jnp.float32),
+        in_specs=in_specs,
+        out_specs=vmem,
+        scratch_shapes=[
+            pltpu.VMEM((at, shards * half), jnp.bfloat16),
+            pltpu.SemaphoreType.DMA((shards, len(hidden))),
+        ],
+        compiler_params=pltpu.CompilerParams(vmem_limit_bytes=40 << 20),
+        cost_estimate=pl.CostEstimate(
+            flops=2 * at * half * width * shards,
+            bytes_accessed=shards * 2 * half * (at + width) + 4 * at * width,
+            transcendentals=0,
+        ),
+        name="products",
+    )(*operands)
+
+
+def ring_order(row_count):
+    evens = list(range(0, row_count, 2))
+    odds = list(range(1, row_count, 2))
+    return evens + odds[::-1]
+
+
+def after(value, other):
+    return lax.optimization_barrier((value, other))[0]
 
 
 def body(passages, kv_weight, new_hidden, queries, lengths, destinations):
     tokens = passages.shape[0]
     requests, steps, half_model = new_hidden.shape
+    row_count = lax.axis_size("rows")
+    group_count = lax.axis_size("groups")
     row_index = lax.axis_index("rows")
+    side = lax.axis_index("groups") % 2
+    core = lax.axis_index("tensor")
+    depth = kv_weight.shape[0]
+    half = depth // 2
+    local_heads = kv_weight.shape[2] // HD
+    group = queries.shape[2] // kv_weight.shape[2]
     count = requests * steps
-    padded = -(-(tokens + count) // 16) * 16
-
-    weight = kv_weight.reshape(kv_weight.shape[0], -1)
-    weight = lax.all_gather(weight, "rows", axis=0, tiled=True)
-
-    moved = jnp.concatenate([new_hidden, queries], 1)
-    moved = lax.all_to_all(moved, "rows", split_axis=0, concat_axis=0, tiled=True)
-    moved = jnp.swapaxes(moved, 0, 1)
-    new_rows = moved[:steps].reshape(count, half_model)
-    query_rows = moved[steps:].reshape(count, -1)
-
-    hidden = jnp.concatenate(
-        [passages, new_rows, jnp.zeros((padded - tokens - count, half_model), passages.dtype)], 0
-    )
-    hidden = lax.all_gather(hidden, "tensor", axis=1, tiled=True)
+    new_padded = -(-count // 16) * 16
+    half_rows = row_count // 2
+
+    partners = [(g, g ^ 1) for g in range(group_count)]
+    cores = [(0, 1), (1, 0)]
+    order = ring_order(row_count)
+    onward = [(order[i], order[(i + 1) % row_count]) for i in range(row_count)]
+    back = [(b, a) for a, b in onward]
+    place = {row: i for i, row in enumerate(order)}
+    shard_order = [
+        [order[(place[r] + d) % row_count] for r in range(row_count)]
+        for k in range(half_rows + 1)
+        for d in ([0] if k == 0 else [-k, k] if k < half_rows else [k])
+    ]
+    owners = lax.dynamic_index_in_dim(jnp.array(shard_order, jnp.int32), row_index, 1, keepdims=False)
+    places = ((owners // half_rows) ^ core) * half_rows + owners % half_rows
+
+    chunks = CHUNKS
+    chunk_heads = local_heads // chunks
+    chunk = chunk_heads * HD
+    mine = lax.dynamic_slice_in_dim(kv_weight, side * half, half, 0)
+    own = [
+        mine[:, :, c * chunk : (c + 1) * chunk].reshape(half, 2 * chunk) for c in range(chunks)
+    ]
+
+    sent = [pick_columns(passages, 1 - side, half, at, half_rows // 2) for at in (0, half_rows // 2)]
+    got = [lax.ppermute(sent[0], "groups", partners)]
+
+    right, left = [[] for _ in range(chunks)], [[] for _ in range(chunks)]
+
+    def ring_step(c):
+        k = len(right[c])
+        r, l = (own[c], own[c]) if k == 0 else (right[c][-1], left[c][-1])
+        if k == half_rows - 1:
+            r, l = r[: half // 2], l[half // 2 :]
+        if k == 0 and c == 0:
+            r, l = after((r, l), sent[0])
+        if k == 0 and c > 0:
+            r, l = after((r, l), (right[c - 1][LAG - 1], left[c - 1][LAG - 1]))
+        if k == 2 and c == 0:
+            r, l = after((r, l), got[0])
+        if k == 1 and c == 1:
+            r, l = after((r, l), got[1])
+        right[c].append(lax.ppermute(r, "rows", onward))
+        left[c].append(lax.ppermute(l, "rows", back))
+        if k == 1 and c == 0:
+            got.append(lax.ppermute(after(sent[1], arrived((0, 1))), "groups", partners))
+
+    def arrived(*steps_done):
+        return [side_of[c][k] for c, k in steps_done for side_of in (right, left)]
+
+    for c in range(chunks):
+        for k in range(half_rows):
+            ring_step(c)
+
+    kept = pick_columns(passages, side, half, 0, half_rows)
+    kept_other = lax.ppermute(kept, "tensor", cores)
+    got = [
+        after(got[0], arrived((0, 1))),
+        after(got[1], arrived((0, half_rows - 1), (1, 0))),
+    ]
+    got_other = [lax.ppermute(piece, "tensor", cores) for piece in got]
+
+    def to_replica(held, start, end):
+        moved = lax.all_to_all(after(held, start), "rows", split_axis=0, concat_axis=0, tiled=True)
+        return jnp.swapaxes(after(moved, end), 0, 1).reshape(count, -1)
+
+    new_rows = to_replica(new_hidden, (kept, sent), arrived((0, 1)))
+    new_rows = jnp.pad(new_rows, ((0, new_padded - count), (0, 0)))
+    new_kept = pick_columns(new_rows, side, half, 0, half_rows)
+    new_sent = pick_columns(new_rows, 1 - side, half, 0, half_rows)
+    new_got = lax.ppermute(new_sent, "groups", partners)
+    new_got = after(new_got, arrived((0, 2)))
+    new_kept = jnp.concatenate([new_kept, new_got], 0)
+    new_other = lax.ppermute(new_kept, "tensor", cores)
+    own_hidden = [(0, tokens, (kept, kept_other)), (0, new_padded, (new_kept, new_other))]
+    away_hidden = [(0, tokens, (*got, *got_other)), (new_padded, new_padded, (new_kept, new_other))]
+    query_rows = to_replica(queries, arrived((1, 1)), arrived((1, half_rows - 1)))
 
     position, key_info, query_info = token_tables(
-        lengths, destinations, row_index, tokens, requests, steps, padded
+        lengths, destinations, row_index, tokens, requests, steps, tokens + new_padded
     )
     cosine, sine = angle_tables(position)
-    projected = jnp.dot(hidden, weight, preferred_element_type=jnp.float32)
-    attended = finish(projected, cosine, sine, key_info, query_info, query_rows)
+
+    def project(c, hidden, ready):
+        weights = [(own[c],)]
+        for k in range(half_rows - 1):
+            weights += [(right[c][k],), (left[c][k],)]
+        shards, total = len(weights), None
+        spots = after(places, ready)
+        for at in range(0, shards, MOST_SHARDS):
+            some = weights[at : at + MOST_SHARDS]
+            total = products(total, hidden, some, spots[at : at + len(some)], half)
+        return products(total, hidden, [(right[c][-1], left[c][-1])], spots[shards:], half)
+
+    away = [project(c, away_hidden, ()) for c in range(chunks)]
+    away = [(total * RAISE).astype(jnp.float16) for total in away]
+    homed = [lax.ppermute(total, "groups", partners) for total in away]
+    homed = [total.astype(jnp.float32) * (1.0 / RAISE) for total in homed]
+
+    outs = []
+    for c in range(chunks):
+        held = project(c, own_hidden, away[c])
+        at = c * chunk * group
+        query = query_rows[:, at : at + chunk * group]
+        outs.append(finish(held, homed[c], cosine, sine, key_info, query_info, query))
+    attended = outs[0] if chunks == 1 else jnp.concatenate(outs, 1)
     attended = jnp.swapaxes(attended.reshape(steps, requests, -1), 0, 1)
     return lax.all_to_all(attended, "rows", split_axis=0, concat_axis=0, tiled=True)
 

time: 332 us -> 192 us (0.58)
  waiting for transfers between devices: 262 us -> 53.7 us
  Pallas kernels: 3.04 us -> 41.4 us
  starting transfers between devices: 7.36 us -> 36.5 us
  local copies, waits for them, and re-layouts: 6.79 us -> 35.4 us
  matrix products: 16.7 us -> 0 us
  between operations: 13.5 us -> 0.58 us
    all_gather x2 -> x0, waiting for transfers between devices: 248 us -> none  [the longest x1 231 us: body(): weight = lax.all_gather(weight, 'rows', axis=0, tiled=True)]
    ppermute x0 -> x25, waiting for transfers between devices: none -> 52.3 us  [the longest x8 35.6 us: ring_step(): right[c].append(lax.ppermute(r, 'rows', onward))]
    pallas_call x0 -> x13, Pallas kernels: none -> 37.9 us  [the longest x8 35.3 us: products(): pl.pallas_call(functools.partial(product_kernel, shards, split, tuple(lay...]
    ppermute x0 -> x25, starting transfers between devices: none -> 25.1 us  [the longest x8 16.4 us: ring_step(): right[c].append(lax.ppermute(r, 'rows', onward))]
    dot_general x1 -> x0, matrix products: 16.7 us -> none  [body(): projected = jnp.dot(hidden, weight, preferred_element_type=jnp.float32)]
    unnamed x5 -> x82, local copies, waits for them, and re-layouts: 4.23 us -> 19.2 us
    all_to_all x1 -> x2, waiting for transfers between devices: 14.4 us -> 1.43 us  [to_replica(): lax.all_to_all(after(held, start), 'rows', split_axis=0, concat_axis=0, t...]
    slice x0 -> x9, local copies, waits for them, and re-layouts: none -> 9.05 us  [the longest x4 5.36 us: ring_step(): r, l = (r[:half // 2], l[half // 2:])]
  transfers between devices with their start and end apart: 3 -> 27, of which waited for: 3 -> 11; matrix products, arithmetic and copies ran while one was open for 2% -> 11% of each run, Pallas kernels for 0% -> 21%
where the time goes in v3:
time: 192 us; the launch traced here: 190 us
  waiting for transfers between devices  53.7 us (28%)
  Pallas kernels  41.4 us (22%)
  starting transfers between devices  36.5 us (19%)
  local copies, waits for them, and re-layouts  35.4 us (18%)
  blocking collectives  13.3 us (7%)
  other arithmetic  9.62 us (5%)
    ppermute x8, waiting for transfers between devices, ring_step(): right[c].append(lax.ppermute(r, 'rows', onward))  35.6 us
    pallas_call x8, Pallas kernels, products(): pl.pallas_call(functools.partial(product_kernel, shards, split, tuple(lay...  35.3 us
    unnamed x82, local copies, waits for them, and re-layouts  19.2 us
    ppermute x8, starting transfers between devices, ring_step(): right[c].append(lax.ppermute(r, 'rows', onward))  16.4 us
    all_to_all x1, blocking collectives, body(): lax.all_to_all(attended, 'rows', split_axis=0, concat_axis=0, tiled=True)  13.3 us
    all_to_all x2, starting transfers between devices, to_replica(): lax.all_to_all(after(held, start), 'rows', split_axis=0, concat_axis=0, t...  11.4 us
    ppermute x8, waiting for transfers between devices, ring_step(): left[c].append(lax.ppermute(l, 'rows', back))  9.64 us
    slice x4, local copies, waits for them, and re-layouts, ring_step(): r, l = (r[:half // 2], l[half // 2:])  5.36 us
  transfers between devices with their start and end apart: 27, of which 11 were waited for; matrix products, arithmetic and copies ran while one was open for 11% of the time, Pallas kernels for 21%

profile of v3, /device:TPU:0, one launch (start us, length us, event | category | flops | bytes accessed | tf_op | source)
XLA Modules:
  0.0 190.4 jit_solution(13666874234190302007)
XLA Ops:
  2.0 2.7 %copy-done = bf16[640,4096]{1,0:T(8,128)(2,1)S(1)} copy-done((bf16[640,4096]{1,0:T(8,128)(2,1)S(1)}, bf16[640,4096]{1,0:T(8,128)(2,1)}, u32[]{:S(2)}) %copy-start) | copy-done | bytes 5242904
  5.1 3.1 %collective-permute-start.1 = (bf16[512,512]{1,0:T(8,128)(2,1)S(1)}, bf16[512,512]{1,0:T(8,128)(2,1)S(1)}, u32[]{:S(2)}, u32[]{:S(2)}) collective-permute-start(bf16[512,512]{1,0:T(8,128)(2,1)S(1)} %bitcast.41), channel_id=1, source_target_pairs={{0,4},{4,8},{8,12},{12,14},{14,10},{10,6},{6,2},{2,0},{1,5},{5,9},... | collective-permute-start | bytes 1572872 | tf_op jit(solution)/shard_map/ppermute | solution.py:267
  10.1 9.9 %collective-permute-done.1.refs_8_.refs_6_ = bf16[512,512]{1,0:T(8,128)(2,1)S(1)} collective-permute-done((bf16[512,512]{1,0:T(8,128)(2,1)S(1)}, bf16[512,512]{1,0:T(8,128)(2,1)S(1)}, u32[]{:S(2)}, u32[]{:S(2)}) %collective-permute-start.1) | collective-permute-done | bytes 524320 | tf_op jit(solution)/shard_map/ppermute | solution.py:267
  23.3 9.8 %collective-permute-done.2.refs_10_.refs_8_ = bf16[512,512]{1,0:T(8,128)(2,1)S(1)} collective-permute-done((bf16[512,512]{1,0:T(8,128)(2,1)S(1)}, bf16[512,512]{1,0:T(8,128)(2,1)S(1)}, u32[]{:S(2)}, u32[]{:S(2)}) %collective-permute-start.2) | collective-permute-done | bytes 524320 | tf_op jit(solution)/shard_map/ppermute | solution.py:267
  35.8 4.0 %collective-permute-done.refs_1_ = bf16[640,1024]{1,0:T(8,128)(2,1)S(1)} collective-permute-done((bf16[640,1024]{1,0:T(8,128)(2,1)S(1)}, bf16[640,1024]{1,0:T(8,128)(2,1)S(1)}, u32[]{:S(2)}, u32[]{:S(2)}) %collective-permute-start) | collective-permute-done | bytes 1310752 | tf_op jit(solution)/shard_map/ppermute | solution.py:250
  43.7 7.2 %collective-permute-done.6.refs_12_.refs_10_ = bf16[512,512]{1,0:T(8,128)(2,1)S(1)} collective-permute-done((bf16[512,512]{1,0:T(8,128)(2,1)S(1)}, bf16[512,512]{1,0:T(8,128)(2,1)S(1)}, u32[]{:S(2)}, u32[]{:S(2)}) %collective-permute-start.6) | collective-permute-done | bytes 524320 | tf_op jit(solution)/shard_map/ppermute | solution.py:267
  50.9 2.5 %collective-permute-done.8.refs_13_.refs_11_ = bf16[512,512]{1,0:T(8,128)(2,1)S(1)} collective-permute-done((bf16[512,512]{1,0:T(8,128)(2,1)S(1)}, bf16[512,512]{1,0:T(8,128)(2,1)S(1)}, u32[]{:S(2)}, u32[]{:S(2)}) %collective-permute-start.8) | collective-permute-done | bytes 524320 | tf_op jit(solution)/shard_map/ppermute | solution.py:268
  57.2 5.9 %all-to-all-start = ((bf16[8,3,4096]{2,1,0:T(4,128)(2,1)}), bf16[8,3,4096]{2,1,0:T(4,128)(2,1)}, u32[]{:S(2)}, u32[]{:S(2)}) async-start(bf16[8,3,4096]{2,1,0:T(4,128)(2,1)} %copy.18), calls=%async_computation | async-start | bytes 524288 | tf_op jit(solution)/shard_map/all_to_all | solution.py:288
  70.5 2.1 %collective-permute-start.18 = (bf16[512,512]{1,0:T(8,128)(2,1)}, bf16[512,512]{1,0:T(8,128)(2,1)S(1)}, u32[]{:S(2)}, u32[]{:S(2)}) collective-permute-start(bf16[512,512]{1,0:T(8,128)(2,1)} %collective-permute-done.10.refs_8_.refs_6_), channel_id=1, source_target_pairs={{0,4},{4,8},{8,12},{12,14},{14,10},{10,6},{6,2},{2,0},{1,5},{5,9},... | collective-permute-start | bytes 1572872 | tf_op jit(solution)/shard_map/ppermute | solution.py:267
  77.5 3.0 %collective-permute-done.14 = bf16[32,2048]{1,0:T(8,128)(2,1)S(1)} collective-permute-done((bf16[32,2048]{1,0:T(8,128)(2,1)S(1)}, bf16[32,2048]{1,0:T(8,128)(2,1)S(1)}, u32[]{:S(2)}, u32[]{:S(2)}) %collective-permute-start.14) | collective-permute-done | bytes 131104 | tf_op jit(solution)/shard_map/ppermute | solution.py:295
  81.6 3.8 %collective-permute-done.18.refs_10_.refs_8_ = bf16[512,512]{1,0:T(8,128)(2,1)S(1)} collective-permute-done((bf16[512,512]{1,0:T(8,128)(2,1)}, bf16[512,512]{1,0:T(8,128)(2,1)S(1)}, u32[]{:S(2)}, u32[]{:S(2)}) %collective-permute-start.18) | collective-permute-done | bytes 524320 | tf_op jit(solution)/shard_map/ppermute | solution.py:267
  87.3 5.9 %collective-permute-done.19.refs_11_.refs_9_ = bf16[512,512]{1,0:T(8,128)(2,1)} collective-permute-done((bf16[512,512]{1,0:T(8,128)(2,1)}, bf16[512,512]{1,0:T(8,128)(2,1)}, u32[]{:S(2)}, u32[]{:S(2)}) %collective-permute-start.19) | collective-permute-done | bytes 524320 | tf_op jit(solution)/shard_map/ppermute | solution.py:268
  94.4 4.9 %collective-permute-done.20.refs_12_.refs_10_ = bf16[512,512]{1,0:T(8,128)(2,1)} collective-permute-done((bf16[512,512]{1,0:T(8,128)(2,1)S(1)}, bf16[512,512]{1,0:T(8,128)(2,1)}, u32[]{:S(2)}, u32[]{:S(2)}) %collective-permute-start.20) | collective-permute-done | bytes 524320 | tf_op jit(solution)/shard_map/ppermute | solution.py:267
  104.5 5.5 %all-to-all-start.1 = ((bf16[8,3,4096]{2,1,0:T(4,128)(2,1)}), bf16[8,3,4096]{2,1,0:T(4,128)(2,1)}, u32[]{:S(2)}, u32[]{:S(2)}) async-start(bf16[8,3,4096]{2,1,0:T(4,128)(2,1)} %copy.20), calls=%async_computation.1 | async-start | bytes 524288 | tf_op jit(solution)/shard_map/all_to_all | solution.py:288
  111.1 2.1 %collective-permute-start.21 = (bf16[256,512]{1,0:T(8,128)(2,1)S(1)}, bf16[256,512]{1,0:T(8,128)(2,1)S(1)}, u32[]{:S(2)}, u32[]{:S(2)}) collective-permute-start(bf16[256,512]{1,0:T(8,128)(2,1)S(1)} %slice.60), channel_id=1, source_target_pairs={{0,4},{4,8},{8,12},{12,14},{14,10},{10,6},{6,2},{2,0},{1,5},{5,9},... | collective-permute-start | bytes 786440 | tf_op jit(solution)/shard_map/ppermute | solution.py:267
  120.8 5.5 %products.8.refs_9_ = f32[672,512]{1,0:T(8,128)S(1)} custom-call(s32[7]{0:T(128)S(1)} %bitcast.49, bf16[640,1024]{1,0:T(8,128)(2,1)S(1)} %copy-done.2, bf16[640,1024]{1,0:T(8,128)(2,1)} %collective-permute-done.5.refs_2_, bf16[640,1024]{1,0:T(8,128)(2,1)} %collective-permute-done.12.refs_3_, bf16[640,1024]{1,0:T(8,128)(2,1)} %collective-permute-done.13.refs_4_, ...), custom_call_target="tpu_custom_call" | custom-call | flops 2466250752 | bytes 9863168 | tf_op jit(solution)/shard_map/products/pallas_call | solution.py:182
  126.3 3.3 %products.9 = f32[672,512]{1,0:T(8,128)S(1)} custom-call(s32[1]{0:T(128)} %slice.44.refs_0_, bf16[640,1024]{1,0:T(8,128)(2,1)S(1)} %copy-done.3, bf16[640,1024]{1,0:T(8,128)(2,1)} %collective-permute-done.5.refs_2_, bf16[640,1024]{1,0:T(8,128)(2,1)} %collective-permute-done.12.refs_3_, bf16[640,1024]{1,0:T(8,128)(2,1)} %collective-permute-done.13.refs_4_, ...), custom_call_target="tpu_custom_call" | custom-call | flops 352321536 | bytes 2588672 | tf_op jit(solution)/shard_map/products/pallas_call | solution.py:182
  132.2 6.6 %products.12.refs_9_ = f32[672,512]{1,0:T(8,128)S(1)} custom-call(s32[7]{0:T(128)S(1)} %bitcast.50, bf16[640,1024]{1,0:T(8,128)(2,1)S(1)} %copy-done.3, bf16[640,1024]{1,0:T(8,128)(2,1)} %collective-permute-done.5.refs_2_, bf16[640,1024]{1,0:T(8,128)(2,1)} %collective-permute-done.12.refs_3_, bf16[640,1024]{1,0:T(8,128)(2,1)} %collective-permute-done.13.refs_4_, ...), custom_call_target="tpu_custom_call" | custom-call | flops 2466250752 | bytes 9863168 | tf_op jit(solution)/shard_map/products/pallas_call | solution.py:182
  138.9 2.3 %products.13 = f32[672,512]{1,0:T(8,128)S(1)} custom-call(s32[1]{0:T(128)} %slice.44.refs_0_, bf16[640,1024]{1,0:T(8,128)(2,1)S(1)} %copy-done.3, bf16[640,1024]{1,0:T(8,128)(2,1)} %collective-permute-done.5.refs_2_, bf16[640,1024]{1,0:T(8,128)(2,1)} %collective-permute-done.12.refs_3_, bf16[640,1024]{1,0:T(8,128)(2,1)} %collective-permute-done.13.refs_4_, ...), custom_call_target="tpu_custom_call" | custom-call | flops 352321536 | bytes 2588672 | tf_op jit(solution)/shard_map/products/pallas_call | solution.py:182
  152.4 5.4 %products.10.refs_7_ = f32[672,512]{1,0:T(8,128)S(1)} custom-call(s32[7]{0:T(128)S(1)} %bitcast.51, bf16[640,2048]{1,0:T(8,128)(2,1)S(1)} %pick_columns.7.refs_1_, bf16[640,2048]{1,0:T(8,128)(2,1)} %collective-permute-done.16.refs_2_, bf16[64,2048]{1,0:T(8,128)(2,1)S(1)} %pad_maximum_fusion.refs_5_.refs_3_, ...), custom_call_target="tpu_custom_call" | custom-call | flops 2466250752 | bytes 9863168 | tf_op jit(solution)/shard_map/products/pallas_call | solution.py:182
  157.7 3.3 %products.11.held_ref = f32[672,512]{1,0:T(8,128)S(1)} custom-call(s32[1]{0:T(128)} %slice.50.refs_0_, bf16[640,2048]{1,0:T(8,128)(2,1)S(1)} %pick_columns.7.refs_1_, bf16[640,2048]{1,0:T(8,128)(2,1)} %collective-permute-done.16.refs_2_, bf16[64,2048]{1,0:T(8,128)(2,1)S(1)} %pad_maximum_fusion.refs_5_.refs_3_, ...), custom_call_target="tpu_custom_call" | custom-call | flops 352321536 | bytes 2588672 | tf_op jit(solution)/shard_map/products/pallas_call | solution.py:182
  161.1 6.6 %products.14.refs_7_ = f32[672,512]{1,0:T(8,128)S(1)} custom-call(s32[7]{0:T(128)S(1)} %bitcast.52, bf16[640,2048]{1,0:T(8,128)(2,1)S(1)} %pick_columns.7.refs_1_, bf16[640,2048]{1,0:T(8,128)(2,1)} %collective-permute-done.16.refs_2_, bf16[64,2048]{1,0:T(8,128)(2,1)S(1)} %pad_maximum_fusion.refs_5_.refs_3_, ...), custom_call_target="tpu_custom_call" | custom-call | flops 2466250752 | bytes 9863168 | tf_op jit(solution)/shard_map/products/pallas_call | solution.py:182
  167.7 2.3 %products.15.held_ref = f32[672,512]{1,0:T(8,128)S(1)} custom-call(s32[1]{0:T(128)} %slice.55.refs_0_, bf16[640,2048]{1,0:T(8,128)(2,1)S(1)} %pick_columns.7.refs_1_, bf16[640,2048]{1,0:T(8,128)(2,1)} %collective-permute-done.16.refs_2_, bf16[64,2048]{1,0:T(8,128)(2,1)S(1)} %pad_maximum_fusion.refs_5_.refs_3_, ...), custom_call_target="tpu_custom_call" | custom-call | flops 352321536 | bytes 2588672 | tf_op jit(solution)/shard_map/products/pallas_call | solution.py:182
  176.3 13.3 %all_to_all.15 = bf16[8,3,4096]{2,1,0:T(4,128)(2,1)S(1)} all-to-all(bf16[8,3,4096]{2,1,0:T(4,128)(2,1)S(1)} %bitcast.55), channel_id=1, replica_groups=mesh['groups'=2,'rows'=8,'tensor'=2] {'rows'}, dimensions={0} | all-to-all | bytes 393216 | tf_op jit(solution)/shard_map/all_to_all | solution.py:332
  (181 shorter events, 69.0 us)
Async XLA Ops:
  5.1 14.9 %collective-permute-start.1 = (bf16[512,512]{1,0:T(8,128)(2,1)S(1)}, bf16[512,512]{1,0:T(8,128)(2,1)S(1)}, u32[]{:S(2)}, u32[]{:S(2)}) collective-permute-start(bf16[512,512]{1,0:T(8,128)(2,1)S(1)} %bitcast.41), channel_id=1, source_target_pairs={{0,4},{4,8},{8,12},{12,14},{14,10},{10,6},{6,2},{2,0},{1,5},{5,9},... | collective-permute-start | bytes 1572872 | tf_op jit(solution)/shard_map/ppermute | solution.py:267
  8.1 13.7 %collective-permute-start.3 = (bf16[512,512]{1,0:T(8,128)(2,1)S(1)}, bf16[512,512]{1,0:T(8,128)(2,1)S(1)}, u32[]{:S(2)}, u32[]{:S(2)}) collective-permute-start(bf16[512,512]{1,0:T(8,128)(2,1)S(1)} %bitcast.42), channel_id=1, source_target_pairs={{4,0},{8,4},{12,8},{14,12},{10,14},{6,10},{2,6},{0,2},{5,1},{9,5},... | collective-permute-start | bytes 1572872 | tf_op jit(solution)/shard_map/ppermute | solution.py:268
  8.2 31.7 %collective-permute-start = (bf16[640,1024]{1,0:T(8,128)(2,1)S(1)}, bf16[640,1024]{1,0:T(8,128)(2,1)S(1)}, u32[]{:S(2)}, u32[]{:S(2)}) collective-permute-start(bf16[640,1024]{1,0:T(8,128)(2,1)S(1)} %pick_columns.5), channel_id=1, source_target_pairs={{0,16},{16,0},{1,17},{17,1},{2,18},{18,2},{3,19},{19,3},{4,20},{20... | collective-permute-start | bytes 3932168 | tf_op jit(solution)/shard_map/ppermute | solution.py:250
  20.0 13.1 %collective-permute-start.2 = (bf16[512,512]{1,0:T(8,128)(2,1)S(1)}, bf16[512,512]{1,0:T(8,128)(2,1)S(1)}, u32[]{:S(2)}, u32[]{:S(2)}) collective-permute-start(bf16[512,512]{1,0:T(8,128)(2,1)S(1)} %collective-permute-done.1.refs_8_.refs_6_), channel_id=1, source_target_pairs={{0,4},{4,8},{8,12},{12,14},{14,10},{10,6},{6,2},{2,0},{1,5},{5,9},... | collective-permute-start | bytes 1572872 | tf_op jit(solution)/shard_map/ppermute | solution.py:267
  21.8 12.5 %collective-permute-start.4 = (bf16[512,512]{1,0:T(8,128)(2,1)S(1)}, bf16[512,512]{1,0:T(8,128)(2,1)S(1)}, u32[]{:S(2)}, u32[]{:S(2)}) collective-permute-start(bf16[512,512]{1,0:T(8,128)(2,1)S(1)} %collective-permute-done.3.refs_9_.refs_7_), channel_id=1, source_target_pairs={{4,0},{8,4},{12,8},{14,12},{10,14},{6,10},{2,6},{0,2},{5,1},{9,5},... | collective-permute-start | bytes 1572872 | tf_op jit(solution)/shard_map/ppermute | solution.py:268
  34.3 35.8 %collective-permute-start.5 = (bf16[640,1024]{1,0:T(8,128)(2,1)}, bf16[640,1024]{1,0:T(8,128)(2,1)}, u32[]{:S(2)}, u32[]{:S(2)}) collective-permute-start(bf16[640,1024]{1,0:T(8,128)(2,1)} %pick_columns.6), channel_id=1, source_target_pairs={{0,16},{16,0},{1,17},{17,1},{2,18},{18,2},{3,19},{19,3},{4,20},{20... | collective-permute-start | bytes 3932168 | tf_op jit(solution)/shard_map/ppermute | solution.py:270
  39.9 11.0 %collective-permute-start.6 = (bf16[512,512]{1,0:T(8,128)(2,1)S(1)}, bf16[512,512]{1,0:T(8,128)(2,1)S(1)}, u32[]{:S(2)}, u32[]{:S(2)}) collective-permute-start(bf16[512,512]{1,0:T(8,128)(2,1)S(1)} %collective-permute-done.2.refs_10_.refs_8_), channel_id=1, source_target_pairs={{0,4},{4,8},{8,12},{12,14},{14,10},{10,6},{6,2},{2,0},{1,5},{5,9},... | collective-permute-start | bytes 1572872 | tf_op jit(solution)/shard_map/ppermute | solution.py:267
  53.4 17.1 %collective-permute-start.10 = (bf16[512,512]{1,0:T(8,128)(2,1)S(1)}, bf16[512,512]{1,0:T(8,128)(2,1)}, u32[]{:S(2)}, u32[]{:S(2)}) collective-permute-start(bf16[512,512]{1,0:T(8,128)(2,1)S(1)} %bitcast.45), channel_id=1, source_target_pairs={{0,4},{4,8},{8,12},{12,14},{14,10},{10,6},{6,2},{2,0},{1,5},{5,9},... | collective-permute-start | bytes 1572872 | tf_op jit(solution)/shard_map/ppermute | solution.py:267
  55.0 15.5 %collective-permute-start.11 = (bf16[512,512]{1,0:T(8,128)(2,1)S(1)}, bf16[512,512]{1,0:T(8,128)(2,1)}, u32[]{:S(2)}, u32[]{:S(2)}) collective-permute-start(bf16[512,512]{1,0:T(8,128)(2,1)S(1)} %bitcast.46), channel_id=1, source_target_pairs={{4,0},{8,4},{12,8},{14,12},{10,14},{6,10},{2,6},{0,2},{5,1},{9,5},... | collective-permute-start | bytes 1572872 | tf_op jit(solution)/shard_map/ppermute | solution.py:268
  57.2 16.8 %all-to-all-start = ((bf16[8,3,4096]{2,1,0:T(4,128)(2,1)}), bf16[8,3,4096]{2,1,0:T(4,128)(2,1)}, u32[]{:S(2)}, u32[]{:S(2)}) async-start(bf16[8,3,4096]{2,1,0:T(4,128)(2,1)} %copy.18), calls=%async_computation | async-start | bytes 524288 | tf_op jit(solution)/shard_map/all_to_all | solution.py:288
  65.7 11.2 %collective-permute-start.7 = (bf16[256,512]{1,0:T(8,128)(2,1)}, bf16[256,512]{1,0:T(8,128)(2,1)}, u32[]{:S(2)}, u32[]{:S(2)}) collective-permute-start(bf16[256,512]{1,0:T(8,128)(2,1)} %slice.58), channel_id=1, source_target_pairs={{0,4},{4,8},{8,12},{12,14},{14,10},{10,6},{6,2},{2,0},{1,5},{5,9},... | collective-permute-start | bytes 786440 | tf_op jit(solution)/shard_map/ppermute | solution.py:267
  70.1 75.0 %collective-permute-start.16 = (bf16[640,2048]{1,0:T(8,128)(2,1)S(1)}, bf16[640,2048]{1,0:T(8,128)(2,1)}, u32[]{:S(2)}, u32[]{:S(2)}) collective-permute-start(bf16[640,2048]{1,0:T(8,128)(2,1)S(1)} %pick_columns.7.refs_1_), channel_id=1, source_target_pairs={{0,1},{1,0},{2,3},{3,2},{4,5},{5,4},{6,7},{7,6},{8,9},{9,8},{10,11... | collective-permute-start | bytes 7864328 | tf_op jit(solution)/shard_map/ppermute | solution.py:280
  70.5 14.9 %collective-permute-start.18 = (bf16[512,512]{1,0:T(8,128)(2,1)}, bf16[512,512]{1,0:T(8,128)(2,1)S(1)}, u32[]{:S(2)}, u32[]{:S(2)}) collective-permute-start(bf16[512,512]{1,0:T(8,128)(2,1)} %collective-permute-done.10.refs_8_.refs_6_), channel_id=1, source_target_pairs={{0,4},{4,8},{8,12},{12,14},{14,10},{10,6},{6,2},{2,0},{1,5},{5,9},... | collective-permute-start | bytes 1572872 | tf_op jit(solution)/shard_map/ppermute | solution.py:267
  76.9 37.3 %collective-permute-start.12 = (bf16[640,1024]{1,0:T(8,128)(2,1)}, bf16[640,1024]{1,0:T(8,128)(2,1)}, u32[]{:S(2)}, u32[]{:S(2)}) collective-permute-start(bf16[640,1024]{1,0:T(8,128)(2,1)} %copy-done.1), channel_id=1, source_target_pairs={{0,1},{1,0},{2,3},{3,2},{4,5},{5,4},{6,7},{7,6},{8,9},{9,8},{10,11... | collective-permute-start | bytes 3932168 | tf_op jit(solution)/shard_map/ppermute | solution.py:285
  76.9 37.3 %collective-permute-start.13 = (bf16[640,1024]{1,0:T(8,128)(2,1)}, bf16[640,1024]{1,0:T(8,128)(2,1)}, u32[]{:S(2)}, u32[]{:S(2)}) collective-permute-start(bf16[640,1024]{1,0:T(8,128)(2,1)} %collective-permute-done.5.refs_2_), channel_id=1, source_target_pairs={{0,1},{1,0},{2,3},{3,2},{4,5},{5,4},{6,7},{7,6},{8,9},{9,8},{10,11... | collective-permute-start | bytes 3932168 | tf_op jit(solution)/shard_map/ppermute | solution.py:285
  81.1 12.2 %collective-permute-start.19 = (bf16[512,512]{1,0:T(8,128)(2,1)}, bf16[512,512]{1,0:T(8,128)(2,1)}, u32[]{:S(2)}, u32[]{:S(2)}) collective-permute-start(bf16[512,512]{1,0:T(8,128)(2,1)} %collective-permute-done.11.refs_9_.refs_7_), channel_id=1, source_target_pairs={{4,0},{8,4},{12,8},{14,12},{10,14},{6,10},{2,6},{0,2},{5,1},{9,5},... | collective-permute-start | bytes 1572872 | tf_op jit(solution)/shard_map/ppermute | solution.py:268
  85.3 14.0 %collective-permute-start.20 = (bf16[512,512]{1,0:T(8,128)(2,1)S(1)}, bf16[512,512]{1,0:T(8,128)(2,1)}, u32[]{:S(2)}, u32[]{:S(2)}) collective-permute-start(bf16[512,512]{1,0:T(8,128)(2,1)S(1)} %collective-permute-done.18.refs_10_.refs_8_), channel_id=1, source_target_pairs={{0,4},{4,8},{8,12},{12,14},{14,10},{10,6},{6,2},{2,0},{1,5},{5,9},... | collective-permute-start | bytes 1572872 | tf_op jit(solution)/shard_map/ppermute | solution.py:267
  93.2 17.9 %collective-permute-start.22 = (bf16[512,512]{1,0:T(8,128)(2,1)}, bf16[512,512]{1,0:T(8,128)(2,1)}, u32[]{:S(2)}, u32[]{:S(2)}) collective-permute-start(bf16[512,512]{1,0:T(8,128)(2,1)} %collective-permute-done.19.refs_11_.refs_9_), channel_id=1, source_target_pairs={{4,0},{8,4},{12,8},{14,12},{10,14},{6,10},{2,6},{0,2},{5,1},{9,5},... | collective-permute-start | bytes 1572872 | tf_op jit(solution)/shard_map/ppermute | solution.py:268
  99.3 14.8 %collective-permute-start.15 = (bf16[64,2048]{1,0:T(8,128)(2,1)S(1)}, bf16[64,2048]{1,0:T(8,128)(2,1)S(1)}, u32[]{:S(2)}, u32[]{:S(2)}) collective-permute-start(bf16[64,2048]{1,0:T(8,128)(2,1)S(1)} %pad_maximum_fusion.refs_5_.refs_3_), channel_id=1, source_target_pairs={{0,1},{1,0},{2,3},{3,2},{4,5},{5,4},{6,7},{7,6},{8,9},{9,8},{10,11... | collective-permute-start | bytes 786440 | tf_op jit(solution)/shard_map/ppermute | solution.py:298
  104.5 38.9 %all-to-all-start.1 = ((bf16[8,3,4096]{2,1,0:T(4,128)(2,1)}), bf16[8,3,4096]{2,1,0:T(4,128)(2,1)}, u32[]{:S(2)}, u32[]{:S(2)}) async-start(bf16[8,3,4096]{2,1,0:T(4,128)(2,1)} %copy.20), calls=%async_computation.1 | async-start | bytes 524288 | tf_op jit(solution)/shard_map/all_to_all | solution.py:288
  111.1 27.7 %collective-permute-start.21 = (bf16[256,512]{1,0:T(8,128)(2,1)S(1)}, bf16[256,512]{1,0:T(8,128)(2,1)S(1)}, u32[]{:S(2)}, u32[]{:S(2)}) collective-permute-start(bf16[256,512]{1,0:T(8,128)(2,1)S(1)} %slice.60), channel_id=1, source_target_pairs={{0,4},{4,8},{8,12},{12,14},{14,10},{10,6},{6,2},{2,0},{1,5},{5,9},... | collective-permute-start | bytes 786440 | tf_op jit(solution)/shard_map/ppermute | solution.py:267
  114.2 24.7 %collective-permute-start.23 = (bf16[256,512]{1,0:T(8,128)(2,1)S(1)}, bf16[256,512]{1,0:T(8,128)(2,1)S(1)}, u32[]{:S(2)}, u32[]{:S(2)}) collective-permute-start(bf16[256,512]{1,0:T(8,128)(2,1)S(1)} %slice.61), channel_id=1, source_target_pairs={{4,0},{8,4},{12,8},{14,12},{10,14},{6,10},{2,6},{0,2},{5,1},{9,5},... | collective-permute-start | bytes 786440 | tf_op jit(solution)/shard_map/ppermute | solution.py:268
  130.7 39.3 %collective-permute-start.17 = (f16[672,512]{1,0:T(8,128)(2,1)}, f16[672,512]{1,0:T(8,128)(2,1)}, u32[]{:S(2)}, u32[]{:S(2)}) collective-permute-start(f16[672,512]{1,0:T(8,128)(2,1)} %multiply_convert_fusion.1), channel_id=1, source_target_pairs={{0,16},{16,0},{1,17},{17,1},{2,18},{18,2},{3,19},{19,3},{4,20},{20... | collective-permute-start | bytes 2064392 | tf_op jit(solution)/shard_map/ppermute | solution.py:321
  142.3 30.8 %collective-permute-start.24 = (f16[672,512]{1,0:T(8,128)(2,1)}, f16[672,512]{1,0:T(8,128)(2,1)}, u32[]{:S(2)}, u32[]{:S(2)}) collective-permute-start(f16[672,512]{1,0:T(8,128)(2,1)} %multiply_convert_fusion), channel_id=1, source_target_pairs={{0,16},{16,0},{1,17},{17,1},{2,18},{18,2},{3,19},{19,3},{4,20},{20... | collective-permute-start | bytes 2064392 | tf_op jit(solution)/shard_map/ppermute | solution.py:321
  (43 other events, 244.4 us)

commit v4 on v3

--- a/solution.py
+++ b/solution.py
@@ -11,8 +11,8 @@
 HD = 128
 HALF = HD // 2
 CHUNKS = 2
-LAG = 3
 MOST_SHARDS = 8
+VMEM_BYTES = 56 << 20
 MERGED = 4
 RAISE = 16.0
 
@@ -102,37 +102,62 @@
     )(projected, back, cosine, sine, key_info, query_info, queries)
 
 
-def pick_kernel(side_ref, source_ref, out_ref):
-    out_ref[...] = source_ref[...]
-
-
-def pick_columns(source, side, half, first, count):
-    rows = source.shape[0]
+def pick_kernel(half, first, side_ref, source_ref, out_ref, sems):
+    rows, width = out_ref.shape
+    copies = []
+    for j in range(width // half):
+        at = pl.multiple_of((2 * j + side_ref[0]) * half, half)
+        copies.append(
+            pltpu.make_async_copy(
+                source_ref.at[first : first + rows, pl.ds(at, half)],
+                out_ref.at[:, j * half : (j + 1) * half],
+                sems.at[j],
+            )
+        )
+        copies[-1].start()
+    for copy in copies:
+        copy.wait()
+
+
+def pick_columns(source, side, half, first, end):
+    count = source.shape[1] // (2 * half)
     return pl.pallas_call(
-        pick_kernel,
-        out_shape=jax.ShapeDtypeStruct((rows, count * half), source.dtype),
-        grid_spec=pltpu.PrefetchScalarGridSpec(
-            num_scalar_prefetch=1,
-            grid=(count,),
-            in_specs=[pl.BlockSpec((rows, half), lambda j, s: (0, 2 * (first + j) + s[0]))],
-            out_specs=pl.BlockSpec((rows, half), lambda j, s: (0, j)),
-        ),
-        compiler_params=pltpu.CompilerParams(vmem_limit_bytes=24 << 20),
+        functools.partial(pick_kernel, half, first),
+        out_shape=jax.ShapeDtypeStruct((end - first, count * half), source.dtype),
+        in_specs=[pl.BlockSpec(memory_space=pltpu.SMEM), pl.BlockSpec(memory_space=pl.ANY)],
+        out_specs=pl.BlockSpec(memory_space=pl.ANY),
+        scratch_shapes=[pltpu.SemaphoreType.DMA((count,))],
+        compiler_params=pltpu.CompilerParams(vmem_limit_bytes=VMEM_BYTES),
         cost_estimate=pl.CostEstimate(
-            flops=0, bytes_accessed=4 * rows * count * half, transcendentals=0
+            flops=0, bytes_accessed=4 * (end - first) * count * half, transcendentals=0
         ),
         name="pick_columns",
     )(side.reshape(1), source)
 
 
-def product_kernel(shards, split, layout, has_total, *refs):
+def product_kernel(depths, layout, column, has_total, *refs):
     place_ref, refs = refs[0], refs[1:]
     hidden, refs = refs[: len(layout)], refs[len(layout) :]
-    weights, refs = refs[: shards * split], refs[shards * split :]
-    out_ref, held, sems = refs[-3:]
+    flat = [depth for pieces in depths for depth in pieces]
+    weights, refs = refs[: len(flat)], refs[len(flat) :]
+    out_ref, held, piece, sems, piece_sems = refs[-5:]
+    shards = len(depths)
     half = held.shape[1] // shards
     spans = sorted({(part, at, rows) for part, at, rows, _, _, _ in layout})
+    tops = [sum(flat[:i]) for i in range(len(flat))]
+    copies = [
+        pltpu.make_async_copy(
+            w.at[:, column : column + piece.shape[1]] if w.shape[1] > piece.shape[1] else w,
+            piece.at[top : top + depth, :],
+            piece_sems.at[i],
+        )
+        for i, (w, top, depth) in enumerate(zip(weights, tops, flat))
+    ]
+    done = 0
     for p in range(shards):
+        for _ in depths[p]:
+            copies[done].start()
+            done += 1
         for (part, at, rows, row, first, blocks), source in zip(layout, hidden):
             block = place_ref[p] - first
 
@@ -146,23 +171,27 @@
                 ).start()
 
     total = refs[0][...] if has_total else None
+    waited = 0
     for begin in range(0, shards, MERGED):
         end = min(begin + MERGED, shards)
         for p in range(begin, end):
             for part, at, rows in spans:
                 target = held.at[at : at + rows, p * half : (p + 1) * half]
                 pltpu.make_async_copy(target, target, sems.at[p, part]).wait()
-        piece = jnp.concatenate([w[...] for w in weights[begin * split : end * split]], 0)
-        term = jnp.dot(
-            held[:, begin * half : end * half], piece, preferred_element_type=jnp.float32
-        )
+            for _ in depths[p]:
+                copies[waited].wait()
+                waited += 1
+        span = slice(begin * half, end * half)
+        term = jnp.dot(held[:, span], piece[span, :], preferred_element_type=jnp.float32)
         total = term if total is None else total + term
     out_ref[...] = total
 
 
-def products(total, hidden, weights, places, half):
-    split, shards = len(weights[0]), len(weights)
-    width = weights[0][0].shape[1]
+def products(total, hidden, weights, places, column, width):
+    shards = len(weights)
+    flat = [w for shard in weights for w in shard]
+    depths = tuple(tuple(w.shape[0] for w in shard) for shard in weights)
+    half = sum(depths[0])
     operands, layout, at = [places], [], 0
     for part, (row, rows, pieces) in enumerate(hidden):
         first = 0
@@ -171,24 +200,25 @@
             layout.append((part, at, rows, row, first, piece.shape[1] // half))
             first += piece.shape[1] // half
         at += rows
-    flat = [w for shard in weights for w in shard]
     operands += flat
     vmem = pl.BlockSpec(memory_space=pltpu.VMEM)
     in_specs = [pl.BlockSpec(memory_space=pltpu.SMEM)]
-    in_specs += [pl.BlockSpec(memory_space=pl.ANY)] * len(layout) + [vmem] * len(flat)
+    in_specs += [pl.BlockSpec(memory_space=pl.ANY)] * (len(layout) + len(flat))
     if total is not None:
         operands.append(total)
         in_specs.append(vmem)
     return pl.pallas_call(
-        functools.partial(product_kernel, shards, split, tuple(layout), total is not None),
+        functools.partial(product_kernel, depths, tuple(layout), column, total is not None),
         out_shape=jax.ShapeDtypeStruct((at, width), jnp.float32),
         in_specs=in_specs,
         out_specs=vmem,
         scratch_shapes=[
             pltpu.VMEM((at, shards * half), jnp.bfloat16),
+            pltpu.VMEM((shards * half, width), jnp.bfloat16),
             pltpu.SemaphoreType.DMA((shards, len(hidden))),
+            pltpu.SemaphoreType.DMA((len(flat),)),
         ],
-        compiler_params=pltpu.CompilerParams(vmem_limit_bytes=40 << 20),
+        compiler_params=pltpu.CompilerParams(vmem_limit_bytes=VMEM_BYTES),
         cost_estimate=pl.CostEstimate(
             flops=2 * at * half * width * shards,
             bytes_accessed=shards * 2 * half * (at + width) + 4 * at * width,
@@ -204,8 +234,8 @@
     return evens + odds[::-1]
 
 
-def after(value, other):
-    return lax.optimization_barrier((value, other))[0]
+def fence(*values):
+    return lax.optimization_barrier(values)
 
 
 def body(passages, kv_weight, new_hidden, queries, lengths, destinations):
@@ -238,96 +268,109 @@
     owners = lax.dynamic_index_in_dim(jnp.array(shard_order, jnp.int32), row_index, 1, keepdims=False)
     places = ((owners // half_rows) ^ core) * half_rows + owners % half_rows
 
-    chunks = CHUNKS
-    chunk_heads = local_heads // chunks
-    chunk = chunk_heads * HD
-    mine = lax.dynamic_slice_in_dim(kv_weight, side * half, half, 0)
-    own = [
-        mine[:, :, c * chunk : (c + 1) * chunk].reshape(half, 2 * chunk) for c in range(chunks)
-    ]
-
-    sent = [pick_columns(passages, 1 - side, half, at, half_rows // 2) for at in (0, half_rows // 2)]
+    chunk = kv_weight.shape[2] // CHUNKS
+    own = lax.dynamic_slice_in_dim(kv_weight, side * half, half, 0)
+    own = own.reshape(half, 2, CHUNKS, chunk).swapaxes(1, 2).reshape(half, -1)
+    width = 2 * chunk
+
+    def step(pair):
+        return lax.ppermute(pair[0], "rows", onward), lax.ppermute(pair[1], "rows", back)
+
+    third = -(-tokens // 48) * 16
+    cuts = (0, third, 2 * third, tokens)
+    sent = [pick_columns(passages, 1 - side, half, cuts[0], cuts[1])]
+    own, sent[0], passages, new_hidden = fence(own, sent[0], passages, new_hidden)
     got = [lax.ppermute(sent[0], "groups", partners)]
-
-    right, left = [[] for _ in range(chunks)], [[] for _ in range(chunks)]
-
-    def ring_step(c):
-        k = len(right[c])
-        r, l = (own[c], own[c]) if k == 0 else (right[c][-1], left[c][-1])
-        if k == half_rows - 1:
-            r, l = r[: half // 2], l[half // 2 :]
-        if k == 0 and c == 0:
-            r, l = after((r, l), sent[0])
-        if k == 0 and c > 0:
-            r, l = after((r, l), (right[c - 1][LAG - 1], left[c - 1][LAG - 1]))
-        if k == 2 and c == 0:
-            r, l = after((r, l), got[0])
-        if k == 1 and c == 1:
-            r, l = after((r, l), got[1])
-        right[c].append(lax.ppermute(r, "rows", onward))
-        left[c].append(lax.ppermute(l, "rows", back))
-        if k == 1 and c == 0:
-            got.append(lax.ppermute(after(sent[1], arrived((0, 1))), "groups", partners))
-
-    def arrived(*steps_done):
-        return [side_of[c][k] for c, k in steps_done for side_of in (right, left)]
-
-    for c in range(chunks):
-        for k in range(half_rows):
-            ring_step(c)
-
-    kept = pick_columns(passages, side, half, 0, half_rows)
+    ring = [step((own, own))]
+    sent += [pick_columns(passages, 1 - side, half, *cuts[i : i + 2]) for i in (1, 2)]
+    kept = pick_columns(passages, side, half, 0, tokens)
     kept_other = lax.ppermute(kept, "tensor", cores)
-    got = [
-        after(got[0], arrived((0, 1))),
-        after(got[1], arrived((0, half_rows - 1), (1, 0))),
-    ]
-    got_other = [lax.ppermute(piece, "tensor", cores) for piece in got]
-
-    def to_replica(held, start, end):
-        moved = lax.all_to_all(after(held, start), "rows", split_axis=0, concat_axis=0, tiled=True)
-        return jnp.swapaxes(after(moved, end), 0, 1).reshape(count, -1)
-
-    new_rows = to_replica(new_hidden, (kept, sent), arrived((0, 1)))
+    new_hidden, kept = fence(new_hidden, kept)
+    moved = lax.all_to_all(new_hidden, "rows", split_axis=0, concat_axis=0, tiled=True)
+    ring[0], got[0], moved, kept_other, sent, queries = fence(
+        ring[0], got[0], moved, kept_other, sent, queries
+    )
+
+    got.append(lax.ppermute(sent[1], "groups", partners))
+    ring.append(step(ring[-1]))
+    new_rows = jnp.swapaxes(moved, 0, 1).reshape(count, half_model)
     new_rows = jnp.pad(new_rows, ((0, new_padded - count), (0, 0)))
-    new_kept = pick_columns(new_rows, side, half, 0, half_rows)
-    new_sent = pick_columns(new_rows, 1 - side, half, 0, half_rows)
+    new_sent = pick_columns(new_rows, 1 - side, half, 0, new_padded)
     new_got = lax.ppermute(new_sent, "groups", partners)
-    new_got = after(new_got, arrived((0, 2)))
+    new_kept = pick_columns(new_rows, side, half, 0, new_padded)
     new_kept = jnp.concatenate([new_kept, new_got], 0)
     new_other = lax.ppermute(new_kept, "tensor", cores)
+    got_other = [lax.ppermute(got[0], "tensor", cores)]
+    ring[1], got[1], new_other, got_other, places, queries = fence(
+        ring[1], got[1], new_other, got_other, places, queries
+    )
+
+    def project(hidden, total, begin, end, column, width):
+        weights = [(own,)] + [(w,) for pair in ring for w in pair]
+        weights = weights[: row_count - 1] + [last[column // width] if last else ()]
+        for at in range(begin, end, MOST_SHARDS):
+            some = weights[at : min(at + MOST_SHARDS, end)]
+            spots = places[at : at + len(some)]
+            total = products(total, hidden, some, spots, column, width)
+        return total
+
+    def homeward(total):
+        return (total * RAISE).astype(jnp.float16)
+
+    last = []
     own_hidden = [(0, tokens, (kept, kept_other)), (0, new_padded, (new_kept, new_other))]
-    away_hidden = [(0, tokens, (*got, *got_other)), (new_padded, new_padded, (new_kept, new_other))]
-    query_rows = to_replica(queries, arrived((1, 1)), arrived((1, half_rows - 1)))
-
+    early = row_count - 3
+    for k in range(2, half_rows - 1):
+        if k > 2:
+            ring[-1] = fence(*ring[-1])
+        else:
+            got.append(lax.ppermute(sent[2], "groups", partners))
+            got_other.append(lax.ppermute(got[1], "tensor", cores))
+            moved = lax.all_to_all(queries, "rows", split_axis=0, concat_axis=0, tiled=True)
+        ring.append(step(ring[-1]))
+    held = project(own_hidden, None, 0, early, 0, 2 * width)
     position, key_info, query_info = token_tables(
         lengths, destinations, row_index, tokens, requests, steps, tokens + new_padded
     )
     cosine, sine = angle_tables(position)
 
-    def project(c, hidden, ready):
-        weights = [(own[c],)]
-        for k in range(half_rows - 1):
-            weights += [(right[c][k],), (left[c][k],)]
-        shards, total = len(weights), None
-        spots = after(places, ready)
-        for at in range(0, shards, MOST_SHARDS):
-            some = weights[at : at + MOST_SHARDS]
-            total = products(total, hidden, some, spots[at : at + len(some)], half)
-        return products(total, hidden, [(right[c][-1], left[c][-1])], spots[shards:], half)
-
-    away = [project(c, away_hidden, ()) for c in range(chunks)]
-    away = [(total * RAISE).astype(jnp.float16) for total in away]
-    homed = [lax.ppermute(total, "groups", partners) for total in away]
-    homed = [total.astype(jnp.float32) * (1.0 / RAISE) for total in homed]
-
+    def halved(c):
+        columns = slice(c * width, (c + 1) * width)
+        return ring[-1][0][: half // 2, columns], ring[-1][1][half // 2 :, columns]
+
+    ends = [halved(0)]
+    ring[-1], got[2], got_other, moved, held, ends, places, cosine, sine = fence(
+        ring[-1], got[2], got_other, moved, held, ends, places, cosine, sine
+    )
+    query_rows = jnp.swapaxes(moved, 0, 1).reshape(count, -1)
+
+    last.append(step(ends[0]))
+    got_other.append(lax.ppermute(got[2], "tensor", cores))
+    away_hidden = [
+        (0, piece.shape[0], (piece, other)) for piece, other in zip(got, got_other)
+    ] + [(new_padded, new_padded, (new_kept, new_other))]
+    away = [project(away_hidden, None, 0, row_count - 1, 0, width)]
+    ends.append(halved(1))
+    last[0], away, ends, places = fence(last[0], away, ends, places)
+
+    last.append(step(ends[1]))
+    away[0] = homeward(project(away_hidden, away[0], row_count - 1, row_count, 0, width))
+    away[0], places = fence(away[0], places)
+    homed = [lax.ppermute(away[0], "groups", partners)]
+    away.append(project(away_hidden, None, 0, row_count - 1, width, width))
+    away[1] = homeward(project(away_hidden, away[1], row_count - 1, row_count, width, width))
+    homed[0], away[1], places = fence(homed[0], away[1], places)
+
+    homed.append(lax.ppermute(away[1], "groups", partners))
     outs = []
-    for c in range(chunks):
-        held = project(c, own_hidden, away[c])
+    for c in range(CHUNKS):
+        back_home = homed[c].astype(jnp.float32) * (1.0 / RAISE)
+        mine = held[:, c * width : (c + 1) * width]
+        mine = project(own_hidden, mine, early, row_count, c * width, width)
         at = c * chunk * group
         query = query_rows[:, at : at + chunk * group]
-        outs.append(finish(held, homed[c], cosine, sine, key_info, query_info, query))
-    attended = outs[0] if chunks == 1 else jnp.concatenate(outs, 1)
+        outs.append(finish(mine, back_home, cosine, sine, key_info, query_info, query))
+    attended = jnp.concatenate(outs, 1)
     attended = jnp.swapaxes(attended.reshape(steps, requests, -1), 0, 1)
     return lax.all_to_all(attended, "rows", split_axis=0, concat_axis=0, tiled=True)
 

time: 192 us -> 320 us (1.67)
  Pallas kernels: 41.4 us -> 225 us
  waiting for transfers between devices: 53.7 us -> 19.8 us
  local copies, waits for them, and re-layouts: 35.4 us -> 23.9 us
  starting transfers between devices: 36.5 us -> 29.8 us
    pallas_call x13, Pallas kernels: 37.9 us -> 222 us  [the longest x6 174 us: pick_columns(): pl.pallas_call(functools.partial(pick_kernel, half, first), out_shape=jax...]
    ppermute x21 -> x17, waiting for transfers between devices: 45.3 us -> 5.71 us  [the longest x5 5.61 us: step(): lax.ppermute(pair[0], 'rows', onward)]
    unnamed x82 -> x30, local copies, waits for them, and re-layouts: 19.2 us -> 5.37 us
    ppermute x21 -> x17, starting transfers between devices: 21.5 us -> 14.3 us  [the longest x5 6.9 us: step(): lax.ppermute(pair[1], 'rows', back)]
    ppermute x1, waiting for transfers between devices: 2.95 us -> 9.96 us  [body(): new_got = lax.ppermute(new_sent, 'groups', partners)]
    ppermute x1, waiting for transfers between devices: 4.04 us -> 0.01 us  [body(): got = [lax.ppermute(sent[0], 'groups', partners)]]
  transfers between devices with their start and end apart: 27 -> 23, of which waited for: 11 -> 4; matrix products, arithmetic and copies ran while one was open for 11% -> 6% of each run, Pallas kernels for 21% -> 34%
where the time goes in v4:
time: 320 us; the launch traced here: 319 us
  Pallas kernels  225 us (70%)
  starting transfers between devices  29.8 us (9%)
  local copies, waits for them, and re-layouts  23.9 us (7%)
  waiting for transfers between devices  19.8 us (6%)
  blocking collectives  11.7 us (4%)
  other arithmetic  8.1 us (3%)
    pallas_call x6, Pallas kernels, pick_columns(): pl.pallas_call(functools.partial(pick_kernel, half, first), out_shape=jax...  174 us
    pallas_call x7, Pallas kernels, products(): pl.pallas_call(functools.partial(product_kernel, depths, tuple(layout), c...  48.3 us
    all_to_all x1, blocking collectives, body(): lax.all_to_all(attended, 'rows', split_axis=0, concat_axis=0, tiled=True)  11.7 us
    ppermute x1, waiting for transfers between devices, body(): new_got = lax.ppermute(new_sent, 'groups', partners)  9.96 us
    ppermute x5, starting transfers between devices, step(): lax.ppermute(pair[1], 'rows', back)  6.9 us
  transfers between devices with their start and end apart: 23, of which 4 were waited for; matrix products, arithmetic and copies ran while one was open for 6% of the time, Pallas kernels for 34%

profile of v4, /device:TPU:0, one launch (start us, length us, event | category | flops | bytes accessed | tf_op | source)
XLA Modules:
  0.0 319.3 jit_solution(7860939481312955088)
XLA Ops:
  5.1 28.9 %pick_columns.6 = bf16[224,2048]{1,0:T(8,128)(2,1)} custom-call(s32[1]{0:T(128)} %bitcast.2.side_ref, bf16[640,4096]{1,0:T(8,128)(2,1)} %source_ref.4), custom_call_target="tpu_custom_call" | custom-call | bytes 1835008 | tf_op jit(solution)/shard_map/pick_columns/pallas_call | solution.py:124
  34.1 80.6 %pick_columns.7.refs_1_ = bf16[640,2048]{1,0:T(8,128)(2,1)} custom-call(s32[1]{0:T(128)} %bitcast.3.side_ref, bf16[640,4096]{1,0:T(8,128)(2,1)} %source_ref.4), custom_call_target="tpu_custom_call" | custom-call | bytes 5242880 | tf_op jit(solution)/shard_map/pick_columns/pallas_call | solution.py:124
  115.1 2.6 collective-permute-start.1
  117.9 1.9 collective-permute-start.2
  120.6 5.8 %all-to-all-start = ((bf16[8,3,4096]{2,1,0:T(4,128)(2,1)}), bf16[8,3,4096]{2,1,0:T(4,128)(2,1)S(1)}, u32[]{:S(2)}, u32[]{:S(2)}) async-start(bf16[8,3,4096]{2,1,0:T(4,128)(2,1)} %copy.18), calls=%async_computation | async-start | bytes 524288 | tf_op jit(solution)/shard_map/all_to_all | solution.py:289
  126.4 25.0 %pick_columns.9 = bf16[192,2048]{1,0:T(8,128)(2,1)} custom-call(s32[1]{0:T(128)} %bitcast.2.side_ref, bf16[640,4096]{1,0:T(8,128)(2,1)} %source_ref.4), custom_call_target="tpu_custom_call" | custom-call | bytes 1572864 | tf_op jit(solution)/shard_map/pick_columns/pallas_call | solution.py:124
  151.4 28.9 %pick_columns.8 = bf16[224,2048]{1,0:T(8,128)(2,1)} custom-call(s32[1]{0:T(128)} %bitcast.2.side_ref, bf16[640,4096]{1,0:T(8,128)(2,1)} %source_ref.4), custom_call_target="tpu_custom_call" | custom-call | bytes 1835008 | tf_op jit(solution)/shard_map/pick_columns/pallas_call | solution.py:124
  180.4 2.1 collective-permute-start.4
  184.0 5.1 %pick_columns.11 = bf16[32,2048]{1,0:T(8,128)(2,1)} custom-call(s32[1]{0:T(128)} %bitcast.2.side_ref, bf16[32,4096]{1,0:T(8,128)(2,1)} %pad.4.source_ref), custom_call_target="tpu_custom_call" | custom-call | bytes 262144 | tf_op jit(solution)/shard_map/pick_columns/pallas_call | solution.py:124
  191.5 5.1 %pick_columns.10 = bf16[32,2048]{1,0:T(8,128)(2,1)} custom-call(s32[1]{0:T(128)} %bitcast.3.side_ref, bf16[32,4096]{1,0:T(8,128)(2,1)} %pad.4.source_ref), custom_call_target="tpu_custom_call" | custom-call | bytes 262144 | tf_op jit(solution)/shard_map/pick_columns/pallas_call | solution.py:124
  196.6 10.0 %collective-permute-done.7 = bf16[32,2048]{1,0:T(8,128)(2,1)S(1)} collective-permute-done((bf16[32,2048]{1,0:T(8,128)(2,1)}, bf16[32,2048]{1,0:T(8,128)(2,1)S(1)}, u32[]{:S(2)}, u32[]{:S(2)}) %collective-permute-start.7) | collective-permute-done | bytes 131104 | tf_op jit(solution)/shard_map/ppermute | solution.py:299
  213.7 5.7 %all-to-all-start.1 = ((bf16[8,3,4096]{2,1,0:T(4,128)(2,1)}), bf16[8,3,4096]{2,1,0:T(4,128)(2,1)}, u32[]{:S(2)}, u32[]{:S(2)}) async-start(bf16[8,3,4096]{2,1,0:T(4,128)(2,1)} %copy.20), calls=%async_computation.1 | async-start | bytes 524288 | tf_op jit(solution)/shard_map/all_to_all | solution.py:329
  220.6 9.7 %products.7 = f32[672,1024]{1,0:T(8,128)} custom-call(s32[5]{0:T(128)} %bitcast.43, bf16[640,2048]{1,0:T(8,128)(2,1)} %pick_columns.7.refs_1_, bf16[640,2048]{1,0:T(8,128)(2,1)} %collective-permute-done.3.refs_2_, bf16[64,2048]{1,0:T(8,128)(2,1)} %copy-done.3, bf16[64,2048]{1,0:T(8,128)(2,1)} %copy-done.5, bf16[512,1024]{1,0:T(8,128)(2,1)} %copy-done.4, ...), custom_call_target="tpu_custom_call" | custom-call | flops 3523215360 | bytes 11436032 | tf_op jit(solution)/shard_map/products/pallas_call | solution.py:210
  230.4 5.6 %collective-permute-done.10.refs_14_.refs_5_ = bf16[512,1024]{1,0:T(8,128)(2,1)} collective-permute-done((bf16[512,1024]{1,0:T(8,128)(2,1)}, bf16[512,1024]{1,0:T(8,128)(2,1)}, u32[]{:S(2)}, u32[]{:S(2)}) %collective-permute-start.10) | collective-permute-done | bytes 1048608 | tf_op jit(solution)/shard_map/ppermute | solution.py:277
  239.4 4.1 %all-to-all-done.1 = bf16[8,3,4096]{2,1,0:T(4,128)(2,1)} async-done(((bf16[8,3,4096]{2,1,0:T(4,128)(2,1)}), bf16[8,3,4096]{2,1,0:T(4,128)(2,1)}, u32[]{:S(2)}, u32[]{:S(2)}) %all-to-all-start.1) | async-done | bytes 196640 | tf_op jit(solution)/shard_map/all_to_all | solution.py:329
  244.0 2.0 collective-permute-start.15
  249.2 8.4 %products.8.refs_11_ = f32[672,512]{1,0:T(8,128)} custom-call(s32[7]{0:T(128)} %bitcast.44, bf16[224,2048]{1,0:T(8,128)(2,1)} %collective-permute-done.2.refs_1_, bf16[224,2048]{1,0:T(8,128)(2,1)} %collective-permute-done.9.refs_2_, bf16[224,2048]{1,0:T(8,128)(2,1)} %collective-permute-done.6.refs_3_, bf16[224,2048]{1,0:T(8,128)(2,1)} %collective-permute-done.13.refs_4_, ...), custom_call_target="tpu_custom_call" | custom-call | flops 2466250752 | bytes 9863168 | tf_op jit(solution)/shard_map/products/pallas_call | solution.py:210
  258.4 5.0 %products.9 = f32[672,512]{1,0:T(8,128)} custom-call(s32[1]{0:T(128)} %slice.49.refs_0_, bf16[224,2048]{1,0:T(8,128)(2,1)} %collective-permute-done.2.refs_1_, bf16[224,2048]{1,0:T(8,128)(2,1)} %collective-permute-done.9.refs_2_, bf16[224,2048]{1,0:T(8,128)(2,1)} %collective-permute-done.6.refs_3_, bf16[224,2048]{1,0:T(8,128)(2,1)} %collective-permute-done.13.refs_4_, ...), custom_call_target="tpu_custom_call" | custom-call | flops 352321536 | bytes 2588672 | tf_op jit(solution)/shard_map/products/pallas_call | solution.py:210
  265.1 2.0 collective-permute-start.19
  268.3 8.4 %products.10.refs_11_ = f32[672,512]{1,0:T(8,128)} custom-call(s32[7]{0:T(128)} %bitcast.45, bf16[224,2048]{1,0:T(8,128)(2,1)} %collective-permute-done.2.refs_1_, bf16[224,2048]{1,0:T(8,128)(2,1)} %collective-permute-done.9.refs_2_, bf16[224,2048]{1,0:T(8,128)(2,1)} %collective-permute-done.6.refs_3_, bf16[224,2048]{1,0:T(8,128)(2,1)} %collective-permute-done.13.refs_4_, ...), custom_call_target="tpu_custom_call" | custom-call | flops 2466250752 | bytes 9863168 | tf_op jit(solution)/shard_map/products/pallas_call | solution.py:210
  278.1 5.2 %products.11 = f32[672,512]{1,0:T(8,128)} custom-call(s32[1]{0:T(128)} %slice.50.refs_0_, bf16[224,2048]{1,0:T(8,128)(2,1)} %collective-permute-done.2.refs_1_, bf16[224,2048]{1,0:T(8,128)(2,1)} %collective-permute-done.9.refs_2_, bf16[224,2048]{1,0:T(8,128)(2,1)} %collective-permute-done.6.refs_3_, bf16[224,2048]{1,0:T(8,128)(2,1)} %collective-permute-done.13.refs_4_, ...), custom_call_target="tpu_custom_call" | custom-call | flops 352321536 | bytes 2588672 | tf_op jit(solution)/shard_map/products/pallas_call | solution.py:210
  288.8 5.8 %products.12.held_ref = f32[672,512]{1,0:T(8,128)} custom-call(s32[3]{0:T(128)} %slice.52.refs_0_, bf16[640,2048]{1,0:T(8,128)(2,1)} %pick_columns.7.refs_1_, bf16[640,2048]{1,0:T(8,128)(2,1)} %collective-permute-done.3.refs_2_, bf16[64,2048]{1,0:T(8,128)(2,1)} %copy-done.3, bf16[64,2048]{1,0:T(8,128)(2,1)} %copy-done.5, ...), custom_call_target="tpu_custom_call" | custom-call | flops 1056964608 | bytes 5013504 | tf_op jit(solution)/shard_map/products/pallas_call | solution.py:210
  297.7 5.8 %products.13.held_ref = f32[672,512]{1,0:T(8,128)} custom-call(s32[3]{0:T(128)} %slice.52.refs_0_, bf16[640,2048]{1,0:T(8,128)(2,1)} %pick_columns.7.refs_1_, bf16[640,2048]{1,0:T(8,128)(2,1)} %collective-permute-done.3.refs_2_, bf16[64,2048]{1,0:T(8,128)(2,1)} %copy-done.3, bf16[64,2048]{1,0:T(8,128)(2,1)} %copy-done.5, ...), custom_call_target="tpu_custom_call" | custom-call | flops 1056964608 | bytes 5013504 | tf_op jit(solution)/shard_map/products/pallas_call | solution.py:210
  306.7 11.7 %all_to_all.15 = bf16[8,3,4096]{2,1,0:T(4,128)(2,1)S(1)} all-to-all(bf16[8,3,4096]{2,1,0:T(4,128)(2,1)S(1)} %bitcast.40), channel_id=1, replica_groups=mesh['groups'=2,'rows'=8,'tensor'=2] {'rows'}, dimensions={0} | all-to-all | bytes 393216 | tf_op jit(solution)/shard_map/all_to_all | solution.py:375
  (122 shorter events, 43.5 us)
Async XLA Ops:
  5.1 112.6 %copy-start.4 = (bf16[512,1024]{1,0:T(8,128)(2,1)}, bf16[512,1024]{1,0:T(8,128)(2,1)S(1)}, u32[]{:S(2)}) copy-start(bf16[512,1024]{1,0:T(8,128)(2,1)S(1)} %reshape.68.refs_5_.refs_9_) | copy-start | bytes 3145732
  114.6 65.8 %collective-permute-start.3 = (bf16[640,2048]{1,0:T(8,128)(2,1)}, bf16[640,2048]{1,0:T(8,128)(2,1)}, u32[]{:S(2)}, u32[]{:S(2)}) collective-permute-start(bf16[640,2048]{1,0:T(8,128)(2,1)} %pick_columns.7.refs_1_), channel_id=1, source_target_pairs={{0,1},{1,0},{2,3},{3,2},{4,5},{5,4},{6,7},{7,6},{8,9},{9,8},{10,11... | collective-permute-start | bytes 7864328 | tf_op jit(solution)/shard_map/ppermute | solution.py:287
  115.1 65.2 %collective-permute-start.1 = (bf16[512,1024]{1,0:T(8,128)(2,1)S(1)}, bf16[512,1024]{1,0:T(8,128)(2,1)}, u32[]{:S(2)}, u32[]{:S(2)}) collective-permute-start(bf16[512,1024]{1,0:T(8,128)(2,1)S(1)} %reshape.68.refs_5_.refs_9_), channel_id=1, source_target_pairs={{4,0},{8,4},{12,8},{14,12},{10,14},{6,10},{2,6},{0,2},{5,1},{9,5},... | collective-permute-start | bytes 3145736 | tf_op jit(solution)/shard_map/ppermute | solution.py:277
  117.7 62.7 %collective-permute-start = (bf16[512,1024]{1,0:T(8,128)(2,1)S(1)}, bf16[512,1024]{1,0:T(8,128)(2,1)}, u32[]{:S(2)}, u32[]{:S(2)}) collective-permute-start(bf16[512,1024]{1,0:T(8,128)(2,1)S(1)} %reshape.68.refs_5_.refs_9_), channel_id=1, source_target_pairs={{0,4},{4,8},{8,12},{12,14},{14,10},{10,6},{6,2},{2,0},{1,5},{5,9},... | collective-permute-start | bytes 3145736 | tf_op jit(solution)/shard_map/ppermute | solution.py:277
  117.9 62.5 %collective-permute-start.2 = (bf16[224,2048]{1,0:T(8,128)(2,1)}, bf16[224,2048]{1,0:T(8,128)(2,1)}, u32[]{:S(2)}, u32[]{:S(2)}) collective-permute-start(bf16[224,2048]{1,0:T(8,128)(2,1)} %pick_columns.6), channel_id=1, source_target_pairs={{0,16},{16,0},{1,17},{17,1},{2,18},{18,2},{3,19},{19,3},{4,20},{20... | collective-permute-start | bytes 2752520 | tf_op jit(solution)/shard_map/ppermute | solution.py:283
  120.6 59.7 %all-to-all-start = ((bf16[8,3,4096]{2,1,0:T(4,128)(2,1)}), bf16[8,3,4096]{2,1,0:T(4,128)(2,1)S(1)}, u32[]{:S(2)}, u32[]{:S(2)}) async-start(bf16[8,3,4096]{2,1,0:T(4,128)(2,1)} %copy.18), calls=%async_computation | async-start | bytes 524288 | tf_op jit(solution)/shard_map/all_to_all | solution.py:289
  180.4 29.3 %collective-permute-start.4 = (bf16[512,1024]{1,0:T(8,128)(2,1)}, bf16[512,1024]{1,0:T(8,128)(2,1)}, u32[]{:S(2)}, u32[]{:S(2)}) collective-permute-start(bf16[512,1024]{1,0:T(8,128)(2,1)} %collective-permute-done.refs_6_.refs_10_), channel_id=1, source_target_pairs={{0,4},{4,8},{8,12},{12,14},{14,10},{10,6},{6,2},{2,0},{1,5},{5,9},... | collective-permute-start | bytes 3145736 | tf_op jit(solution)/shard_map/ppermute | solution.py:277
  182.5 27.2 %collective-permute-start.5 = (bf16[512,1024]{1,0:T(8,128)(2,1)}, bf16[512,1024]{1,0:T(8,128)(2,1)}, u32[]{:S(2)}, u32[]{:S(2)}) collective-permute-start(bf16[512,1024]{1,0:T(8,128)(2,1)} %collective-permute-done.1.refs_7_.refs_11_), channel_id=1, source_target_pairs={{4,0},{8,4},{12,8},{14,12},{10,14},{6,10},{2,6},{0,2},{5,1},{9,5},... | collective-permute-start | bytes 3145736 | tf_op jit(solution)/shard_map/ppermute | solution.py:277
  182.6 27.1 %collective-permute-start.6 = (bf16[224,2048]{1,0:T(8,128)(2,1)}, bf16[224,2048]{1,0:T(8,128)(2,1)}, u32[]{:S(2)}, u32[]{:S(2)}) collective-permute-start(bf16[224,2048]{1,0:T(8,128)(2,1)} %pick_columns.8), channel_id=1, source_target_pairs={{0,16},{16,0},{1,17},{17,1},{2,18},{18,2},{3,19},{19,3},{4,20},{20... | collective-permute-start | bytes 2752520 | tf_op jit(solution)/shard_map/ppermute | solution.py:294
  183.1 26.6 %collective-permute-start.9 = (bf16[224,2048]{1,0:T(8,128)(2,1)}, bf16[224,2048]{1,0:T(8,128)(2,1)}, u32[]{:S(2)}, u32[]{:S(2)}) collective-permute-start(bf16[224,2048]{1,0:T(8,128)(2,1)} %collective-permute-done.2.refs_1_), channel_id=1, source_target_pairs={{0,1},{1,0},{2,3},{3,2},{4,5},{5,4},{6,7},{7,6},{8,9},{9,8},{10,11... | collective-permute-start | bytes 2752520 | tf_op jit(solution)/shard_map/ppermute | solution.py:303
  189.1 17.5 %collective-permute-start.7 = (bf16[32,2048]{1,0:T(8,128)(2,1)}, bf16[32,2048]{1,0:T(8,128)(2,1)S(1)}, u32[]{:S(2)}, u32[]{:S(2)}) collective-permute-start(bf16[32,2048]{1,0:T(8,128)(2,1)} %pick_columns.11), channel_id=1, source_target_pairs={{0,16},{16,0},{1,17},{17,1},{2,18},{18,2},{3,19},{19,3},{4,20},{20... | collective-permute-start | bytes 393224 | tf_op jit(solution)/shard_map/ppermute | solution.py:299
  207.5 2.1 collective-permute-start.8
  209.7 26.3 %collective-permute-start.10 = (bf16[512,1024]{1,0:T(8,128)(2,1)}, bf16[512,1024]{1,0:T(8,128)(2,1)}, u32[]{:S(2)}, u32[]{:S(2)}) collective-permute-start(bf16[512,1024]{1,0:T(8,128)(2,1)} %collective-permute-done.4.refs_8_.refs_12_), channel_id=1, source_target_pairs={{0,4},{4,8},{8,12},{12,14},{14,10},{10,6},{6,2},{2,0},{1,5},{5,9},... | collective-permute-start | bytes 3145736 | tf_op jit(solution)/shard_map/ppermute | solution.py:277
  211.4 26.3 %collective-permute-start.11 = (bf16[512,1024]{1,0:T(8,128)(2,1)}, bf16[512,1024]{1,0:T(8,128)(2,1)}, u32[]{:S(2)}, u32[]{:S(2)}) collective-permute-start(bf16[512,1024]{1,0:T(8,128)(2,1)} %collective-permute-done.5.refs_9_.refs_13_), channel_id=1, source_target_pairs={{4,0},{8,4},{12,8},{14,12},{10,14},{6,10},{2,6},{0,2},{5,1},{9,5},... | collective-permute-start | bytes 3145736 | tf_op jit(solution)/shard_map/ppermute | solution.py:277
  212.1 31.5 %collective-permute-start.13 = (bf16[224,2048]{1,0:T(8,128)(2,1)}, bf16[224,2048]{1,0:T(8,128)(2,1)}, u32[]{:S(2)}, u32[]{:S(2)}) collective-permute-start(bf16[224,2048]{1,0:T(8,128)(2,1)} %collective-permute-done.6.refs_3_), channel_id=1, source_target_pairs={{0,1},{1,0},{2,3},{3,2},{4,5},{5,4},{6,7},{7,6},{8,9},{9,8},{10,11... | collective-permute-start | bytes 2752520 | tf_op jit(solution)/shard_map/ppermute | solution.py:328
  212.1 27.3 %collective-permute-start.12 = (bf16[192,2048]{1,0:T(8,128)(2,1)}, bf16[192,2048]{1,0:T(8,128)(2,1)}, u32[]{:S(2)}, u32[]{:S(2)}) collective-permute-start(bf16[192,2048]{1,0:T(8,128)(2,1)} %pick_columns.9), channel_id=1, source_target_pairs={{0,16},{16,0},{1,17},{17,1},{2,18},{18,2},{3,19},{19,3},{4,20},{20... | collective-permute-start | bytes 2359304 | tf_op jit(solution)/shard_map/ppermute | solution.py:327
  213.7 29.8 %all-to-all-start.1 = ((bf16[8,3,4096]{2,1,0:T(4,128)(2,1)}), bf16[8,3,4096]{2,1,0:T(4,128)(2,1)}, u32[]{:S(2)}, u32[]{:S(2)}) async-start(bf16[8,3,4096]{2,1,0:T(4,128)(2,1)} %copy.20), calls=%async_computation.1 | async-start | bytes 524288 | tf_op jit(solution)/shard_map/all_to_all | solution.py:329
  243.5 5.6 %collective-permute-start.16 = (bf16[192,2048]{1,0:T(8,128)(2,1)}, bf16[192,2048]{1,0:T(8,128)(2,1)}, u32[]{:S(2)}, u32[]{:S(2)}) collective-permute-start(bf16[192,2048]{1,0:T(8,128)(2,1)} %collective-permute-done.12.refs_5_), channel_id=1, source_target_pairs={{0,1},{1,0},{2,3},{3,2},{4,5},{5,4},{6,7},{7,6},{8,9},{9,8},{10,11... | collective-permute-start | bytes 2359304 | tf_op jit(solution)/shard_map/ppermute | solution.py:348
  243.9 13.7 %collective-permute-start.14 = (bf16[256,512]{1,0:T(8,128)(2,1)}, bf16[256,512]{1,0:T(8,128)(2,1)S(1)}, u32[]{:S(2)}, u32[]{:S(2)}) collective-permute-start(bf16[256,512]{1,0:T(8,128)(2,1)} %slice.57), channel_id=1, source_target_pairs={{0,4},{4,8},{8,12},{12,14},{14,10},{10,6},{6,2},{2,0},{1,5},{5,9},... | collective-permute-start | bytes 786440 | tf_op jit(solution)/shard_map/ppermute | solution.py:277
  244.0 13.6 %collective-permute-start.15 = (bf16[256,512]{1,0:T(8,128)(2,1)}, bf16[256,512]{1,0:T(8,128)(2,1)S(1)}, u32[]{:S(2)}, u32[]{:S(2)}) collective-permute-start(bf16[256,512]{1,0:T(8,128)(2,1)} %slice.58), channel_id=1, source_target_pairs={{4,0},{8,4},{12,8},{14,12},{10,14},{6,10},{2,6},{0,2},{5,1},{9,5},... | collective-permute-start | bytes 786440 | tf_op jit(solution)/shard_map/ppermute | solution.py:277
  265.0 11.7 %collective-permute-start.18 = (bf16[256,512]{1,0:T(8,128)(2,1)S(1)}, bf16[256,512]{1,0:T(8,128)(2,1)S(1)}, u32[]{:S(2)}, u32[]{:S(2)}) collective-permute-start(bf16[256,512]{1,0:T(8,128)(2,1)S(1)} %slice.47), channel_id=1, source_target_pairs={{0,4},{4,8},{8,12},{12,14},{14,10},{10,6},{6,2},{2,0},{1,5},{5,9},... | collective-permute-start | bytes 786440 | tf_op jit(solution)/shard_map/ppermute | solution.py:277
  265.1 11.6 %collective-permute-start.19 = (bf16[256,512]{1,0:T(8,128)(2,1)S(1)}, bf16[256,512]{1,0:T(8,128)(2,1)S(1)}, u32[]{:S(2)}, u32[]{:S(2)}) collective-permute-start(bf16[256,512]{1,0:T(8,128)(2,1)S(1)} %slice.48), channel_id=1, source_target_pairs={{4,0},{8,4},{12,8},{14,12},{10,14},{6,10},{2,6},{0,2},{5,1},{9,5},... | collective-permute-start | bytes 786440 | tf_op jit(solution)/shard_map/ppermute | solution.py:277
  267.1 17.7 %collective-permute-start.17 = (f16[672,512]{1,0:T(8,128)(2,1)S(1)}, f16[672,512]{1,0:T(8,128)(2,1)S(1)}, u32[]{:S(2)}, u32[]{:S(2)}) collective-permute-start(f16[672,512]{1,0:T(8,128)(2,1)S(1)} %multiply_convert_fusion.1), channel_id=1, source_target_pairs={{0,16},{16,0},{1,17},{17,1},{2,18},{18,2},{3,19},{19,3},{4,20},{20... | collective-permute-start | bytes 2064392 | tf_op jit(solution)/shard_map/ppermute | solution.py:359
  284.8 18.6 %collective-permute-start.20 = (f16[672,512]{1,0:T(8,128)(2,1)S(1)}, f16[672,512]{1,0:T(8,128)(2,1)S(1)}, u32[]{:S(2)}, u32[]{:S(2)}) collective-permute-start(f16[672,512]{1,0:T(8,128)(2,1)S(1)} %multiply_convert_fusion), channel_id=1, source_target_pairs={{0,16},{16,0},{1,17},{17,1},{2,18},{18,2},{3,19},{19,3},{4,20},{20... | collective-permute-start | bytes 2064392 | tf_op jit(solution)/shard_map/ppermute | solution.py:364
  (14 other events, 169.6 us)

commit v5 on v4

--- a/solution.py
+++ b/solution.py
@@ -12,7 +12,7 @@
 HALF = HD // 2
 CHUNKS = 2
 MOST_SHARDS = 8
-VMEM_BYTES = 56 << 20
+VMEM_BYTES = 32 << 20
 MERGED = 4
 RAISE = 16.0
 
@@ -102,55 +102,51 @@
     )(projected, back, cosine, sine, key_info, query_info, queries)
 
 
-def pick_kernel(half, first, side_ref, source_ref, out_ref, sems):
-    rows, width = out_ref.shape
-    copies = []
-    for j in range(width // half):
-        at = pl.multiple_of((2 * j + side_ref[0]) * half, half)
-        copies.append(
-            pltpu.make_async_copy(
-                source_ref.at[first : first + rows, pl.ds(at, half)],
-                out_ref.at[:, j * half : (j + 1) * half],
-                sems.at[j],
-            )
-        )
-        copies[-1].start()
-    for copy in copies:
-        copy.wait()
+def pick_kernel(side_ref, source_ref, out_ref):
+    out_ref[...] = source_ref[...]
 
 
 def pick_columns(source, side, half, first, end):
-    count = source.shape[1] // (2 * half)
+    blocks = source.shape[1] // (2 * half)
+    rows = math.gcd(first, end) if first else end
     return pl.pallas_call(
-        functools.partial(pick_kernel, half, first),
-        out_shape=jax.ShapeDtypeStruct((end - first, count * half), source.dtype),
-        in_specs=[pl.BlockSpec(memory_space=pltpu.SMEM), pl.BlockSpec(memory_space=pl.ANY)],
-        out_specs=pl.BlockSpec(memory_space=pl.ANY),
-        scratch_shapes=[pltpu.SemaphoreType.DMA((count,))],
+        pick_kernel,
+        out_shape=jax.ShapeDtypeStruct((end - first, blocks * half), source.dtype),
+        grid_spec=pltpu.PrefetchScalarGridSpec(
+            num_scalar_prefetch=1,
+            grid=((end - first) // rows, blocks),
+            in_specs=[
+                pl.BlockSpec((rows, half), lambda i, j, s: (first // rows + i, 2 * j + s[0]))
+            ],
+            out_specs=pl.BlockSpec((rows, half), lambda i, j, s: (i, j)),
+        ),
         compiler_params=pltpu.CompilerParams(vmem_limit_bytes=VMEM_BYTES),
         cost_estimate=pl.CostEstimate(
-            flops=0, bytes_accessed=4 * (end - first) * count * half, transcendentals=0
+            flops=0, bytes_accessed=4 * (end - first) * blocks * half, transcendentals=0
         ),
         name="pick_columns",
     )(side.reshape(1), source)
 
 
-def product_kernel(depths, layout, column, has_total, *refs):
+def product_kernel(depths, layout, base, column, has_total, *refs):
     place_ref, refs = refs[0], refs[1:]
-    hidden, refs = refs[: len(layout)], refs[len(layout) :]
+    hidden, refs = refs[: 2 * len(layout)], refs[2 * len(layout) :]
     flat = [depth for pieces in depths for depth in pieces]
     weights, refs = refs[: len(flat)], refs[len(flat) :]
-    out_ref, held, piece, sems, piece_sems = refs[-5:]
-    shards = len(depths)
+    out_ref, held, piece, sems, piece_sems, total_sem = refs[-6:]
+    shards, width = len(depths), out_ref.shape[1]
     half = held.shape[1] // shards
-    spans = sorted({(part, at, rows) for part, at, rows, _, _, _ in layout})
+    blocks = hidden[0].shape[1] // half
+
+    def window(ref):
+        return ref if ref.shape[1] == width else ref.at[:, column : column + width]
+
+    if has_total:
+        total_copy = pltpu.make_async_copy(window(refs[0]), out_ref, total_sem)
+        total_copy.start()
     tops = [sum(flat[:i]) for i in range(len(flat))]
     copies = [
-        pltpu.make_async_copy(
-            w.at[:, column : column + piece.shape[1]] if w.shape[1] > piece.shape[1] else w,
-            piece.at[top : top + depth, :],
-            piece_sems.at[i],
-        )
+        pltpu.make_async_copy(window(w), piece.at[top : top + depth, :], piece_sems.at[i])
         for i, (w, top, depth) in enumerate(zip(weights, tops, flat))
     ]
     done = 0
@@ -158,24 +154,24 @@
         for _ in depths[p]:
             copies[done].start()
             done += 1
-        for (part, at, rows, row, first, blocks), source in zip(layout, hidden):
-            block = place_ref[p] - first
-
-            @pl.when((block >= 0) & (block < blocks))
+        place = place_ref[base + p]
+        for core in range(2):
+
+            @pl.when(place // blocks == core)
             def _():
-                columns = pl.ds(pl.multiple_of(block * half, half), half)
-                pltpu.make_async_copy(
-                    source.at[row : row + rows, columns],
-                    held.at[at : at + rows, p * half : (p + 1) * half],
-                    sems.at[p, part],
-                ).start()
-
-    total = refs[0][...] if has_total else None
-    waited = 0
+                columns = pl.ds(pl.multiple_of((place - core * blocks) * half, half), half)
+                for part, (row, at, rows) in enumerate(layout):
+                    pltpu.make_async_copy(
+                        hidden[2 * part + core].at[row : row + rows, columns],
+                        held.at[at : at + rows, p * half : (p + 1) * half],
+                        sems.at[p, part],
+                    ).start()
+
+    total, waited = None, 0
     for begin in range(0, shards, MERGED):
         end = min(begin + MERGED, shards)
         for p in range(begin, end):
-            for part, at, rows in spans:
+            for part, (_, at, rows) in enumerate(layout):
                 target = held.at[at : at + rows, p * half : (p + 1) * half]
                 pltpu.make_async_copy(target, target, sems.at[p, part]).wait()
             for _ in depths[p]:
@@ -184,39 +180,39 @@
         span = slice(begin * half, end * half)
         term = jnp.dot(held[:, span], piece[span, :], preferred_element_type=jnp.float32)
         total = term if total is None else total + term
+    if has_total:
+        total_copy.wait()
+        total = out_ref[...] + total
     out_ref[...] = total
 
 
-def products(total, hidden, weights, places, column, width):
+def products(total, hidden, weights, places, base, column, width):
     shards = len(weights)
     flat = [w for shard in weights for w in shard]
     depths = tuple(tuple(w.shape[0] for w in shard) for shard in weights)
     half = sum(depths[0])
     operands, layout, at = [places], [], 0
-    for part, (row, rows, pieces) in enumerate(hidden):
-        first = 0
-        for piece in pieces:
-            operands.append(piece)
-            layout.append((part, at, rows, row, first, piece.shape[1] // half))
-            first += piece.shape[1] // half
+    for row, rows, pair in hidden:
+        operands += pair
+        layout.append((row, at, rows))
         at += rows
     operands += flat
-    vmem = pl.BlockSpec(memory_space=pltpu.VMEM)
-    in_specs = [pl.BlockSpec(memory_space=pltpu.SMEM)]
-    in_specs += [pl.BlockSpec(memory_space=pl.ANY)] * (len(layout) + len(flat))
     if total is not None:
         operands.append(total)
-        in_specs.append(vmem)
     return pl.pallas_call(
-        functools.partial(product_kernel, depths, tuple(layout), column, total is not None),
+        functools.partial(
+            product_kernel, depths, tuple(layout), base, column, total is not None
+        ),
         out_shape=jax.ShapeDtypeStruct((at, width), jnp.float32),
-        in_specs=in_specs,
-        out_specs=vmem,
+        in_specs=[pl.BlockSpec(memory_space=pltpu.SMEM)]
+        + [pl.BlockSpec(memory_space=pl.ANY)] * (len(operands) - 1),
+        out_specs=pl.BlockSpec(memory_space=pltpu.VMEM),
         scratch_shapes=[
             pltpu.VMEM((at, shards * half), jnp.bfloat16),
             pltpu.VMEM((shards * half, width), jnp.bfloat16),
             pltpu.SemaphoreType.DMA((shards, len(hidden))),
             pltpu.SemaphoreType.DMA((len(flat),)),
+            pltpu.SemaphoreType.DMA,
         ],
         compiler_params=pltpu.CompilerParams(vmem_limit_bytes=VMEM_BYTES),
         cost_estimate=pl.CostEstimate(
@@ -276,8 +272,7 @@
     def step(pair):
         return lax.ppermute(pair[0], "rows", onward), lax.ppermute(pair[1], "rows", back)
 
-    third = -(-tokens // 48) * 16
-    cuts = (0, third, 2 * third, tokens)
+    cuts = (0, 2 * tokens // 5, 4 * tokens // 5, tokens)
     sent = [pick_columns(passages, 1 - side, half, cuts[0], cuts[1])]
     own, sent[0], passages, new_hidden = fence(own, sent[0], passages, new_hidden)
     got = [lax.ppermute(sent[0], "groups", partners)]
@@ -301,17 +296,18 @@
     new_kept = jnp.concatenate([new_kept, new_got], 0)
     new_other = lax.ppermute(new_kept, "tensor", cores)
     got_other = [lax.ppermute(got[0], "tensor", cores)]
-    ring[1], got[1], new_other, got_other, places, queries = fence(
-        ring[1], got[1], new_other, got_other, places, queries
-    )
+    moved = lax.all_to_all(queries, "rows", split_axis=0, concat_axis=0, tiled=True)
+    ring[1], got[1], new_other, got_other, places, moved = fence(
+        ring[1], got[1], new_other, got_other, places, moved
+    )
+    query_rows = jnp.swapaxes(moved, 0, 1).reshape(count, -1)
 
     def project(hidden, total, begin, end, column, width):
         weights = [(own,)] + [(w,) for pair in ring for w in pair]
         weights = weights[: row_count - 1] + [last[column // width] if last else ()]
         for at in range(begin, end, MOST_SHARDS):
             some = weights[at : min(at + MOST_SHARDS, end)]
-            spots = places[at : at + len(some)]
-            total = products(total, hidden, some, spots, column, width)
+            total = products(total, hidden, some, places, at, column, width)
         return total
 
     def homeward(total):
@@ -326,7 +322,6 @@
         else:
             got.append(lax.ppermute(sent[2], "groups", partners))
             got_other.append(lax.ppermute(got[1], "tensor", cores))
-            moved = lax.all_to_all(queries, "rows", split_axis=0, concat_axis=0, tiled=True)
         ring.append(step(ring[-1]))
     held = project(own_hidden, None, 0, early, 0, 2 * width)
     position, key_info, query_info = token_tables(
@@ -339,10 +334,9 @@
         return ring[-1][0][: half // 2, columns], ring[-1][1][half // 2 :, columns]
 
     ends = [halved(0)]
-    ring[-1], got[2], got_other, moved, held, ends, places, cosine, sine = fence(
-        ring[-1], got[2], got_other, moved, held, ends, places, cosine, sine
-    )
-    query_rows = jnp.swapaxes(moved, 0, 1).reshape(count, -1)
+    ring[-1], got[2], got_other, held, ends, places, cosine, sine = fence(
+        ring[-1], got[2], got_other, held, ends, places, cosine, sine
+    )
 
     last.append(step(ends[0]))
     got_other.append(lax.ppermute(got[2], "tensor", cores))
@@ -365,8 +359,7 @@
     outs = []
     for c in range(CHUNKS):
         back_home = homed[c].astype(jnp.float32) * (1.0 / RAISE)
-        mine = held[:, c * width : (c + 1) * width]
-        mine = project(own_hidden, mine, early, row_count, c * width, width)
+        mine = project(own_hidden, held, early, row_count, c * width, width)
         at = c * chunk * group
         query = query_rows[:, at : at + chunk * group]
         outs.append(finish(mine, back_home, cosine, sine, key_info, query_info, query))

time: 320 us -> 171 us (0.53)
  Pallas kernels: 225 us -> 43.9 us
  waiting for transfers between devices: 19.8 us -> 52.2 us
    pallas_call x13, Pallas kernels: 222 us -> 40.4 us  [the longest x7 34.4 us: products(): pl.pallas_call(functools.partial(product_kernel, depths, tuple(layout), b...]
    all_to_all x1, waiting for transfers between devices: 0.01 us -> 20.1 us  [body(): lax.all_to_all(new_hidden, 'rows', split_axis=0, concat_axis=0, tiled=True)]
    unnamed x30 -> x38, local copies, waits for them, and re-layouts: 5.37 us -> 12.3 us
    ppermute x1, waiting for transfers between devices: 0.01 us -> 4.6 us  [body(): homed.append(lax.ppermute(away[1], 'groups', partners))]
    ppermute x1, waiting for transfers between devices: 9.96 us -> 14.2 us  [body(): new_got = lax.ppermute(new_sent, 'groups', partners)]
    slice x4 -> x0, local copies, waits for them, and re-layouts: 3.77 us -> none  [the longest x3 1.95 us: project(): spots = places[at:at + len(some)]]
    ppermute x5, waiting for transfers between devices: 5.61 us -> 9.14 us  [step(): lax.ppermute(pair[0], 'rows', onward)]
  transfers between devices with their start and end apart: 23 -> 23, of which waited for: 4 -> 6; matrix products, arithmetic and copies ran while one was open for 6% -> 10% of each run, Pallas kernels for 34% -> 21%
where the time goes in v5:
time: 171 us
  waiting for transfers between devices  52.2 us (31%)
  Pallas kernels  43.9 us (26%)
  starting transfers between devices  27.7 us (16%)
  local copies, waits for them, and re-layouts  25.5 us (15%)
  blocking collectives  11.8 us (7%)
  other arithmetic  8.87 us (5%)
    pallas_call x7, Pallas kernels, products(): pl.pallas_call(functools.partial(product_kernel, depths, tuple(layout), b...  34.4 us
    all_to_all x1, waiting for transfers between devices, body(): lax.all_to_all(new_hidden, 'rows', split_axis=0, concat_axis=0, tiled=True)  20.1 us
    ppermute x1, waiting for transfers between devices, body(): new_got = lax.ppermute(new_sent, 'groups', partners)  14.2 us
    unnamed x38, local copies, waits for them, and re-layouts  12.3 us
    all_to_all x1, blocking collectives, body(): lax.all_to_all(attended, 'rows', split_axis=0, concat_axis=0, tiled=True)  11.8 us
    ppermute x5, waiting for transfers between devices, step(): lax.ppermute(pair[0], 'rows', onward)  9.14 us
    ppermute x5, starting transfers between devices, step(): lax.ppermute(pair[1], 'rows', back)  7.15 us
    pallas_call x6, Pallas kernels, pick_columns(): pl.pallas_call(pick_kernel, out_shape=jax.ShapeDtypeStruct((end - first,...  6.03 us
  transfers between devices with their start and end apart: 23, of which 6 were waited for; matrix products, arithmetic and copies ran while one was open for 10% of the time, Pallas kernels for 21%

profile of v5, /device:TPU:0, one launch (start us, length us, event | category | flops | bytes accessed | tf_op | source)
XLA Modules:
  0.0 170.5 jit_solution(9205762828083283042)
XLA Ops:
  3.9 2.5 %copy-done.1 = bf16[640,4096]{1,0:T(8,128)(2,1)S(1)} copy-done((bf16[640,4096]{1,0:T(8,128)(2,1)S(1)}, bf16[640,4096]{1,0:T(8,128)(2,1)}, u32[]{:S(2)}) %copy-start.1) | copy-done | bytes 5242904
  9.3 2.4 %pick_columns.7.refs_1_ = bf16[640,2048]{1,0:T(8,128)(2,1)} custom-call(s32[1]{0:T(128)} %bitcast.3.side_ref, bf16[640,4096]{1,0:T(8,128)(2,1)S(1)} %copy-done.2), custom_call_target="tpu_custom_call" | custom-call | bytes 5242880 | tf_op jit(solution)/shard_map/pick_columns/pallas_call | solution.py:112
  12.1 2.5 %collective-permute-start.2 = (bf16[256,2048]{1,0:T(8,128)(2,1)}, bf16[256,2048]{1,0:T(8,128)(2,1)S(1)}, u32[]{:S(2)}, u32[]{:S(2)}) collective-permute-start(bf16[256,2048]{1,0:T(8,128)(2,1)} %pick_columns.6), channel_id=1, source_target_pairs={{0,16},{16,0},{1,17},{17,1},{2,18},{18,2},{3,19},{19,3},{4,20},{20... | collective-permute-start | bytes 3145736 | tf_op jit(solution)/shard_map/ppermute | solution.py:278
  17.4 5.8 %all-to-all-start = ((bf16[8,3,4096]{2,1,0:T(4,128)(2,1)}), bf16[8,3,4096]{2,1,0:T(4,128)(2,1)S(1)}, u32[]{:S(2)}, u32[]{:S(2)}) async-start(bf16[8,3,4096]{2,1,0:T(4,128)(2,1)} %copy.18), calls=%async_computation | async-start | bytes 524288 | tf_op jit(solution)/shard_map/all_to_all | solution.py:284
  23.3 2.5 %copy-done.3 = bf16[640,4096]{1,0:T(8,128)(2,1)S(1)} copy-done((bf16[640,4096]{1,0:T(8,128)(2,1)S(1)}, bf16[640,4096]{1,0:T(8,128)(2,1)}, u32[]{:S(2)}) %copy-start.3) | copy-done | bytes 5242904
  28.1 20.1 %all-to-all-done = bf16[8,3,4096]{2,1,0:T(4,128)(2,1)S(1)} async-done(((bf16[8,3,4096]{2,1,0:T(4,128)(2,1)}), bf16[8,3,4096]{2,1,0:T(4,128)(2,1)S(1)}, u32[]{:S(2)}, u32[]{:S(2)}) %all-to-all-start) | async-done | bytes 196640 | tf_op jit(solution)/shard_map/all_to_all | solution.py:284
  54.9 1.8 %copy.20 = bf16[8,3,4096]{2,1,0:T(4,128)(2,1)} copy(bf16[8,3,4096]{2,0,1:T(8,128)(2,1)} %param.10) | data formatting | bytes 393216 | tf_op jit(solution)/shard_map/optimization_barrier | solution.py:234
  56.7 4.0 %all-to-all-start.1 = ((bf16[8,3,4096]{2,1,0:T(4,128)(2,1)}), bf16[8,3,4096]{2,1,0:T(4,128)(2,1)}, u32[]{:S(2)}, u32[]{:S(2)}) async-start(bf16[8,3,4096]{2,1,0:T(4,128)(2,1)} %copy.20), calls=%async_computation.1 | async-start | bytes 524288 | tf_op jit(solution)/shard_map/all_to_all | solution.py:299
  60.7 14.2 %collective-permute-done.7 = bf16[32,2048]{1,0:T(8,128)(2,1)} collective-permute-done((bf16[32,2048]{1,0:T(8,128)(2,1)}, bf16[32,2048]{1,0:T(8,128)(2,1)}, u32[]{:S(2)}, u32[]{:S(2)}) %collective-permute-start.7) | collective-permute-done | bytes 131104 | tf_op jit(solution)/shard_map/ppermute | solution.py:294
  79.0 1.8 %collective-permute-start.11 = (bf16[512,1024]{1,0:T(8,128)(2,1)}, bf16[512,1024]{1,0:T(8,128)(2,1)}, u32[]{:S(2)}, u32[]{:S(2)}) collective-permute-start(bf16[512,1024]{1,0:T(8,128)(2,1)} %collective-permute-done.5.refs_9_.refs_13_), channel_id=1, source_target_pairs={{4,0},{8,4},{12,8},{14,12},{10,14},{6,10},{2,6},{0,2},{5,1},{9,5},... | collective-permute-start | bytes 3145736 | tf_op jit(solution)/shard_map/ppermute | solution.py:273
  82.7 2.1 %multiply_sine_fusion = (f32[672,64]{1,0:T(8,128)}, f32[672,64]{1,0:T(8,128)}) fusion(f32[64]{0:T(128)S(1)} %multiply_exponential_fusion, f32[672]{0:T(1024)S(1)} %get-tuple-element.100), kind=kLoop, calls=%fused_computation.4 | loop fusion | flops 43008 | bytes 347008 | tf_op jit(solution)/shard_map/sin | solution.py:24
  84.8 7.9 %products.7.refs_9_ = f32[672,1024]{1,0:T(8,128)S(1)} custom-call(s32[8]{0:T(128)S(1)} %fusion.2.refs_0_, bf16[640,2048]{1,0:T(8,128)(2,1)} %pick_columns.7.refs_1_, bf16[640,2048]{1,0:T(8,128)(2,1)} %collective-permute-done.3.refs_2_, bf16[64,2048]{1,0:T(8,128)(2,1)S(1)} %pad_maximum_fusion.refs_3_.refs_7_, ...), custom_call_target="tpu_custom_call" | custom-call | flops 3523215360 | bytes 11436032 | tf_op jit(solution)/shard_map/products/pallas_call | solution.py:202
  94.2 9.1 %collective-permute-done.10.refs_14_.refs_5_ = bf16[512,1024]{1,0:T(8,128)(2,1)S(1)} collective-permute-done((bf16[512,1024]{1,0:T(8,128)(2,1)}, bf16[512,1024]{1,0:T(8,128)(2,1)S(1)}, u32[]{:S(2)}, u32[]{:S(2)}) %collective-permute-start.10) | collective-permute-done | bytes 1048608 | tf_op jit(solution)/shard_map/ppermute | solution.py:273
  110.4 6.5 %products.8.refs_11_ = f32[672,512]{1,0:T(8,128)S(1)} custom-call(s32[8]{0:T(128)S(1)} %fusion.2.refs_0_, bf16[256,2048]{1,0:T(8,128)(2,1)S(1)} %copy-done.7, bf16[256,2048]{1,0:T(8,128)(2,1)} %collective-permute-done.9.refs_2_, bf16[256,2048]{1,0:T(8,128)(2,1)} %collective-permute-done.6.refs_3_, bf16[256,2048]{1,0:T(8,128)(2,1)} %collective-permute-done.13.refs_4_, ...), custom_call_target="tpu_custom_call" | custom-call | flops 2466250752 | bytes 9863168 | tf_op jit(solution)/shard_map/products/pallas_call | solution.py:202
  116.9 2.6 %products.9 = f32[672,512]{1,0:T(8,128)S(1)} custom-call(s32[8]{0:T(128)S(1)} %fusion.2.refs_0_, bf16[256,2048]{1,0:T(8,128)(2,1)S(1)} %copy-done.7, bf16[256,2048]{1,0:T(8,128)(2,1)} %collective-permute-done.9.refs_2_, bf16[256,2048]{1,0:T(8,128)(2,1)} %collective-permute-done.6.refs_3_, bf16[256,2048]{1,0:T(8,128)(2,1)} %collective-permute-done.13.refs_4_, ...), custom_call_target="tpu_custom_call" | custom-call | flops 352321536 | bytes 2588672 | tf_op jit(solution)/shard_map/products/pallas_call | solution.py:202
  125.7 6.5 %products.10.refs_11_ = f32[672,512]{1,0:T(8,128)S(1)} custom-call(s32[8]{0:T(128)S(1)} %fusion.2.refs_0_, bf16[256,2048]{1,0:T(8,128)(2,1)S(1)} %copy-done.8, bf16[256,2048]{1,0:T(8,128)(2,1)} %collective-permute-done.9.refs_2_, bf16[256,2048]{1,0:T(8,128)(2,1)} %collective-permute-done.6.refs_3_, bf16[256,2048]{1,0:T(8,128)(2,1)} %collective-permute-done.13.refs_4_, ...), custom_call_target="tpu_custom_call" | custom-call | flops 2466250752 | bytes 9863168 | tf_op jit(solution)/shard_map/products/pallas_call | solution.py:202
  132.3 2.8 %products.11 = f32[672,512]{1,0:T(8,128)S(1)} custom-call(s32[8]{0:T(128)S(1)} %fusion.2.refs_0_, bf16[256,2048]{1,0:T(8,128)(2,1)S(1)} %copy-done.9, bf16[256,2048]{1,0:T(8,128)(2,1)} %collective-permute-done.9.refs_2_, bf16[256,2048]{1,0:T(8,128)(2,1)} %collective-permute-done.6.refs_3_, bf16[256,2048]{1,0:T(8,128)(2,1)} %collective-permute-done.13.refs_4_, ...), custom_call_target="tpu_custom_call" | custom-call | flops 352321536 | bytes 2588672 | tf_op jit(solution)/shard_map/products/pallas_call | solution.py:202
  135.2 2.9 %collective-permute-done.17 = f16[672,512]{1,0:T(8,128)(2,1)} collective-permute-done((f16[672,512]{1,0:T(8,128)(2,1)}, f16[672,512]{1,0:T(8,128)(2,1)}, u32[]{:S(2)}, u32[]{:S(2)}) %collective-permute-start.17) | collective-permute-done | bytes 688160 | tf_op jit(solution)/shard_map/ppermute | solution.py:353
  138.7 4.0 %products.12.held_ref = f32[672,512]{1,0:T(8,128)S(1)} custom-call(s32[8]{0:T(128)S(1)} %fusion.2.refs_0_, bf16[640,2048]{1,0:T(8,128)(2,1)} %pick_columns.7.refs_1_, bf16[640,2048]{1,0:T(8,128)(2,1)} %collective-permute-done.3.refs_2_, bf16[64,2048]{1,0:T(8,128)(2,1)S(1)} %pad_maximum_fusion.refs_3_.refs_7_, ...), custom_call_target="tpu_custom_call" | custom-call | flops 1056964608 | bytes 5013504 | tf_op jit(solution)/shard_map/products/pallas_call | solution.py:202
  144.2 1.7 %rotate_attend.2 = bf16[24,2048]{1,0:T(8,128)(2,1)S(1)} custom-call(f32[672,512]{1,0:T(8,128)S(1)} %products.12.held_ref, f32[672,512]{1,0:T(8,128)S(1)} %convert_multiply_fusion.1.back_ref, f32[672,64]{1,0:T(8,128)S(1)} %copy-done.11, f32[672,64]{1,0:T(8,128)S(1)} %copy-done.10, s32[2,672]{1,0:T(2,128)S(1)} %pad_add_fusion.keys_ref, ...), custom_call_target="tpu_custom_call" | custom-call | flops 132120576 | bytes 2949120 | tf_op jit(solution)/shard_map/rotate_attend/pallas_call | solution.py:90
  145.9 4.2 %products.13.held_ref = f32[672,512]{1,0:T(8,128)S(1)} custom-call(s32[8]{0:T(128)S(1)} %fusion.2.refs_0_, bf16[640,2048]{1,0:T(8,128)(2,1)} %pick_columns.7.refs_1_, bf16[640,2048]{1,0:T(8,128)(2,1)} %collective-permute-done.3.refs_2_, bf16[64,2048]{1,0:T(8,128)(2,1)S(1)} %pad_maximum_fusion.refs_3_.refs_7_, ...), custom_call_target="tpu_custom_call" | custom-call | flops 1056964608 | bytes 5013504 | tf_op jit(solution)/shard_map/products/pallas_call | solution.py:202
  150.1 4.6 %collective-permute-done.20 = f16[672,512]{1,0:T(8,128)(2,1)} collective-permute-done((f16[672,512]{1,0:T(8,128)(2,1)S(1)}, f16[672,512]{1,0:T(8,128)(2,1)}, u32[]{:S(2)}, u32[]{:S(2)}) %collective-permute-start.20) | collective-permute-done | bytes 688160 | tf_op jit(solution)/shard_map/ppermute | solution.py:358
  156.0 1.7 %rotate_attend.3 = bf16[24,2048]{1,0:T(8,128)(2,1)S(1)} custom-call(f32[672,512]{1,0:T(8,128)S(1)} %products.13.held_ref, f32[672,512]{1,0:T(8,128)S(1)} %convert_multiply_fusion.back_ref, f32[672,64]{1,0:T(8,128)S(1)} %copy-done.11, f32[672,64]{1,0:T(8,128)S(1)} %copy-done.10, s32[2,672]{1,0:T(2,128)S(1)} %pad_add_fusion.keys_ref, ...), custom_call_target="tpu_custom_call" | custom-call | flops 132120576 | bytes 2949120 | tf_op jit(solution)/shard_map/rotate_attend/pallas_call | solution.py:90
  157.9 11.8 %all_to_all.15 = bf16[8,3,4096]{2,1,0:T(4,128)(2,1)S(1)} all-to-all(bf16[8,3,4096]{2,1,0:T(4,128)(2,1)S(1)} %bitcast.37), channel_id=1, replica_groups=mesh['groups'=2,'rows'=8,'tensor'=2] {'rows'}, dimensions={0} | all-to-all | bytes 393216 | tf_op jit(solution)/shard_map/all_to_all | solution.py:368
  (126 shorter events, 44.0 us)
Async XLA Ops:
  11.6 36.6 %collective-permute-start.3 = (bf16[640,2048]{1,0:T(8,128)(2,1)}, bf16[640,2048]{1,0:T(8,128)(2,1)}, u32[]{:S(2)}, u32[]{:S(2)}) collective-permute-start(bf16[640,2048]{1,0:T(8,128)(2,1)} %pick_columns.7.refs_1_), channel_id=1, source_target_pairs={{0,1},{1,0},{2,3},{3,2},{4,5},{5,4},{6,7},{7,6},{8,9},{9,8},{10,11... | collective-permute-start | bytes 7864328 | tf_op jit(solution)/shard_map/ppermute | solution.py:282
  12.1 36.1 %collective-permute-start.2 = (bf16[256,2048]{1,0:T(8,128)(2,1)}, bf16[256,2048]{1,0:T(8,128)(2,1)S(1)}, u32[]{:S(2)}, u32[]{:S(2)}) collective-permute-start(bf16[256,2048]{1,0:T(8,128)(2,1)} %pick_columns.6), channel_id=1, source_target_pairs={{0,16},{16,0},{1,17},{17,1},{2,18},{18,2},{3,19},{19,3},{4,20},{20... | collective-permute-start | bytes 3145736 | tf_op jit(solution)/shard_map/ppermute | solution.py:278
  14.6 33.7 %collective-permute-start.1 = (bf16[512,1024]{1,0:T(8,128)(2,1)}, bf16[512,1024]{1,0:T(8,128)(2,1)}, u32[]{:S(2)}, u32[]{:S(2)}) collective-permute-start(bf16[512,1024]{1,0:T(8,128)(2,1)} %reshape.68.refs_5_.refs_9_), channel_id=1, source_target_pairs={{4,0},{8,4},{12,8},{14,12},{10,14},{6,10},{2,6},{0,2},{5,1},{9,5},... | collective-permute-start | bytes 3145736 | tf_op jit(solution)/shard_map/ppermute | solution.py:273
  16.1 32.1 %collective-permute-start = (bf16[512,1024]{1,0:T(8,128)(2,1)}, bf16[512,1024]{1,0:T(8,128)(2,1)}, u32[]{:S(2)}, u32[]{:S(2)}) collective-permute-start(bf16[512,1024]{1,0:T(8,128)(2,1)} %reshape.68.refs_5_.refs_9_), channel_id=1, source_target_pairs={{0,4},{4,8},{8,12},{12,14},{14,10},{10,6},{6,2},{2,0},{1,5},{5,9},... | collective-permute-start | bytes 3145736 | tf_op jit(solution)/shard_map/ppermute | solution.py:273
  17.4 30.7 %all-to-all-start = ((bf16[8,3,4096]{2,1,0:T(4,128)(2,1)}), bf16[8,3,4096]{2,1,0:T(4,128)(2,1)S(1)}, u32[]{:S(2)}, u32[]{:S(2)}) async-start(bf16[8,3,4096]{2,1,0:T(4,128)(2,1)} %copy.18), calls=%async_computation | async-start | bytes 524288 | tf_op jit(solution)/shard_map/all_to_all | solution.py:284
  48.2 27.7 %copy-start.6 = (bf16[256,2048]{1,0:T(8,128)(2,1)}, bf16[256,2048]{1,0:T(8,128)(2,1)S(1)}, u32[]{:S(2)}) copy-start(bf16[256,2048]{1,0:T(8,128)(2,1)S(1)} %collective-permute-done.2.refs_1_) | copy-start | bytes 3145732
  48.2 30.5 %collective-permute-start.6 = (bf16[256,2048]{1,0:T(8,128)(2,1)}, bf16[256,2048]{1,0:T(8,128)(2,1)}, u32[]{:S(2)}, u32[]{:S(2)}) collective-permute-start(bf16[256,2048]{1,0:T(8,128)(2,1)} %copy-done.12), channel_id=1, source_target_pairs={{0,16},{16,0},{1,17},{17,1},{2,18},{18,2},{3,19},{19,3},{4,20},{20... | collective-permute-start | bytes 3145736 | tf_op jit(solution)/shard_map/ppermute | solution.py:289
  48.8 29.9 %collective-permute-start.4 = (bf16[512,1024]{1,0:T(8,128)(2,1)}, bf16[512,1024]{1,0:T(8,128)(2,1)}, u32[]{:S(2)}, u32[]{:S(2)}) collective-permute-start(bf16[512,1024]{1,0:T(8,128)(2,1)} %collective-permute-done.refs_6_.refs_10_), channel_id=1, source_target_pairs={{0,4},{4,8},{8,12},{12,14},{14,10},{10,6},{6,2},{2,0},{1,5},{5,9},... | collective-permute-start | bytes 3145736 | tf_op jit(solution)/shard_map/ppermute | solution.py:273
  49.8 28.9 %collective-permute-start.5 = (bf16[512,1024]{1,0:T(8,128)(2,1)}, bf16[512,1024]{1,0:T(8,128)(2,1)}, u32[]{:S(2)}, u32[]{:S(2)}) collective-permute-start(bf16[512,1024]{1,0:T(8,128)(2,1)} %collective-permute-done.1.refs_7_.refs_11_), channel_id=1, source_target_pairs={{4,0},{8,4},{12,8},{14,12},{10,14},{6,10},{2,6},{0,2},{5,1},{9,5},... | collective-permute-start | bytes 3145736 | tf_op jit(solution)/shard_map/ppermute | solution.py:273
  50.9 27.9 %collective-permute-start.9 = (bf16[256,2048]{1,0:T(8,128)(2,1)S(1)}, bf16[256,2048]{1,0:T(8,128)(2,1)}, u32[]{:S(2)}, u32[]{:S(2)}) collective-permute-start(bf16[256,2048]{1,0:T(8,128)(2,1)S(1)} %collective-permute-done.2.refs_1_), channel_id=1, source_target_pairs={{0,1},{1,0},{2,3},{3,2},{4,5},{5,4},{6,7},{7,6},{8,9},{9,8},{10,11... | collective-permute-start | bytes 3145736 | tf_op jit(solution)/shard_map/ppermute | solution.py:298
  52.4 22.6 %collective-permute-start.7 = (bf16[32,2048]{1,0:T(8,128)(2,1)}, bf16[32,2048]{1,0:T(8,128)(2,1)}, u32[]{:S(2)}, u32[]{:S(2)}) collective-permute-start(bf16[32,2048]{1,0:T(8,128)(2,1)} %pick_columns.11), channel_id=1, source_target_pairs={{0,16},{16,0},{1,17},{17,1},{2,18},{18,2},{3,19},{19,3},{4,20},{20... | collective-permute-start | bytes 393224 | tf_op jit(solution)/shard_map/ppermute | solution.py:294
  56.7 22.0 %all-to-all-start.1 = ((bf16[8,3,4096]{2,1,0:T(4,128)(2,1)}), bf16[8,3,4096]{2,1,0:T(4,128)(2,1)}, u32[]{:S(2)}, u32[]{:S(2)}) async-start(bf16[8,3,4096]{2,1,0:T(4,128)(2,1)} %copy.20), calls=%async_computation.1 | async-start | bytes 524288 | tf_op jit(solution)/shard_map/all_to_all | solution.py:299
  75.9 2.8 %collective-permute-start.8 = (bf16[64,2048]{1,0:T(8,128)(2,1)S(1)}, bf16[64,2048]{1,0:T(8,128)(2,1)}, u32[]{:S(2)}, u32[]{:S(2)}) collective-permute-start(bf16[64,2048]{1,0:T(8,128)(2,1)S(1)} %pad_maximum_fusion.refs_3_.refs_7_), channel_id=1, source_target_pairs={{0,1},{1,0},{2,3},{3,2},{4,5},{5,4},{6,7},{7,6},{8,9},{9,8},{10,11... | collective-permute-start | bytes 786440 | tf_op jit(solution)/shard_map/ppermute | solution.py:297
  78.7 24.6 %collective-permute-start.10 = (bf16[512,1024]{1,0:T(8,128)(2,1)}, bf16[512,1024]{1,0:T(8,128)(2,1)S(1)}, u32[]{:S(2)}, u32[]{:S(2)}) collective-permute-start(bf16[512,1024]{1,0:T(8,128)(2,1)} %collective-permute-done.4.refs_8_.refs_12_), channel_id=1, source_target_pairs={{0,4},{4,8},{8,12},{12,14},{14,10},{10,6},{6,2},{2,0},{1,5},{5,9},... | collective-permute-start | bytes 3145736 | tf_op jit(solution)/shard_map/ppermute | solution.py:273
  79.0 25.1 %collective-permute-start.11 = (bf16[512,1024]{1,0:T(8,128)(2,1)}, bf16[512,1024]{1,0:T(8,128)(2,1)}, u32[]{:S(2)}, u32[]{:S(2)}) collective-permute-start(bf16[512,1024]{1,0:T(8,128)(2,1)} %collective-permute-done.5.refs_9_.refs_13_), channel_id=1, source_target_pairs={{4,0},{8,4},{12,8},{14,12},{10,14},{6,10},{2,6},{0,2},{5,1},{9,5},... | collective-permute-start | bytes 3145736 | tf_op jit(solution)/shard_map/ppermute | solution.py:273
  80.8 24.9 %collective-permute-start.13 = (bf16[256,2048]{1,0:T(8,128)(2,1)}, bf16[256,2048]{1,0:T(8,128)(2,1)}, u32[]{:S(2)}, u32[]{:S(2)}) collective-permute-start(bf16[256,2048]{1,0:T(8,128)(2,1)} %collective-permute-done.6.refs_3_), channel_id=1, source_target_pairs={{0,1},{1,0},{2,3},{3,2},{4,5},{5,4},{6,7},{7,6},{8,9},{9,8},{10,11... | collective-permute-start | bytes 3145736 | tf_op jit(solution)/shard_map/ppermute | solution.py:324
  81.2 24.5 %collective-permute-start.12 = (bf16[128,2048]{1,0:T(8,128)(2,1)}, bf16[128,2048]{1,0:T(8,128)(2,1)}, u32[]{:S(2)}, u32[]{:S(2)}) collective-permute-start(bf16[128,2048]{1,0:T(8,128)(2,1)} %copy-done.17), channel_id=1, source_target_pairs={{0,16},{16,0},{1,17},{17,1},{2,18},{18,2},{3,19},{19,3},{4,20},{20... | collective-permute-start | bytes 1572872 | tf_op jit(solution)/shard_map/ppermute | solution.py:323
  105.7 4.6 %collective-permute-start.16 = (bf16[128,2048]{1,0:T(8,128)(2,1)}, bf16[128,2048]{1,0:T(8,128)(2,1)}, u32[]{:S(2)}, u32[]{:S(2)}) collective-permute-start(bf16[128,2048]{1,0:T(8,128)(2,1)} %collective-permute-done.12.refs_5_), channel_id=1, source_target_pairs={{0,1},{1,0},{2,3},{3,2},{4,5},{5,4},{6,7},{7,6},{8,9},{9,8},{10,11... | collective-permute-start | bytes 1572872 | tf_op jit(solution)/shard_map/ppermute | solution.py:342
  105.9 11.0 %collective-permute-start.14 = (bf16[256,512]{1,0:T(8,128)(2,1)}, bf16[256,512]{1,0:T(8,128)(2,1)S(1)}, u32[]{:S(2)}, u32[]{:S(2)}) collective-permute-start(bf16[256,512]{1,0:T(8,128)(2,1)} %slice.24), channel_id=1, source_target_pairs={{0,4},{4,8},{8,12},{12,14},{14,10},{10,6},{6,2},{2,0},{1,5},{5,9},... | collective-permute-start | bytes 786440 | tf_op jit(solution)/shard_map/ppermute | solution.py:273
  106.5 10.4 %collective-permute-start.15 = (bf16[256,512]{1,0:T(8,128)(2,1)}, bf16[256,512]{1,0:T(8,128)(2,1)S(1)}, u32[]{:S(2)}, u32[]{:S(2)}) collective-permute-start(bf16[256,512]{1,0:T(8,128)(2,1)} %slice.25), channel_id=1, source_target_pairs={{4,0},{8,4},{12,8},{14,12},{10,14},{6,10},{2,6},{0,2},{5,1},{9,5},... | collective-permute-start | bytes 786440 | tf_op jit(solution)/shard_map/ppermute | solution.py:273
  120.5 17.6 %collective-permute-start.17 = (f16[672,512]{1,0:T(8,128)(2,1)}, f16[672,512]{1,0:T(8,128)(2,1)}, u32[]{:S(2)}, u32[]{:S(2)}) collective-permute-start(f16[672,512]{1,0:T(8,128)(2,1)} %multiply_convert_fusion.1), channel_id=1, source_target_pairs={{0,16},{16,0},{1,17},{17,1},{2,18},{18,2},{3,19},{19,3},{4,20},{20... | collective-permute-start | bytes 2064392 | tf_op jit(solution)/shard_map/ppermute | solution.py:353
  121.2 11.0 %collective-permute-start.18 = (bf16[256,512]{1,0:T(8,128)(2,1)}, bf16[256,512]{1,0:T(8,128)(2,1)}, u32[]{:S(2)}, u32[]{:S(2)}) collective-permute-start(bf16[256,512]{1,0:T(8,128)(2,1)} %slice.20), channel_id=1, source_target_pairs={{0,4},{4,8},{8,12},{12,14},{14,10},{10,6},{6,2},{2,0},{1,5},{5,9},... | collective-permute-start | bytes 786440 | tf_op jit(solution)/shard_map/ppermute | solution.py:273
  121.9 10.3 %collective-permute-start.19 = (bf16[256,512]{1,0:T(8,128)(2,1)}, bf16[256,512]{1,0:T(8,128)(2,1)}, u32[]{:S(2)}, u32[]{:S(2)}) collective-permute-start(bf16[256,512]{1,0:T(8,128)(2,1)} %slice.21), channel_id=1, source_target_pairs={{4,0},{8,4},{12,8},{14,12},{10,14},{6,10},{2,6},{0,2},{5,1},{9,5},... | collective-permute-start | bytes 786440 | tf_op jit(solution)/shard_map/ppermute | solution.py:273
  138.1 16.6 %collective-permute-start.20 = (f16[672,512]{1,0:T(8,128)(2,1)S(1)}, f16[672,512]{1,0:T(8,128)(2,1)}, u32[]{:S(2)}, u32[]{:S(2)}) collective-permute-start(f16[672,512]{1,0:T(8,128)(2,1)S(1)} %multiply_convert_fusion), channel_id=1, source_target_pairs={{0,16},{16,0},{1,17},{17,1},{2,18},{18,2},{3,19},{19,3},{4,20},{20... | collective-permute-start | bytes 2064392 | tf_op jit(solution)/shard_map/ppermute | solution.py:358
  (18 other events, 54.0 us)

commit v6 on v5

v6 whole, which is shorter than its diff:
```python
import functools
import math

import jax
import jax.numpy as jnp
from jax import lax
from jax.experimental import pallas as pl
from jax.experimental.pallas import tpu as pltpu
from jax.sharding import PartitionSpec as P

HD = 128
HALF = HD // 2
CHUNKS = 2
MOST_SHARDS = 8
VMEM_BYTES = 32 << 20
MERGED = 4
RAISE = 16.0


def angle_tables(positions):
    index_float = jnp.arange(HALF, dtype=jnp.float32)
    inverse = jnp.exp(index_float * (-2.0 * math.log(1000000.0) / HD))
    angles = positions.astype(jnp.float32)[:, None] * inverse
    return jnp.cos(angles), jnp.sin(angles)


def token_tables(lengths, destinations, row_index, tokens, requests, steps, padded):
    my_lengths = lax.dynamic_index_in_dim(lengths, row_index, 0, keepdims=False)
    my_targets = lax.dynamic_index_in_dim(destinations, row_index, 0, keepdims=False)
    ends = jnp.cumsum(my_lengths)
    starts = ends - my_lengths
    token = jnp.arange(tokens, dtype=jnp.int32)[:, None]
    inside = (starts[None, :] <= token) & (token < ends[None, :])
    token_position = token[:, 0] - jnp.sum(jnp.where(inside, starts[None, :], 0), axis=1)
    token_target = jnp.sum(jnp.where(inside, my_targets[None, :], 0), axis=1)
    received = jnp.sum(jnp.where(destinations == row_index, lengths, 0), axis=1)
    step = jnp.repeat(jnp.arange(steps, dtype=jnp.int32), requests)
    new_target = jnp.tile(jnp.arange(requests, dtype=jnp.int32), steps)
    new_position = jnp.tile(received, steps) + step
    spare = jnp.zeros((padded - requests * steps,), jnp.int32)
    target = jnp.concatenate([token_target, new_target, spare - 1])
    seen_from = jnp.concatenate([jnp.zeros_like(token_target), step, spare])
    query_info = jnp.stack([new_target, step], 1)
    return token_position, new_position, jnp.stack([target, seen_from], 0), query_info


def rotate(first, second, cosine, sine):
    return [first * cosine - second * sine, second * cosine + first * sine]


def finish_kernel(chunks, group, *refs):
    held, homed, refs = refs[:chunks], refs[chunks : 2 * chunks], refs[2 * chunks :]
    cos_ref, sin_ref, keys_ref, rows_ref, new_ref, query_ref, out_ref = refs
    cosine, sine = cos_ref[...], sin_ref[...]
    allowed = (keys_ref[0:1, :] == rows_ref[:, 0:1]) & (keys_ref[1:2, :] <= rows_ref[:, 1:2])
    allowed = jnp.concatenate([allowed.astype(jnp.float32)] * group, 0) > 0.5
    queries = query_ref[...].astype(jnp.float32)
    count = queries.shape[0]
    width = held[0].shape[1]
    heads = width // (2 * HD)
    for h in range(chunks * heads):
        c, local = h // heads, h % heads
        key_at = slice(local * HD, (local + 1) * HD)
        value_at = slice((heads + local) * HD, (heads + local + 1) * HD)
        new_at = c * width
        both = held[c][:, key_at] + homed[c][:, key_at]
        keys = jnp.concatenate(rotate(both[:, :HALF], both[:, HALF:], cosine, sine), -1)
        values = held[c][:, value_at] + homed[c][:, value_at]
        keys, values = (
            jnp.concatenate(
                [cached.astype(jnp.bfloat16), new_ref[:, new_at + at.start : new_at + at.stop]], 0
            )
            for cached, at in ((keys, key_at), (values, value_at))
        )
        at = h * group * HD
        query = jnp.concatenate(
            [queries[:, at + g * HD : at + (g + 1) * HD] for g in range(group)], 0
        ).astype(jnp.bfloat16)
        scores = lax.dot_general(
            query, keys, (((1,), (1,)), ((), ())), preferred_element_type=jnp.float32
        )
        scores = jnp.where(allowed, scores * (1.0 / math.sqrt(HD)), jnp.float32(-1e30))
        raised = jnp.exp(scores - jnp.max(scores, axis=-1, keepdims=True))
        total = jnp.sum(raised, axis=-1, keepdims=True)
        weights = (raised / total).astype(jnp.bfloat16)
        output = jnp.dot(weights, values, preferred_element_type=jnp.float32)
        for g in range(group):
            out_ref[:, at + g * HD : at + (g + 1) * HD] = output[
                g * count : (g + 1) * count
            ].astype(jnp.bfloat16)


def finish(held, homed, cosine, sine, key_info, query_info, new_pairs, queries):
    rows, width = held[0].shape
    heads = len(held) * width // (2 * HD)
    group = queries.shape[1] // (heads * HD)
    count = queries.shape[0]
    vmem = pl.BlockSpec(memory_space=pltpu.VMEM)
    operands = [*held, *homed, cosine, sine, key_info, query_info, new_pairs, queries]
    return pl.pallas_call(
        functools.partial(finish_kernel, len(held), group),
        out_shape=jax.ShapeDtypeStruct(queries.shape, jnp.bfloat16),
        in_specs=[vmem] * len(operands),
        out_specs=vmem,
        compiler_params=pltpu.CompilerParams(vmem_limit_bytes=VMEM_BYTES),
        cost_estimate=pl.CostEstimate(
            flops=4 * heads * group * count * rows * HD,
            bytes_accessed=8 * len(held) * rows * width + 4 * queries.size,
            transcendentals=heads * group * count * rows,
        ),
        name="rotate_attend",
    )(*operands)


def pick_kernel(side_ref, source_ref, out_ref):
    out_ref[...] = source_ref[...]


def pick_columns(source, side, half, first, end):
    blocks = source.shape[1] // (2 * half)
    rows = math.gcd(first, end) if first else end
    return pl.pallas_call(
        pick_kernel,
        out_shape=jax.ShapeDtypeStruct((end - first, blocks * half), source.dtype),
        grid_spec=pltpu.PrefetchScalarGridSpec(
            num_scalar_prefetch=1,
            grid=((end - first) // rows, blocks),
            in_specs=[
                pl.BlockSpec((rows, half), lambda i, j, s: (first // rows + i, 2 * j + s[0]))
            ],
            out_specs=pl.BlockSpec((rows, half), lambda i, j, s: (i, j)),
        ),
        compiler_params=pltpu.CompilerParams(vmem_limit_bytes=VMEM_BYTES),
        cost_estimate=pl.CostEstimate(
            flops=0, bytes_accessed=4 * (end - first) * blocks * half, transcendentals=0
        ),
        name="pick_columns",
    )(side.reshape(1), source)


def product_kernel(depths, parts, base, column, has_total, *refs):
    place_ref, refs = refs[0], refs[1:]
    hidden, refs = refs[: 2 * parts], refs[2 * parts :]
    weights, out_ref = refs[: sum(len(pieces) for pieces in depths)], refs[-1]
    width = out_ref.shape[1]
    half = sum(depths[0])
    blocks = hidden[0].shape[1] // half

    def window(ref):
        return ref[...] if ref.shape[1] == width else ref[:, column : column + width]

    total, used = window(refs[-2]) if has_total else None, 0
    for p, pieces in enumerate(depths):
        place = place_ref[base + p]
        here = place < blocks
        columns = pl.ds(pl.multiple_of(jnp.where(here, place, place - blocks) * half, half), half)
        rows = [
            jnp.where(here, hidden[2 * q][:, columns], hidden[2 * q + 1][:, columns])
            for q in range(parts)
        ]
        rows = rows[0] if parts == 1 else jnp.concatenate(rows, 0)
        piece = [window(w) for w in weights[used : used + len(pieces)]]
        piece = piece[0] if len(piece) == 1 else jnp.concatenate(piece, 0)
        used += len(pieces)
        term = jnp.dot(rows, piece, preferred_element_type=jnp.float32)
        total = term if total is None else total + term
    out_ref[...] = total


def products(total, hidden, weights, places, base, column, width):
    shards = len(weights)
    flat = [w for shard in weights for w in shard]
    depths = tuple(tuple(w.shape[0] for w in shard) for shard in weights)
    half = sum(depths[0])
    rows = sum(pair[0].shape[0] for pair in hidden)
    operands = [places] + [array for pair in hidden for array in pair] + flat
    if total is not None:
        operands.append(total)
    vmem = pl.BlockSpec(memory_space=pltpu.VMEM)
    return pl.pallas_call(
        functools.partial(
            product_kernel, depths, len(hidden), base, column, total is not None
        ),
        out_shape=jax.ShapeDtypeStruct((rows, width), jnp.float32),
        in_specs=[pl.BlockSpec(memory_space=pltpu.SMEM)] + [vmem] * (len(operands) - 1),
        out_specs=vmem,
        compiler_params=pltpu.CompilerParams(vmem_limit_bytes=VMEM_BYTES),
        cost_estimate=pl.CostEstimate(
            flops=2 * rows * half * width * shards,
            bytes_accessed=shards * 2 * half * (rows + width) + 4 * rows * width,
            transcendentals=0,
        ),
        name="products",
    )(*operands)


def ring_order(row_count):
    evens = list(range(0, row_count, 2))
    odds = list(range(1, row_count, 2))
    return evens + odds[::-1]


def fence(*values):
    return lax.optimization_barrier(values)


def body(passages, kv_weight, new_hidden, queries, lengths, destinations):
    tokens = passages.shape[0]
    requests, steps, half_model = new_hidden.shape
    row_count = lax.axis_size("rows")
    group_count = lax.axis_size("groups")
    row_index = lax.axis_index("rows")
    side = lax.axis_index("groups") % 2
    core = lax.axis_index("tensor")
    depth = kv_weight.shape[0]
    half = depth // 2
    local_heads = kv_weight.shape[2] // HD
    group = queries.shape[2] // kv_weight.shape[2]
    count = requests * steps
    new_padded = -(-count // 16) * 16
    half_rows = row_count // 2

    partners = [(g, g ^ 1) for g in range(group_count)]
    cores = [(0, 1), (1, 0)]
    order = ring_order(row_count)
    onward = [(order[i], order[(i + 1) % row_count]) for i in range(row_count)]
    back = [(b, a) for a, b in onward]
    place = {row: i for i, row in enumerate(order)}
    shard_order = [
        [order[(place[r] + d) % row_count] for r in range(row_count)]
        for k in range(half_rows + 1)
        for d in ([0] if k == 0 else [-k, k] if k < half_rows else [k])
    ]
    owners = lax.dynamic_index_in_dim(jnp.array(shard_order, jnp.int32), row_index, 1, keepdims=False)
    places = ((owners // half_rows) ^ core) * half_rows + owners % half_rows

    chunk = kv_weight.shape[2] // CHUNKS
    own = lax.dynamic_slice_in_dim(kv_weight, side * half, half, 0)
    own = own.reshape(half, 2, CHUNKS, chunk).swapaxes(1, 2).reshape(half, -1)
    width = 2 * chunk

    def step(pair):
        return lax.ppermute(pair[0], "rows", onward), lax.ppermute(pair[1], "rows", back)

    cuts = (0, 2 * tokens // 5, 4 * tokens // 5, tokens)
    sent = [pick_columns(passages, 1 - side, half, cuts[0], cuts[1])]
    own, sent[0], passages, new_hidden = fence(own, sent[0], passages, new_hidden)
    got = [lax.ppermute(sent[0], "groups", partners)]
    ring = [step((own, own))]
    sent += [pick_columns(passages, 1 - side, half, *cuts[i : i + 2]) for i in (1, 2)]
    kept = pick_columns(passages, side, half, 0, tokens)
    new_rows = jnp.swapaxes(new_hidden, 0, 1).reshape(count, half_model)
    new_rows = jnp.pad(new_rows, ((0, new_padded - count), (0, 0)))
    new_sent = pick_columns(new_rows, 1 - side, half, 0, new_padded)
    new_kept = pick_columns(new_rows, side, half, 0, new_padded)
    ring[0], got[0], sent, kept, new_sent, new_kept, lengths, destinations = fence(
        ring[0], got[0], sent, kept, new_sent, new_kept, lengths, destinations
    )

    got.append(lax.ppermute(sent[1], "groups", partners))
    ring.append(step(ring[-1]))
    kept_other = lax.ppermute(kept, "tensor", cores)
    new_got = lax.ppermute(new_sent, "groups", partners)
    position, new_position, key_info, query_info = token_tables(
        lengths, destinations, row_index, tokens, requests, steps, new_padded
    )
    cosine, sine = angle_tables(position)
    new_cosine, new_sine = angle_tables(new_position)
    tables = (cosine, sine, new_cosine, new_sine, key_info, query_info)
    ring[1], got[1], kept_other, new_got, tables, places = fence(
        ring[1], got[1], kept_other, new_got, tables, places
    )

    def project(hidden, total, begin, end, column, width):
        weights = [(own,)] + [(w,) for pair in ring for w in pair]
        weights = weights[: row_count - 1] + [last[column // width] if last else ()]
        for at in range(begin, end, MOST_SHARDS):
            some = weights[at : min(at + MOST_SHARDS, end)]
            total = products(total, hidden, some, places, at, column, width)
        return total

    def homeward(total):
        tokens_total = (total[:tokens] * RAISE).astype(jnp.float16)
        return tokens_total, total[tokens + new_padded :], total[tokens : tokens + count]

    last = []
    own_hidden = [(kept, kept_other)]
    early = row_count - 3
    got_other = []
    for k in range(2, half_rows - 1):
        if k > 2:
            ring[-1] = fence(*ring[-1])
        else:
            got.append(lax.ppermute(sent[2], "groups", partners))
            got_other += [lax.ppermute(piece, "tensor", cores) for piece in got[:2]]
        ring.append(step(ring[-1]))
    held = project(own_hidden, None, 0, early, 0, 2 * width)
    new_kept = jnp.concatenate([new_kept, new_got], 0)

    def halved(c):
        columns = slice(c * width, (c + 1) * width)
        return ring[-1][0][: half // 2, columns], ring[-1][1][half // 2 :, columns]

    ends = [halved(0)]
    ring[-1], got[2], got_other, new_kept, held, ends, places = fence(
        ring[-1], got[2], got_other, new_kept, held, ends, places
    )

    last.append(step(ends[0]))
    got_other.append(lax.ppermute(got[2], "tensor", cores))
    new_other = lax.ppermute(new_kept, "tensor", cores)
    away_hidden = list(zip(got, got_other)) + [(new_kept, new_other)]
    away = project(away_hidden, None, 0, row_count - 1, 0, width)
    ends.append(halved(1))
    last[0], away, ends, places = fence(last[0], away, ends, places)

    last.append(step(ends[1]))
    away = project(away_hidden, away, row_count - 1, row_count, 0, width)
    away, places = fence(homeward(away), places)
    homed = [lax.ppermute(away[0], "groups", partners)]
    new_totals = [away[2] + lax.ppermute(away[1], "groups", partners)[:count]]
    away = project(away_hidden, None, 0, row_count - 1, width, width)
    away = homeward(project(away_hidden, away, row_count - 1, row_count, width, width))
    new_totals.append(away[2] + lax.ppermute(away[1], "groups", partners)[:count])
    mine = [project(own_hidden, held, early, row_count, 0, width)]
    homed[0], away, mine, new_totals, held, queries, places = fence(
        homed[0], away, mine, new_totals, held, queries, places
    )

    homed.append(lax.ppermute(away[0], "groups", partners))
    cosine, sine, new_cosine, new_sine, key_info, query_info = tables
    moved = [jnp.swapaxes(queries, 0, 1).reshape(count, -1)]
    for total in new_totals:
        pairs = total.reshape(count, 2, -1, 2, HALF)
        keys = rotate(
            pairs[:, 0, :, 0], pairs[:, 0, :, 1], new_cosine[:, None, :], new_sine[:, None, :]
        )
        keys = jnp.stack(keys, 2).reshape(count, chunk)
        moved += [keys.astype(jnp.bfloat16), total[:, chunk:].astype(jnp.bfloat16)]
    moved = jnp.concatenate(moved, 1).reshape(steps, requests, -1)
    moved = jnp.swapaxes(moved, 0, 1)
    moved = lax.all_to_all(moved, "rows", split_axis=0, concat_axis=0, tiled=True)
    moved = jnp.swapaxes(moved, 0, 1).reshape(count, -1)
    heads_width = queries.shape[2]
    query_rows, new_pairs = moved[:, :heads_width], moved[:, heads_width:]
    new_pairs = jnp.pad(new_pairs, ((0, new_padded - count), (0, 0)))
    mine.append(project(own_hidden, held, early, row_count, width, width))
    homed = [total.astype(jnp.float32) * (1.0 / RAISE) for total in homed]
    attended = finish(mine, homed, cosine, sine, key_info, query_info, new_pairs, query_rows)
    attended = jnp.swapaxes(attended.reshape(steps, requests, -1), 0, 1)
    return lax.all_to_all(attended, "rows", split_axis=0, concat_axis=0, tiled=True)


def solution(mesh):
    placed = (
        P(("groups", "rows"), "tensor"),
        P("rows", None, "tensor"),
        P(("groups", "rows"), None, "tensor"),
        P(("groups", "rows"), None, "tensor"),
        P("groups", None),
        P("groups", None),
    )
    return jax.shard_map(
        body,
        mesh=mesh,
        in_specs=placed,
        out_specs=P(("groups", "rows"), None, "tensor"),
        check_vma=False,
    )
```

time: 171 us -> 171 us (level)
  Pallas kernels: 43.9 us -> 33.7 us
  waiting for transfers between devices: 52.2 us -> 59.7 us
  blocking collectives: 11.8 us -> 13.9 us
    all_to_all x2 -> x1, waiting for transfers between devices: 21.3 us -> 0.01 us  [body(): lax.all_to_all(moved, 'rows', split_axis=0, concat_axis=0, tiled=True)]
    ppermute x5, waiting for transfers between devices: 9.14 us -> 29.7 us  [step(): lax.ppermute(pair[0], 'rows', onward)]
    ppermute x1, waiting for transfers between devices: 14.2 us -> 23.5 us  [body(): new_got = lax.ppermute(new_sent, 'groups', partners)]
    pallas_call x9 -> x8, Pallas kernels: 37.9 us -> 30.2 us  [the longest x7 27.2 us: products(): pl.pallas_call(functools.partial(product_kernel, depths, len(hidden), bas...]
    ppermute x5, starting transfers between devices: 3.03 us -> 9.8 us  [step(): lax.ppermute(pair[0], 'rows', onward)]
    all_to_all x2 -> x1, starting transfers between devices: 9.87 us -> 4.08 us  [body(): lax.all_to_all(moved, 'rows', split_axis=0, concat_axis=0, tiled=True)]
    ppermute x5, starting transfers between devices: 7.15 us -> 1.51 us  [step(): lax.ppermute(pair[1], 'rows', back)]
    unnamed x38 -> x54, local copies, waits for them, and re-layouts: 12.3 us -> 17.4 us
  transfers between devices with their start and end apart: 23 -> 24, of which waited for: 6 -> 8; matrix products, arithmetic and copies ran while one was open for 10% -> 6% of each run, Pallas kernels for 21% -> 17%
where the time goes in v6:
time: 171 us
  waiting for transfers between devices  59.7 us (35%)
  Pallas kernels  33.7 us (20%)
  starting transfers between devices  26.9 us (16%)
  local copies, waits for them, and re-layouts  26.7 us (16%)
  blocking collectives  13.9 us (8%)
  other arithmetic  9.09 us (5%)
    ppermute x5, waiting for transfers between devices, step(): lax.ppermute(pair[0], 'rows', onward)  29.7 us
    pallas_call x7, Pallas kernels, products(): pl.pallas_call(functools.partial(product_kernel, depths, len(hidden), bas...  27.2 us
    ppermute x1, waiting for transfers between devices, body(): new_got = lax.ppermute(new_sent, 'groups', partners)  23.5 us
    unnamed x54, local copies, waits for them, and re-layouts  17.4 us
    all_to_all x1, blocking collectives, body(): lax.all_to_all(attended, 'rows', split_axis=0, concat_axis=0, tiled=True)  13.9 us
    ppermute x5, starting transfers between devices, step(): lax.ppermute(pair[0], 'rows', onward)  9.8 us
    ppermute x5, waiting for transfers between devices, step(): lax.ppermute(pair[1], 'rows', back)  4.25 us
    all_to_all x1, starting transfers between devices, body(): lax.all_to_all(moved, 'rows', split_axis=0, concat_axis=0, tiled=True)  4.08 us
  transfers between devices with their start and end apart: 24, of which 8 were waited for; matrix products, arithmetic and copies ran while one was open for 6% of the time, Pallas kernels for 17%

profile of v6, /device:TPU:0, one launch (start us, length us, event | category | flops | bytes accessed | tf_op | source)
XLA Modules:
  0.0 170.6 jit_solution(17722464526230404612)
XLA Ops:
  1.6 1.7 %constant_dynamic-slice_fusion.3 = bf16[512,2,512]{2,1,0:T(2,128)(2,1)} fusion(bf16[1024,2,512]{2,1,0:T(2,128)(2,1)S(1)} %copy-done, s32[]{:T(128)S(6)} %select_n.40), kind=kLoop, calls=%fused_computation.53 | loop fusion | bytes 2097156 | tf_op jit(solution)/shard_map/dynamic_slice | solution.py:238
  3.3 1.8 %reshape.180.refs_3_.refs_9_ = bf16[512,1024]{1,0:T(8,128)(2,1)S(1)} reshape(bf16[512,2,2,256]{3,2,1,0:T(2,128)(2,1)} %bitcast.73) | data formatting | bytes 2097152 | tf_op jit(solution)/shard_map/reshape | solution.py:239
  5.1 2.9 %copy-done.1 = bf16[640,4096]{1,0:T(8,128)(2,1)S(1)} copy-done((bf16[640,4096]{1,0:T(8,128)(2,1)S(1)}, bf16[640,4096]{1,0:T(8,128)(2,1)}, u32[]{:S(2)}) %copy-start.1) | copy-done | bytes 5242904
  8.3 3.1 %collective-permute-start = (bf16[512,1024]{1,0:T(8,128)(2,1)S(1)}, bf16[512,1024]{1,0:T(8,128)(2,1)}, u32[]{:S(2)}, u32[]{:S(2)}) collective-permute-start(bf16[512,1024]{1,0:T(8,128)(2,1)S(1)} %reshape.180.refs_3_.refs_9_), channel_id=1, source_target_pairs={{0,4},{4,8},{8,12},{12,14},{14,10},{10,6},{6,2},{2,0},{1,5},{5,9},... | collective-permute-start | bytes 3145736 | tf_op jit(solution)/shard_map/ppermute | solution.py:243
  11.4 1.9 %collective-permute-start.2 = (bf16[256,2048]{1,0:T(8,128)(2,1)S(1)}, bf16[256,2048]{1,0:T(8,128)(2,1)}, u32[]{:S(2)}, u32[]{:S(2)}) collective-permute-start(bf16[256,2048]{1,0:T(8,128)(2,1)S(1)} %pick_columns.6), channel_id=1, source_target_pairs={{0,16},{16,0},{1,17},{17,1},{2,18},{18,2},{3,19},{19,3},{4,20},{20... | collective-permute-start | bytes 3145736 | tf_op jit(solution)/shard_map/ppermute | solution.py:248
  15.8 2.3 %pick_columns.9.refs_1_ = bf16[640,2048]{1,0:T(8,128)(2,1)} custom-call(s32[1]{0:T(128)} %bitcast.3.side_ref, bf16[640,4096]{1,0:T(8,128)(2,1)S(1)} %bitcast.71), custom_call_target="tpu_custom_call" | custom-call | bytes 5242880 | tf_op jit(solution)/shard_map/pick_columns/pallas_call | solution.py:122
  18.4 16.2 %collective-permute-done.refs_4_.refs_10_ = bf16[512,1024]{1,0:T(8,128)(2,1)} collective-permute-done((bf16[512,1024]{1,0:T(8,128)(2,1)S(1)}, bf16[512,1024]{1,0:T(8,128)(2,1)}, u32[]{:S(2)}, u32[]{:S(2)}) %collective-permute-start) | collective-permute-done | bytes 1048608 | tf_op jit(solution)/shard_map/ppermute | solution.py:243
  38.3 1.7 %collective-permute-start.3 = (bf16[512,1024]{1,0:T(8,128)(2,1)}, bf16[512,1024]{1,0:T(8,128)(2,1)S(1)}, u32[]{:S(2)}, u32[]{:S(2)}) collective-permute-start(bf16[512,1024]{1,0:T(8,128)(2,1)} %collective-permute-done.refs_4_.refs_10_), channel_id=1, source_target_pairs={{0,4},{4,8},{8,12},{12,14},{14,10},{10,6},{6,2},{2,0},{1,5},{5,9},... | collective-permute-start | bytes 3145736 | tf_op jit(solution)/shard_map/ppermute | solution.py:243
  42.7 2.1 %multiply_sine_fusion = (f32[640,64]{1,0:T(8,128)}, f32[640,64]{1,0:T(8,128)}) fusion(f32[64]{0:T(128)S(1)} %multiply_exponential_fusion, f32[640]{0:T(1024)S(1)} %subtract_convert_fusion.2), kind=kLoop, calls=%fused_computation.6 | loop fusion | flops 40960 | bytes 330496 | tf_op jit(solution)/shard_map/sin | solution.py:24
  44.9 23.5 %collective-permute-done.7 = bf16[32,2048]{1,0:T(8,128)(2,1)S(1)} collective-permute-done((bf16[32,2048]{1,0:T(8,128)(2,1)S(1)}, bf16[32,2048]{1,0:T(8,128)(2,1)S(1)}, u32[]{:S(2)}, u32[]{:S(2)}) %collective-permute-start.7) | collective-permute-done | bytes 131104 | tf_op jit(solution)/shard_map/ppermute | solution.py:263
  68.4 1.8 %collective-permute-start.8 = (bf16[512,1024]{1,0:T(8,128)(2,1)S(1)}, bf16[512,1024]{1,0:T(8,128)(2,1)S(1)}, u32[]{:S(2)}, u32[]{:S(2)}) collective-permute-start(bf16[512,1024]{1,0:T(8,128)(2,1)S(1)} %collective-permute-done.3.refs_6_.refs_12_), channel_id=1, source_target_pairs={{0,4},{4,8},{8,12},{12,14},{14,10},{10,6},{6,2},{2,0},{1,5},{5,9},... | collective-permute-start | bytes 3145736 | tf_op jit(solution)/shard_map/ppermute | solution.py:243
  73.9 6.7 %products.7.refs_7_ = f32[640,1024]{1,0:T(8,128)S(1)} custom-call(s32[8]{0:T(128)S(1)} %fusion.5.refs_0_, bf16[640,2048]{1,0:T(8,128)(2,1)} %pick_columns.9.refs_1_, bf16[640,2048]{1,0:T(8,128)(2,1)} %collective-permute-done.6.refs_2_, bf16[512,1024]{1,0:T(8,128)(2,1)S(1)} %copy-done.7, bf16[512,1024]{1,0:T(8,128)(2,1)} %collective-permute-done.refs_4_.refs_10_, ...), custom_call_target="tpu_custom_call" | custom-call | flops 3355443200 | bytes 11141120 | tf_op jit(solution)/shard_map/products/pallas_call | solution.py:180
  80.6 12.0 %collective-permute-done.8.refs_14_.refs_3_ = bf16[512,1024]{1,0:T(8,128)(2,1)S(1)} collective-permute-done((bf16[512,1024]{1,0:T(8,128)(2,1)S(1)}, bf16[512,1024]{1,0:T(8,128)(2,1)S(1)}, u32[]{:S(2)}, u32[]{:S(2)}) %collective-permute-start.8) | collective-permute-done | bytes 1048608 | tf_op jit(solution)/shard_map/ppermute | solution.py:243
  96.8 4.6 %products.8.refs_11_ = f32[704,512]{1,0:T(8,128)S(1)} custom-call(s32[8]{0:T(128)S(1)} %fusion.5.refs_0_, bf16[256,2048]{1,0:T(8,128)(2,1)} %collective-permute-done.2.refs_1_, bf16[256,2048]{1,0:T(8,128)(2,1)S(1)} %collective-permute-done.11.refs_2_, bf16[256,2048]{1,0:T(8,128)(2,1)S(1)} %collective-permute-done.5.refs_3_, ...), custom_call_target="tpu_custom_call" | custom-call | flops 2583691264 | bytes 10158080 | tf_op jit(solution)/shard_map/products/pallas_call | solution.py:180
  104.3 1.8 %products.9 = f32[704,512]{1,0:T(8,128)S(1)} custom-call(s32[8]{0:T(128)S(1)} %fusion.5.refs_0_, bf16[256,2048]{1,0:T(8,128)(2,1)} %collective-permute-done.2.refs_1_, bf16[256,2048]{1,0:T(8,128)(2,1)S(1)} %collective-permute-done.11.refs_2_, bf16[256,2048]{1,0:T(8,128)(2,1)S(1)} %collective-permute-done.5.refs_3_, ...), custom_call_target="tpu_custom_call" | custom-call | flops 369098752 | bytes 2686976 | tf_op jit(solution)/shard_map/products/pallas_call | solution.py:180
  110.4 3.7 %products.12.refs_0_ = f32[640,512]{1,0:T(8,128)S(1)} custom-call(s32[8]{0:T(128)S(1)} %fusion.5.refs_0_, bf16[640,2048]{1,0:T(8,128)(2,1)} %pick_columns.9.refs_1_, bf16[640,2048]{1,0:T(8,128)(2,1)} %collective-permute-done.6.refs_2_, bf16[512,1024]{1,0:T(8,128)(2,1)S(1)} %collective-permute-done.8.refs_14_.refs_3_, ...), custom_call_target="tpu_custom_call" | custom-call | flops 1006632960 | bytes 4849664 | tf_op jit(solution)/shard_map/products/pallas_call | solution.py:180
  115.3 4.7 %products.10.refs_11_ = f32[704,512]{1,0:T(8,128)S(1)} custom-call(s32[8]{0:T(128)S(1)} %fusion.5.refs_0_, bf16[256,2048]{1,0:T(8,128)(2,1)} %collective-permute-done.2.refs_1_, bf16[256,2048]{1,0:T(8,128)(2,1)S(1)} %collective-permute-done.11.refs_2_, bf16[256,2048]{1,0:T(8,128)(2,1)S(1)} %collective-permute-done.5.refs_3_, ...), custom_call_target="tpu_custom_call" | custom-call | flops 2583691264 | bytes 10158080 | tf_op jit(solution)/shard_map/products/pallas_call | solution.py:180
  120.0 1.9 %products.11 = f32[704,512]{1,0:T(8,128)S(1)} custom-call(s32[8]{0:T(128)S(1)} %fusion.5.refs_0_, bf16[256,2048]{1,0:T(8,128)(2,1)} %collective-permute-done.2.refs_1_, bf16[256,2048]{1,0:T(8,128)(2,1)S(1)} %collective-permute-done.11.refs_2_, bf16[256,2048]{1,0:T(8,128)(2,1)S(1)} %collective-permute-done.5.refs_3_, ...), custom_call_target="tpu_custom_call" | custom-call | flops 369098752 | bytes 2686976 | tf_op jit(solution)/shard_map/products/pallas_call | solution.py:180
  124.5 2.2 %collective-permute-done.21 = f32[32,512]{1,0:T(8,128)S(1)} collective-permute-done((f32[32,512]{1,0:T(8,128)S(1)}, f32[32,512]{1,0:T(8,128)S(1)}, u32[]{:S(2)}, u32[]{:S(2)}) %collective-permute-start.21) | collective-permute-done | bytes 65568 | tf_op jit(solution)/shard_map/ppermute | solution.py:324
  134.0 4.1 %all-to-all-start = ((bf16[8,3,5120]{2,1,0:T(4,128)(2,1)}), bf16[8,3,5120]{2,1,0:T(4,128)(2,1)}, u32[]{:S(2)}, u32[]{:S(2)}) async-start(bf16[8,3,5120]{2,1,0:T(4,128)(2,1)} %bitcast.74), calls=%async_computation | async-start | bytes 655360 | tf_op jit(solution)/shard_map/all_to_all | solution.py:342
  138.8 1.7 %copy-done.3 = f32[640,1024]{1,0:T(8,128)S(1)} copy-done((f32[640,1024]{1,0:T(8,128)S(1)}, f32[640,1024]{1,0:T(8,128)}, u32[]{:S(2)}) %copy-start.3) | copy-done | bytes 2621464
  142.7 3.7 %products.13.refs_1_ = f32[640,512]{1,0:T(8,128)S(1)} custom-call(s32[8]{0:T(128)S(1)} %fusion.5.refs_0_, bf16[640,2048]{1,0:T(8,128)(2,1)} %pick_columns.9.refs_1_, bf16[640,2048]{1,0:T(8,128)(2,1)} %collective-permute-done.6.refs_2_, bf16[512,1024]{1,0:T(8,128)(2,1)S(1)} %collective-permute-done.8.refs_14_.refs_3_, bf16[512,1024]{1,0:T(8,128)(2,1)S(1)} %copy-done.5, ...), custom_call_target="tpu_custom_call" | custom-call | flops 1006632960 | bytes 4849664 | tf_op jit(solution)/shard_map/products/pallas_call | solution.py:180
  152.6 3.0 %rotate_attend.1 = bf16[24,4096]{1,0:T(8,128)(2,1)S(1)} custom-call(f32[640,512]{1,0:T(8,128)S(1)} %copy-done.10, f32[640,512]{1,0:T(8,128)S(1)} %copy-done.12, f32[640,512]{1,0:T(8,128)S(1)} %convert_multiply_fusion.1.refs_2_, f32[640,512]{1,0:T(8,128)S(1)} %convert_multiply_fusion.refs_3_, f32[640,64]{1,0:T(8,128)S(1)} %copy-done.14, ...), custom_call_target="tpu_custom_call" | custom-call | flops 251658240 | bytes 5636096 | tf_op jit(solution)/shard_map/rotate_attend/pallas_call | solution.py:100
  155.8 13.9 %all_to_all.10 = bf16[8,3,4096]{2,1,0:T(4,128)(2,1)S(1)} all-to-all(bf16[8,3,4096]{2,1,0:T(4,128)(2,1)S(1)} %bitcast.75), channel_id=1, replica_groups=mesh['groups'=2,'rows'=8,'tensor'=2] {'rows'}, dimensions={0} | all-to-all | bytes 393216 | tf_op jit(solution)/shard_map/all_to_all | solution.py:351
  (158 shorter events, 47.0 us)
Async XLA Ops:
  8.3 26.3 %collective-permute-start = (bf16[512,1024]{1,0:T(8,128)(2,1)S(1)}, bf16[512,1024]{1,0:T(8,128)(2,1)}, u32[]{:S(2)}, u32[]{:S(2)}) collective-permute-start(bf16[512,1024]{1,0:T(8,128)(2,1)S(1)} %reshape.180.refs_3_.refs_9_), channel_id=1, source_target_pairs={{0,4},{4,8},{8,12},{12,14},{14,10},{10,6},{6,2},{2,0},{1,5},{5,9},... | collective-permute-start | bytes 3145736 | tf_op jit(solution)/shard_map/ppermute | solution.py:243
  11.4 24.7 %collective-permute-start.1 = (bf16[512,1024]{1,0:T(8,128)(2,1)S(1)}, bf16[512,1024]{1,0:T(8,128)(2,1)}, u32[]{:S(2)}, u32[]{:S(2)}) collective-permute-start(bf16[512,1024]{1,0:T(8,128)(2,1)S(1)} %reshape.180.refs_3_.refs_9_), channel_id=1, source_target_pairs={{4,0},{8,4},{12,8},{14,12},{10,14},{6,10},{2,6},{0,2},{5,1},{9,5},... | collective-permute-start | bytes 3145736 | tf_op jit(solution)/shard_map/ppermute | solution.py:243
  11.4 24.7 %collective-permute-start.2 = (bf16[256,2048]{1,0:T(8,128)(2,1)S(1)}, bf16[256,2048]{1,0:T(8,128)(2,1)}, u32[]{:S(2)}, u32[]{:S(2)}) collective-permute-start(bf16[256,2048]{1,0:T(8,128)(2,1)S(1)} %pick_columns.6), channel_id=1, source_target_pairs={{0,16},{16,0},{1,17},{17,1},{2,18},{18,2},{3,19},{19,3},{4,20},{20... | collective-permute-start | bytes 3145736 | tf_op jit(solution)/shard_map/ppermute | solution.py:248
  36.2 32.2 %collective-permute-start.6 = (bf16[640,2048]{1,0:T(8,128)(2,1)}, bf16[640,2048]{1,0:T(8,128)(2,1)}, u32[]{:S(2)}, u32[]{:S(2)}) collective-permute-start(bf16[640,2048]{1,0:T(8,128)(2,1)} %pick_columns.9.refs_1_), channel_id=1, source_target_pairs={{0,1},{1,0},{2,3},{3,2},{4,5},{5,4},{6,7},{7,6},{8,9},{9,8},{10,11... | collective-permute-start | bytes 7864328 | tf_op jit(solution)/shard_map/ppermute | solution.py:262
  38.3 30.1 %collective-permute-start.3 = (bf16[512,1024]{1,0:T(8,128)(2,1)}, bf16[512,1024]{1,0:T(8,128)(2,1)S(1)}, u32[]{:S(2)}, u32[]{:S(2)}) collective-permute-start(bf16[512,1024]{1,0:T(8,128)(2,1)} %collective-permute-done.refs_4_.refs_10_), channel_id=1, source_target_pairs={{0,4},{4,8},{8,12},{12,14},{14,10},{10,6},{6,2},{2,0},{1,5},{5,9},... | collective-permute-start | bytes 3145736 | tf_op jit(solution)/shard_map/ppermute | solution.py:243
  40.1 28.3 %collective-permute-start.4 = (bf16[512,1024]{1,0:T(8,128)(2,1)}, bf16[512,1024]{1,0:T(8,128)(2,1)S(1)}, u32[]{:S(2)}, u32[]{:S(2)}) collective-permute-start(bf16[512,1024]{1,0:T(8,128)(2,1)} %collective-permute-done.1.refs_5_.refs_11_), channel_id=1, source_target_pairs={{4,0},{8,4},{12,8},{14,12},{10,14},{6,10},{2,6},{0,2},{5,1},{9,5},... | collective-permute-start | bytes 3145736 | tf_op jit(solution)/shard_map/ppermute | solution.py:243
  40.4 28.0 %collective-permute-start.5 = (bf16[256,2048]{1,0:T(8,128)(2,1)}, bf16[256,2048]{1,0:T(8,128)(2,1)S(1)}, u32[]{:S(2)}, u32[]{:S(2)}) collective-permute-start(bf16[256,2048]{1,0:T(8,128)(2,1)} %copy-done.15), channel_id=1, source_target_pairs={{0,16},{16,0},{1,17},{17,1},{2,18},{18,2},{3,19},{19,3},{4,20},{20... | collective-permute-start | bytes 3145736 | tf_op jit(solution)/shard_map/ppermute | solution.py:260
  42.0 26.4 %collective-permute-start.7 = (bf16[32,2048]{1,0:T(8,128)(2,1)S(1)}, bf16[32,2048]{1,0:T(8,128)(2,1)S(1)}, u32[]{:S(2)}, u32[]{:S(2)}) collective-permute-start(bf16[32,2048]{1,0:T(8,128)(2,1)S(1)} %pick_columns.10), channel_id=1, source_target_pairs={{0,16},{16,0},{1,17},{17,1},{2,18},{18,2},{3,19},{19,3},{4,20},{20... | collective-permute-start | bytes 393224 | tf_op jit(solution)/shard_map/ppermute | solution.py:263
  68.4 24.2 %collective-permute-start.8 = (bf16[512,1024]{1,0:T(8,128)(2,1)S(1)}, bf16[512,1024]{1,0:T(8,128)(2,1)S(1)}, u32[]{:S(2)}, u32[]{:S(2)}) collective-permute-start(bf16[512,1024]{1,0:T(8,128)(2,1)S(1)} %collective-permute-done.3.refs_6_.refs_12_), channel_id=1, source_target_pairs={{0,4},{4,8},{8,12},{12,14},{14,10},{10,6},{6,2},{2,0},{1,5},{5,9},... | collective-permute-start | bytes 3145736 | tf_op jit(solution)/shard_map/ppermute | solution.py:243
  70.2 23.9 %collective-permute-start.9 = (bf16[512,1024]{1,0:T(8,128)(2,1)S(1)}, bf16[512,1024]{1,0:T(8,128)(2,1)S(1)}, u32[]{:S(2)}, u32[]{:S(2)}) collective-permute-start(bf16[512,1024]{1,0:T(8,128)(2,1)S(1)} %collective-permute-done.4.refs_7_.refs_13_), channel_id=1, source_target_pairs={{4,0},{8,4},{12,8},{14,12},{10,14},{6,10},{2,6},{0,2},{5,1},{9,5},... | collective-permute-start | bytes 3145736 | tf_op jit(solution)/shard_map/ppermute | solution.py:243
  70.5 23.6 %collective-permute-start.11 = (bf16[256,2048]{1,0:T(8,128)(2,1)}, bf16[256,2048]{1,0:T(8,128)(2,1)S(1)}, u32[]{:S(2)}, u32[]{:S(2)}) collective-permute-start(bf16[256,2048]{1,0:T(8,128)(2,1)} %collective-permute-done.2.refs_1_), channel_id=1, source_target_pairs={{0,1},{1,0},{2,3},{3,2},{4,5},{5,4},{6,7},{7,6},{8,9},{9,8},{10,11... | collective-permute-start | bytes 3145736 | tf_op jit(solution)/shard_map/ppermute | solution.py:295
  70.5 23.6 %collective-permute-start.12 = (bf16[256,2048]{1,0:T(8,128)(2,1)S(1)}, bf16[256,2048]{1,0:T(8,128)(2,1)S(1)}, u32[]{:S(2)}, u32[]{:S(2)}) collective-permute-start(bf16[256,2048]{1,0:T(8,128)(2,1)S(1)} %collective-permute-done.5.refs_3_), channel_id=1, source_target_pairs={{0,1},{1,0},{2,3},{3,2},{4,5},{5,4},{6,7},{7,6},{8,9},{9,8},{10,11... | collective-permute-start | bytes 3145736 | tf_op jit(solution)/shard_map/ppermute | solution.py:295
  71.0 23.1 %collective-permute-start.10 = (bf16[128,2048]{1,0:T(8,128)(2,1)}, bf16[128,2048]{1,0:T(8,128)(2,1)S(1)}, u32[]{:S(2)}, u32[]{:S(2)}) collective-permute-start(bf16[128,2048]{1,0:T(8,128)(2,1)} %copy-done.18), channel_id=1, source_target_pairs={{0,16},{16,0},{1,17},{17,1},{2,18},{18,2},{3,19},{19,3},{4,20},{20... | collective-permute-start | bytes 1572872 | tf_op jit(solution)/shard_map/ppermute | solution.py:294
  94.1 2.7 %collective-permute-start.15 = (bf16[128,2048]{1,0:T(8,128)(2,1)S(1)}, bf16[128,2048]{1,0:T(8,128)(2,1)S(1)}, u32[]{:S(2)}, u32[]{:S(2)}) collective-permute-start(bf16[128,2048]{1,0:T(8,128)(2,1)S(1)} %collective-permute-done.10.refs_5_), channel_id=1, source_target_pairs={{0,1},{1,0},{2,3},{3,2},{4,5},{5,4},{6,7},{7,6},{8,9},{9,8},{10,11... | collective-permute-start | bytes 1572872 | tf_op jit(solution)/shard_map/ppermute | solution.py:310
  94.2 2.6 %collective-permute-start.16 = (bf16[64,2048]{1,0:T(8,128)(2,1)S(1)}, bf16[64,2048]{1,0:T(8,128)(2,1)S(1)}, u32[]{:S(2)}, u32[]{:S(2)}) collective-permute-start(bf16[64,2048]{1,0:T(8,128)(2,1)S(1)} %pad_maximum_fusion.refs_7_), channel_id=1, source_target_pairs={{0,1},{1,0},{2,3},{3,2},{4,5},{5,4},{6,7},{7,6},{8,9},{9,8},{10,11... | collective-permute-start | bytes 786440 | tf_op jit(solution)/shard_map/ppermute | solution.py:311
  94.7 8.3 %collective-permute-start.13 = (bf16[256,512]{1,0:T(8,128)(2,1)S(1)}, bf16[256,512]{1,0:T(8,128)(2,1)S(1)}, u32[]{:S(2)}, u32[]{:S(2)}) collective-permute-start(bf16[256,512]{1,0:T(8,128)(2,1)S(1)} %slice.82), channel_id=1, source_target_pairs={{0,4},{4,8},{8,12},{12,14},{14,10},{10,6},{6,2},{2,0},{1,5},{5,9},... | collective-permute-start | bytes 786440 | tf_op jit(solution)/shard_map/ppermute | solution.py:243
  96.3 8.0 %collective-permute-start.14 = (bf16[256,512]{1,0:T(8,128)(2,1)S(1)}, bf16[256,512]{1,0:T(8,128)(2,1)S(1)}, u32[]{:S(2)}, u32[]{:S(2)}) collective-permute-start(bf16[256,512]{1,0:T(8,128)(2,1)S(1)} %slice.83), channel_id=1, source_target_pairs={{4,0},{8,4},{12,8},{14,12},{10,14},{6,10},{2,6},{0,2},{5,1},{9,5},... | collective-permute-start | bytes 786440 | tf_op jit(solution)/shard_map/ppermute | solution.py:243
  106.3 13.7 %collective-permute-start.18 = (bf16[256,512]{1,0:T(8,128)(2,1)S(1)}, bf16[256,512]{1,0:T(8,128)(2,1)S(1)}, u32[]{:S(2)}, u32[]{:S(2)}) collective-permute-start(bf16[256,512]{1,0:T(8,128)(2,1)S(1)} %slice.64), channel_id=1, source_target_pairs={{0,4},{4,8},{8,12},{12,14},{14,10},{10,6},{6,2},{2,0},{1,5},{5,9},... | collective-permute-start | bytes 786440 | tf_op jit(solution)/shard_map/ppermute | solution.py:243
  107.9 12.1 %collective-permute-start.19 = (bf16[256,512]{1,0:T(8,128)(2,1)S(1)}, bf16[256,512]{1,0:T(8,128)(2,1)S(1)}, u32[]{:S(2)}, u32[]{:S(2)}) collective-permute-start(bf16[256,512]{1,0:T(8,128)(2,1)S(1)} %slice.65), channel_id=1, source_target_pairs={{4,0},{8,4},{12,8},{14,12},{10,14},{6,10},{2,6},{0,2},{5,1},{9,5},... | collective-permute-start | bytes 786440 | tf_op jit(solution)/shard_map/ppermute | solution.py:243
  108.4 11.6 %collective-permute-start.20 = (f32[32,512]{1,0:T(8,128)S(1)}, f32[32,512]{1,0:T(8,128)S(1)}, u32[]{:S(2)}, u32[]{:S(2)}) collective-permute-start(f32[32,512]{1,0:T(8,128)S(1)} %slice.85), channel_id=1, source_target_pairs={{0,16},{16,0},{1,17},{17,1},{2,18},{18,2},{3,19},{19,3},{4,20},{20... | collective-permute-start | bytes 196616 | tf_op jit(solution)/shard_map/ppermute | solution.py:321
  109.9 16.8 %collective-permute-start.17 = (f16[640,512]{1,0:T(8,128)(2,1)S(1)}, f16[640,512]{1,0:T(8,128)(2,1)}, u32[]{:S(2)}, u32[]{:S(2)}) collective-permute-start(f16[640,512]{1,0:T(8,128)(2,1)S(1)} %fusion.1), channel_id=1, source_target_pairs={{0,16},{16,0},{1,17},{17,1},{2,18},{18,2},{3,19},{19,3},{4,20},{20... | collective-permute-start | bytes 1966088 | tf_op jit(solution)/shard_map/ppermute | solution.py:320
  122.0 4.7 %collective-permute-start.21 = (f32[32,512]{1,0:T(8,128)S(1)}, f32[32,512]{1,0:T(8,128)S(1)}, u32[]{:S(2)}, u32[]{:S(2)}) collective-permute-start(f32[32,512]{1,0:T(8,128)S(1)} %slice.88), channel_id=1, source_target_pairs={{0,16},{16,0},{1,17},{17,1},{2,18},{18,2},{3,19},{19,3},{4,20},{20... | collective-permute-start | bytes 196616 | tf_op jit(solution)/shard_map/ppermute | solution.py:324
  131.3 18.8 %collective-permute-start.22 = (f16[640,512]{1,0:T(8,128)(2,1)}, f16[640,512]{1,0:T(8,128)(2,1)}, u32[]{:S(2)}, u32[]{:S(2)}) collective-permute-start(f16[640,512]{1,0:T(8,128)(2,1)} %fusion), channel_id=1, source_target_pairs={{0,16},{16,0},{1,17},{17,1},{2,18},{18,2},{3,19},{19,3},{4,20},{20... | collective-permute-start | bytes 1966088 | tf_op jit(solution)/shard_map/ppermute | solution.py:330
  134.0 14.9 %all-to-all-start = ((bf16[8,3,5120]{2,1,0:T(4,128)(2,1)}), bf16[8,3,5120]{2,1,0:T(4,128)(2,1)}, u32[]{:S(2)}, u32[]{:S(2)}) async-start(bf16[8,3,5120]{2,1,0:T(4,128)(2,1)} %bitcast.74), calls=%async_computation | async-start | bytes 655360 | tf_op jit(solution)/shard_map/all_to_all | solution.py:342
  (25 other events, 145.6 us)

commit v7 on v6

--- a/solution.py
+++ b/solution.py
@@ -112,6 +112,72 @@
     )(*operands)
 
 
+def own_kernel(side_ref, weight_ref, out_ref):
+    chunk = out_ref.shape[1] // (2 * CHUNKS)
+    for kind in range(2):
+        columns = weight_ref[:, kind, :]
+        for c in range(CHUNKS):
+            at = (2 * c + kind) * chunk
+            out_ref[:, at : at + chunk] = columns[:, c * chunk : (c + 1) * chunk]
+
+
+def own_half(weight, side):
+    depth, kinds, width = weight.shape
+    half = depth // 2
+    return pl.pallas_call(
+        own_kernel,
+        out_shape=jax.ShapeDtypeStruct((half, kinds * width), weight.dtype),
+        grid_spec=pltpu.PrefetchScalarGridSpec(
+            num_scalar_prefetch=1,
+            grid=(2,),
+            in_specs=[
+                pl.BlockSpec((half // 2, kinds, width), lambda i, s: (2 * s[0] + i, 0, 0))
+            ],
+            out_specs=pl.BlockSpec((half // 2, kinds * width), lambda i, s: (i, 0)),
+        ),
+        compiler_params=pltpu.CompilerParams(vmem_limit_bytes=VMEM_BYTES),
+        cost_estimate=pl.CostEstimate(
+            flops=0, bytes_accessed=8 * half * width * kinds, transcendentals=0
+        ),
+        name="own_half",
+    )(side.reshape(1), weight)
+
+
+def pack_kernel(chunks, own_ref, *refs):
+    owns, (got_ref, cos_ref, sin_ref, query_ref, out_ref) = (own_ref, *refs[: chunks - 1]), refs[chunks - 1 :]
+    cosine, sine = cos_ref[...], sin_ref[...]
+    count, base = query_ref.shape
+    width = owns[0].shape[1]
+    half = width // 2
+    out_ref[:, :base] = query_ref[...]
+    for c in range(chunks):
+        for h in range(half // HD):
+            at = h * HD
+            both = owns[c][:, at : at + HD] + got_ref[:count, c * width + at : c * width + at + HD]
+            both = jnp.concatenate(rotate(both[:, :HALF], both[:, HALF:], cosine, sine), -1)
+            at += base + c * width
+            out_ref[:, at : at + HD] = both.astype(jnp.bfloat16)
+        values = owns[c][:, half:] + got_ref[:count, c * width + half : (c + 1) * width]
+        at = base + c * width + half
+        out_ref[:, at : at + half] = values.astype(jnp.bfloat16)
+
+
+def pack(owns, got, cosine, sine, queries):
+    vmem = pl.BlockSpec(memory_space=pltpu.VMEM)
+    width = queries.shape[1] + got.shape[1]
+    return pl.pallas_call(
+        functools.partial(pack_kernel, len(owns)),
+        out_shape=jax.ShapeDtypeStruct((queries.shape[0], width), jnp.bfloat16),
+        in_specs=[vmem] * (len(owns) + 4),
+        out_specs=vmem,
+        compiler_params=pltpu.CompilerParams(vmem_limit_bytes=VMEM_BYTES),
+        cost_estimate=pl.CostEstimate(
+            flops=0, bytes_accessed=4 * queries.size + 10 * got.size, transcendentals=0
+        ),
+        name="pack_new",
+    )(*owns, got, cosine, sine, queries)
+
+
 def pick_kernel(side_ref, source_ref, out_ref):
     out_ref[...] = source_ref[...]
 
@@ -235,18 +301,18 @@
     places = ((owners // half_rows) ^ core) * half_rows + owners % half_rows
 
     chunk = kv_weight.shape[2] // CHUNKS
-    own = lax.dynamic_slice_in_dim(kv_weight, side * half, half, 0)
-    own = own.reshape(half, 2, CHUNKS, chunk).swapaxes(1, 2).reshape(half, -1)
     width = 2 * chunk
+    own = own_half(kv_weight, side)
 
     def step(pair):
         return lax.ppermute(pair[0], "rows", onward), lax.ppermute(pair[1], "rows", back)
 
     cuts = (0, 2 * tokens // 5, 4 * tokens // 5, tokens)
     sent = [pick_columns(passages, 1 - side, half, cuts[0], cuts[1])]
-    own, sent[0], passages, new_hidden = fence(own, sent[0], passages, new_hidden)
+    own, passages_later, new_hidden = fence(own, passages, new_hidden)
     got = [lax.ppermute(sent[0], "groups", partners)]
     ring = [step((own, own))]
+    passages = passages_later
     sent += [pick_columns(passages, 1 - side, half, *cuts[i : i + 2]) for i in (1, 2)]
     kept = pick_columns(passages, side, half, 0, tokens)
     new_rows = jnp.swapaxes(new_hidden, 0, 1).reshape(count, half_model)
@@ -260,15 +326,15 @@
     got.append(lax.ppermute(sent[1], "groups", partners))
     ring.append(step(ring[-1]))
     kept_other = lax.ppermute(kept, "tensor", cores)
-    new_got = lax.ppermute(new_sent, "groups", partners)
+    got_other = [lax.ppermute(got[0], "tensor", cores)]
     position, new_position, key_info, query_info = token_tables(
         lengths, destinations, row_index, tokens, requests, steps, new_padded
     )
     cosine, sine = angle_tables(position)
     new_cosine, new_sine = angle_tables(new_position)
     tables = (cosine, sine, new_cosine, new_sine, key_info, query_info)
-    ring[1], got[1], kept_other, new_got, tables, places = fence(
-        ring[1], got[1], kept_other, new_got, tables, places
+    ring[1], got[1], kept_other, got_other, tables, places = fence(
+        ring[1], got[1], kept_other, got_other, tables, places
     )
 
     def project(hidden, total, begin, end, column, width):
@@ -286,13 +352,13 @@
     last = []
     own_hidden = [(kept, kept_other)]
     early = row_count - 3
-    got_other = []
     for k in range(2, half_rows - 1):
         if k > 2:
             ring[-1] = fence(*ring[-1])
         else:
             got.append(lax.ppermute(sent[2], "groups", partners))
-            got_other += [lax.ppermute(piece, "tensor", cores) for piece in got[:2]]
+            got_other.append(lax.ppermute(got[1], "tensor", cores))
+            new_got = lax.ppermute(new_sent, "groups", partners)
         ring.append(step(ring[-1]))
     held = project(own_hidden, None, 0, early, 0, 2 * width)
     new_kept = jnp.concatenate([new_kept, new_got], 0)
@@ -318,33 +384,28 @@
     away = project(away_hidden, away, row_count - 1, row_count, 0, width)
     away, places = fence(homeward(away), places)
     homed = [lax.ppermute(away[0], "groups", partners)]
-    new_totals = [away[2] + lax.ppermute(away[1], "groups", partners)[:count]]
+    new_own, new_away = [away[2]], [away[1]]
     away = project(away_hidden, None, 0, row_count - 1, width, width)
     away = homeward(project(away_hidden, away, row_count - 1, row_count, width, width))
-    new_totals.append(away[2] + lax.ppermute(away[1], "groups", partners)[:count])
-    mine = [project(own_hidden, held, early, row_count, 0, width)]
-    homed[0], away, mine, new_totals, held, queries, places = fence(
-        homed[0], away, mine, new_totals, held, queries, places
+    new_own.append(away[2])
+    new_away.append(away[1])
+    new_back = lax.ppermute(jnp.concatenate(new_away, 1), "groups", partners)
+    mine = [project(own_hidden, held, early, row_count, c * width, width) for c in range(CHUNKS)]
+    queries = jnp.swapaxes(queries, 0, 1).reshape(count, -1)
+    homed[0], away, mine, new_own, new_back, queries = fence(
+        homed[0], away, mine, new_own, new_back, queries
     )
 
     homed.append(lax.ppermute(away[0], "groups", partners))
     cosine, sine, new_cosine, new_sine, key_info, query_info = tables
-    moved = [jnp.swapaxes(queries, 0, 1).reshape(count, -1)]
-    for total in new_totals:
-        pairs = total.reshape(count, 2, -1, 2, HALF)
-        keys = rotate(
-            pairs[:, 0, :, 0], pairs[:, 0, :, 1], new_cosine[:, None, :], new_sine[:, None, :]
-        )
-        keys = jnp.stack(keys, 2).reshape(count, chunk)
-        moved += [keys.astype(jnp.bfloat16), total[:, chunk:].astype(jnp.bfloat16)]
-    moved = jnp.concatenate(moved, 1).reshape(steps, requests, -1)
+    moved = pack(new_own, new_back, new_cosine, new_sine, queries)
+    moved = moved.reshape(steps, requests, -1)
     moved = jnp.swapaxes(moved, 0, 1)
     moved = lax.all_to_all(moved, "rows", split_axis=0, concat_axis=0, tiled=True)
     moved = jnp.swapaxes(moved, 0, 1).reshape(count, -1)
-    heads_width = queries.shape[2]
+    heads_width = queries.shape[1]
     query_rows, new_pairs = moved[:, :heads_width], moved[:, heads_width:]
     new_pairs = jnp.pad(new_pairs, ((0, new_padded - count), (0, 0)))
-    mine.append(project(own_hidden, held, early, row_count, width, width))
     homed = [total.astype(jnp.float32) * (1.0 / RAISE) for total in homed]
     attended = finish(mine, homed, cosine, sine, key_info, query_info, new_pairs, query_rows)
     attended = jnp.swapaxes(attended.reshape(steps, requests, -1), 0, 1)

time: 171 us -> 157 us (0.918)
  local copies, waits for them, and re-layouts: 26.7 us -> 11.1 us
  Pallas kernels: 33.7 us -> 38.8 us
  waiting for transfers between devices: 59.7 us -> 64.2 us
  other arithmetic: 9.09 us -> 5.93 us
  blocking collectives: 13.9 us -> 11.7 us
  starting transfers between devices: 26.9 us -> 24.7 us
    ppermute x1, waiting for transfers between devices: 23.5 us -> 4.27 us  [body(): new_got = lax.ppermute(new_sent, 'groups', partners)]
    ppermute x5, waiting for transfers between devices: 29.7 us -> 44.4 us  [step(): lax.ppermute(pair[0], 'rows', onward)]
    unnamed x54 -> x32, local copies, waits for them, and re-layouts: 17.4 us -> 8.34 us
    all_to_all x1, waiting for transfers between devices: 0.01 us -> 7.32 us  [body(): lax.all_to_all(moved, 'rows', split_axis=0, concat_axis=0, tiled=True)]
    pallas_call x7, Pallas kernels: 27.2 us -> 30.5 us  [products(): pl.pallas_call(functools.partial(product_kernel, depths, len(hidden), bas...]
    pallas_call x0 -> x2, Pallas kernels: none -> 3.3 us  [the longest x1 3.15 us: own_half(): pl.pallas_call(own_kernel, out_shape=jax.ShapeDtypeStruct((half, kinds *...]
    ppermute x4 -> x3, starting transfers between devices: 3.57 us -> 0.62 us  [the longest x1 0.61 us: body(): new_back = lax.ppermute(jnp.concatenate(new_away, 1), 'groups', partners)]
    ppermute x1, waiting for transfers between devices: 0.02 us -> 2.68 us  [body(): got = [lax.ppermute(sent[0], 'groups', partners)]]
  transfers between devices with their start and end apart: 24 -> 23, of which waited for: 8 -> 10; matrix products, arithmetic and copies ran while one was open for 6% -> 5% of each run, Pallas kernels for 17% -> 19%
where the time goes in v7:
time: 157 us
  waiting for transfers between devices  64.2 us (41%)
  Pallas kernels  38.8 us (25%)
  starting transfers between devices  24.7 us (16%)
  blocking collectives  11.7 us (7%)
  local copies, waits for them, and re-layouts  11.1 us (7%)
  other arithmetic  5.93 us (4%)
    ppermute x5, waiting for transfers between devices, step(): lax.ppermute(pair[0], 'rows', onward)  44.4 us
    pallas_call x7, Pallas kernels, products(): pl.pallas_call(functools.partial(product_kernel, depths, len(hidden), bas...  30.5 us
    all_to_all x1, blocking collectives, body(): lax.all_to_all(attended, 'rows', split_axis=0, concat_axis=0, tiled=True)  11.7 us
    ppermute x5, starting transfers between devices, step(): lax.ppermute(pair[0], 'rows', onward)  9.66 us
    unnamed x32, local copies, waits for them, and re-layouts  8.34 us
    all_to_all x1, waiting for transfers between devices, body(): lax.all_to_all(moved, 'rows', split_axis=0, concat_axis=0, tiled=True)  7.32 us
    ppermute x5, waiting for transfers between devices, step(): lax.ppermute(pair[1], 'rows', back)  5.53 us
    ppermute x1, waiting for transfers between devices, body(): new_got = lax.ppermute(new_sent, 'groups', partners)  4.27 us
  transfers between devices with their start and end apart: 23, of which 10 were waited for; matrix products, arithmetic and copies ran while one was open for 5% of the time, Pallas kernels for 19%

profile of v7, /device:TPU:0, one launch (start us, length us, event | category | flops | bytes accessed | tf_op | source)
XLA Modules:
  0.0 156.9 jit_solution(7372718961243424792)
XLA Ops:
  1.6 3.1 %own_half.1.refs_3_.refs_9_ = bf16[512,1024]{1,0:T(8,128)(2,1)} custom-call(s32[1]{0:T(128)} %bitcast.side_ref, bf16[1024,2,512]{2,1,0:T(2,128)(2,1)S(1)} %copy-done.7), custom_call_target="tpu_custom_call" | custom-call | bytes 4194304 | tf_op jit(solution)/shard_map/own_half/pallas_call | solution.py:127
  4.7 3.0 %collective-permute-start = (bf16[512,1024]{1,0:T(8,128)(2,1)}, bf16[512,1024]{1,0:T(8,128)(2,1)}, u32[]{:S(2)}, u32[]{:S(2)}) collective-permute-start(bf16[512,1024]{1,0:T(8,128)(2,1)} %own_half.1.refs_3_.refs_9_), channel_id=1, source_target_pairs={{0,4},{4,8},{8,12},{12,14},{14,10},{10,6},{6,2},{2,0},{1,5},{5,9},... | collective-permute-start | bytes 3145736 | tf_op jit(solution)/shard_map/ppermute | solution.py:308
  7.8 2.5 %copy-done = bf16[640,4096]{1,0:T(8,128)(2,1)S(1)} copy-done((bf16[640,4096]{1,0:T(8,128)(2,1)S(1)}, bf16[640,4096]{1,0:T(8,128)(2,1)}, u32[]{:S(2)}) %copy-start) | copy-done | bytes 5242904
  10.6 2.0 %collective-permute-start.2 = (bf16[256,2048]{1,0:T(8,128)(2,1)S(1)}, bf16[256,2048]{1,0:T(8,128)(2,1)}, u32[]{:S(2)}, u32[]{:S(2)}) collective-permute-start(bf16[256,2048]{1,0:T(8,128)(2,1)S(1)} %pick_columns.6), channel_id=1, source_target_pairs={{0,16},{16,0},{1,17},{17,1},{2,18},{18,2},{3,19},{19,3},{4,20},{20... | collective-permute-start | bytes 3145736 | tf_op jit(solution)/shard_map/ppermute | solution.py:313
  16.0 15.1 %collective-permute-done.refs_4_.refs_10_ = bf16[512,1024]{1,0:T(8,128)(2,1)} collective-permute-done((bf16[512,1024]{1,0:T(8,128)(2,1)}, bf16[512,1024]{1,0:T(8,128)(2,1)}, u32[]{:S(2)}, u32[]{:S(2)}) %collective-permute-start) | collective-permute-done | bytes 1048608 | tf_op jit(solution)/shard_map/ppermute | solution.py:308
  32.7 2.7 %collective-permute-done.2.refs_1_ = bf16[256,2048]{1,0:T(8,128)(2,1)} collective-permute-done((bf16[256,2048]{1,0:T(8,128)(2,1)S(1)}, bf16[256,2048]{1,0:T(8,128)(2,1)}, u32[]{:S(2)}, u32[]{:S(2)}) %collective-permute-start.2) | collective-permute-done | bytes 1048608 | tf_op jit(solution)/shard_map/ppermute | solution.py:313
  36.8 1.7 %collective-permute-start.3 = (bf16[512,1024]{1,0:T(8,128)(2,1)}, bf16[512,1024]{1,0:T(8,128)(2,1)}, u32[]{:S(2)}, u32[]{:S(2)}) collective-permute-start(bf16[512,1024]{1,0:T(8,128)(2,1)} %collective-permute-done.refs_4_.refs_10_), channel_id=1, source_target_pairs={{0,4},{4,8},{8,12},{12,14},{14,10},{10,6},{6,2},{2,0},{1,5},{5,9},... | collective-permute-start | bytes 3145736 | tf_op jit(solution)/shard_map/ppermute | solution.py:308
  38.8 1.7 %collective-permute-start.5 = (bf16[256,2048]{1,0:T(8,128)(2,1)}, bf16[256,2048]{1,0:T(8,128)(2,1)}, u32[]{:S(2)}, u32[]{:S(2)}) collective-permute-start(bf16[256,2048]{1,0:T(8,128)(2,1)} %copy-done.8), channel_id=1, source_target_pairs={{0,16},{16,0},{1,17},{17,1},{2,18},{18,2},{3,19},{19,3},{4,20},{20... | collective-permute-start | bytes 3145736 | tf_op jit(solution)/shard_map/ppermute | solution.py:326
  41.1 1.9 %multiply_sine_fusion = (f32[640,64]{1,0:T(8,128)S(1)}, f32[640,64]{1,0:T(8,128)S(1)}) fusion(f32[64]{0:T(128)} %copy-done.15, f32[640]{0:T(1024)S(1)} %subtract_convert_fusion), kind=kLoop, calls=%fused_computation.6 | loop fusion | flops 40960 | bytes 330496 | tf_op jit(solution)/shard_map/sin | solution.py:24
  42.9 19.7 %collective-permute-done.3.refs_6_.refs_12_ = bf16[512,1024]{1,0:T(8,128)(2,1)} collective-permute-done((bf16[512,1024]{1,0:T(8,128)(2,1)}, bf16[512,1024]{1,0:T(8,128)(2,1)}, u32[]{:S(2)}, u32[]{:S(2)}) %collective-permute-start.3) | collective-permute-done | bytes 1048608 | tf_op jit(solution)/shard_map/ppermute | solution.py:308
  64.1 1.7 %collective-permute-start.8 = (bf16[512,1024]{1,0:T(8,128)(2,1)}, bf16[512,1024]{1,0:T(8,128)(2,1)S(1)}, u32[]{:S(2)}, u32[]{:S(2)}) collective-permute-start(bf16[512,1024]{1,0:T(8,128)(2,1)} %collective-permute-done.3.refs_6_.refs_12_), channel_id=1, source_target_pairs={{0,4},{4,8},{8,12},{12,14},{14,10},{10,6},{6,2},{2,0},{1,5},{5,9},... | collective-permute-start | bytes 3145736 | tf_op jit(solution)/shard_map/ppermute | solution.py:308
  68.3 4.3 %collective-permute-done.12 = bf16[32,2048]{1,0:T(8,128)(2,1)S(1)} collective-permute-done((bf16[32,2048]{1,0:T(8,128)(2,1)S(1)}, bf16[32,2048]{1,0:T(8,128)(2,1)S(1)}, u32[]{:S(2)}, u32[]{:S(2)}) %collective-permute-start.12) | collective-permute-done | bytes 131104 | tf_op jit(solution)/shard_map/ppermute | solution.py:361
  72.5 6.8 %products.7.refs_7_ = f32[640,1024]{1,0:T(8,128)S(1)} custom-call(s32[8]{0:T(128)S(1)} %fusion.3.refs_0_, bf16[640,2048]{1,0:T(8,128)(2,1)S(1)} %pick_columns.9.refs_1_, bf16[640,2048]{1,0:T(8,128)(2,1)} %collective-permute-done.6.refs_2_, bf16[512,1024]{1,0:T(8,128)(2,1)} %own_half.1.refs_3_.refs_9_, ...), custom_call_target="tpu_custom_call" | custom-call | flops 3355443200 | bytes 11141120 | tf_op jit(solution)/shard_map/products/pallas_call | solution.py:246
  79.4 9.5 %collective-permute-done.8.refs_14_.refs_3_ = bf16[512,1024]{1,0:T(8,128)(2,1)S(1)} collective-permute-done((bf16[512,1024]{1,0:T(8,128)(2,1)}, bf16[512,1024]{1,0:T(8,128)(2,1)S(1)}, u32[]{:S(2)}, u32[]{:S(2)}) %collective-permute-start.8) | collective-permute-done | bytes 1048608 | tf_op jit(solution)/shard_map/ppermute | solution.py:308
  92.9 6.2 %products.8.refs_11_ = f32[704,512]{1,0:T(8,128)S(1)} custom-call(s32[8]{0:T(128)S(1)} %fusion.3.refs_0_, bf16[256,2048]{1,0:T(8,128)(2,1)} %collective-permute-done.2.refs_1_, bf16[256,2048]{1,0:T(8,128)(2,1)} %collective-permute-done.7.refs_2_, bf16[256,2048]{1,0:T(8,128)(2,1)} %collective-permute-done.5.refs_3_, ...), custom_call_target="tpu_custom_call" | custom-call | flops 2583691264 | bytes 10158080 | tf_op jit(solution)/shard_map/products/pallas_call | solution.py:246
  100.4 2.4 %products.9 = f32[704,512]{1,0:T(8,128)S(1)} custom-call(s32[8]{0:T(128)S(1)} %fusion.3.refs_0_, bf16[256,2048]{1,0:T(8,128)(2,1)} %collective-permute-done.2.refs_1_, bf16[256,2048]{1,0:T(8,128)(2,1)} %collective-permute-done.7.refs_2_, bf16[256,2048]{1,0:T(8,128)(2,1)} %collective-permute-done.5.refs_3_, ...), custom_call_target="tpu_custom_call" | custom-call | flops 369098752 | bytes 2686976 | tf_op jit(solution)/shard_map/products/pallas_call | solution.py:246
  106.6 6.2 %products.10.refs_11_ = f32[704,512]{1,0:T(8,128)S(1)} custom-call(s32[8]{0:T(128)S(1)} %fusion.3.refs_0_, bf16[256,2048]{1,0:T(8,128)(2,1)} %collective-permute-done.2.refs_1_, bf16[256,2048]{1,0:T(8,128)(2,1)} %collective-permute-done.7.refs_2_, bf16[256,2048]{1,0:T(8,128)(2,1)} %collective-permute-done.5.refs_3_, ...), custom_call_target="tpu_custom_call" | custom-call | flops 2583691264 | bytes 10158080 | tf_op jit(solution)/shard_map/products/pallas_call | solution.py:246
  112.8 3.0 %products.12.refs_0_ = f32[640,512]{1,0:T(8,128)S(1)} custom-call(s32[8]{0:T(128)S(1)} %fusion.3.refs_0_, bf16[640,2048]{1,0:T(8,128)(2,1)S(1)} %pick_columns.9.refs_1_, bf16[640,2048]{1,0:T(8,128)(2,1)} %collective-permute-done.6.refs_2_, bf16[512,1024]{1,0:T(8,128)(2,1)S(1)} %collective-permute-done.8.refs_14_.refs_3_, ...), custom_call_target="tpu_custom_call" | custom-call | flops 1006632960 | bytes 4849664 | tf_op jit(solution)/shard_map/products/pallas_call | solution.py:246
  115.8 2.9 %products.11 = f32[704,512]{1,0:T(8,128)S(1)} custom-call(s32[8]{0:T(128)S(1)} %fusion.3.refs_0_, bf16[256,2048]{1,0:T(8,128)(2,1)} %collective-permute-done.2.refs_1_, bf16[256,2048]{1,0:T(8,128)(2,1)} %collective-permute-done.7.refs_2_, bf16[256,2048]{1,0:T(8,128)(2,1)} %collective-permute-done.5.refs_3_, ...), custom_call_target="tpu_custom_call" | custom-call | flops 369098752 | bytes 2686976 | tf_op jit(solution)/shard_map/products/pallas_call | solution.py:246
  120.4 3.0 %products.13.refs_1_ = f32[640,512]{1,0:T(8,128)S(1)} custom-call(s32[8]{0:T(128)S(1)} %fusion.3.refs_0_, bf16[640,2048]{1,0:T(8,128)(2,1)S(1)} %pick_columns.9.refs_1_, bf16[640,2048]{1,0:T(8,128)(2,1)} %collective-permute-done.6.refs_2_, bf16[512,1024]{1,0:T(8,128)(2,1)S(1)} %collective-permute-done.8.refs_14_.refs_3_, ...), custom_call_target="tpu_custom_call" | custom-call | flops 1006632960 | bytes 4849664 | tf_op jit(solution)/shard_map/products/pallas_call | solution.py:246
  127.2 3.6 %all-to-all-start = ((bf16[8,3,5120]{2,1,0:T(4,128)(2,1)}), bf16[8,3,5120]{2,1,0:T(4,128)(2,1)S(1)}, u32[]{:S(2)}, u32[]{:S(2)}) async-start(bf16[8,3,5120]{2,1,0:T(4,128)(2,1)} %bitcast.32), calls=%async_computation | async-start | bytes 655360 | tf_op jit(solution)/shard_map/all_to_all | solution.py:404
  132.1 7.3 %all-to-all-done = bf16[8,3,5120]{2,1,0:T(4,128)(2,1)S(1)} async-done(((bf16[8,3,5120]{2,1,0:T(4,128)(2,1)}), bf16[8,3,5120]{2,1,0:T(4,128)(2,1)S(1)}, u32[]{:S(2)}, u32[]{:S(2)}) %all-to-all-start) | async-done | bytes 245792 | tf_op jit(solution)/shard_map/all_to_all | solution.py:404
  141.2 3.0 %rotate_attend.1 = bf16[24,4096]{1,0:T(8,128)(2,1)S(1)} custom-call(f32[640,512]{1,0:T(8,128)S(1)} %copy-done.4, f32[640,512]{1,0:T(8,128)S(1)} %copy-done.6, f32[640,512]{1,0:T(8,128)S(1)} %convert_multiply_fusion.1.refs_2_, f32[640,512]{1,0:T(8,128)S(1)} %convert_multiply_fusion.refs_3_, f32[640,64]{1,0:T(8,128)S(1)} %get-tuple-element.101.refs_4_, ...), custom_call_target="tpu_custom_call" | custom-call | flops 251658240 | bytes 5636096 | tf_op jit(solution)/shard_map/rotate_attend/pallas_call | solution.py:100
  144.4 11.7 %all_to_all.10 = bf16[8,3,4096]{2,1,0:T(4,128)(2,1)S(1)} all-to-all(bf16[8,3,4096]{2,1,0:T(4,128)(2,1)S(1)} %bitcast.39), channel_id=1, replica_groups=mesh['groups'=2,'rows'=8,'tensor'=2] {'rows'}, dimensions={0} | all-to-all | bytes 393216 | tf_op jit(solution)/shard_map/all_to_all | solution.py:412
  (125 shorter events, 31.3 us)
Async XLA Ops:
  4.7 26.4 %collective-permute-start = (bf16[512,1024]{1,0:T(8,128)(2,1)}, bf16[512,1024]{1,0:T(8,128)(2,1)}, u32[]{:S(2)}, u32[]{:S(2)}) collective-permute-start(bf16[512,1024]{1,0:T(8,128)(2,1)} %own_half.1.refs_3_.refs_9_), channel_id=1, source_target_pairs={{0,4},{4,8},{8,12},{12,14},{14,10},{10,6},{6,2},{2,0},{1,5},{5,9},... | collective-permute-start | bytes 3145736 | tf_op jit(solution)/shard_map/ppermute | solution.py:308
  7.8 24.9 %collective-permute-start.1 = (bf16[512,1024]{1,0:T(8,128)(2,1)}, bf16[512,1024]{1,0:T(8,128)(2,1)}, u32[]{:S(2)}, u32[]{:S(2)}) collective-permute-start(bf16[512,1024]{1,0:T(8,128)(2,1)} %own_half.1.refs_3_.refs_9_), channel_id=1, source_target_pairs={{4,0},{8,4},{12,8},{14,12},{10,14},{6,10},{2,6},{0,2},{5,1},{9,5},... | collective-permute-start | bytes 3145736 | tf_op jit(solution)/shard_map/ppermute | solution.py:308
  10.6 24.8 %collective-permute-start.2 = (bf16[256,2048]{1,0:T(8,128)(2,1)S(1)}, bf16[256,2048]{1,0:T(8,128)(2,1)}, u32[]{:S(2)}, u32[]{:S(2)}) collective-permute-start(bf16[256,2048]{1,0:T(8,128)(2,1)S(1)} %pick_columns.6), channel_id=1, source_target_pairs={{0,16},{16,0},{1,17},{17,1},{2,18},{18,2},{3,19},{19,3},{4,20},{20... | collective-permute-start | bytes 3145736 | tf_op jit(solution)/shard_map/ppermute | solution.py:313
  15.0 25.5 %copy-start.13 = (s32[8,8]{1,0:T(8,128)S(1)}, s32[8,8]{1,0:T(8,128)}, u32[]{:S(2)}) copy-start(s32[8,8]{1,0:T(8,128)} %param.12) | copy-start | bytes 772
  35.4 28.8 %collective-permute-start.6 = (bf16[640,2048]{1,0:T(8,128)(2,1)S(1)}, bf16[640,2048]{1,0:T(8,128)(2,1)}, u32[]{:S(2)}, u32[]{:S(2)}) collective-permute-start(bf16[640,2048]{1,0:T(8,128)(2,1)S(1)} %pick_columns.9.refs_1_), channel_id=1, source_target_pairs={{0,1},{1,0},{2,3},{3,2},{4,5},{5,4},{6,7},{7,6},{8,9},{9,8},{10,11... | collective-permute-start | bytes 7864328 | tf_op jit(solution)/shard_map/ppermute | solution.py:328
  36.8 25.9 %collective-permute-start.3 = (bf16[512,1024]{1,0:T(8,128)(2,1)}, bf16[512,1024]{1,0:T(8,128)(2,1)}, u32[]{:S(2)}, u32[]{:S(2)}) collective-permute-start(bf16[512,1024]{1,0:T(8,128)(2,1)} %collective-permute-done.refs_4_.refs_10_), channel_id=1, source_target_pairs={{0,4},{4,8},{8,12},{12,14},{14,10},{10,6},{6,2},{2,0},{1,5},{5,9},... | collective-permute-start | bytes 3145736 | tf_op jit(solution)/shard_map/ppermute | solution.py:308
  38.5 25.6 %collective-permute-start.4 = (bf16[512,1024]{1,0:T(8,128)(2,1)}, bf16[512,1024]{1,0:T(8,128)(2,1)}, u32[]{:S(2)}, u32[]{:S(2)}) collective-permute-start(bf16[512,1024]{1,0:T(8,128)(2,1)} %collective-permute-done.1.refs_5_.refs_11_), channel_id=1, source_target_pairs={{4,0},{8,4},{12,8},{14,12},{10,14},{6,10},{2,6},{0,2},{5,1},{9,5},... | collective-permute-start | bytes 3145736 | tf_op jit(solution)/shard_map/ppermute | solution.py:308
  38.8 25.3 %collective-permute-start.5 = (bf16[256,2048]{1,0:T(8,128)(2,1)}, bf16[256,2048]{1,0:T(8,128)(2,1)}, u32[]{:S(2)}, u32[]{:S(2)}) collective-permute-start(bf16[256,2048]{1,0:T(8,128)(2,1)} %copy-done.8), channel_id=1, source_target_pairs={{0,16},{16,0},{1,17},{17,1},{2,18},{18,2},{3,19},{19,3},{4,20},{20... | collective-permute-start | bytes 3145736 | tf_op jit(solution)/shard_map/ppermute | solution.py:326
  40.5 23.7 %collective-permute-start.7 = (bf16[256,2048]{1,0:T(8,128)(2,1)}, bf16[256,2048]{1,0:T(8,128)(2,1)}, u32[]{:S(2)}, u32[]{:S(2)}) collective-permute-start(bf16[256,2048]{1,0:T(8,128)(2,1)} %collective-permute-done.2.refs_1_), channel_id=1, source_target_pairs={{0,1},{1,0},{2,3},{3,2},{4,5},{5,4},{6,7},{7,6},{8,9},{9,8},{10,11... | collective-permute-start | bytes 3145736 | tf_op jit(solution)/shard_map/ppermute | solution.py:329
  64.1 24.7 %collective-permute-start.8 = (bf16[512,1024]{1,0:T(8,128)(2,1)}, bf16[512,1024]{1,0:T(8,128)(2,1)S(1)}, u32[]{:S(2)}, u32[]{:S(2)}) collective-permute-start(bf16[512,1024]{1,0:T(8,128)(2,1)} %collective-permute-done.3.refs_6_.refs_12_), channel_id=1, source_target_pairs={{0,4},{4,8},{8,12},{12,14},{14,10},{10,6},{6,2},{2,0},{1,5},{5,9},... | collective-permute-start | bytes 3145736 | tf_op jit(solution)/shard_map/ppermute | solution.py:308
  65.9 24.3 %collective-permute-start.9 = (bf16[512,1024]{1,0:T(8,128)(2,1)}, bf16[512,1024]{1,0:T(8,128)(2,1)S(1)}, u32[]{:S(2)}, u32[]{:S(2)}) collective-permute-start(bf16[512,1024]{1,0:T(8,128)(2,1)} %collective-permute-done.4.refs_7_.refs_13_), channel_id=1, source_target_pairs={{4,0},{8,4},{12,8},{14,12},{10,14},{6,10},{2,6},{0,2},{5,1},{9,5},... | collective-permute-start | bytes 3145736 | tf_op jit(solution)/shard_map/ppermute | solution.py:308
  66.2 24.0 %collective-permute-start.11 = (bf16[256,2048]{1,0:T(8,128)(2,1)}, bf16[256,2048]{1,0:T(8,128)(2,1)S(1)}, u32[]{:S(2)}, u32[]{:S(2)}) collective-permute-start(bf16[256,2048]{1,0:T(8,128)(2,1)} %collective-permute-done.5.refs_3_), channel_id=1, source_target_pairs={{0,1},{1,0},{2,3},{3,2},{4,5},{5,4},{6,7},{7,6},{8,9},{9,8},{10,11... | collective-permute-start | bytes 3145736 | tf_op jit(solution)/shard_map/ppermute | solution.py:360
  66.2 6.3 %collective-permute-start.12 = (bf16[32,2048]{1,0:T(8,128)(2,1)S(1)}, bf16[32,2048]{1,0:T(8,128)(2,1)S(1)}, u32[]{:S(2)}, u32[]{:S(2)}) collective-permute-start(bf16[32,2048]{1,0:T(8,128)(2,1)S(1)} %pick_columns.10), channel_id=1, source_target_pairs={{0,16},{16,0},{1,17},{17,1},{2,18},{18,2},{3,19},{19,3},{4,20},{20... | collective-permute-start | bytes 393224 | tf_op jit(solution)/shard_map/ppermute | solution.py:361
  67.8 22.4 %collective-permute-start.10 = (bf16[128,2048]{1,0:T(8,128)(2,1)}, bf16[128,2048]{1,0:T(8,128)(2,1)S(1)}, u32[]{:S(2)}, u32[]{:S(2)}) collective-permute-start(bf16[128,2048]{1,0:T(8,128)(2,1)} %copy-done.9), channel_id=1, source_target_pairs={{0,16},{16,0},{1,17},{17,1},{2,18},{18,2},{3,19},{19,3},{4,20},{20... | collective-permute-start | bytes 1572872 | tf_op jit(solution)/shard_map/ppermute | solution.py:359
  90.2 2.7 %collective-permute-start.15 = (bf16[128,2048]{1,0:T(8,128)(2,1)S(1)}, bf16[128,2048]{1,0:T(8,128)(2,1)S(1)}, u32[]{:S(2)}, u32[]{:S(2)}) collective-permute-start(bf16[128,2048]{1,0:T(8,128)(2,1)S(1)} %collective-permute-done.10.refs_5_), channel_id=1, source_target_pairs={{0,1},{1,0},{2,3},{3,2},{4,5},{5,4},{6,7},{7,6},{8,9},{9,8},{10,11... | collective-permute-start | bytes 1572872 | tf_op jit(solution)/shard_map/ppermute | solution.py:376
  90.3 2.6 %collective-permute-start.16 = (bf16[64,2048]{1,0:T(8,128)(2,1)S(1)}, bf16[64,2048]{1,0:T(8,128)(2,1)S(1)}, u32[]{:S(2)}, u32[]{:S(2)}) collective-permute-start(bf16[64,2048]{1,0:T(8,128)(2,1)S(1)} %pad_maximum_fusion.refs_7_), channel_id=1, source_target_pairs={{0,1},{1,0},{2,3},{3,2},{4,5},{5,4},{6,7},{7,6},{8,9},{9,8},{10,11... | collective-permute-start | bytes 786440 | tf_op jit(solution)/shard_map/ppermute | solution.py:377
  90.8 8.3 %collective-permute-start.13 = (bf16[256,512]{1,0:T(8,128)(2,1)S(1)}, bf16[256,512]{1,0:T(8,128)(2,1)S(1)}, u32[]{:S(2)}, u32[]{:S(2)}) collective-permute-start(bf16[256,512]{1,0:T(8,128)(2,1)S(1)} %slice.48), channel_id=1, source_target_pairs={{0,4},{4,8},{8,12},{12,14},{14,10},{10,6},{6,2},{2,0},{1,5},{5,9},... | collective-permute-start | bytes 786440 | tf_op jit(solution)/shard_map/ppermute | solution.py:308
  92.4 8.0 %collective-permute-start.14 = (bf16[256,512]{1,0:T(8,128)(2,1)S(1)}, bf16[256,512]{1,0:T(8,128)(2,1)S(1)}, u32[]{:S(2)}, u32[]{:S(2)}) collective-permute-start(bf16[256,512]{1,0:T(8,128)(2,1)S(1)} %slice.49), channel_id=1, source_target_pairs={{4,0},{8,4},{12,8},{14,12},{10,14},{6,10},{2,6},{0,2},{5,1},{9,5},... | collective-permute-start | bytes 786440 | tf_op jit(solution)/shard_map/ppermute | solution.py:308
  103.0 12.8 %collective-permute-start.18 = (bf16[256,512]{1,0:T(8,128)(2,1)S(1)}, bf16[256,512]{1,0:T(8,128)(2,1)S(1)}, u32[]{:S(2)}, u32[]{:S(2)}) collective-permute-start(bf16[256,512]{1,0:T(8,128)(2,1)S(1)} %slice.38), channel_id=1, source_target_pairs={{0,4},{4,8},{8,12},{12,14},{14,10},{10,6},{6,2},{2,0},{1,5},{5,9},... | collective-permute-start | bytes 786440 | tf_op jit(solution)/shard_map/ppermute | solution.py:308
  104.6 11.2 %collective-permute-start.19 = (bf16[256,512]{1,0:T(8,128)(2,1)S(1)}, bf16[256,512]{1,0:T(8,128)(2,1)S(1)}, u32[]{:S(2)}, u32[]{:S(2)}) collective-permute-start(bf16[256,512]{1,0:T(8,128)(2,1)S(1)} %slice.39), channel_id=1, source_target_pairs={{4,0},{8,4},{12,8},{14,12},{10,14},{6,10},{2,6},{0,2},{5,1},{9,5},... | collective-permute-start | bytes 786440 | tf_op jit(solution)/shard_map/ppermute | solution.py:308
  105.1 19.4 %collective-permute-start.17 = (f16[640,512]{1,0:T(8,128)(2,1)S(1)}, f16[640,512]{1,0:T(8,128)(2,1)S(1)}, u32[]{:S(2)}, u32[]{:S(2)}) collective-permute-start(f16[640,512]{1,0:T(8,128)(2,1)S(1)} %fusion.1), channel_id=1, source_target_pairs={{0,16},{16,0},{1,17},{17,1},{2,18},{18,2},{3,19},{19,3},{4,20},{20... | collective-permute-start | bytes 1966088 | tf_op jit(solution)/shard_map/ppermute | solution.py:386
  118.8 5.7 %collective-permute-start.20 = (f32[32,1024]{1,0:T(8,128)S(1)}, f32[32,1024]{1,0:T(8,128)S(1)}, u32[]{:S(2)}, u32[]{:S(2)}) collective-permute-start(f32[32,1024]{1,0:T(8,128)S(1)} %pad_maximum_fusion.1), channel_id=1, source_target_pairs={{0,16},{16,0},{1,17},{17,1},{2,18},{18,2},{3,19},{19,3},{4,20},{20... | collective-permute-start | bytes 393224 | tf_op jit(solution)/shard_map/ppermute | solution.py:392
  124.5 15.1 %collective-permute-start.21 = (f16[640,512]{1,0:T(8,128)(2,1)}, f16[640,512]{1,0:T(8,128)(2,1)S(1)}, u32[]{:S(2)}, u32[]{:S(2)}) collective-permute-start(f16[640,512]{1,0:T(8,128)(2,1)} %fusion), channel_id=1, source_target_pairs={{0,16},{16,0},{1,17},{17,1},{2,18},{18,2},{3,19},{19,3},{4,20},{20... | collective-permute-start | bytes 1966088 | tf_op jit(solution)/shard_map/ppermute | solution.py:399
  127.2 12.3 %all-to-all-start = ((bf16[8,3,5120]{2,1,0:T(4,128)(2,1)}), bf16[8,3,5120]{2,1,0:T(4,128)(2,1)S(1)}, u32[]{:S(2)}, u32[]{:S(2)}) async-start(bf16[8,3,5120]{2,1,0:T(4,128)(2,1)} %bitcast.32), calls=%async_computation | async-start | bytes 655360 | tf_op jit(solution)/shard_map/all_to_all | solution.py:404
  (16 other events, 83.8 us)

commit v8 on v7

--- a/solution.py
+++ b/solution.py
@@ -112,28 +112,28 @@
     )(*operands)
 
 
-def own_kernel(side_ref, weight_ref, out_ref):
-    chunk = out_ref.shape[1] // (2 * CHUNKS)
+def own_kernel(side_ref, weight_ref, *out_refs):
+    chunk = out_refs[0].shape[1] // 2
     for kind in range(2):
         columns = weight_ref[:, kind, :]
-        for c in range(CHUNKS):
-            at = (2 * c + kind) * chunk
-            out_ref[:, at : at + chunk] = columns[:, c * chunk : (c + 1) * chunk]
+        for c, out_ref in enumerate(out_refs):
+            out_ref[:, kind * chunk : (kind + 1) * chunk] = columns[:, c * chunk : (c + 1) * chunk]
 
 
 def own_half(weight, side):
     depth, kinds, width = weight.shape
     half = depth // 2
+    chunk = kinds * width // CHUNKS
     return pl.pallas_call(
         own_kernel,
-        out_shape=jax.ShapeDtypeStruct((half, kinds * width), weight.dtype),
+        out_shape=[jax.ShapeDtypeStruct((half, chunk), weight.dtype)] * CHUNKS,
         grid_spec=pltpu.PrefetchScalarGridSpec(
             num_scalar_prefetch=1,
             grid=(2,),
             in_specs=[
                 pl.BlockSpec((half // 2, kinds, width), lambda i, s: (2 * s[0] + i, 0, 0))
             ],
-            out_specs=pl.BlockSpec((half // 2, kinds * width), lambda i, s: (i, 0)),
+            out_specs=[pl.BlockSpec((half // 2, chunk), lambda i, s: (i, 0))] * CHUNKS,
         ),
         compiler_params=pltpu.CompilerParams(vmem_limit_bytes=VMEM_BYTES),
         cost_estimate=pl.CostEstimate(
@@ -178,23 +178,20 @@
     )(*owns, got, cosine, sine, queries)
 
 
-def pick_kernel(side_ref, source_ref, out_ref):
-    out_ref[...] = source_ref[...]
+def pick_kernel(first, side_ref, source_ref, out_ref):
+    out_ref[...] = source_ref[first : first + out_ref.shape[0], :]
 
 
 def pick_columns(source, side, half, first, end):
-    blocks = source.shape[1] // (2 * half)
-    rows = math.gcd(first, end) if first else end
+    rows, blocks = source.shape[0], source.shape[1] // (2 * half)
     return pl.pallas_call(
-        pick_kernel,
+        functools.partial(pick_kernel, first),
         out_shape=jax.ShapeDtypeStruct((end - first, blocks * half), source.dtype),
         grid_spec=pltpu.PrefetchScalarGridSpec(
             num_scalar_prefetch=1,
-            grid=((end - first) // rows, blocks),
-            in_specs=[
-                pl.BlockSpec((rows, half), lambda i, j, s: (first // rows + i, 2 * j + s[0]))
-            ],
-            out_specs=pl.BlockSpec((rows, half), lambda i, j, s: (i, j)),
+            grid=(blocks,),
+            in_specs=[pl.BlockSpec((rows, half), lambda j, s: (0, 2 * j + s[0]))],
+            out_specs=pl.BlockSpec((end - first, half), lambda j, s: (0, j)),
         ),
         compiler_params=pltpu.CompilerParams(vmem_limit_bytes=VMEM_BYTES),
         cost_estimate=pl.CostEstimate(
@@ -204,18 +201,14 @@
     )(side.reshape(1), source)
 
 
-def product_kernel(depths, parts, base, column, has_total, *refs):
+def product_kernel(depths, parts, base, has_total, *refs):
     place_ref, refs = refs[0], refs[1:]
     hidden, refs = refs[: 2 * parts], refs[2 * parts :]
     weights, out_ref = refs[: sum(len(pieces) for pieces in depths)], refs[-1]
-    width = out_ref.shape[1]
     half = sum(depths[0])
     blocks = hidden[0].shape[1] // half
 
-    def window(ref):
-        return ref[...] if ref.shape[1] == width else ref[:, column : column + width]
-
-    total, used = window(refs[-2]) if has_total else None, 0
+    total, used = refs[-2][...] if has_total else None, 0
     for p, pieces in enumerate(depths):
         place = place_ref[base + p]
         here = place < blocks
@@ -225,7 +218,7 @@
             for q in range(parts)
         ]
         rows = rows[0] if parts == 1 else jnp.concatenate(rows, 0)
-        piece = [window(w) for w in weights[used : used + len(pieces)]]
+        piece = [w[...] for w in weights[used : used + len(pieces)]]
         piece = piece[0] if len(piece) == 1 else jnp.concatenate(piece, 0)
         used += len(pieces)
         term = jnp.dot(rows, piece, preferred_element_type=jnp.float32)
@@ -233,11 +226,11 @@
     out_ref[...] = total
 
 
-def products(total, hidden, weights, places, base, column, width):
+def products(total, hidden, weights, places, base):
     shards = len(weights)
     flat = [w for shard in weights for w in shard]
     depths = tuple(tuple(w.shape[0] for w in shard) for shard in weights)
-    half = sum(depths[0])
+    half, width = sum(depths[0]), flat[0].shape[1]
     rows = sum(pair[0].shape[0] for pair in hidden)
     operands = [places] + [array for pair in hidden for array in pair] + flat
     if total is not None:
@@ -245,7 +238,7 @@
     vmem = pl.BlockSpec(memory_space=pltpu.VMEM)
     return pl.pallas_call(
         functools.partial(
-            product_kernel, depths, len(hidden), base, column, total is not None
+            product_kernel, depths, len(hidden), base, total is not None
         ),
         out_shape=jax.ShapeDtypeStruct((rows, width), jnp.float32),
         in_specs=[pl.BlockSpec(memory_space=pltpu.SMEM)] + [vmem] * (len(operands) - 1),
@@ -300,18 +293,40 @@
     owners = lax.dynamic_index_in_dim(jnp.array(shard_order, jnp.int32), row_index, 1, keepdims=False)
     places = ((owners // half_rows) ^ core) * half_rows + owners % half_rows
 
-    chunk = kv_weight.shape[2] // CHUNKS
-    width = 2 * chunk
     own = own_half(kv_weight, side)
 
-    def step(pair):
-        return lax.ppermute(pair[0], "rows", onward), lax.ppermute(pair[1], "rows", back)
-
-    cuts = (0, 2 * tokens // 5, 4 * tokens // 5, tokens)
+    ring, ends = [[(piece, piece)] for piece in own], [None, None]
+
+    def halved(pair):
+        return pair[0][: half // 2], pair[1][half // 2 :]
+
+    def step(c):
+        pair = ring[c][-1]
+        if len(ring[c]) == half_rows:
+            pair = ends[c]
+        ring[c].append((lax.ppermute(pair[0], "rows", onward), lax.ppermute(pair[1], "rows", back)))
+
+    def fence_with(c, *others):
+        ring[c][-1], others = fence(ring[c][-1], others)
+        return others
+
+    def project(c, hidden, total, begin, end):
+        weights = [(own[c],)] + [(w,) for pair in ring[c][1:half_rows] for w in pair]
+        weights += ring[c][half_rows:]
+        for at in range(begin, end, MOST_SHARDS):
+            some = weights[at : min(at + MOST_SHARDS, end)]
+            total = products(total, hidden, some, places, at)
+        return total
+
+    def homeward(total):
+        tokens_total = (total[:tokens] * RAISE).astype(jnp.float16)
+        return tokens_total, total[tokens + new_padded :], total[tokens : tokens + count]
+
+    cuts = (0, tokens // 10, tokens // 20 * 11, tokens)
     sent = [pick_columns(passages, 1 - side, half, cuts[0], cuts[1])]
-    own, passages_later, new_hidden = fence(own, passages, new_hidden)
+    (passages_later, new_hidden) = fence_with(0, passages, new_hidden)
     got = [lax.ppermute(sent[0], "groups", partners)]
-    ring = [step((own, own))]
+    step(0)
     passages = passages_later
     sent += [pick_columns(passages, 1 - side, half, *cuts[i : i + 2]) for i in (1, 2)]
     kept = pick_columns(passages, side, half, 0, tokens)
@@ -319,84 +334,71 @@
     new_rows = jnp.pad(new_rows, ((0, new_padded - count), (0, 0)))
     new_sent = pick_columns(new_rows, 1 - side, half, 0, new_padded)
     new_kept = pick_columns(new_rows, side, half, 0, new_padded)
-    ring[0], got[0], sent, kept, new_sent, new_kept, lengths, destinations = fence(
-        ring[0], got[0], sent, kept, new_sent, new_kept, lengths, destinations
-    )
+    new_got = lax.ppermute(new_sent, "groups", partners)
+    got[0], sent, kept, new_got, new_kept, lengths, destinations = fence_with(
+        0, got[0], sent, kept, new_got, new_kept, lengths, destinations
+    )
+    new_kept = jnp.concatenate([new_kept, new_got], 0)
 
     got.append(lax.ppermute(sent[1], "groups", partners))
-    ring.append(step(ring[-1]))
+    step(0)
     kept_other = lax.ppermute(kept, "tensor", cores)
     got_other = [lax.ppermute(got[0], "tensor", cores)]
+    kept_other, got_other = fence_with(1, kept_other, got_other)
+    step(1)
     position, new_position, key_info, query_info = token_tables(
         lengths, destinations, row_index, tokens, requests, steps, new_padded
     )
     cosine, sine = angle_tables(position)
     new_cosine, new_sine = angle_tables(new_position)
     tables = (cosine, sine, new_cosine, new_sine, key_info, query_info)
-    ring[1], got[1], kept_other, got_other, tables, places = fence(
-        ring[1], got[1], kept_other, got_other, tables, places
-    )
-
-    def project(hidden, total, begin, end, column, width):
-        weights = [(own,)] + [(w,) for pair in ring for w in pair]
-        weights = weights[: row_count - 1] + [last[column // width] if last else ()]
-        for at in range(begin, end, MOST_SHARDS):
-            some = weights[at : min(at + MOST_SHARDS, end)]
-            total = products(total, hidden, some, places, at, column, width)
-        return total
-
-    def homeward(total):
-        tokens_total = (total[:tokens] * RAISE).astype(jnp.float16)
-        return tokens_total, total[tokens + new_padded :], total[tokens : tokens + count]
-
-    last = []
+    got[1], tables, places, ring[1][-1] = fence_with(0, got[1], tables, places, ring[1][-1])
+
     own_hidden = [(kept, kept_other)]
     early = row_count - 3
-    for k in range(2, half_rows - 1):
-        if k > 2:
-            ring[-1] = fence(*ring[-1])
-        else:
-            got.append(lax.ppermute(sent[2], "groups", partners))
-            got_other.append(lax.ppermute(got[1], "tensor", cores))
-            new_got = lax.ppermute(new_sent, "groups", partners)
-        ring.append(step(ring[-1]))
-    held = project(own_hidden, None, 0, early, 0, 2 * width)
-    new_kept = jnp.concatenate([new_kept, new_got], 0)
-
-    def halved(c):
-        columns = slice(c * width, (c + 1) * width)
-        return ring[-1][0][: half // 2, columns], ring[-1][1][half // 2 :, columns]
-
-    ends = [halved(0)]
-    ring[-1], got[2], got_other, new_kept, held, ends, places = fence(
-        ring[-1], got[2], got_other, new_kept, held, ends, places
-    )
-
-    last.append(step(ends[0]))
+    got.append(lax.ppermute(sent[2], "groups", partners))
+    step(0)
+    got_other.append(lax.ppermute(got[1], "tensor", cores))
+    (got_other[1],) = fence_with(1, got_other[1])
+    step(1)
+    for k in range(3, half_rows - 1):
+        (ring[1][-1],) = fence_with(0, ring[1][-1])
+        step(0)
+        step(1)
+    held = [project(0, own_hidden, None, 0, early)]
+    ends[0] = halved(ring[0][-1])
+    got[2], new_kept, held, places, ring[1][-1], ends[0] = fence_with(
+        0, got[2], new_kept, held, places, ring[1][-1], ends[0]
+    )
+
+    step(0)
     got_other.append(lax.ppermute(got[2], "tensor", cores))
     new_other = lax.ppermute(new_kept, "tensor", cores)
+    new_other, got_other[2] = fence_with(1, new_other, got_other[2])
+    step(1)
     away_hidden = list(zip(got, got_other)) + [(new_kept, new_other)]
-    away = project(away_hidden, None, 0, row_count - 1, 0, width)
-    ends.append(halved(1))
-    last[0], away, ends, places = fence(last[0], away, ends, places)
-
-    last.append(step(ends[1]))
-    away = project(away_hidden, away, row_count - 1, row_count, 0, width)
+    held.append(project(1, own_hidden, None, 0, early))
+    places, held = fence(places, held)
+    away = project(0, away_hidden, None, 0, row_count)
     away, places = fence(homeward(away), places)
+    (places,) = fence_with(1, places)
+    ends[1] = halved(ring[1][-1])
+    step(1)
     homed = [lax.ppermute(away[0], "groups", partners)]
     new_own, new_away = [away[2]], [away[1]]
-    away = project(away_hidden, None, 0, row_count - 1, width, width)
-    away = homeward(project(away_hidden, away, row_count - 1, row_count, width, width))
+    away = project(1, away_hidden, None, 0, row_count - 1)
+    away = homeward(project(1, away_hidden, away, row_count - 1, row_count))
     new_own.append(away[2])
     new_away.append(away[1])
     new_back = lax.ppermute(jnp.concatenate(new_away, 1), "groups", partners)
-    mine = [project(own_hidden, held, early, row_count, c * width, width) for c in range(CHUNKS)]
+    held[0] = project(0, own_hidden, held[0], early, row_count)
     queries = jnp.swapaxes(queries, 0, 1).reshape(count, -1)
-    homed[0], away, mine, new_own, new_back, queries = fence(
-        homed[0], away, mine, new_own, new_back, queries
+    homed[0], away, held, new_own, new_back, queries, places = fence(
+        homed[0], away, held, new_own, new_back, queries, places
     )
 
     homed.append(lax.ppermute(away[0], "groups", partners))
+    held[1] = project(1, own_hidden, held[1], early, row_count)
     cosine, sine, new_cosine, new_sine, key_info, query_info = tables
     moved = pack(new_own, new_back, new_cosine, new_sine, queries)
     moved = moved.reshape(steps, requests, -1)
@@ -407,7 +409,7 @@
     query_rows, new_pairs = moved[:, :heads_width], moved[:, heads_width:]
     new_pairs = jnp.pad(new_pairs, ((0, new_padded - count), (0, 0)))
     homed = [total.astype(jnp.float32) * (1.0 / RAISE) for total in homed]
-    attended = finish(mine, homed, cosine, sine, key_info, query_info, new_pairs, query_rows)
+    attended = finish(held, homed, cosine, sine, key_info, query_info, new_pairs, query_rows)
     attended = jnp.swapaxes(attended.reshape(steps, requests, -1), 0, 1)
     return lax.all_to_all(attended, "rows", split_axis=0, concat_axis=0, tiled=True)
 

time: 157 us -> 157 us (level)
  waiting for transfers between devices: 64.2 us -> 50.8 us
  starting transfers between devices: 24.7 us -> 33.9 us
  local copies, waits for them, and re-layouts: 11.1 us -> 18.2 us
  Pallas kernels: 38.8 us -> 32.5 us
    ppermute x5 -> x8, waiting for transfers between devices: 44.4 us -> 16.5 us  [step(): lax.ppermute(pair[0], 'rows', onward)]
    ppermute x1, waiting for transfers between devices: 0.01 us -> 10.6 us  [body(): got.append(lax.ppermute(sent[2], 'groups', partners))]
    ppermute x1, waiting for transfers between devices: 0.01 us -> 9.5 us  [body(): got.append(lax.ppermute(sent[1], 'groups', partners))]
    all_to_all x1, waiting for transfers between devices: 7.32 us -> 1.06 us  [body(): lax.all_to_all(moved, 'rows', split_axis=0, concat_axis=0, tiled=True)]
    unnamed x32 -> x62, local copies, waits for them, and re-layouts: 8.34 us -> 14.4 us
    pallas_call x7, Pallas kernels: 30.5 us -> 24.6 us  [products(): pl.pallas_call(functools.partial(product_kernel, depths, len(hidden), bas...]
    ppermute x5 -> x8, starting transfers between devices: 9.66 us -> 13 us  [step(): lax.ppermute(pair[0], 'rows', onward)]
    ppermute x5 -> x8, starting transfers between devices: 1.58 us -> 4.5 us  [step(): lax.ppermute(pair[1], 'rows', back)]
  transfers between devices with their start and end apart: 23 -> 29, of which waited for: 10 -> 14; matrix products, arithmetic and copies ran while one was open for 5% -> 6% of each run, Pallas kernels for 19% -> 17%
where the time goes in v8:
time: 157 us; the launch traced here: 156 us
  waiting for transfers between devices  50.8 us (32%)
  starting transfers between devices  33.9 us (22%)
  Pallas kernels  32.5 us (21%)
  local copies, waits for them, and re-layouts  18.2 us (12%)
  blocking collectives  13 us (8%)
  other arithmetic  7.17 us (5%)
    pallas_call x7, Pallas kernels, products(): pl.pallas_call(functools.partial(product_kernel, depths, len(hidden), bas...  24.6 us
    ppermute x8, waiting for transfers between devices, step(): lax.ppermute(pair[0], 'rows', onward)  16.5 us
    unnamed x62, local copies, waits for them, and re-layouts  14.4 us
    ppermute x8, starting transfers between devices, step(): lax.ppermute(pair[0], 'rows', onward)  13 us
    all_to_all x1, blocking collectives, body(): lax.all_to_all(attended, 'rows', split_axis=0, concat_axis=0, tiled=True)  13 us
    ppermute x1, waiting for transfers between devices, body(): got.append(lax.ppermute(sent[2], 'groups', partners))  10.6 us
    ppermute x1, waiting for transfers between devices, body(): got.append(lax.ppermute(sent[1], 'groups', partners))  9.5 us
    ppermute x8, waiting for transfers between devices, step(): lax.ppermute(pair[1], 'rows', back)  5.96 us
  transfers between devices with their start and end apart: 29, of which 14 were waited for; matrix products, arithmetic and copies ran while one was open for 6% of the time, Pallas kernels for 17%

profile of v8, /device:TPU:0, one launch (start us, length us, event | category | flops | bytes accessed | tf_op | source)
XLA Modules:
  0.0 156.0 jit_solution(10622465846248024904)
XLA Ops:
  1.6 2.5 %own_half.1 = (bf16[512,512]{1,0:T(8,128)(2,1)}, bf16[512,512]{1,0:T(8,128)(2,1)S(1)}) custom-call(s32[1]{0:T(128)} %bitcast.side_ref, bf16[1024,2,512]{2,1,0:T(2,128)(2,1)S(1)} %copy-done.15), custom_call_target="tpu_custom_call" | custom-call | bytes 4194304 | tf_op jit(solution)/shard_map/own_half/pallas_call | solution.py:127
  4.8 3.0 %collective-permute-start = (bf16[512,512]{1,0:T(8,128)(2,1)}, bf16[512,512]{1,0:T(8,128)(2,1)}, u32[]{:S(2)}, u32[]{:S(2)}) collective-permute-start(bf16[512,512]{1,0:T(8,128)(2,1)} %get-tuple-element.75.refs_3_.refs_9_), channel_id=1, source_target_pairs={{0,4},{4,8},{8,12},{12,14},{14,10},{10,6},{6,2},{2,0},{1,5},{5,9},... | collective-permute-start | bytes 1572872 | tf_op jit(solution)/shard_map/ppermute | solution.py:307
  7.9 2.5 %copy-done = bf16[640,4096]{1,0:T(8,128)(2,1)S(1)} copy-done((bf16[640,4096]{1,0:T(8,128)(2,1)S(1)}, bf16[640,4096]{1,0:T(8,128)(2,1)}, u32[]{:S(2)}) %copy-start) | copy-done | bytes 5242904
  10.7 2.0 %collective-permute-start.2 = (bf16[64,2048]{1,0:T(8,128)(2,1)S(1)}, bf16[64,2048]{1,0:T(8,128)(2,1)S(1)}, u32[]{:S(2)}, u32[]{:S(2)}) collective-permute-start(bf16[64,2048]{1,0:T(8,128)(2,1)S(1)} %pick_columns.6), channel_id=1, source_target_pairs={{0,16},{16,0},{1,17},{17,1},{2,18},{18,2},{3,19},{19,3},{4,20},{20... | collective-permute-start | bytes 786440 | tf_op jit(solution)/shard_map/ppermute | solution.py:328
  17.3 4.1 %collective-permute-done.3 = bf16[32,2048]{1,0:T(8,128)(2,1)S(1)} collective-permute-done((bf16[32,2048]{1,0:T(8,128)(2,1)S(1)}, bf16[32,2048]{1,0:T(8,128)(2,1)S(1)}, u32[]{:S(2)}, u32[]{:S(2)}) %collective-permute-start.3) | collective-permute-done | bytes 131104 | tf_op jit(solution)/shard_map/ppermute | solution.py:337
  23.9 1.7 %collective-permute-start.6 = (bf16[288,2048]{1,0:T(8,128)(2,1)}, bf16[288,2048]{1,0:T(8,128)(2,1)}, u32[]{:S(2)}, u32[]{:S(2)}) collective-permute-start(bf16[288,2048]{1,0:T(8,128)(2,1)} %copy-done.19), channel_id=1, source_target_pairs={{0,16},{16,0},{1,17},{17,1},{2,18},{18,2},{3,19},{19,3},{4,20},{20... | collective-permute-start | bytes 3538952 | tf_op jit(solution)/shard_map/ppermute | solution.py:343
  30.3 2.1 %multiply_sine_fusion = (f32[640,64]{1,0:T(8,128)}, f32[640,64]{1,0:T(8,128)}) fusion(f32[64]{0:T(128)S(1)} %multiply_exponential_fusion, f32[640]{0:T(1024)S(1)} %subtract_convert_fusion), kind=kLoop, calls=%fused_computation.6 | loop fusion | flops 40960 | bytes 330496 | tf_op jit(solution)/shard_map/sin | solution.py:24
  32.4 8.7 %collective-permute-done.4.refs_6_.refs_12_ = bf16[512,512]{1,0:T(8,128)(2,1)S(1)} collective-permute-done((bf16[512,512]{1,0:T(8,128)(2,1)}, bf16[512,512]{1,0:T(8,128)(2,1)S(1)}, u32[]{:S(2)}, u32[]{:S(2)}) %collective-permute-start.4) | collective-permute-done | bytes 524320 | tf_op jit(solution)/shard_map/ppermute | solution.py:307
  42.7 9.5 %collective-permute-done.6.refs_3_ = bf16[288,2048]{1,0:T(8,128)(2,1)} collective-permute-done((bf16[288,2048]{1,0:T(8,128)(2,1)}, bf16[288,2048]{1,0:T(8,128)(2,1)}, u32[]{:S(2)}, u32[]{:S(2)}) %collective-permute-start.6) | collective-permute-done | bytes 1179680 | tf_op jit(solution)/shard_map/ppermute | solution.py:343
  58.9 4.0 %products.7.refs_7_ = f32[640,512]{1,0:T(8,128)S(1)} custom-call(s32[8]{0:T(128)S(1)} %fusion.3.refs_0_, bf16[640,2048]{1,0:T(8,128)(2,1)S(1)} %pick_columns.9.refs_1_, bf16[640,2048]{1,0:T(8,128)(2,1)} %collective-permute-done.7.refs_2_, bf16[512,512]{1,0:T(8,128)(2,1)} %get-tuple-element.75.refs_3_.refs_9_, ...), custom_call_target="tpu_custom_call" | custom-call | flops 1677721600 | bytes 7208960 | tf_op jit(solution)/shard_map/products/pallas_call | solution.py:239
  62.9 5.7 %collective-permute-done.11.refs_14_.refs_3_ = bf16[512,512]{1,0:T(8,128)(2,1)S(1)} collective-permute-done((bf16[512,512]{1,0:T(8,128)(2,1)S(1)}, bf16[512,512]{1,0:T(8,128)(2,1)S(1)}, u32[]{:S(2)}, u32[]{:S(2)}) %collective-permute-start.11) | collective-permute-done | bytes 524320 | tf_op jit(solution)/shard_map/ppermute | solution.py:307
  70.3 10.6 %collective-permute-done.13.refs_5_ = bf16[288,2048]{1,0:T(8,128)(2,1)S(1)} collective-permute-done((bf16[288,2048]{1,0:T(8,128)(2,1)}, bf16[288,2048]{1,0:T(8,128)(2,1)S(1)}, u32[]{:S(2)}, u32[]{:S(2)}) %collective-permute-start.13) | collective-permute-done | bytes 1179680 | tf_op jit(solution)/shard_map/ppermute | solution.py:359
  86.2 3.7 %products.8.refs_7_ = f32[640,512]{1,0:T(8,128)S(1)} custom-call(s32[8]{0:T(128)S(1)} %fusion.3.refs_0_, bf16[640,2048]{1,0:T(8,128)(2,1)S(1)} %pick_columns.9.refs_1_, bf16[640,2048]{1,0:T(8,128)(2,1)} %collective-permute-done.7.refs_2_, bf16[512,512]{1,0:T(8,128)(2,1)S(1)} %copy-done.14, bf16[512,512]{1,0:T(8,128)(2,1)S(1)} %collective-permute-done.9.refs_4_.refs_10_, ...), custom_call_target="tpu_custom_call" | custom-call | flops 1677721600 | bytes 7208960 | tf_op jit(solution)/shard_map/products/pallas_call | solution.py:239
  92.2 4.9 %products.9 = f32[704,512]{1,0:T(8,128)S(1)} custom-call(s32[8]{0:T(128)S(1)} %fusion.3.refs_0_, bf16[64,2048]{1,0:T(8,128)(2,1)S(1)} %collective-permute-done.2.refs_1_, bf16[64,2048]{1,0:T(8,128)(2,1)S(1)} %copy-done.12, bf16[288,2048]{1,0:T(8,128)(2,1)} %collective-permute-done.6.refs_3_, bf16[288,2048]{1,0:T(8,128)(2,1)S(1)} %collective-permute-done.14.refs_4_, ...), custom_call_target="tpu_custom_call" | custom-call | flops 2952790016 | bytes 11403264 | tf_op jit(solution)/shard_map/products/pallas_call | solution.py:239
  98.9 2.1 %collective-permute-done.22.refs_14_.refs_3_ = bf16[512,512]{1,0:T(8,128)(2,1)S(1)} collective-permute-done((bf16[512,512]{1,0:T(8,128)(2,1)S(1)}, bf16[512,512]{1,0:T(8,128)(2,1)S(1)}, u32[]{:S(2)}, u32[]{:S(2)}) %collective-permute-start.22) | collective-permute-done | bytes 524320 | tf_op jit(solution)/shard_map/ppermute | solution.py:307
  102.3 1.6 %collective-permute-start.24 = (bf16[256,512]{1,0:T(8,128)(2,1)S(1)}, bf16[256,512]{1,0:T(8,128)(2,1)S(1)}, u32[]{:S(2)}, u32[]{:S(2)}) collective-permute-start(bf16[256,512]{1,0:T(8,128)(2,1)S(1)} %slice.41), channel_id=1, source_target_pairs={{0,4},{4,8},{8,12},{12,14},{14,10},{10,6},{6,2},{2,0},{1,5},{5,9},... | collective-permute-start | bytes 786440 | tf_op jit(solution)/shard_map/ppermute | solution.py:307
  104.6 3.0 %products.12.refs_0_ = f32[640,512]{1,0:T(8,128)S(1)} custom-call(s32[8]{0:T(128)S(1)} %fusion.3.refs_0_, bf16[640,2048]{1,0:T(8,128)(2,1)S(1)} %pick_columns.9.refs_1_, bf16[640,2048]{1,0:T(8,128)(2,1)} %collective-permute-done.7.refs_2_, bf16[512,512]{1,0:T(8,128)(2,1)S(1)} %collective-permute-done.11.refs_14_.refs_3_, ...), custom_call_target="tpu_custom_call" | custom-call | flops 1006632960 | bytes 4849664 | tf_op jit(solution)/shard_map/products/pallas_call | solution.py:239
  108.7 4.1 %products.10.refs_11_ = f32[704,512]{1,0:T(8,128)S(1)} custom-call(s32[8]{0:T(128)S(1)} %fusion.3.refs_0_, bf16[64,2048]{1,0:T(8,128)(2,1)S(1)} %collective-permute-done.2.refs_1_, bf16[64,2048]{1,0:T(8,128)(2,1)S(1)} %copy-done.12, bf16[288,2048]{1,0:T(8,128)(2,1)} %collective-permute-done.6.refs_3_, bf16[288,2048]{1,0:T(8,128)(2,1)S(1)} %collective-permute-done.14.refs_4_, ...), custom_call_target="tpu_custom_call" | custom-call | flops 2583691264 | bytes 10158080 | tf_op jit(solution)/shard_map/products/pallas_call | solution.py:239
  112.8 2.0 %products.11 = f32[704,512]{1,0:T(8,128)S(1)} custom-call(s32[8]{0:T(128)S(1)} %fusion.3.refs_0_, bf16[64,2048]{1,0:T(8,128)(2,1)S(1)} %collective-permute-done.2.refs_1_, bf16[64,2048]{1,0:T(8,128)(2,1)S(1)} %copy-done.12, bf16[288,2048]{1,0:T(8,128)(2,1)} %collective-permute-done.6.refs_3_, bf16[288,2048]{1,0:T(8,128)(2,1)S(1)} %collective-permute-done.14.refs_4_, ...), custom_call_target="tpu_custom_call" | custom-call | flops 369098752 | bytes 2686976 | tf_op jit(solution)/shard_map/products/pallas_call | solution.py:239
  117.5 2.4 %collective-permute-done.26.refs_1_ = f32[32,1024]{1,0:T(8,128)S(1)} collective-permute-done((f32[32,1024]{1,0:T(8,128)S(1)}, f32[32,1024]{1,0:T(8,128)S(1)}, u32[]{:S(2)}, u32[]{:S(2)}) %collective-permute-start.26) | collective-permute-done | bytes 131104 | tf_op jit(solution)/shard_map/ppermute | solution.py:393
  122.6 4.8 %all-to-all-start = ((bf16[8,3,5120]{2,1,0:T(4,128)(2,1)}), bf16[8,3,5120]{2,1,0:T(4,128)(2,1)}, u32[]{:S(2)}, u32[]{:S(2)}) async-start(bf16[8,3,5120]{2,1,0:T(4,128)(2,1)} %bitcast.38), calls=%async_computation | async-start | bytes 655360 | tf_op jit(solution)/shard_map/all_to_all | solution.py:406
  130.8 3.0 %products.13.refs_1_ = f32[640,512]{1,0:T(8,128)S(1)} custom-call(s32[8]{0:T(128)S(1)} %fusion.3.refs_0_, bf16[640,2048]{1,0:T(8,128)(2,1)S(1)} %pick_columns.9.refs_1_, bf16[640,2048]{1,0:T(8,128)(2,1)} %collective-permute-done.7.refs_2_, bf16[512,512]{1,0:T(8,128)(2,1)S(1)} %collective-permute-done.22.refs_14_.refs_3_, bf16[512,512]{1,0:T(8,128)(2,1)S(1)} %copy-done.10, ...), custom_call_target="tpu_custom_call" | custom-call | flops 1006632960 | bytes 4849664 | tf_op jit(solution)/shard_map/products/pallas_call | solution.py:239
  139.0 3.0 %rotate_attend.1 = bf16[24,4096]{1,0:T(8,128)(2,1)S(1)} custom-call(f32[640,512]{1,0:T(8,128)S(1)} %copy-done.6, f32[640,512]{1,0:T(8,128)S(1)} %copy-done.8, f32[640,512]{1,0:T(8,128)S(1)} %convert_multiply_fusion.1.refs_2_, f32[640,512]{1,0:T(8,128)S(1)} %convert_multiply_fusion.refs_3_, f32[640,64]{1,0:T(8,128)S(1)} %copy-done.17, ...), custom_call_target="tpu_custom_call" | custom-call | flops 251658240 | bytes 5636096 | tf_op jit(solution)/shard_map/rotate_attend/pallas_call | solution.py:100
  142.2 13.0 %all_to_all.10 = bf16[8,3,4096]{2,1,0:T(4,128)(2,1)S(1)} all-to-all(bf16[8,3,4096]{2,1,0:T(4,128)(2,1)S(1)} %bitcast.39), channel_id=1, replica_groups=mesh['groups'=2,'rows'=8,'tensor'=2] {'rows'}, dimensions={0} | all-to-all | bytes 393216 | tf_op jit(solution)/shard_map/all_to_all | solution.py:414
  (167 shorter events, 51.6 us)
Async XLA Ops:
  4.8 16.5 %collective-permute-start = (bf16[512,512]{1,0:T(8,128)(2,1)}, bf16[512,512]{1,0:T(8,128)(2,1)}, u32[]{:S(2)}, u32[]{:S(2)}) collective-permute-start(bf16[512,512]{1,0:T(8,128)(2,1)} %get-tuple-element.75.refs_3_.refs_9_), channel_id=1, source_target_pairs={{0,4},{4,8},{8,12},{12,14},{14,10},{10,6},{6,2},{2,0},{1,5},{5,9},... | collective-permute-start | bytes 1572872 | tf_op jit(solution)/shard_map/ppermute | solution.py:307
  7.9 14.1 %collective-permute-start.1 = (bf16[512,512]{1,0:T(8,128)(2,1)}, bf16[512,512]{1,0:T(8,128)(2,1)}, u32[]{:S(2)}, u32[]{:S(2)}) collective-permute-start(bf16[512,512]{1,0:T(8,128)(2,1)} %get-tuple-element.75.refs_3_.refs_9_), channel_id=1, source_target_pairs={{4,0},{8,4},{12,8},{14,12},{10,14},{6,10},{2,6},{0,2},{5,1},{9,5},... | collective-permute-start | bytes 1572872 | tf_op jit(solution)/shard_map/ppermute | solution.py:307
  10.7 10.6 %collective-permute-start.2 = (bf16[64,2048]{1,0:T(8,128)(2,1)S(1)}, bf16[64,2048]{1,0:T(8,128)(2,1)S(1)}, u32[]{:S(2)}, u32[]{:S(2)}) collective-permute-start(bf16[64,2048]{1,0:T(8,128)(2,1)S(1)} %pick_columns.6), channel_id=1, source_target_pairs={{0,16},{16,0},{1,17},{17,1},{2,18},{18,2},{3,19},{19,3},{4,20},{20... | collective-permute-start | bytes 786440 | tf_op jit(solution)/shard_map/ppermute | solution.py:328
  12.9 8.4 %collective-permute-start.3 = (bf16[32,2048]{1,0:T(8,128)(2,1)S(1)}, bf16[32,2048]{1,0:T(8,128)(2,1)S(1)}, u32[]{:S(2)}, u32[]{:S(2)}) collective-permute-start(bf16[32,2048]{1,0:T(8,128)(2,1)S(1)} %pick_columns.10), channel_id=1, source_target_pairs={{0,16},{16,0},{1,17},{17,1},{2,18},{18,2},{3,19},{19,3},{4,20},{20... | collective-permute-start | bytes 393224 | tf_op jit(solution)/shard_map/ppermute | solution.py:337
  22.0 6.1 %collective-permute-start.7 = (bf16[640,2048]{1,0:T(8,128)(2,1)S(1)}, bf16[640,2048]{1,0:T(8,128)(2,1)}, u32[]{:S(2)}, u32[]{:S(2)}) collective-permute-start(bf16[640,2048]{1,0:T(8,128)(2,1)S(1)} %pick_columns.9.refs_1_), channel_id=1, source_target_pairs={{0,1},{1,0},{2,3},{3,2},{4,5},{5,4},{6,7},{7,6},{8,9},{9,8},{10,11... | collective-permute-start | bytes 7864328 | tf_op jit(solution)/shard_map/ppermute | solution.py:345
  23.9 28.2 %collective-permute-start.6 = (bf16[288,2048]{1,0:T(8,128)(2,1)}, bf16[288,2048]{1,0:T(8,128)(2,1)}, u32[]{:S(2)}, u32[]{:S(2)}) collective-permute-start(bf16[288,2048]{1,0:T(8,128)(2,1)} %copy-done.19), channel_id=1, source_target_pairs={{0,16},{16,0},{1,17},{17,1},{2,18},{18,2},{3,19},{19,3},{4,20},{20... | collective-permute-start | bytes 3538952 | tf_op jit(solution)/shard_map/ppermute | solution.py:343
  26.0 15.0 %collective-permute-start.4 = (bf16[512,512]{1,0:T(8,128)(2,1)}, bf16[512,512]{1,0:T(8,128)(2,1)S(1)}, u32[]{:S(2)}, u32[]{:S(2)}) collective-permute-start(bf16[512,512]{1,0:T(8,128)(2,1)} %collective-permute-done.refs_4_.refs_10_), channel_id=1, source_target_pairs={{0,4},{4,8},{8,12},{12,14},{14,10},{10,6},{6,2},{2,0},{1,5},{5,9},... | collective-permute-start | bytes 1572872 | tf_op jit(solution)/shard_map/ppermute | solution.py:307
  27.6 15.1 %collective-permute-start.5 = (bf16[512,512]{1,0:T(8,128)(2,1)}, bf16[512,512]{1,0:T(8,128)(2,1)S(1)}, u32[]{:S(2)}, u32[]{:S(2)}) collective-permute-start(bf16[512,512]{1,0:T(8,128)(2,1)} %collective-permute-done.1.refs_5_.refs_11_), channel_id=1, source_target_pairs={{4,0},{8,4},{12,8},{14,12},{10,14},{6,10},{2,6},{0,2},{5,1},{9,5},... | collective-permute-start | bytes 1572872 | tf_op jit(solution)/shard_map/ppermute | solution.py:307
  28.1 24.3 %collective-permute-start.10 = (bf16[512,512]{1,0:T(8,128)(2,1)}, bf16[512,512]{1,0:T(8,128)(2,1)S(1)}, u32[]{:S(2)}, u32[]{:S(2)}) collective-permute-start(bf16[512,512]{1,0:T(8,128)(2,1)} %copy-done.13), channel_id=1, source_target_pairs={{4,0},{8,4},{12,8},{14,12},{10,14},{6,10},{2,6},{0,2},{5,1},{9,5},... | collective-permute-start | bytes 1572872 | tf_op jit(solution)/shard_map/ppermute | solution.py:307
  29.6 22.7 %collective-permute-start.9 = (bf16[512,512]{1,0:T(8,128)(2,1)}, bf16[512,512]{1,0:T(8,128)(2,1)S(1)}, u32[]{:S(2)}, u32[]{:S(2)}) collective-permute-start(bf16[512,512]{1,0:T(8,128)(2,1)} %copy-done.13), channel_id=1, source_target_pairs={{0,4},{4,8},{8,12},{12,14},{14,10},{10,6},{6,2},{2,0},{1,5},{5,9},... | collective-permute-start | bytes 1572872 | tf_op jit(solution)/shard_map/ppermute | solution.py:307
  52.3 28.6 %collective-permute-start.13 = (bf16[288,2048]{1,0:T(8,128)(2,1)}, bf16[288,2048]{1,0:T(8,128)(2,1)S(1)}, u32[]{:S(2)}, u32[]{:S(2)}) collective-permute-start(bf16[288,2048]{1,0:T(8,128)(2,1)} %copy-done.18), channel_id=1, source_target_pairs={{0,16},{16,0},{1,17},{17,1},{2,18},{18,2},{3,19},{19,3},{4,20},{20... | collective-permute-start | bytes 3538952 | tf_op jit(solution)/shard_map/ppermute | solution.py:359
  53.9 14.8 %collective-permute-start.11 = (bf16[512,512]{1,0:T(8,128)(2,1)S(1)}, bf16[512,512]{1,0:T(8,128)(2,1)S(1)}, u32[]{:S(2)}, u32[]{:S(2)}) collective-permute-start(bf16[512,512]{1,0:T(8,128)(2,1)S(1)} %collective-permute-done.4.refs_6_.refs_12_), channel_id=1, source_target_pairs={{0,4},{4,8},{8,12},{12,14},{14,10},{10,6},{6,2},{2,0},{1,5},{5,9},... | collective-permute-start | bytes 1572872 | tf_op jit(solution)/shard_map/ppermute | solution.py:307
  55.5 14.8 %collective-permute-start.12 = (bf16[512,512]{1,0:T(8,128)(2,1)S(1)}, bf16[512,512]{1,0:T(8,128)(2,1)S(1)}, u32[]{:S(2)}, u32[]{:S(2)}) collective-permute-start(bf16[512,512]{1,0:T(8,128)(2,1)S(1)} %collective-permute-done.5.refs_7_.refs_13_), channel_id=1, source_target_pairs={{4,0},{8,4},{12,8},{14,12},{10,14},{6,10},{2,6},{0,2},{5,1},{9,5},... | collective-permute-start | bytes 1572872 | tf_op jit(solution)/shard_map/ppermute | solution.py:307
  55.9 25.0 %collective-permute-start.15 = (bf16[512,512]{1,0:T(8,128)(2,1)S(1)}, bf16[512,512]{1,0:T(8,128)(2,1)S(1)}, u32[]{:S(2)}, u32[]{:S(2)}) collective-permute-start(bf16[512,512]{1,0:T(8,128)(2,1)S(1)} %collective-permute-done.9.refs_4_.refs_10_), channel_id=1, source_target_pairs={{0,4},{4,8},{8,12},{12,14},{14,10},{10,6},{6,2},{2,0},{1,5},{5,9},... | collective-permute-start | bytes 1572872 | tf_op jit(solution)/shard_map/ppermute | solution.py:307
  57.5 23.4 %collective-permute-start.16 = (bf16[512,512]{1,0:T(8,128)(2,1)S(1)}, bf16[512,512]{1,0:T(8,128)(2,1)S(1)}, u32[]{:S(2)}, u32[]{:S(2)}) collective-permute-start(bf16[512,512]{1,0:T(8,128)(2,1)S(1)} %collective-permute-done.10.refs_5_.refs_11_), channel_id=1, source_target_pairs={{4,0},{8,4},{12,8},{14,12},{10,14},{6,10},{2,6},{0,2},{5,1},{9,5},... | collective-permute-start | bytes 1572872 | tf_op jit(solution)/shard_map/ppermute | solution.py:307
  81.5 9.5 %collective-permute-start.19 = (bf16[256,512]{1,0:T(8,128)(2,1)S(1)}, bf16[256,512]{1,0:T(8,128)(2,1)S(1)}, u32[]{:S(2)}, u32[]{:S(2)}) collective-permute-start(bf16[256,512]{1,0:T(8,128)(2,1)S(1)} %slice.48), channel_id=1, source_target_pairs={{0,4},{4,8},{8,12},{12,14},{14,10},{10,6},{6,2},{2,0},{1,5},{5,9},... | collective-permute-start | bytes 786440 | tf_op jit(solution)/shard_map/ppermute | solution.py:307
  83.0 9.2 %collective-permute-start.20 = (bf16[256,512]{1,0:T(8,128)(2,1)S(1)}, bf16[256,512]{1,0:T(8,128)(2,1)S(1)}, u32[]{:S(2)}, u32[]{:S(2)}) collective-permute-start(bf16[256,512]{1,0:T(8,128)(2,1)S(1)} %slice.49), channel_id=1, source_target_pairs={{4,0},{8,4},{12,8},{14,12},{10,14},{6,10},{2,6},{0,2},{5,1},{9,5},... | collective-permute-start | bytes 786440 | tf_op jit(solution)/shard_map/ppermute | solution.py:307
  84.2 16.8 %collective-permute-start.22 = (bf16[512,512]{1,0:T(8,128)(2,1)S(1)}, bf16[512,512]{1,0:T(8,128)(2,1)S(1)}, u32[]{:S(2)}, u32[]{:S(2)}) collective-permute-start(bf16[512,512]{1,0:T(8,128)(2,1)S(1)} %collective-permute-done.15.refs_6_.refs_12_), channel_id=1, source_target_pairs={{0,4},{4,8},{8,12},{12,14},{14,10},{10,6},{6,2},{2,0},{1,5},{5,9},... | collective-permute-start | bytes 1572872 | tf_op jit(solution)/shard_map/ppermute | solution.py:307
  85.7 16.5 %collective-permute-start.23 = (bf16[512,512]{1,0:T(8,128)(2,1)S(1)}, bf16[512,512]{1,0:T(8,128)(2,1)S(1)}, u32[]{:S(2)}, u32[]{:S(2)}) collective-permute-start(bf16[512,512]{1,0:T(8,128)(2,1)S(1)} %collective-permute-done.16.refs_7_.refs_13_), channel_id=1, source_target_pairs={{4,0},{8,4},{12,8},{14,12},{10,14},{6,10},{2,6},{0,2},{5,1},{9,5},... | collective-permute-start | bytes 1572872 | tf_op jit(solution)/shard_map/ppermute | solution.py:307
  97.3 20.2 %collective-permute-start.21 = (f16[640,512]{1,0:T(8,128)(2,1)S(1)}, f16[640,512]{1,0:T(8,128)(2,1)S(1)}, u32[]{:S(2)}, u32[]{:S(2)}) collective-permute-start(f16[640,512]{1,0:T(8,128)(2,1)S(1)} %fusion.1), channel_id=1, source_target_pairs={{0,16},{16,0},{1,17},{17,1},{2,18},{18,2},{3,19},{19,3},{4,20},{20... | collective-permute-start | bytes 1966088 | tf_op jit(solution)/shard_map/ppermute | solution.py:387
  102.3 10.5 %collective-permute-start.24 = (bf16[256,512]{1,0:T(8,128)(2,1)S(1)}, bf16[256,512]{1,0:T(8,128)(2,1)S(1)}, u32[]{:S(2)}, u32[]{:S(2)}) collective-permute-start(bf16[256,512]{1,0:T(8,128)(2,1)S(1)} %slice.41), channel_id=1, source_target_pairs={{0,4},{4,8},{8,12},{12,14},{14,10},{10,6},{6,2},{2,0},{1,5},{5,9},... | collective-permute-start | bytes 786440 | tf_op jit(solution)/shard_map/ppermute | solution.py:307
  104.0 8.8 %collective-permute-start.25 = (bf16[256,512]{1,0:T(8,128)(2,1)S(1)}, bf16[256,512]{1,0:T(8,128)(2,1)S(1)}, u32[]{:S(2)}, u32[]{:S(2)}) collective-permute-start(bf16[256,512]{1,0:T(8,128)(2,1)S(1)} %slice.42), channel_id=1, source_target_pairs={{4,0},{8,4},{12,8},{14,12},{10,14},{6,10},{2,6},{0,2},{5,1},{9,5},... | collective-permute-start | bytes 786440 | tf_op jit(solution)/shard_map/ppermute | solution.py:307
  120.0 17.5 %collective-permute-start.27 = (f16[640,512]{1,0:T(8,128)(2,1)}, f16[640,512]{1,0:T(8,128)(2,1)}, u32[]{:S(2)}, u32[]{:S(2)}) collective-permute-start(f16[640,512]{1,0:T(8,128)(2,1)} %fusion), channel_id=1, source_target_pairs={{0,16},{16,0},{1,17},{17,1},{2,18},{18,2},{3,19},{19,3},{4,20},{20... | collective-permute-start | bytes 1966088 | tf_op jit(solution)/shard_map/ppermute | solution.py:400
  122.6 13.6 %all-to-all-start = ((bf16[8,3,5120]{2,1,0:T(4,128)(2,1)}), bf16[8,3,5120]{2,1,0:T(4,128)(2,1)}, u32[]{:S(2)}, u32[]{:S(2)}) async-start(bf16[8,3,5120]{2,1,0:T(4,128)(2,1)} %bitcast.38), calls=%async_computation | async-start | bytes 655360 | tf_op jit(solution)/shard_map/all_to_all | solution.py:406
  (37 other events, 189.9 us)

commit v9 on v8

--- a/solution.py
+++ b/solution.py
@@ -12,7 +12,7 @@
 HALF = HD // 2
 CHUNKS = 2
 MOST_SHARDS = 8
-VMEM_BYTES = 32 << 20
+VMEM_BYTES = 20 << 20
 MERGED = 4
 RAISE = 16.0
 
@@ -322,7 +322,7 @@
         tokens_total = (total[:tokens] * RAISE).astype(jnp.float16)
         return tokens_total, total[tokens + new_padded :], total[tokens : tokens + count]
 
-    cuts = (0, tokens // 10, tokens // 20 * 11, tokens)
+    cuts = (0, 3 * tokens // 20, 23 * tokens // 40, tokens)
     sent = [pick_columns(passages, 1 - side, half, cuts[0], cuts[1])]
     (passages_later, new_hidden) = fence_with(0, passages, new_hidden)
     got = [lax.ppermute(sent[0], "groups", partners)]
@@ -334,11 +334,9 @@
     new_rows = jnp.pad(new_rows, ((0, new_padded - count), (0, 0)))
     new_sent = pick_columns(new_rows, 1 - side, half, 0, new_padded)
     new_kept = pick_columns(new_rows, side, half, 0, new_padded)
-    new_got = lax.ppermute(new_sent, "groups", partners)
-    got[0], sent, kept, new_got, new_kept, lengths, destinations = fence_with(
-        0, got[0], sent, kept, new_got, new_kept, lengths, destinations
+    got[0], sent, kept, new_sent, new_kept, lengths, destinations = fence_with(
+        0, got[0], sent, kept, new_sent, new_kept, lengths, destinations
     )
-    new_kept = jnp.concatenate([new_kept, new_got], 0)
 
     got.append(lax.ppermute(sent[1], "groups", partners))
     step(0)
@@ -367,14 +365,15 @@
         step(1)
     held = [project(0, own_hidden, None, 0, early)]
     ends[0] = halved(ring[0][-1])
-    got[2], new_kept, held, places, ring[1][-1], ends[0] = fence_with(
-        0, got[2], new_kept, held, places, ring[1][-1], ends[0]
+    got[2], new_sent, held, places, ring[1][-1], ends[0] = fence_with(
+        0, got[2], new_sent, held, places, ring[1][-1], ends[0]
     )
 
     step(0)
     got_other.append(lax.ppermute(got[2], "tensor", cores))
+    new_kept = jnp.concatenate([new_kept, lax.ppermute(new_sent, "groups", partners)], 0)
     new_other = lax.ppermute(new_kept, "tensor", cores)
-    new_other, got_other[2] = fence_with(1, new_other, got_other[2])
+    (got_other[2],) = fence_with(1, got_other[2])
     step(1)
     away_hidden = list(zip(got, got_other)) + [(new_kept, new_other)]
     held.append(project(1, own_hidden, None, 0, early))
@@ -393,14 +392,12 @@
     new_back = lax.ppermute(jnp.concatenate(new_away, 1), "groups", partners)
     held[0] = project(0, own_hidden, held[0], early, row_count)
     queries = jnp.swapaxes(queries, 0, 1).reshape(count, -1)
-    homed[0], away, held, new_own, new_back, queries, places = fence(
-        homed[0], away, held, new_own, new_back, queries, places
-    )
-
+    held, queries, places = fence(held, queries, places)
     homed.append(lax.ppermute(away[0], "groups", partners))
-    held[1] = project(1, own_hidden, held[1], early, row_count)
     cosine, sine, new_cosine, new_sine, key_info, query_info = tables
     moved = pack(new_own, new_back, new_cosine, new_sine, queries)
+    moved, places = fence(moved, places)
+    held[1] = project(1, own_hidden, held[1], early, row_count)
     moved = moved.reshape(steps, requests, -1)
     moved = jnp.swapaxes(moved, 0, 1)
     moved = lax.all_to_all(moved, "rows", split_axis=0, concat_axis=0, tiled=True)

time: 157 us -> 173 us (1.10)
  waiting for transfers between devices: 50.8 us -> 68.2 us
  starting transfers between devices: 33.9 us -> 30.9 us
  Pallas kernels: 32.5 us -> 30 us
  other arithmetic: 7.17 us -> 9.51 us
    ppermute x1, waiting for transfers between devices: 2.44 us -> 17.3 us  [body(): new_back = lax.ppermute(jnp.concatenate(new_away, 1), 'groups', partners)]
    ppermute x1, waiting for transfers between devices: 0.01 us -> 3.84 us  [body(): got = [lax.ppermute(sent[0], 'groups', partners)]]
    pallas_call x7, Pallas kernels: 24.6 us -> 22.3 us  [products(): pl.pallas_call(functools.partial(product_kernel, depths, len(hidden), bas...]
    mul x2, other arithmetic: 1.52 us -> 3.83 us  [body(): homed = [total.astype(jnp.float32) * (1.0 / RAISE) for total in homed]]
    ppermute x8, waiting for transfers between devices: 16.5 us -> 18.5 us  [step(): lax.ppermute(pair[0], 'rows', onward)]
    unnamed x62 -> x73, local copies, waits for them, and re-layouts: 14.4 us -> 15.4 us
  transfers between devices with their start and end apart: 29 -> 29, of which waited for: 14 -> 17; matrix products, arithmetic and copies ran while one was open for 6% -> 6% of each run, Pallas kernels for 17% -> 14%
where the time goes in v9:
time: 173 us; the launch traced here: 172 us
  waiting for transfers between devices  68.2 us (39%)
  starting transfers between devices  30.9 us (18%)
  Pallas kernels  30 us (17%)
  local copies, waits for them, and re-layouts  19.2 us (11%)
  blocking collectives  13.8 us (8%)
  other arithmetic  9.51 us (5%)
    pallas_call x7, Pallas kernels, products(): pl.pallas_call(functools.partial(product_kernel, depths, len(hidden), bas...  22.3 us
    ppermute x8, waiting for transfers between devices, step(): lax.ppermute(pair[0], 'rows', onward)  18.5 us
    ppermute x1, waiting for transfers between devices, body(): new_back = lax.ppermute(jnp.concatenate(new_away, 1), 'groups', partners)  17.3 us
    unnamed x73, local copies, waits for them, and re-layouts  15.4 us
    ppermute x8, starting transfers between devices, step(): lax.ppermute(pair[0], 'rows', onward)  14.2 us
    all_to_all x1, blocking collectives, body(): lax.all_to_all(attended, 'rows', split_axis=0, concat_axis=0, tiled=True)  13.8 us
    ppermute x1, waiting for transfers between devices, body(): got.append(lax.ppermute(sent[2], 'groups', partners))  10.3 us
    ppermute x1, waiting for transfers between devices, body(): got.append(lax.ppermute(sent[1], 'groups', partners))  8.2 us
  transfers between devices with their start and end apart: 29, of which 17 were waited for; matrix products, arithmetic and copies ran while one was open for 6% of the time, Pallas kernels for 14%

profile of v9, /device:TPU:0, one launch (start us, length us, event | category | flops | bytes accessed | tf_op | source)
XLA Modules:
  0.0 172.2 jit_solution(17569506878986861166)
XLA Ops:
  1.6 2.3 %own_half.1 = (bf16[512,512]{1,0:T(8,128)(2,1)S(1)}, bf16[512,512]{1,0:T(8,128)(2,1)S(1)}) custom-call(s32[1]{0:T(128)} %bitcast.side_ref, bf16[1024,2,512]{2,1,0:T(2,128)(2,1)S(1)} %copy-done.19), custom_call_target="tpu_custom_call" | custom-call | bytes 4194304 | tf_op jit(solution)/shard_map/own_half/pallas_call | solution.py:127
  4.7 3.0 %collective-permute-start = (bf16[512,512]{1,0:T(8,128)(2,1)S(1)}, bf16[512,512]{1,0:T(8,128)(2,1)}, u32[]{:S(2)}, u32[]{:S(2)}) collective-permute-start(bf16[512,512]{1,0:T(8,128)(2,1)S(1)} %get-tuple-element.71.refs_3_.refs_9_), channel_id=1, source_target_pairs={{0,4},{4,8},{8,12},{12,14},{14,10},{10,6},{6,2},{2,0},{1,5},{5,9},... | collective-permute-start | bytes 1572872 | tf_op jit(solution)/shard_map/ppermute | solution.py:307
  7.7 2.5 %copy-done = bf16[640,4096]{1,0:T(8,128)(2,1)S(1)} copy-done((bf16[640,4096]{1,0:T(8,128)(2,1)S(1)}, bf16[640,4096]{1,0:T(8,128)(2,1)}, u32[]{:S(2)}) %copy-start) | copy-done | bytes 5242904
  10.6 2.0 %collective-permute-start.2 = (bf16[96,2048]{1,0:T(8,128)(2,1)S(1)}, bf16[96,2048]{1,0:T(8,128)(2,1)S(1)}, u32[]{:S(2)}, u32[]{:S(2)}) collective-permute-start(bf16[96,2048]{1,0:T(8,128)(2,1)S(1)} %pick_columns.6), channel_id=1, source_target_pairs={{0,16},{16,0},{1,17},{17,1},{2,18},{18,2},{3,19},{19,3},{4,20},{20... | collective-permute-start | bytes 1179656 | tf_op jit(solution)/shard_map/ppermute | solution.py:328
  17.4 3.8 %collective-permute-done.2.refs_1_ = bf16[96,2048]{1,0:T(8,128)(2,1)S(1)} collective-permute-done((bf16[96,2048]{1,0:T(8,128)(2,1)S(1)}, bf16[96,2048]{1,0:T(8,128)(2,1)S(1)}, u32[]{:S(2)}, u32[]{:S(2)}) %collective-permute-start.2) | collective-permute-done | bytes 393248 | tf_op jit(solution)/shard_map/ppermute | solution.py:328
  23.5 1.7 collective-permute-start.5
  29.6 2.1 %multiply_sine_fusion = (f32[640,64]{1,0:T(8,128)}, f32[640,64]{1,0:T(8,128)}) fusion(f32[64]{0:T(128)S(1)} %multiply_exponential_fusion, f32[640]{0:T(1024)S(1)} %subtract_convert_fusion), kind=kLoop, calls=%fused_computation.6 | loop fusion | flops 40960 | bytes 330496 | tf_op jit(solution)/shard_map/sin | solution.py:24
  31.7 8.7 %collective-permute-done.3.refs_6_.refs_12_ = bf16[512,512]{1,0:T(8,128)(2,1)S(1)} collective-permute-done((bf16[512,512]{1,0:T(8,128)(2,1)}, bf16[512,512]{1,0:T(8,128)(2,1)S(1)}, u32[]{:S(2)}, u32[]{:S(2)}) %collective-permute-start.3) | collective-permute-done | bytes 524320 | tf_op jit(solution)/shard_map/ppermute | solution.py:307
  42.0 8.2 %collective-permute-done.5.refs_3_ = bf16[272,2048]{1,0:T(8,128)(2,1)S(1)} collective-permute-done((bf16[272,2048]{1,0:T(8,128)(2,1)}, bf16[272,2048]{1,0:T(8,128)(2,1)S(1)}, u32[]{:S(2)}, u32[]{:S(2)}) %collective-permute-start.5) | collective-permute-done | bytes 1114144 | tf_op jit(solution)/shard_map/ppermute | solution.py:341
  57.5 3.9 %products.7.refs_7_ = f32[640,512]{1,0:T(8,128)S(1)} custom-call(s32[8]{0:T(128)S(1)} %fusion.3.refs_0_, bf16[640,2048]{1,0:T(8,128)(2,1)S(1)} %pick_columns.9.refs_1_, bf16[640,2048]{1,0:T(8,128)(2,1)} %collective-permute-done.6.refs_2_, bf16[512,512]{1,0:T(8,128)(2,1)S(1)} %copy-done.17, bf16[512,512]{1,0:T(8,128)(2,1)} %collective-permute-done.refs_4_.refs_10_, ...), custom_call_target="tpu_custom_call" | custom-call | flops 1677721600 | bytes 7208960 | tf_op jit(solution)/shard_map/products/pallas_call | solution.py:239
  61.4 5.5 %collective-permute-done.10.refs_14_.refs_3_ = bf16[512,512]{1,0:T(8,128)(2,1)S(1)} collective-permute-done((bf16[512,512]{1,0:T(8,128)(2,1)S(1)}, bf16[512,512]{1,0:T(8,128)(2,1)S(1)}, u32[]{:S(2)}, u32[]{:S(2)}) %collective-permute-start.10) | collective-permute-done | bytes 524320 | tf_op jit(solution)/shard_map/ppermute | solution.py:307
  68.6 10.3 %collective-permute-done.12.refs_5_ = bf16[272,2048]{1,0:T(8,128)(2,1)S(1)} collective-permute-done((bf16[272,2048]{1,0:T(8,128)(2,1)}, bf16[272,2048]{1,0:T(8,128)(2,1)S(1)}, u32[]{:S(2)}, u32[]{:S(2)}) %collective-permute-start.12) | collective-permute-done | bytes 1114144 | tf_op jit(solution)/shard_map/ppermute | solution.py:357
  82.4 2.4 %collective-permute-done.19 = bf16[32,2048]{1,0:T(8,128)(2,1)S(1)} collective-permute-done((bf16[32,2048]{1,0:T(8,128)(2,1)S(1)}, bf16[32,2048]{1,0:T(8,128)(2,1)S(1)}, u32[]{:S(2)}, u32[]{:S(2)}) %collective-permute-start.19) | collective-permute-done | bytes 131104 | tf_op jit(solution)/shard_map/ppermute | solution.py:374
  87.0 3.6 %products.8.refs_7_ = f32[640,512]{1,0:T(8,128)S(1)} custom-call(s32[8]{0:T(128)S(1)} %fusion.3.refs_0_, bf16[640,2048]{1,0:T(8,128)(2,1)S(1)} %pick_columns.9.refs_1_, bf16[640,2048]{1,0:T(8,128)(2,1)} %collective-permute-done.6.refs_2_, bf16[512,512]{1,0:T(8,128)(2,1)S(1)} %copy-done.15, bf16[512,512]{1,0:T(8,128)(2,1)S(1)} %collective-permute-done.8.refs_4_.refs_10_, ...), custom_call_target="tpu_custom_call" | custom-call | flops 1677721600 | bytes 7208960 | tf_op jit(solution)/shard_map/products/pallas_call | solution.py:239
  91.7 4.4 %products.9 = f32[704,512]{1,0:T(8,128)S(1)} custom-call(s32[8]{0:T(128)S(1)} %fusion.3.refs_0_, bf16[96,2048]{1,0:T(8,128)(2,1)S(1)} %collective-permute-done.2.refs_1_, bf16[96,2048]{1,0:T(8,128)(2,1)S(1)} %collective-permute-done.7.refs_2_, bf16[272,2048]{1,0:T(8,128)(2,1)S(1)} %collective-permute-done.5.refs_3_, ...), custom_call_target="tpu_custom_call" | custom-call | flops 2952790016 | bytes 11403264 | tf_op jit(solution)/shard_map/products/pallas_call | solution.py:239
  97.3 2.7 %collective-permute-done.17.refs_14_.refs_3_ = bf16[512,512]{1,0:T(8,128)(2,1)S(1)} collective-permute-done((bf16[512,512]{1,0:T(8,128)(2,1)S(1)}, bf16[512,512]{1,0:T(8,128)(2,1)S(1)}, u32[]{:S(2)}, u32[]{:S(2)}) %collective-permute-start.17) | collective-permute-done | bytes 524320 | tf_op jit(solution)/shard_map/ppermute | solution.py:307
  104.3 3.3 %products.11.refs_11_ = f32[704,512]{1,0:T(8,128)S(1)} custom-call(s32[8]{0:T(128)S(1)} %fusion.3.refs_0_, bf16[96,2048]{1,0:T(8,128)(2,1)S(1)} %collective-permute-done.2.refs_1_, bf16[96,2048]{1,0:T(8,128)(2,1)S(1)} %collective-permute-done.7.refs_2_, bf16[272,2048]{1,0:T(8,128)(2,1)S(1)} %collective-permute-done.5.refs_3_, ...), custom_call_target="tpu_custom_call" | custom-call | flops 2583691264 | bytes 10158080 | tf_op jit(solution)/shard_map/products/pallas_call | solution.py:239
  114.8 3.0 %products.10.refs_0_ = f32[640,512]{1,0:T(8,128)S(1)} custom-call(s32[8]{0:T(128)S(1)} %fusion.3.refs_0_, bf16[640,2048]{1,0:T(8,128)(2,1)S(1)} %pick_columns.9.refs_1_, bf16[640,2048]{1,0:T(8,128)(2,1)} %collective-permute-done.6.refs_2_, bf16[512,512]{1,0:T(8,128)(2,1)S(1)} %collective-permute-done.10.refs_14_.refs_3_, ...), custom_call_target="tpu_custom_call" | custom-call | flops 1006632960 | bytes 4849664 | tf_op jit(solution)/shard_map/products/pallas_call | solution.py:239
  118.9 17.3 %collective-permute-done.25.refs_1_ = f32[32,1024]{1,0:T(8,128)S(1)} collective-permute-done((f32[32,1024]{1,0:T(8,128)S(1)}, f32[32,1024]{1,0:T(8,128)S(1)}, u32[]{:S(2)}, u32[]{:S(2)}) %collective-permute-start.25) | collective-permute-done | bytes 131104 | tf_op jit(solution)/shard_map/ppermute | solution.py:392
  137.3 4.2 %all-to-all-start = ((bf16[8,3,5120]{2,1,0:T(4,128)(2,1)}), bf16[8,3,5120]{2,1,0:T(4,128)(2,1)}, u32[]{:S(2)}, u32[]{:S(2)}) async-start(bf16[8,3,5120]{2,1,0:T(4,128)(2,1)} %bitcast.32), calls=%async_computation | async-start | bytes 655360 | tf_op jit(solution)/shard_map/all_to_all | solution.py:403
  141.6 2.5 %convert_multiply_fusion.1.refs_2_ = f32[640,512]{1,0:T(8,128)} fusion(f16[640,512]{1,0:T(8,128)(2,1)} %collective-permute-done.26), kind=kLoop, calls=%fused_computation.5 | loop fusion | flops 655360 | bytes 1966080 | tf_op jit(solution)/shard_map/mul | solution.py:408
  146.0 3.0 %products.13.refs_1_ = f32[640,512]{1,0:T(8,128)S(1)} custom-call(s32[8]{0:T(128)S(1)} %fusion.3.refs_0_, bf16[640,2048]{1,0:T(8,128)(2,1)S(1)} %pick_columns.9.refs_1_, bf16[640,2048]{1,0:T(8,128)(2,1)} %collective-permute-done.6.refs_2_, bf16[512,512]{1,0:T(8,128)(2,1)S(1)} %copy-done.11, bf16[512,512]{1,0:T(8,128)(2,1)S(1)} %copy-done.13, ...), custom_call_target="tpu_custom_call" | custom-call | flops 1006632960 | bytes 4849664 | tf_op jit(solution)/shard_map/products/pallas_call | solution.py:239
  154.4 3.0 %rotate_attend.1 = bf16[24,4096]{1,0:T(8,128)(2,1)S(1)} custom-call(f32[640,512]{1,0:T(8,128)S(1)} %copy-done.6, f32[640,512]{1,0:T(8,128)S(1)} %copy-done.8, f32[640,512]{1,0:T(8,128)S(1)} %copy-done.9, f32[640,512]{1,0:T(8,128)S(1)} %convert_multiply_fusion.refs_3_, f32[640,64]{1,0:T(8,128)S(1)} %copy-done.21, f32[640,64]{1,0:T(8,128)S(1)} %copy-done.20, ...), custom_call_target="tpu_custom_call" | custom-call | flops 251658240 | bytes 5636096 | tf_op jit(solution)/shard_map/rotate_attend/pallas_call | solution.py:100
  157.6 13.8 %all_to_all.10 = bf16[8,3,4096]{2,1,0:T(4,128)(2,1)S(1)} all-to-all(bf16[8,3,4096]{2,1,0:T(4,128)(2,1)S(1)} %bitcast.38), channel_id=1, replica_groups=mesh['groups'=2,'rows'=8,'tensor'=2] {'rows'}, dimensions={0} | all-to-all | bytes 393216 | tf_op jit(solution)/shard_map/all_to_all | solution.py:411
  (178 shorter events, 54.3 us)
Async XLA Ops:
  4.7 16.5 %collective-permute-start = (bf16[512,512]{1,0:T(8,128)(2,1)S(1)}, bf16[512,512]{1,0:T(8,128)(2,1)}, u32[]{:S(2)}, u32[]{:S(2)}) collective-permute-start(bf16[512,512]{1,0:T(8,128)(2,1)S(1)} %get-tuple-element.71.refs_3_.refs_9_), channel_id=1, source_target_pairs={{0,4},{4,8},{8,12},{12,14},{14,10},{10,6},{6,2},{2,0},{1,5},{5,9},... | collective-permute-start | bytes 1572872 | tf_op jit(solution)/shard_map/ppermute | solution.py:307
  7.7 13.5 %collective-permute-start.1 = (bf16[512,512]{1,0:T(8,128)(2,1)S(1)}, bf16[512,512]{1,0:T(8,128)(2,1)}, u32[]{:S(2)}, u32[]{:S(2)}) collective-permute-start(bf16[512,512]{1,0:T(8,128)(2,1)S(1)} %get-tuple-element.71.refs_3_.refs_9_), channel_id=1, source_target_pairs={{4,0},{8,4},{12,8},{14,12},{10,14},{6,10},{2,6},{0,2},{5,1},{9,5},... | collective-permute-start | bytes 1572872 | tf_op jit(solution)/shard_map/ppermute | solution.py:307
  10.6 10.6 %collective-permute-start.2 = (bf16[96,2048]{1,0:T(8,128)(2,1)S(1)}, bf16[96,2048]{1,0:T(8,128)(2,1)S(1)}, u32[]{:S(2)}, u32[]{:S(2)}) collective-permute-start(bf16[96,2048]{1,0:T(8,128)(2,1)S(1)} %pick_columns.6), channel_id=1, source_target_pairs={{0,16},{16,0},{1,17},{17,1},{2,18},{18,2},{3,19},{19,3},{4,20},{20... | collective-permute-start | bytes 1179656 | tf_op jit(solution)/shard_map/ppermute | solution.py:328
  23.5 26.7 %collective-permute-start.5 = (bf16[272,2048]{1,0:T(8,128)(2,1)}, bf16[272,2048]{1,0:T(8,128)(2,1)S(1)}, u32[]{:S(2)}, u32[]{:S(2)}) collective-permute-start(bf16[272,2048]{1,0:T(8,128)(2,1)} %copy-done.23), channel_id=1, source_target_pairs={{0,16},{16,0},{1,17},{17,1},{2,18},{18,2},{3,19},{19,3},{4,20},{20... | collective-permute-start | bytes 3342344 | tf_op jit(solution)/shard_map/ppermute | solution.py:341
  25.3 15.0 %collective-permute-start.3 = (bf16[512,512]{1,0:T(8,128)(2,1)}, bf16[512,512]{1,0:T(8,128)(2,1)S(1)}, u32[]{:S(2)}, u32[]{:S(2)}) collective-permute-start(bf16[512,512]{1,0:T(8,128)(2,1)} %collective-permute-done.refs_4_.refs_10_), channel_id=1, source_target_pairs={{0,4},{4,8},{8,12},{12,14},{14,10},{10,6},{6,2},{2,0},{1,5},{5,9},... | collective-permute-start | bytes 1572872 | tf_op jit(solution)/shard_map/ppermute | solution.py:307
  26.9 15.1 %collective-permute-start.4 = (bf16[512,512]{1,0:T(8,128)(2,1)}, bf16[512,512]{1,0:T(8,128)(2,1)S(1)}, u32[]{:S(2)}, u32[]{:S(2)}) collective-permute-start(bf16[512,512]{1,0:T(8,128)(2,1)} %collective-permute-done.1.refs_5_.refs_11_), channel_id=1, source_target_pairs={{4,0},{8,4},{12,8},{14,12},{10,14},{6,10},{2,6},{0,2},{5,1},{9,5},... | collective-permute-start | bytes 1572872 | tf_op jit(solution)/shard_map/ppermute | solution.py:307
  27.4 23.0 %collective-permute-start.8 = (bf16[512,512]{1,0:T(8,128)(2,1)}, bf16[512,512]{1,0:T(8,128)(2,1)S(1)}, u32[]{:S(2)}, u32[]{:S(2)}) collective-permute-start(bf16[512,512]{1,0:T(8,128)(2,1)} %copy-done.14), channel_id=1, source_target_pairs={{0,4},{4,8},{8,12},{12,14},{14,10},{10,6},{6,2},{2,0},{1,5},{5,9},... | collective-permute-start | bytes 1572872 | tf_op jit(solution)/shard_map/ppermute | solution.py:307
  29.0 22.6 %collective-permute-start.9 = (bf16[512,512]{1,0:T(8,128)(2,1)}, bf16[512,512]{1,0:T(8,128)(2,1)S(1)}, u32[]{:S(2)}, u32[]{:S(2)}) collective-permute-start(bf16[512,512]{1,0:T(8,128)(2,1)} %copy-done.14), channel_id=1, source_target_pairs={{4,0},{8,4},{12,8},{14,12},{10,14},{6,10},{2,6},{0,2},{5,1},{9,5},... | collective-permute-start | bytes 1572872 | tf_op jit(solution)/shard_map/ppermute | solution.py:307
  51.7 27.2 %collective-permute-start.12 = (bf16[272,2048]{1,0:T(8,128)(2,1)}, bf16[272,2048]{1,0:T(8,128)(2,1)S(1)}, u32[]{:S(2)}, u32[]{:S(2)}) collective-permute-start(bf16[272,2048]{1,0:T(8,128)(2,1)} %copy-done.22), channel_id=1, source_target_pairs={{0,16},{16,0},{1,17},{17,1},{2,18},{18,2},{3,19},{19,3},{4,20},{20... | collective-permute-start | bytes 3342344 | tf_op jit(solution)/shard_map/ppermute | solution.py:357
  52.2 14.8 %collective-permute-start.10 = (bf16[512,512]{1,0:T(8,128)(2,1)S(1)}, bf16[512,512]{1,0:T(8,128)(2,1)S(1)}, u32[]{:S(2)}, u32[]{:S(2)}) collective-permute-start(bf16[512,512]{1,0:T(8,128)(2,1)S(1)} %collective-permute-done.3.refs_6_.refs_12_), channel_id=1, source_target_pairs={{0,4},{4,8},{8,12},{12,14},{14,10},{10,6},{6,2},{2,0},{1,5},{5,9},... | collective-permute-start | bytes 1572872 | tf_op jit(solution)/shard_map/ppermute | solution.py:307
  53.8 14.8 %collective-permute-start.11 = (bf16[512,512]{1,0:T(8,128)(2,1)S(1)}, bf16[512,512]{1,0:T(8,128)(2,1)S(1)}, u32[]{:S(2)}, u32[]{:S(2)}) collective-permute-start(bf16[512,512]{1,0:T(8,128)(2,1)S(1)} %collective-permute-done.4.refs_7_.refs_13_), channel_id=1, source_target_pairs={{4,0},{8,4},{12,8},{14,12},{10,14},{6,10},{2,6},{0,2},{5,1},{9,5},... | collective-permute-start | bytes 1572872 | tf_op jit(solution)/shard_map/ppermute | solution.py:307
  54.4 24.4 %collective-permute-start.14 = (bf16[512,512]{1,0:T(8,128)(2,1)S(1)}, bf16[512,512]{1,0:T(8,128)(2,1)S(1)}, u32[]{:S(2)}, u32[]{:S(2)}) collective-permute-start(bf16[512,512]{1,0:T(8,128)(2,1)S(1)} %collective-permute-done.8.refs_4_.refs_10_), channel_id=1, source_target_pairs={{0,4},{4,8},{8,12},{12,14},{14,10},{10,6},{6,2},{2,0},{1,5},{5,9},... | collective-permute-start | bytes 1572872 | tf_op jit(solution)/shard_map/ppermute | solution.py:307
  56.0 22.9 %collective-permute-start.15 = (bf16[512,512]{1,0:T(8,128)(2,1)S(1)}, bf16[512,512]{1,0:T(8,128)(2,1)S(1)}, u32[]{:S(2)}, u32[]{:S(2)}) collective-permute-start(bf16[512,512]{1,0:T(8,128)(2,1)S(1)} %collective-permute-done.9.refs_5_.refs_11_), channel_id=1, source_target_pairs={{4,0},{8,4},{12,8},{14,12},{10,14},{6,10},{2,6},{0,2},{5,1},{9,5},... | collective-permute-start | bytes 1572872 | tf_op jit(solution)/shard_map/ppermute | solution.py:307
  80.3 11.4 %collective-permute-start.21 = (bf16[256,512]{1,0:T(8,128)(2,1)S(1)}, bf16[256,512]{1,0:T(8,128)(2,1)S(1)}, u32[]{:S(2)}, u32[]{:S(2)}) collective-permute-start(bf16[256,512]{1,0:T(8,128)(2,1)S(1)} %slice.48), channel_id=1, source_target_pairs={{0,4},{4,8},{8,12},{12,14},{14,10},{10,6},{6,2},{2,0},{1,5},{5,9},... | collective-permute-start | bytes 786440 | tf_op jit(solution)/shard_map/ppermute | solution.py:307
  81.9 9.8 %collective-permute-start.22 = (bf16[256,512]{1,0:T(8,128)(2,1)S(1)}, bf16[256,512]{1,0:T(8,128)(2,1)S(1)}, u32[]{:S(2)}, u32[]{:S(2)}) collective-permute-start(bf16[256,512]{1,0:T(8,128)(2,1)S(1)} %slice.49), channel_id=1, source_target_pairs={{4,0},{8,4},{12,8},{14,12},{10,14},{6,10},{2,6},{0,2},{5,1},{9,5},... | collective-permute-start | bytes 786440 | tf_op jit(solution)/shard_map/ppermute | solution.py:307
  84.8 6.9 %collective-permute-start.20 = (bf16[64,2048]{1,0:T(8,128)(2,1)S(1)}, bf16[64,2048]{1,0:T(8,128)(2,1)S(1)}, u32[]{:S(2)}, u32[]{:S(2)}) collective-permute-start(bf16[64,2048]{1,0:T(8,128)(2,1)S(1)} %constant_dynamic-update-slice_fusion.refs_7_), channel_id=1, source_target_pairs={{0,1},{1,0},{2,3},{3,2},{4,5},{5,4},{6,7},{7,6},{8,9},{9,8},{10,11... | collective-permute-start | bytes 786440 | tf_op jit(solution)/shard_map/ppermute | solution.py:375
  84.9 15.1 %collective-permute-start.17 = (bf16[512,512]{1,0:T(8,128)(2,1)S(1)}, bf16[512,512]{1,0:T(8,128)(2,1)S(1)}, u32[]{:S(2)}, u32[]{:S(2)}) collective-permute-start(bf16[512,512]{1,0:T(8,128)(2,1)S(1)} %collective-permute-done.14.refs_6_.refs_12_), channel_id=1, source_target_pairs={{0,4},{4,8},{8,12},{12,14},{14,10},{10,6},{6,2},{2,0},{1,5},{5,9},... | collective-permute-start | bytes 1572872 | tf_op jit(solution)/shard_map/ppermute | solution.py:307
  86.5 14.8 %collective-permute-start.18 = (bf16[512,512]{1,0:T(8,128)(2,1)S(1)}, bf16[512,512]{1,0:T(8,128)(2,1)S(1)}, u32[]{:S(2)}, u32[]{:S(2)}) collective-permute-start(bf16[512,512]{1,0:T(8,128)(2,1)S(1)} %collective-permute-done.15.refs_7_.refs_13_), channel_id=1, source_target_pairs={{4,0},{8,4},{12,8},{14,12},{10,14},{6,10},{2,6},{0,2},{5,1},{9,5},... | collective-permute-start | bytes 1572872 | tf_op jit(solution)/shard_map/ppermute | solution.py:307
  101.4 7.6 %collective-permute-start.23 = (bf16[256,512]{1,0:T(8,128)(2,1)S(1)}, bf16[256,512]{1,0:T(8,128)(2,1)S(1)}, u32[]{:S(2)}, u32[]{:S(2)}) collective-permute-start(bf16[256,512]{1,0:T(8,128)(2,1)S(1)} %slice.41), channel_id=1, source_target_pairs={{0,4},{4,8},{8,12},{12,14},{14,10},{10,6},{6,2},{2,0},{1,5},{5,9},... | collective-permute-start | bytes 786440 | tf_op jit(solution)/shard_map/ppermute | solution.py:307
  103.0 7.6 %collective-permute-start.24 = (bf16[256,512]{1,0:T(8,128)(2,1)S(1)}, bf16[256,512]{1,0:T(8,128)(2,1)S(1)}, u32[]{:S(2)}, u32[]{:S(2)}) collective-permute-start(bf16[256,512]{1,0:T(8,128)(2,1)S(1)} %slice.42), channel_id=1, source_target_pairs={{4,0},{8,4},{12,8},{14,12},{10,14},{6,10},{2,6},{0,2},{5,1},{9,5},... | collective-permute-start | bytes 786440 | tf_op jit(solution)/shard_map/ppermute | solution.py:307
  103.7 37.9 %collective-permute-start.26 = (f16[640,512]{1,0:T(8,128)(2,1)}, f16[640,512]{1,0:T(8,128)(2,1)}, u32[]{:S(2)}, u32[]{:S(2)}) collective-permute-start(f16[640,512]{1,0:T(8,128)(2,1)} %fusion.1), channel_id=1, source_target_pairs={{0,16},{16,0},{1,17},{17,1},{2,18},{18,2},{3,19},{19,3},{4,20},{20... | collective-permute-start | bytes 1966088 | tf_op jit(solution)/shard_map/ppermute | solution.py:386
  112.7 38.8 %collective-permute-start.27 = (f16[640,512]{1,0:T(8,128)(2,1)}, f16[640,512]{1,0:T(8,128)(2,1)}, u32[]{:S(2)}, u32[]{:S(2)}) collective-permute-start(f16[640,512]{1,0:T(8,128)(2,1)} %fusion), channel_id=1, source_target_pairs={{0,16},{16,0},{1,17},{17,1},{2,18},{18,2},{3,19},{19,3},{4,20},{20... | collective-permute-start | bytes 1966088 | tf_op jit(solution)/shard_map/ppermute | solution.py:396
  113.4 22.8 %collective-permute-start.25 = (f32[32,1024]{1,0:T(8,128)S(1)}, f32[32,1024]{1,0:T(8,128)S(1)}, u32[]{:S(2)}, u32[]{:S(2)}) collective-permute-start(f32[32,1024]{1,0:T(8,128)S(1)} %pad_maximum_fusion), channel_id=1, source_target_pairs={{0,16},{16,0},{1,17},{17,1},{2,18},{18,2},{3,19},{19,3},{4,20},{20... | collective-permute-start | bytes 393224 | tf_op jit(solution)/shard_map/ppermute | solution.py:392
  137.3 12.9 %all-to-all-start = ((bf16[8,3,5120]{2,1,0:T(4,128)(2,1)}), bf16[8,3,5120]{2,1,0:T(4,128)(2,1)}, u32[]{:S(2)}, u32[]{:S(2)}) async-start(bf16[8,3,5120]{2,1,0:T(4,128)(2,1)} %bitcast.32), calls=%async_computation | async-start | bytes 655360 | tf_op jit(solution)/shard_map/all_to_all | solution.py:403
  (42 other events, 219.7 us)

commit v10 on v9

--- a/solution.py
+++ b/solution.py
@@ -17,11 +17,11 @@
 RAISE = 16.0
 
 
-def angle_tables(positions):
+def angle_table(positions):
     index_float = jnp.arange(HALF, dtype=jnp.float32)
     inverse = jnp.exp(index_float * (-2.0 * math.log(1000000.0) / HD))
     angles = positions.astype(jnp.float32)[:, None] * inverse
-    return jnp.cos(angles), jnp.sin(angles)
+    return jnp.concatenate([jnp.cos(angles), jnp.sin(angles)], 1)
 
 
 def token_tables(lengths, destinations, row_index, tokens, requests, steps, padded):
@@ -50,8 +50,8 @@
 
 def finish_kernel(chunks, group, *refs):
     held, homed, refs = refs[:chunks], refs[chunks : 2 * chunks], refs[2 * chunks :]
-    cos_ref, sin_ref, keys_ref, rows_ref, new_ref, query_ref, out_ref = refs
-    cosine, sine = cos_ref[...], sin_ref[...]
+    angle_ref, keys_ref, rows_ref, new_ref, query_ref, out_ref = refs
+    cosine, sine = angle_ref[:, :HALF], angle_ref[:, HALF:]
     allowed = (keys_ref[0:1, :] == rows_ref[:, 0:1]) & (keys_ref[1:2, :] <= rows_ref[:, 1:2])
     allowed = jnp.concatenate([allowed.astype(jnp.float32)] * group, 0) > 0.5
     queries = query_ref[...].astype(jnp.float32)
@@ -90,13 +90,13 @@
             ].astype(jnp.bfloat16)
 
 
-def finish(held, homed, cosine, sine, key_info, query_info, new_pairs, queries):
+def finish(held, homed, angles, key_info, query_info, new_pairs, queries):
     rows, width = held[0].shape
     heads = len(held) * width // (2 * HD)
     group = queries.shape[1] // (heads * HD)
     count = queries.shape[0]
     vmem = pl.BlockSpec(memory_space=pltpu.VMEM)
-    operands = [*held, *homed, cosine, sine, key_info, query_info, new_pairs, queries]
+    operands = [*held, *homed, angles, key_info, query_info, new_pairs, queries]
     return pl.pallas_call(
         functools.partial(finish_kernel, len(held), group),
         out_shape=jax.ShapeDtypeStruct(queries.shape, jnp.bfloat16),
@@ -144,8 +144,8 @@
 
 
 def pack_kernel(chunks, own_ref, *refs):
-    owns, (got_ref, cos_ref, sin_ref, query_ref, out_ref) = (own_ref, *refs[: chunks - 1]), refs[chunks - 1 :]
-    cosine, sine = cos_ref[...], sin_ref[...]
+    owns, (got_ref, angle_ref, query_ref, out_ref) = (own_ref, *refs[: chunks - 1]), refs[chunks - 1 :]
+    cosine, sine = angle_ref[:, :HALF], angle_ref[:, HALF:]
     count, base = query_ref.shape
     width = owns[0].shape[1]
     half = width // 2
@@ -162,20 +162,20 @@
         out_ref[:, at : at + half] = values.astype(jnp.bfloat16)
 
 
-def pack(owns, got, cosine, sine, queries):
+def pack(owns, got, angles, queries):
     vmem = pl.BlockSpec(memory_space=pltpu.VMEM)
     width = queries.shape[1] + got.shape[1]
     return pl.pallas_call(
         functools.partial(pack_kernel, len(owns)),
         out_shape=jax.ShapeDtypeStruct((queries.shape[0], width), jnp.bfloat16),
-        in_specs=[vmem] * (len(owns) + 4),
+        in_specs=[vmem] * (len(owns) + 3),
         out_specs=vmem,
         compiler_params=pltpu.CompilerParams(vmem_limit_bytes=VMEM_BYTES),
         cost_estimate=pl.CostEstimate(
             flops=0, bytes_accessed=4 * queries.size + 10 * got.size, transcendentals=0
         ),
         name="pack_new",
-    )(*owns, got, cosine, sine, queries)
+    )(*owns, got, angles, queries)
 
 
 def pick_kernel(first, side_ref, source_ref, out_ref):
@@ -347,9 +347,8 @@
     position, new_position, key_info, query_info = token_tables(
         lengths, destinations, row_index, tokens, requests, steps, new_padded
     )
-    cosine, sine = angle_tables(position)
-    new_cosine, new_sine = angle_tables(new_position)
-    tables = (cosine, sine, new_cosine, new_sine, key_info, query_info)
+    angles, new_angles = angle_table(position), angle_table(new_position)
+    tables = (angles, new_angles, key_info, query_info)
     got[1], tables, places, ring[1][-1] = fence_with(0, got[1], tables, places, ring[1][-1])
 
     own_hidden = [(kept, kept_other)]
@@ -392,10 +391,12 @@
     new_back = lax.ppermute(jnp.concatenate(new_away, 1), "groups", partners)
     held[0] = project(0, own_hidden, held[0], early, row_count)
     queries = jnp.swapaxes(queries, 0, 1).reshape(count, -1)
-    held, queries, places = fence(held, queries, places)
+    held, queries, places, away, new_back, homed[0] = fence(
+        held, queries, places, away, new_back, homed[0]
+    )
     homed.append(lax.ppermute(away[0], "groups", partners))
-    cosine, sine, new_cosine, new_sine, key_info, query_info = tables
-    moved = pack(new_own, new_back, new_cosine, new_sine, queries)
+    angles, new_angles, key_info, query_info = tables
+    moved = pack(new_own, new_back, new_angles, queries)
     moved, places = fence(moved, places)
     held[1] = project(1, own_hidden, held[1], early, row_count)
     moved = moved.reshape(steps, requests, -1)
@@ -406,7 +407,7 @@
     query_rows, new_pairs = moved[:, :heads_width], moved[:, heads_width:]
     new_pairs = jnp.pad(new_pairs, ((0, new_padded - count), (0, 0)))
     homed = [total.astype(jnp.float32) * (1.0 / RAISE) for total in homed]
-    attended = finish(held, homed, cosine, sine, key_info, query_info, new_pairs, query_rows)
+    attended = finish(held, homed, angles, key_info, query_info, new_pairs, query_rows)
     attended = jnp.swapaxes(attended.reshape(steps, requests, -1), 0, 1)
     return lax.all_to_all(attended, "rows", split_axis=0, concat_axis=0, tiled=True)
 

time: 173 us -> 152 us (0.88)
  waiting for transfers between devices: 68.2 us -> 52.5 us
  other arithmetic: 9.51 us -> 6.32 us
    ppermute x1, waiting for transfers between devices: 17.3 us -> 3.34 us  [body(): new_back = lax.ppermute(jnp.concatenate(new_away, 1), 'groups', partners)]
    mul x2, other arithmetic: 3.83 us -> 1.52 us  [body(): homed = [total.astype(jnp.float32) * (1.0 / RAISE) for total in homed]]
    sin x2 -> x0, other arithmetic: 2.2 us -> none  [angle_tables(): return (jnp.cos(angles), jnp.sin(angles))]
  transfers between devices with their start and end apart: 29 -> 29, of which waited for: 17 -> 16; matrix products, arithmetic and copies ran while one was open for 6% -> 5% of each run, Pallas kernels for 14% -> 16%
where the time goes in v10:
time: 152 us
  waiting for transfers between devices  52.5 us (35%)
  starting transfers between devices  30.9 us (20%)
  Pallas kernels  29.8 us (20%)
  local copies, waits for them, and re-layouts  18.3 us (12%)
  blocking collectives  13 us (9%)
  other arithmetic  6.32 us (4%)
    pallas_call x7, Pallas kernels, products(): pl.pallas_call(functools.partial(product_kernel, depths, len(hidden), bas...  22.3 us
    ppermute x8, waiting for transfers between devices, step(): lax.ppermute(pair[0], 'rows', onward)  17.6 us
    unnamed x73, local copies, waits for them, and re-layouts  14.5 us
    ppermute x8, starting transfers between devices, step(): lax.ppermute(pair[0], 'rows', onward)  14.2 us
    all_to_all x1, blocking collectives, body(): lax.all_to_all(attended, 'rows', split_axis=0, concat_axis=0, tiled=True)  13 us
    ppermute x1, waiting for transfers between devices, body(): got.append(lax.ppermute(sent[2], 'groups', partners))  10 us
    ppermute x1, waiting for transfers between devices, body(): got.append(lax.ppermute(sent[1], 'groups', partners))  8.19 us
    ppermute x8, waiting for transfers between devices, step(): lax.ppermute(pair[1], 'rows', back)  5.95 us
  transfers between devices with their start and end apart: 29, of which 16 were waited for; matrix products, arithmetic and copies ran while one was open for 5% of the time, Pallas kernels for 16%

profile of v10, /device:TPU:0, one launch (start us, length us, event | category | flops | bytes accessed | tf_op | source)
XLA Modules:
  0.0 151.5 jit_solution(15676790632270096406)
XLA Ops:
  1.6 2.3 %own_half.1 = (bf16[512,512]{1,0:T(8,128)(2,1)S(1)}, bf16[512,512]{1,0:T(8,128)(2,1)S(1)}) custom-call(s32[1]{0:T(128)} %bitcast.side_ref, bf16[1024,2,512]{2,1,0:T(2,128)(2,1)S(1)} %copy-done.17), custom_call_target="tpu_custom_call" | custom-call | bytes 4194304 | tf_op jit(solution)/shard_map/own_half/pallas_call | solution.py:127
  4.7 3.0 %collective-permute-start = (bf16[512,512]{1,0:T(8,128)(2,1)S(1)}, bf16[512,512]{1,0:T(8,128)(2,1)}, u32[]{:S(2)}, u32[]{:S(2)}) collective-permute-start(bf16[512,512]{1,0:T(8,128)(2,1)S(1)} %get-tuple-element.72.refs_3_.refs_9_), channel_id=1, source_target_pairs={{0,4},{4,8},{8,12},{12,14},{14,10},{10,6},{6,2},{2,0},{1,5},{5,9},... | collective-permute-start | bytes 1572872 | tf_op jit(solution)/shard_map/ppermute | solution.py:307
  7.8 2.5 %copy-done = bf16[640,4096]{1,0:T(8,128)(2,1)S(1)} copy-done((bf16[640,4096]{1,0:T(8,128)(2,1)S(1)}, bf16[640,4096]{1,0:T(8,128)(2,1)}, u32[]{:S(2)}) %copy-start) | copy-done | bytes 5242904
  10.6 2.0 %collective-permute-start.2 = (bf16[96,2048]{1,0:T(8,128)(2,1)S(1)}, bf16[96,2048]{1,0:T(8,128)(2,1)S(1)}, u32[]{:S(2)}, u32[]{:S(2)}) collective-permute-start(bf16[96,2048]{1,0:T(8,128)(2,1)S(1)} %pick_columns.6), channel_id=1, source_target_pairs={{0,16},{16,0},{1,17},{17,1},{2,18},{18,2},{3,19},{19,3},{4,20},{20... | collective-permute-start | bytes 1179656 | tf_op jit(solution)/shard_map/ppermute | solution.py:328
  17.4 3.8 %collective-permute-done.2.refs_1_ = bf16[96,2048]{1,0:T(8,128)(2,1)S(1)} collective-permute-done((bf16[96,2048]{1,0:T(8,128)(2,1)S(1)}, bf16[96,2048]{1,0:T(8,128)(2,1)S(1)}, u32[]{:S(2)}, u32[]{:S(2)}) %collective-permute-start.2) | collective-permute-done | bytes 393248 | tf_op jit(solution)/shard_map/ppermute | solution.py:328
  23.5 1.7 %collective-permute-start.5 = (bf16[272,2048]{1,0:T(8,128)(2,1)}, bf16[272,2048]{1,0:T(8,128)(2,1)S(1)}, u32[]{:S(2)}, u32[]{:S(2)}) collective-permute-start(bf16[272,2048]{1,0:T(8,128)(2,1)} %copy-done.21), channel_id=1, source_target_pairs={{0,16},{16,0},{1,17},{17,1},{2,18},{18,2},{3,19},{19,3},{4,20},{20... | collective-permute-start | bytes 3342344 | tf_op jit(solution)/shard_map/ppermute | solution.py:341
  27.6 1.6 %collective-permute-start.8 = (bf16[512,512]{1,0:T(8,128)(2,1)}, bf16[512,512]{1,0:T(8,128)(2,1)S(1)}, u32[]{:S(2)}, u32[]{:S(2)}) collective-permute-start(bf16[512,512]{1,0:T(8,128)(2,1)} %copy-done.13), channel_id=1, source_target_pairs={{0,4},{4,8},{8,12},{12,14},{14,10},{10,6},{6,2},{2,0},{1,5},{5,9},... | collective-permute-start | bytes 1572872 | tf_op jit(solution)/shard_map/ppermute | solution.py:307
  31.8 8.6 %collective-permute-done.3.refs_6_.refs_12_ = bf16[512,512]{1,0:T(8,128)(2,1)S(1)} collective-permute-done((bf16[512,512]{1,0:T(8,128)(2,1)}, bf16[512,512]{1,0:T(8,128)(2,1)S(1)}, u32[]{:S(2)}, u32[]{:S(2)}) %collective-permute-start.3) | collective-permute-done | bytes 524320 | tf_op jit(solution)/shard_map/ppermute | solution.py:307
  42.0 8.2 %collective-permute-done.5.refs_3_ = bf16[272,2048]{1,0:T(8,128)(2,1)S(1)} collective-permute-done((bf16[272,2048]{1,0:T(8,128)(2,1)}, bf16[272,2048]{1,0:T(8,128)(2,1)S(1)}, u32[]{:S(2)}, u32[]{:S(2)}) %collective-permute-start.5) | collective-permute-done | bytes 1114144 | tf_op jit(solution)/shard_map/ppermute | solution.py:341
  56.5 3.9 %products.7.refs_7_ = f32[640,512]{1,0:T(8,128)S(1)} custom-call(s32[8]{0:T(128)S(1)} %fusion.3.refs_0_, bf16[640,2048]{1,0:T(8,128)(2,1)S(1)} %pick_columns.9.refs_1_, bf16[640,2048]{1,0:T(8,128)(2,1)} %collective-permute-done.6.refs_2_, bf16[512,512]{1,0:T(8,128)(2,1)S(1)} %copy-done.16, bf16[512,512]{1,0:T(8,128)(2,1)} %collective-permute-done.refs_4_.refs_10_, ...), custom_call_target="tpu_custom_call" | custom-call | flops 1677721600 | bytes 7208960 | tf_op jit(solution)/shard_map/products/pallas_call | solution.py:239
  60.4 6.6 %collective-permute-done.10.refs_14_.refs_3_ = bf16[512,512]{1,0:T(8,128)(2,1)S(1)} collective-permute-done((bf16[512,512]{1,0:T(8,128)(2,1)S(1)}, bf16[512,512]{1,0:T(8,128)(2,1)S(1)}, u32[]{:S(2)}, u32[]{:S(2)}) %collective-permute-start.10) | collective-permute-done | bytes 524320 | tf_op jit(solution)/shard_map/ppermute | solution.py:307
  68.6 10.0 %collective-permute-done.12.refs_5_ = bf16[272,2048]{1,0:T(8,128)(2,1)S(1)} collective-permute-done((bf16[272,2048]{1,0:T(8,128)(2,1)S(1)}, bf16[272,2048]{1,0:T(8,128)(2,1)S(1)}, u32[]{:S(2)}, u32[]{:S(2)}) %collective-permute-start.12) | collective-permute-done | bytes 1114144 | tf_op jit(solution)/shard_map/ppermute | solution.py:356
  80.3 1.6 %collective-permute-start.21 = (bf16[256,512]{1,0:T(8,128)(2,1)S(1)}, bf16[256,512]{1,0:T(8,128)(2,1)S(1)}, u32[]{:S(2)}, u32[]{:S(2)}) collective-permute-start(bf16[256,512]{1,0:T(8,128)(2,1)S(1)} %slice.48), channel_id=1, source_target_pairs={{0,4},{4,8},{8,12},{12,14},{14,10},{10,6},{6,2},{2,0},{1,5},{5,9},... | collective-permute-start | bytes 786440 | tf_op jit(solution)/shard_map/ppermute | solution.py:307
  82.4 2.3 %collective-permute-done.19 = bf16[32,2048]{1,0:T(8,128)(2,1)S(1)} collective-permute-done((bf16[32,2048]{1,0:T(8,128)(2,1)S(1)}, bf16[32,2048]{1,0:T(8,128)(2,1)S(1)}, u32[]{:S(2)}, u32[]{:S(2)}) %collective-permute-start.19) | collective-permute-done | bytes 131104 | tf_op jit(solution)/shard_map/ppermute | solution.py:373
  86.9 3.6 %products.8.refs_7_ = f32[640,512]{1,0:T(8,128)S(1)} custom-call(s32[8]{0:T(128)S(1)} %fusion.3.refs_0_, bf16[640,2048]{1,0:T(8,128)(2,1)S(1)} %pick_columns.9.refs_1_, bf16[640,2048]{1,0:T(8,128)(2,1)} %collective-permute-done.6.refs_2_, bf16[512,512]{1,0:T(8,128)(2,1)S(1)} %copy-done.14, bf16[512,512]{1,0:T(8,128)(2,1)S(1)} %collective-permute-done.8.refs_4_.refs_10_, ...), custom_call_target="tpu_custom_call" | custom-call | flops 1677721600 | bytes 7208960 | tf_op jit(solution)/shard_map/products/pallas_call | solution.py:239
  91.7 4.4 %products.9 = f32[704,512]{1,0:T(8,128)S(1)} custom-call(s32[8]{0:T(128)S(1)} %fusion.3.refs_0_, bf16[96,2048]{1,0:T(8,128)(2,1)S(1)} %collective-permute-done.2.refs_1_, bf16[96,2048]{1,0:T(8,128)(2,1)S(1)} %collective-permute-done.7.refs_2_, bf16[272,2048]{1,0:T(8,128)(2,1)S(1)} %collective-permute-done.5.refs_3_, ...), custom_call_target="tpu_custom_call" | custom-call | flops 2952790016 | bytes 11403264 | tf_op jit(solution)/shard_map/products/pallas_call | solution.py:239
  97.8 2.3 %collective-permute-done.17.refs_14_.refs_3_ = bf16[512,512]{1,0:T(8,128)(2,1)S(1)} collective-permute-done((bf16[512,512]{1,0:T(8,128)(2,1)S(1)}, bf16[512,512]{1,0:T(8,128)(2,1)S(1)}, u32[]{:S(2)}, u32[]{:S(2)}) %collective-permute-start.17) | collective-permute-done | bytes 524320 | tf_op jit(solution)/shard_map/ppermute | solution.py:307
  103.7 3.0 %products.10.refs_0_ = f32[640,512]{1,0:T(8,128)S(1)} custom-call(s32[8]{0:T(128)S(1)} %fusion.3.refs_0_, bf16[640,2048]{1,0:T(8,128)(2,1)S(1)} %pick_columns.9.refs_1_, bf16[640,2048]{1,0:T(8,128)(2,1)} %collective-permute-done.6.refs_2_, bf16[512,512]{1,0:T(8,128)(2,1)S(1)} %collective-permute-done.10.refs_14_.refs_3_, ...), custom_call_target="tpu_custom_call" | custom-call | flops 1006632960 | bytes 4849664 | tf_op jit(solution)/shard_map/products/pallas_call | solution.py:239
  107.8 3.3 %products.11.refs_11_ = f32[704,512]{1,0:T(8,128)S(1)} custom-call(s32[8]{0:T(128)S(1)} %fusion.3.refs_0_, bf16[96,2048]{1,0:T(8,128)(2,1)S(1)} %collective-permute-done.2.refs_1_, bf16[96,2048]{1,0:T(8,128)(2,1)S(1)} %collective-permute-done.7.refs_2_, bf16[272,2048]{1,0:T(8,128)(2,1)S(1)} %collective-permute-done.5.refs_3_, ...), custom_call_target="tpu_custom_call" | custom-call | flops 2583691264 | bytes 10158080 | tf_op jit(solution)/shard_map/products/pallas_call | solution.py:239
  114.0 3.3 %collective-permute-done.25.refs_1_ = f32[32,1024]{1,0:T(8,128)S(1)} collective-permute-done((f32[32,1024]{1,0:T(8,128)S(1)}, f32[32,1024]{1,0:T(8,128)S(1)}, u32[]{:S(2)}, u32[]{:S(2)}) %collective-permute-start.25) | collective-permute-done | bytes 131104 | tf_op jit(solution)/shard_map/ppermute | solution.py:391
  119.1 4.1 %all-to-all-start = ((bf16[8,3,5120]{2,1,0:T(4,128)(2,1)}), bf16[8,3,5120]{2,1,0:T(4,128)(2,1)}, u32[]{:S(2)}, u32[]{:S(2)}) async-start(bf16[8,3,5120]{2,1,0:T(4,128)(2,1)} %bitcast.38), calls=%async_computation | async-start | bytes 655360 | tf_op jit(solution)/shard_map/all_to_all | solution.py:404
  126.6 3.0 %products.13.refs_1_ = f32[640,512]{1,0:T(8,128)S(1)} custom-call(s32[8]{0:T(128)S(1)} %fusion.3.refs_0_, bf16[640,2048]{1,0:T(8,128)(2,1)S(1)} %pick_columns.9.refs_1_, bf16[640,2048]{1,0:T(8,128)(2,1)} %collective-permute-done.6.refs_2_, bf16[512,512]{1,0:T(8,128)(2,1)S(1)} %copy-done.10, bf16[512,512]{1,0:T(8,128)(2,1)S(1)} %copy-done.12, ...), custom_call_target="tpu_custom_call" | custom-call | flops 1006632960 | bytes 4849664 | tf_op jit(solution)/shard_map/products/pallas_call | solution.py:239
  134.7 2.9 %rotate_attend.1 = bf16[24,4096]{1,0:T(8,128)(2,1)S(1)} custom-call(f32[640,512]{1,0:T(8,128)S(1)} %copy-done.6, f32[640,512]{1,0:T(8,128)S(1)} %copy-done.8, f32[640,512]{1,0:T(8,128)S(1)} %convert_multiply_fusion.1.refs_2_, f32[640,512]{1,0:T(8,128)S(1)} %convert_multiply_fusion.refs_3_, f32[640,128]{1,0:T(8,128)S(1)} %copy-done.18, ...), custom_call_target="tpu_custom_call" | custom-call | flops 251658240 | bytes 5636096 | tf_op jit(solution)/shard_map/rotate_attend/pallas_call | solution.py:100
  137.7 13.0 %all_to_all.10 = bf16[8,3,4096]{2,1,0:T(4,128)(2,1)S(1)} all-to-all(bf16[8,3,4096]{2,1,0:T(4,128)(2,1)S(1)} %bitcast.39), channel_id=1, replica_groups=mesh['groups'=2,'rows'=8,'tensor'=2] {'rows'}, dimensions={0} | all-to-all | bytes 393216 | tf_op jit(solution)/shard_map/all_to_all | solution.py:412
  (180 shorter events, 49.8 us)
Async XLA Ops:
  4.7 16.5 %collective-permute-start = (bf16[512,512]{1,0:T(8,128)(2,1)S(1)}, bf16[512,512]{1,0:T(8,128)(2,1)}, u32[]{:S(2)}, u32[]{:S(2)}) collective-permute-start(bf16[512,512]{1,0:T(8,128)(2,1)S(1)} %get-tuple-element.72.refs_3_.refs_9_), channel_id=1, source_target_pairs={{0,4},{4,8},{8,12},{12,14},{14,10},{10,6},{6,2},{2,0},{1,5},{5,9},... | collective-permute-start | bytes 1572872 | tf_op jit(solution)/shard_map/ppermute | solution.py:307
  7.8 13.5 %collective-permute-start.1 = (bf16[512,512]{1,0:T(8,128)(2,1)S(1)}, bf16[512,512]{1,0:T(8,128)(2,1)}, u32[]{:S(2)}, u32[]{:S(2)}) collective-permute-start(bf16[512,512]{1,0:T(8,128)(2,1)S(1)} %get-tuple-element.72.refs_3_.refs_9_), channel_id=1, source_target_pairs={{4,0},{8,4},{12,8},{14,12},{10,14},{6,10},{2,6},{0,2},{5,1},{9,5},... | collective-permute-start | bytes 1572872 | tf_op jit(solution)/shard_map/ppermute | solution.py:307
  10.6 10.6 %collective-permute-start.2 = (bf16[96,2048]{1,0:T(8,128)(2,1)S(1)}, bf16[96,2048]{1,0:T(8,128)(2,1)S(1)}, u32[]{:S(2)}, u32[]{:S(2)}) collective-permute-start(bf16[96,2048]{1,0:T(8,128)(2,1)S(1)} %pick_columns.6), channel_id=1, source_target_pairs={{0,16},{16,0},{1,17},{17,1},{2,18},{18,2},{3,19},{19,3},{4,20},{20... | collective-permute-start | bytes 1179656 | tf_op jit(solution)/shard_map/ppermute | solution.py:328
  21.3 6.3 %collective-permute-start.6 = (bf16[640,2048]{1,0:T(8,128)(2,1)S(1)}, bf16[640,2048]{1,0:T(8,128)(2,1)}, u32[]{:S(2)}, u32[]{:S(2)}) collective-permute-start(bf16[640,2048]{1,0:T(8,128)(2,1)S(1)} %pick_columns.9.refs_1_), channel_id=1, source_target_pairs={{0,1},{1,0},{2,3},{3,2},{4,5},{5,4},{6,7},{7,6},{8,9},{9,8},{10,11... | collective-permute-start | bytes 7864328 | tf_op jit(solution)/shard_map/ppermute | solution.py:343
  23.5 26.7 %collective-permute-start.5 = (bf16[272,2048]{1,0:T(8,128)(2,1)}, bf16[272,2048]{1,0:T(8,128)(2,1)S(1)}, u32[]{:S(2)}, u32[]{:S(2)}) collective-permute-start(bf16[272,2048]{1,0:T(8,128)(2,1)} %copy-done.21), channel_id=1, source_target_pairs={{0,16},{16,0},{1,17},{17,1},{2,18},{18,2},{3,19},{19,3},{4,20},{20... | collective-permute-start | bytes 3342344 | tf_op jit(solution)/shard_map/ppermute | solution.py:341
  25.4 15.0 %collective-permute-start.3 = (bf16[512,512]{1,0:T(8,128)(2,1)}, bf16[512,512]{1,0:T(8,128)(2,1)S(1)}, u32[]{:S(2)}, u32[]{:S(2)}) collective-permute-start(bf16[512,512]{1,0:T(8,128)(2,1)} %collective-permute-done.refs_4_.refs_10_), channel_id=1, source_target_pairs={{0,4},{4,8},{8,12},{12,14},{14,10},{10,6},{6,2},{2,0},{1,5},{5,9},... | collective-permute-start | bytes 1572872 | tf_op jit(solution)/shard_map/ppermute | solution.py:307
  27.0 15.1 %collective-permute-start.4 = (bf16[512,512]{1,0:T(8,128)(2,1)}, bf16[512,512]{1,0:T(8,128)(2,1)S(1)}, u32[]{:S(2)}, u32[]{:S(2)}) collective-permute-start(bf16[512,512]{1,0:T(8,128)(2,1)} %collective-permute-done.1.refs_5_.refs_11_), channel_id=1, source_target_pairs={{4,0},{8,4},{12,8},{14,12},{10,14},{6,10},{2,6},{0,2},{5,1},{9,5},... | collective-permute-start | bytes 1572872 | tf_op jit(solution)/shard_map/ppermute | solution.py:307
  27.6 22.8 %collective-permute-start.8 = (bf16[512,512]{1,0:T(8,128)(2,1)}, bf16[512,512]{1,0:T(8,128)(2,1)S(1)}, u32[]{:S(2)}, u32[]{:S(2)}) collective-permute-start(bf16[512,512]{1,0:T(8,128)(2,1)} %copy-done.13), channel_id=1, source_target_pairs={{0,4},{4,8},{8,12},{12,14},{14,10},{10,6},{6,2},{2,0},{1,5},{5,9},... | collective-permute-start | bytes 1572872 | tf_op jit(solution)/shard_map/ppermute | solution.py:307
  29.2 22.5 %collective-permute-start.9 = (bf16[512,512]{1,0:T(8,128)(2,1)}, bf16[512,512]{1,0:T(8,128)(2,1)S(1)}, u32[]{:S(2)}, u32[]{:S(2)}) collective-permute-start(bf16[512,512]{1,0:T(8,128)(2,1)} %copy-done.13), channel_id=1, source_target_pairs={{4,0},{8,4},{12,8},{14,12},{10,14},{6,10},{2,6},{0,2},{5,1},{9,5},... | collective-permute-start | bytes 1572872 | tf_op jit(solution)/shard_map/ppermute | solution.py:307
  51.7 27.0 %collective-permute-start.12 = (bf16[272,2048]{1,0:T(8,128)(2,1)S(1)}, bf16[272,2048]{1,0:T(8,128)(2,1)S(1)}, u32[]{:S(2)}, u32[]{:S(2)}) collective-permute-start(bf16[272,2048]{1,0:T(8,128)(2,1)S(1)} %copy-done.20), channel_id=1, source_target_pairs={{0,16},{16,0},{1,17},{17,1},{2,18},{18,2},{3,19},{19,3},{4,20},{20... | collective-permute-start | bytes 3342344 | tf_op jit(solution)/shard_map/ppermute | solution.py:356
  52.2 14.8 %collective-permute-start.10 = (bf16[512,512]{1,0:T(8,128)(2,1)S(1)}, bf16[512,512]{1,0:T(8,128)(2,1)S(1)}, u32[]{:S(2)}, u32[]{:S(2)}) collective-permute-start(bf16[512,512]{1,0:T(8,128)(2,1)S(1)} %collective-permute-done.3.refs_6_.refs_12_), channel_id=1, source_target_pairs={{0,4},{4,8},{8,12},{12,14},{14,10},{10,6},{6,2},{2,0},{1,5},{5,9},... | collective-permute-start | bytes 1572872 | tf_op jit(solution)/shard_map/ppermute | solution.py:307
  53.8 14.8 %collective-permute-start.11 = (bf16[512,512]{1,0:T(8,128)(2,1)S(1)}, bf16[512,512]{1,0:T(8,128)(2,1)S(1)}, u32[]{:S(2)}, u32[]{:S(2)}) collective-permute-start(bf16[512,512]{1,0:T(8,128)(2,1)S(1)} %collective-permute-done.4.refs_7_.refs_13_), channel_id=1, source_target_pairs={{4,0},{8,4},{12,8},{14,12},{10,14},{6,10},{2,6},{0,2},{5,1},{9,5},... | collective-permute-start | bytes 1572872 | tf_op jit(solution)/shard_map/ppermute | solution.py:307
  54.5 24.2 %collective-permute-start.14 = (bf16[512,512]{1,0:T(8,128)(2,1)S(1)}, bf16[512,512]{1,0:T(8,128)(2,1)S(1)}, u32[]{:S(2)}, u32[]{:S(2)}) collective-permute-start(bf16[512,512]{1,0:T(8,128)(2,1)S(1)} %collective-permute-done.8.refs_4_.refs_10_), channel_id=1, source_target_pairs={{0,4},{4,8},{8,12},{12,14},{14,10},{10,6},{6,2},{2,0},{1,5},{5,9},... | collective-permute-start | bytes 1572872 | tf_op jit(solution)/shard_map/ppermute | solution.py:307
  56.0 22.8 %collective-permute-start.15 = (bf16[512,512]{1,0:T(8,128)(2,1)S(1)}, bf16[512,512]{1,0:T(8,128)(2,1)S(1)}, u32[]{:S(2)}, u32[]{:S(2)}) collective-permute-start(bf16[512,512]{1,0:T(8,128)(2,1)S(1)} %collective-permute-done.9.refs_5_.refs_11_), channel_id=1, source_target_pairs={{4,0},{8,4},{12,8},{14,12},{10,14},{6,10},{2,6},{0,2},{5,1},{9,5},... | collective-permute-start | bytes 1572872 | tf_op jit(solution)/shard_map/ppermute | solution.py:307
  80.3 11.3 %collective-permute-start.21 = (bf16[256,512]{1,0:T(8,128)(2,1)S(1)}, bf16[256,512]{1,0:T(8,128)(2,1)S(1)}, u32[]{:S(2)}, u32[]{:S(2)}) collective-permute-start(bf16[256,512]{1,0:T(8,128)(2,1)S(1)} %slice.48), channel_id=1, source_target_pairs={{0,4},{4,8},{8,12},{12,14},{14,10},{10,6},{6,2},{2,0},{1,5},{5,9},... | collective-permute-start | bytes 786440 | tf_op jit(solution)/shard_map/ppermute | solution.py:307
  82.0 9.7 %collective-permute-start.22 = (bf16[256,512]{1,0:T(8,128)(2,1)S(1)}, bf16[256,512]{1,0:T(8,128)(2,1)S(1)}, u32[]{:S(2)}, u32[]{:S(2)}) collective-permute-start(bf16[256,512]{1,0:T(8,128)(2,1)S(1)} %slice.49), channel_id=1, source_target_pairs={{4,0},{8,4},{12,8},{14,12},{10,14},{6,10},{2,6},{0,2},{5,1},{9,5},... | collective-permute-start | bytes 786440 | tf_op jit(solution)/shard_map/ppermute | solution.py:307
  84.8 6.9 %collective-permute-start.20 = (bf16[64,2048]{1,0:T(8,128)(2,1)S(1)}, bf16[64,2048]{1,0:T(8,128)(2,1)S(1)}, u32[]{:S(2)}, u32[]{:S(2)}) collective-permute-start(bf16[64,2048]{1,0:T(8,128)(2,1)S(1)} %constant_dynamic-update-slice_fusion.refs_7_), channel_id=1, source_target_pairs={{0,1},{1,0},{2,3},{3,2},{4,5},{5,4},{6,7},{7,6},{8,9},{9,8},{10,11... | collective-permute-start | bytes 786440 | tf_op jit(solution)/shard_map/ppermute | solution.py:374
  84.8 15.2 %collective-permute-start.17 = (bf16[512,512]{1,0:T(8,128)(2,1)S(1)}, bf16[512,512]{1,0:T(8,128)(2,1)S(1)}, u32[]{:S(2)}, u32[]{:S(2)}) collective-permute-start(bf16[512,512]{1,0:T(8,128)(2,1)S(1)} %collective-permute-done.14.refs_6_.refs_12_), channel_id=1, source_target_pairs={{0,4},{4,8},{8,12},{12,14},{14,10},{10,6},{6,2},{2,0},{1,5},{5,9},... | collective-permute-start | bytes 1572872 | tf_op jit(solution)/shard_map/ppermute | solution.py:307
  86.5 14.9 %collective-permute-start.18 = (bf16[512,512]{1,0:T(8,128)(2,1)S(1)}, bf16[512,512]{1,0:T(8,128)(2,1)S(1)}, u32[]{:S(2)}, u32[]{:S(2)}) collective-permute-start(bf16[512,512]{1,0:T(8,128)(2,1)S(1)} %collective-permute-done.15.refs_7_.refs_13_), channel_id=1, source_target_pairs={{4,0},{8,4},{12,8},{14,12},{10,14},{6,10},{2,6},{0,2},{5,1},{9,5},... | collective-permute-start | bytes 1572872 | tf_op jit(solution)/shard_map/ppermute | solution.py:307
  96.2 17.8 %collective-permute-start.26 = (f16[640,512]{1,0:T(8,128)(2,1)S(1)}, f16[640,512]{1,0:T(8,128)(2,1)S(1)}, u32[]{:S(2)}, u32[]{:S(2)}) collective-permute-start(f16[640,512]{1,0:T(8,128)(2,1)S(1)} %fusion.1), channel_id=1, source_target_pairs={{0,16},{16,0},{1,17},{17,1},{2,18},{18,2},{3,19},{19,3},{4,20},{20... | collective-permute-start | bytes 1966088 | tf_op jit(solution)/shard_map/ppermute | solution.py:385
  101.4 9.7 %collective-permute-start.23 = (bf16[256,512]{1,0:T(8,128)(2,1)S(1)}, bf16[256,512]{1,0:T(8,128)(2,1)S(1)}, u32[]{:S(2)}, u32[]{:S(2)}) collective-permute-start(bf16[256,512]{1,0:T(8,128)(2,1)S(1)} %slice.41), channel_id=1, source_target_pairs={{0,4},{4,8},{8,12},{12,14},{14,10},{10,6},{6,2},{2,0},{1,5},{5,9},... | collective-permute-start | bytes 786440 | tf_op jit(solution)/shard_map/ppermute | solution.py:307
  103.0 8.2 %collective-permute-start.24 = (bf16[256,512]{1,0:T(8,128)(2,1)S(1)}, bf16[256,512]{1,0:T(8,128)(2,1)S(1)}, u32[]{:S(2)}, u32[]{:S(2)}) collective-permute-start(bf16[256,512]{1,0:T(8,128)(2,1)S(1)} %slice.42), channel_id=1, source_target_pairs={{4,0},{8,4},{12,8},{14,12},{10,14},{6,10},{2,6},{0,2},{5,1},{9,5},... | collective-permute-start | bytes 786440 | tf_op jit(solution)/shard_map/ppermute | solution.py:307
  117.4 15.7 %collective-permute-start.27 = (f16[640,512]{1,0:T(8,128)(2,1)}, f16[640,512]{1,0:T(8,128)(2,1)}, u32[]{:S(2)}, u32[]{:S(2)}) collective-permute-start(f16[640,512]{1,0:T(8,128)(2,1)} %fusion), channel_id=1, source_target_pairs={{0,16},{16,0},{1,17},{17,1},{2,18},{18,2},{3,19},{19,3},{4,20},{20... | collective-permute-start | bytes 1966088 | tf_op jit(solution)/shard_map/ppermute | solution.py:397
  119.1 12.8 %all-to-all-start = ((bf16[8,3,5120]{2,1,0:T(4,128)(2,1)}), bf16[8,3,5120]{2,1,0:T(4,128)(2,1)}, u32[]{:S(2)}, u32[]{:S(2)}) async-start(bf16[8,3,5120]{2,1,0:T(4,128)(2,1)} %bitcast.38), calls=%async_computation | async-start | bytes 655360 | tf_op jit(solution)/shard_map/all_to_all | solution.py:404
  (42 other events, 312.4 us)

commit v11 on v10

--- a/solution.py
+++ b/solution.py
@@ -349,10 +349,13 @@
     )
     angles, new_angles = angle_table(position), angle_table(new_position)
     tables = (angles, new_angles, key_info, query_info)
-    got[1], tables, places, ring[1][-1] = fence_with(0, got[1], tables, places, ring[1][-1])
-
     own_hidden = [(kept, kept_other)]
-    early = row_count - 3
+    first, early = 5, row_count - 3
+    held = [project(0, own_hidden, None, 0, first)]
+    got[1], tables, places, held, ring[1][-1] = fence_with(
+        0, got[1], tables, places, held, ring[1][-1]
+    )
+
     got.append(lax.ppermute(sent[2], "groups", partners))
     step(0)
     got_other.append(lax.ppermute(got[1], "tensor", cores))
@@ -362,7 +365,8 @@
         (ring[1][-1],) = fence_with(0, ring[1][-1])
         step(0)
         step(1)
-    held = [project(0, own_hidden, None, 0, early)]
+    held[0] = project(0, own_hidden, held[0], first, row_count - 1)
+    held.append(project(1, own_hidden, None, 0, early - 2))
     ends[0] = halved(ring[0][-1])
     got[2], new_sent, held, places, ring[1][-1], ends[0] = fence_with(
         0, got[2], new_sent, held, places, ring[1][-1], ends[0]
@@ -375,10 +379,8 @@
     (got_other[2],) = fence_with(1, got_other[2])
     step(1)
     away_hidden = list(zip(got, got_other)) + [(new_kept, new_other)]
-    held.append(project(1, own_hidden, None, 0, early))
-    places, held = fence(places, held)
     away = project(0, away_hidden, None, 0, row_count)
-    away, places = fence(homeward(away), places)
+    away, places, held = fence(homeward(away), places, held)
     (places,) = fence_with(1, places)
     ends[1] = halved(ring[1][-1])
     step(1)
@@ -389,7 +391,8 @@
     new_own.append(away[2])
     new_away.append(away[1])
     new_back = lax.ppermute(jnp.concatenate(new_away, 1), "groups", partners)
-    held[0] = project(0, own_hidden, held[0], early, row_count)
+    held[0] = project(0, own_hidden, held[0], row_count - 1, row_count)
+    held[1] = project(1, own_hidden, held[1], early - 2, early)
     queries = jnp.swapaxes(queries, 0, 1).reshape(count, -1)
     held, queries, places, away, new_back, homed[0] = fence(
         held, queries, places, away, new_back, homed[0]

time: 152 us -> 157 us (1.033)
  Pallas kernels: 29.8 us -> 34.4 us
  waiting for transfers between devices: 52.5 us -> 49.5 us
  starting transfers between devices: 30.9 us -> 33.7 us
    ppermute x1, waiting for transfers between devices: 10 us -> 2.92 us  [body(): got.append(lax.ppermute(sent[2], 'groups', partners))]
    pallas_call x7 -> x9, Pallas kernels: 22.3 us -> 26.9 us  [products(): pl.pallas_call(functools.partial(product_kernel, depths, len(hidden), bas...]
    ppermute x8, waiting for transfers between devices: 17.6 us -> 21.1 us  [step(): lax.ppermute(pair[0], 'rows', onward)]
  transfers between devices with their start and end apart: 29 -> 29, of which waited for: 16 -> 16; matrix products, arithmetic and copies ran while one was open for 5% -> 5% of each run, Pallas kernels for 16% -> 19%
where the time goes in v11:
time: 157 us; the launch traced here: 156 us
  waiting for transfers between devices  49.5 us (32%)
  Pallas kernels  34.4 us (22%)
  starting transfers between devices  33.7 us (21%)
  local copies, waits for them, and re-layouts  18.3 us (12%)
  blocking collectives  13 us (8%)
  other arithmetic  6.32 us (4%)
    pallas_call x9, Pallas kernels, products(): pl.pallas_call(functools.partial(product_kernel, depths, len(hidden), bas...  26.9 us
    ppermute x8, waiting for transfers between devices, step(): lax.ppermute(pair[0], 'rows', onward)  21.1 us
    unnamed x73, local copies, waits for them, and re-layouts  14.5 us
    ppermute x8, starting transfers between devices, step(): lax.ppermute(pair[0], 'rows', onward)  14.4 us
    all_to_all x1, blocking collectives, body(): lax.all_to_all(attended, 'rows', split_axis=0, concat_axis=0, tiled=True)  13 us
    ppermute x1, waiting for transfers between devices, body(): got.append(lax.ppermute(sent[1], 'groups', partners))  7.57 us
    ppermute x8, waiting for transfers between devices, step(): lax.ppermute(pair[1], 'rows', back)  7.27 us
    all_to_all x1, starting transfers between devices, body(): lax.all_to_all(moved, 'rows', split_axis=0, concat_axis=0, tiled=True)  4.09 us
  transfers between devices with their start and end apart: 29, of which 16 were waited for; matrix products, arithmetic and copies ran while one was open for 5% of the time, Pallas kernels for 19%

profile of v11, /device:TPU:0, one launch (start us, length us, event | category | flops | bytes accessed | tf_op | source)
XLA Modules:
  0.0 155.8 jit_solution(13063557021376155735)
XLA Ops:
  1.6 2.3 %own_half.1 = (bf16[512,512]{1,0:T(8,128)(2,1)S(1)}, bf16[512,512]{1,0:T(8,128)(2,1)S(1)}) custom-call(s32[1]{0:T(128)} %bitcast.side_ref, bf16[1024,2,512]{2,1,0:T(2,128)(2,1)S(1)} %copy-done.17), custom_call_target="tpu_custom_call" | custom-call | bytes 4194304 | tf_op jit(solution)/shard_map/own_half/pallas_call | solution.py:127
  4.7 3.0 %collective-permute-start = (bf16[512,512]{1,0:T(8,128)(2,1)S(1)}, bf16[512,512]{1,0:T(8,128)(2,1)}, u32[]{:S(2)}, u32[]{:S(2)}) collective-permute-start(bf16[512,512]{1,0:T(8,128)(2,1)S(1)} %get-tuple-element.73.refs_3_.refs_9_), channel_id=1, source_target_pairs={{0,4},{4,8},{8,12},{12,14},{14,10},{10,6},{6,2},{2,0},{1,5},{5,9},... | collective-permute-start | bytes 1572872 | tf_op jit(solution)/shard_map/ppermute | solution.py:307
  7.8 2.5 %copy-done = bf16[640,4096]{1,0:T(8,128)(2,1)S(1)} copy-done((bf16[640,4096]{1,0:T(8,128)(2,1)S(1)}, bf16[640,4096]{1,0:T(8,128)(2,1)}, u32[]{:S(2)}) %copy-start) | copy-done | bytes 5242904
  10.6 2.0 %collective-permute-start.2 = (bf16[96,2048]{1,0:T(8,128)(2,1)S(1)}, bf16[96,2048]{1,0:T(8,128)(2,1)S(1)}, u32[]{:S(2)}, u32[]{:S(2)}) collective-permute-start(bf16[96,2048]{1,0:T(8,128)(2,1)S(1)} %pick_columns.6), channel_id=1, source_target_pairs={{0,16},{16,0},{1,17},{17,1},{2,18},{18,2},{3,19},{19,3},{4,20},{20... | collective-permute-start | bytes 1179656 | tf_op jit(solution)/shard_map/ppermute | solution.py:328
  17.4 3.8 %collective-permute-done.2.refs_1_ = bf16[96,2048]{1,0:T(8,128)(2,1)S(1)} collective-permute-done((bf16[96,2048]{1,0:T(8,128)(2,1)S(1)}, bf16[96,2048]{1,0:T(8,128)(2,1)S(1)}, u32[]{:S(2)}, u32[]{:S(2)}) %collective-permute-start.2) | collective-permute-done | bytes 393248 | tf_op jit(solution)/shard_map/ppermute | solution.py:328
  31.8 6.4 %collective-permute-done.3.refs_6_.refs_12_ = bf16[512,512]{1,0:T(8,128)(2,1)} collective-permute-done((bf16[512,512]{1,0:T(8,128)(2,1)}, bf16[512,512]{1,0:T(8,128)(2,1)}, u32[]{:S(2)}, u32[]{:S(2)}) %collective-permute-start.3) | collective-permute-done | bytes 524320 | tf_op jit(solution)/shard_map/ppermute | solution.py:307
  40.0 4.2 %products.9.refs_5_ = f32[640,512]{1,0:T(8,128)S(1)} custom-call(s32[8]{0:T(128)S(1)} %fusion.3.refs_0_, bf16[640,2048]{1,0:T(8,128)(2,1)S(1)} %pick_columns.9.refs_1_, bf16[640,2048]{1,0:T(8,128)(2,1)} %collective-permute-done.6.refs_2_, bf16[512,512]{1,0:T(8,128)(2,1)S(1)} %copy-done.16, bf16[512,512]{1,0:T(8,128)(2,1)} %collective-permute-done.refs_4_.refs_10_, ...), custom_call_target="tpu_custom_call" | custom-call | flops 1677721600 | bytes 7208960 | tf_op jit(solution)/shard_map/products/pallas_call | solution.py:239
  44.2 7.6 %collective-permute-done.5.refs_3_ = bf16[272,2048]{1,0:T(8,128)(2,1)S(1)} collective-permute-done((bf16[272,2048]{1,0:T(8,128)(2,1)}, bf16[272,2048]{1,0:T(8,128)(2,1)S(1)}, u32[]{:S(2)}, u32[]{:S(2)}) %collective-permute-start.5) | collective-permute-done | bytes 1114144 | tf_op jit(solution)/shard_map/ppermute | solution.py:341
  57.5 10.9 %collective-permute-done.10.refs_3_.refs_14_ = bf16[512,512]{1,0:T(8,128)(2,1)S(1)} collective-permute-done((bf16[512,512]{1,0:T(8,128)(2,1)}, bf16[512,512]{1,0:T(8,128)(2,1)S(1)}, u32[]{:S(2)}, u32[]{:S(2)}) %collective-permute-start.10) | collective-permute-done | bytes 524320 | tf_op jit(solution)/shard_map/ppermute | solution.py:307
  70.1 2.7 %products.10.refs_5_ = f32[640,512]{1,0:T(8,128)S(1)} custom-call(s32[8]{0:T(128)S(1)} %fusion.3.refs_0_, bf16[640,2048]{1,0:T(8,128)(2,1)S(1)} %pick_columns.9.refs_1_, bf16[640,2048]{1,0:T(8,128)(2,1)} %collective-permute-done.6.refs_2_, bf16[512,512]{1,0:T(8,128)(2,1)S(1)} %collective-permute-done.10.refs_3_.refs_14_, ...), custom_call_target="tpu_custom_call" | custom-call | flops 671088640 | bytes 3670016 | tf_op jit(solution)/shard_map/products/pallas_call | solution.py:239
  72.8 3.0 %products.11.refs_5_ = f32[640,512]{1,0:T(8,128)S(1)} custom-call(s32[8]{0:T(128)S(1)} %fusion.3.refs_0_, bf16[640,2048]{1,0:T(8,128)(2,1)S(1)} %pick_columns.9.refs_1_, bf16[640,2048]{1,0:T(8,128)(2,1)} %collective-permute-done.6.refs_2_, bf16[512,512]{1,0:T(8,128)(2,1)S(1)} %copy-done.14, bf16[512,512]{1,0:T(8,128)(2,1)S(1)} %collective-permute-done.8.refs_4_.refs_10_, ...), custom_call_target="tpu_custom_call" | custom-call | flops 1006632960 | bytes 4849664 | tf_op jit(solution)/shard_map/products/pallas_call | solution.py:239
  75.8 2.9 %collective-permute-done.12.refs_5_ = bf16[272,2048]{1,0:T(8,128)(2,1)S(1)} collective-permute-done((bf16[272,2048]{1,0:T(8,128)(2,1)S(1)}, bf16[272,2048]{1,0:T(8,128)(2,1)S(1)}, u32[]{:S(2)}, u32[]{:S(2)}) %collective-permute-start.12) | collective-permute-done | bytes 1114144 | tf_op jit(solution)/shard_map/ppermute | solution.py:359
  82.8 3.3 %collective-permute-done.19 = bf16[32,2048]{1,0:T(8,128)(2,1)S(1)} collective-permute-done((bf16[32,2048]{1,0:T(8,128)(2,1)S(1)}, bf16[32,2048]{1,0:T(8,128)(2,1)S(1)}, u32[]{:S(2)}, u32[]{:S(2)}) %collective-permute-start.19) | collective-permute-done | bytes 131104 | tf_op jit(solution)/shard_map/ppermute | solution.py:377
  90.6 4.7 %products.12 = f32[704,512]{1,0:T(8,128)S(1)} custom-call(s32[8]{0:T(128)S(1)} %fusion.3.refs_0_, bf16[96,2048]{1,0:T(8,128)(2,1)S(1)} %collective-permute-done.2.refs_1_, bf16[96,2048]{1,0:T(8,128)(2,1)S(1)} %collective-permute-done.7.refs_2_, bf16[272,2048]{1,0:T(8,128)(2,1)S(1)} %collective-permute-done.5.refs_3_, ...), custom_call_target="tpu_custom_call" | custom-call | flops 2952790016 | bytes 11403264 | tf_op jit(solution)/shard_map/products/pallas_call | solution.py:239
  95.4 2.4 %collective-permute-start.26 = (f16[640,512]{1,0:T(8,128)(2,1)S(1)}, f16[640,512]{1,0:T(8,128)(2,1)S(1)}, u32[]{:S(2)}, u32[]{:S(2)}) collective-permute-start(f16[640,512]{1,0:T(8,128)(2,1)S(1)} %fusion.1), channel_id=1, source_target_pairs={{0,16},{16,0},{1,17},{17,1},{2,18},{18,2},{3,19},{19,3},{4,20},{20... | collective-permute-start | bytes 1966088 | tf_op jit(solution)/shard_map/ppermute | solution.py:387
  97.8 2.7 %collective-permute-done.17.refs_14_.refs_3_ = bf16[512,512]{1,0:T(8,128)(2,1)S(1)} collective-permute-done((bf16[512,512]{1,0:T(8,128)(2,1)S(1)}, bf16[512,512]{1,0:T(8,128)(2,1)S(1)}, u32[]{:S(2)}, u32[]{:S(2)}) %collective-permute-start.17) | collective-permute-done | bytes 524320 | tf_op jit(solution)/shard_map/ppermute | solution.py:307
  104.2 2.6 %products.14.refs_7_ = f32[640,512]{1,0:T(8,128)S(1)} custom-call(s32[8]{0:T(128)S(1)} %fusion.3.refs_0_, bf16[640,2048]{1,0:T(8,128)(2,1)S(1)} %pick_columns.9.refs_1_, bf16[640,2048]{1,0:T(8,128)(2,1)} %collective-permute-done.6.refs_2_, bf16[512,512]{1,0:T(8,128)(2,1)S(1)} %collective-permute-done.14.refs_3_.refs_12_, ...), custom_call_target="tpu_custom_call" | custom-call | flops 671088640 | bytes 3670016 | tf_op jit(solution)/shard_map/products/pallas_call | solution.py:239
  107.9 2.3 %products.13.refs_0_ = f32[640,512]{1,0:T(8,128)S(1)} custom-call(s32[8]{0:T(128)S(1)} %fusion.3.refs_0_, bf16[640,2048]{1,0:T(8,128)(2,1)S(1)} %pick_columns.9.refs_1_, bf16[640,2048]{1,0:T(8,128)(2,1)} %collective-permute-done.6.refs_2_, bf16[256,512]{1,0:T(8,128)(2,1)S(1)} %collective-permute-done.21.refs_16_.refs_3_, ...), custom_call_target="tpu_custom_call" | custom-call | flops 335544320 | bytes 2490368 | tf_op jit(solution)/shard_map/products/pallas_call | solution.py:239
  111.3 3.3 %products.15.refs_11_ = f32[704,512]{1,0:T(8,128)S(1)} custom-call(s32[8]{0:T(128)S(1)} %fusion.3.refs_0_, bf16[96,2048]{1,0:T(8,128)(2,1)S(1)} %collective-permute-done.2.refs_1_, bf16[96,2048]{1,0:T(8,128)(2,1)S(1)} %collective-permute-done.7.refs_2_, bf16[272,2048]{1,0:T(8,128)(2,1)S(1)} %collective-permute-done.5.refs_3_, ...), custom_call_target="tpu_custom_call" | custom-call | flops 2583691264 | bytes 10158080 | tf_op jit(solution)/shard_map/products/pallas_call | solution.py:239
  118.4 2.5 %collective-permute-done.25.refs_1_ = f32[32,1024]{1,0:T(8,128)S(1)} collective-permute-done((f32[32,1024]{1,0:T(8,128)S(1)}, f32[32,1024]{1,0:T(8,128)S(1)}, u32[]{:S(2)}, u32[]{:S(2)}) %collective-permute-start.25) | collective-permute-done | bytes 131104 | tf_op jit(solution)/shard_map/ppermute | solution.py:393
  123.4 4.1 %all-to-all-start = ((bf16[8,3,5120]{2,1,0:T(4,128)(2,1)}), bf16[8,3,5120]{2,1,0:T(4,128)(2,1)}, u32[]{:S(2)}, u32[]{:S(2)}) async-start(bf16[8,3,5120]{2,1,0:T(4,128)(2,1)} %bitcast.38), calls=%async_computation | async-start | bytes 655360 | tf_op jit(solution)/shard_map/all_to_all | solution.py:407
  130.9 3.0 %products.17.refs_1_ = f32[640,512]{1,0:T(8,128)S(1)} custom-call(s32[8]{0:T(128)S(1)} %fusion.3.refs_0_, bf16[640,2048]{1,0:T(8,128)(2,1)S(1)} %pick_columns.9.refs_1_, bf16[640,2048]{1,0:T(8,128)(2,1)} %collective-permute-done.6.refs_2_, bf16[512,512]{1,0:T(8,128)(2,1)S(1)} %copy-done.10, bf16[512,512]{1,0:T(8,128)(2,1)S(1)} %copy-done.12, ...), custom_call_target="tpu_custom_call" | custom-call | flops 1006632960 | bytes 4849664 | tf_op jit(solution)/shard_map/products/pallas_call | solution.py:239
  139.0 2.9 %rotate_attend.1 = bf16[24,4096]{1,0:T(8,128)(2,1)S(1)} custom-call(f32[640,512]{1,0:T(8,128)S(1)} %copy-done.8, f32[640,512]{1,0:T(8,128)S(1)} %copy-done.6, f32[640,512]{1,0:T(8,128)S(1)} %convert_multiply_fusion.1.refs_2_, f32[640,512]{1,0:T(8,128)S(1)} %convert_multiply_fusion.refs_3_, f32[640,128]{1,0:T(8,128)S(1)} %copy-done.18, ...), custom_call_target="tpu_custom_call" | custom-call | flops 251658240 | bytes 5636096 | tf_op jit(solution)/shard_map/rotate_attend/pallas_call | solution.py:100
  142.1 13.0 %all_to_all.10 = bf16[8,3,4096]{2,1,0:T(4,128)(2,1)S(1)} all-to-all(bf16[8,3,4096]{2,1,0:T(4,128)(2,1)S(1)} %bitcast.39), channel_id=1, replica_groups=mesh['groups'=2,'rows'=8,'tensor'=2] {'rows'}, dimensions={0} | all-to-all | bytes 393216 | tf_op jit(solution)/shard_map/all_to_all | solution.py:415
  (182 shorter events, 57.2 us)
Async XLA Ops:
  4.7 16.5 %collective-permute-start = (bf16[512,512]{1,0:T(8,128)(2,1)S(1)}, bf16[512,512]{1,0:T(8,128)(2,1)}, u32[]{:S(2)}, u32[]{:S(2)}) collective-permute-start(bf16[512,512]{1,0:T(8,128)(2,1)S(1)} %get-tuple-element.73.refs_3_.refs_9_), channel_id=1, source_target_pairs={{0,4},{4,8},{8,12},{12,14},{14,10},{10,6},{6,2},{2,0},{1,5},{5,9},... | collective-permute-start | bytes 1572872 | tf_op jit(solution)/shard_map/ppermute | solution.py:307
  7.8 13.5 %collective-permute-start.1 = (bf16[512,512]{1,0:T(8,128)(2,1)S(1)}, bf16[512,512]{1,0:T(8,128)(2,1)}, u32[]{:S(2)}, u32[]{:S(2)}) collective-permute-start(bf16[512,512]{1,0:T(8,128)(2,1)S(1)} %get-tuple-element.73.refs_3_.refs_9_), channel_id=1, source_target_pairs={{4,0},{8,4},{12,8},{14,12},{10,14},{6,10},{2,6},{0,2},{5,1},{9,5},... | collective-permute-start | bytes 1572872 | tf_op jit(solution)/shard_map/ppermute | solution.py:307
  10.6 10.6 %collective-permute-start.2 = (bf16[96,2048]{1,0:T(8,128)(2,1)S(1)}, bf16[96,2048]{1,0:T(8,128)(2,1)S(1)}, u32[]{:S(2)}, u32[]{:S(2)}) collective-permute-start(bf16[96,2048]{1,0:T(8,128)(2,1)S(1)} %pick_columns.6), channel_id=1, source_target_pairs={{0,16},{16,0},{1,17},{17,1},{2,18},{18,2},{3,19},{19,3},{4,20},{20... | collective-permute-start | bytes 1179656 | tf_op jit(solution)/shard_map/ppermute | solution.py:328
  21.3 6.3 %collective-permute-start.6 = (bf16[640,2048]{1,0:T(8,128)(2,1)S(1)}, bf16[640,2048]{1,0:T(8,128)(2,1)}, u32[]{:S(2)}, u32[]{:S(2)}) collective-permute-start(bf16[640,2048]{1,0:T(8,128)(2,1)S(1)} %pick_columns.9.refs_1_), channel_id=1, source_target_pairs={{0,1},{1,0},{2,3},{3,2},{4,5},{5,4},{6,7},{7,6},{8,9},{9,8},{10,11... | collective-permute-start | bytes 7864328 | tf_op jit(solution)/shard_map/ppermute | solution.py:343
  23.1 15.1 %collective-permute-start.3 = (bf16[512,512]{1,0:T(8,128)(2,1)}, bf16[512,512]{1,0:T(8,128)(2,1)}, u32[]{:S(2)}, u32[]{:S(2)}) collective-permute-start(bf16[512,512]{1,0:T(8,128)(2,1)} %collective-permute-done.refs_4_.refs_10_), channel_id=1, source_target_pairs={{0,4},{4,8},{8,12},{12,14},{14,10},{10,6},{6,2},{2,0},{1,5},{5,9},... | collective-permute-start | bytes 1572872 | tf_op jit(solution)/shard_map/ppermute | solution.py:307
  24.8 15.1 %collective-permute-start.4 = (bf16[512,512]{1,0:T(8,128)(2,1)}, bf16[512,512]{1,0:T(8,128)(2,1)}, u32[]{:S(2)}, u32[]{:S(2)}) collective-permute-start(bf16[512,512]{1,0:T(8,128)(2,1)} %collective-permute-done.1.refs_5_.refs_11_), channel_id=1, source_target_pairs={{4,0},{8,4},{12,8},{14,12},{10,14},{6,10},{2,6},{0,2},{5,1},{9,5},... | collective-permute-start | bytes 1572872 | tf_op jit(solution)/shard_map/ppermute | solution.py:307
  25.5 26.2 %collective-permute-start.5 = (bf16[272,2048]{1,0:T(8,128)(2,1)}, bf16[272,2048]{1,0:T(8,128)(2,1)S(1)}, u32[]{:S(2)}, u32[]{:S(2)}) collective-permute-start(bf16[272,2048]{1,0:T(8,128)(2,1)} %copy-done.21), channel_id=1, source_target_pairs={{0,16},{16,0},{1,17},{17,1},{2,18},{18,2},{3,19},{19,3},{4,20},{20... | collective-permute-start | bytes 3342344 | tf_op jit(solution)/shard_map/ppermute | solution.py:341
  27.6 24.1 %collective-permute-start.8 = (bf16[512,512]{1,0:T(8,128)(2,1)}, bf16[512,512]{1,0:T(8,128)(2,1)S(1)}, u32[]{:S(2)}, u32[]{:S(2)}) collective-permute-start(bf16[512,512]{1,0:T(8,128)(2,1)} %copy-done.13), channel_id=1, source_target_pairs={{0,4},{4,8},{8,12},{12,14},{14,10},{10,6},{6,2},{2,0},{1,5},{5,9},... | collective-permute-start | bytes 1572872 | tf_op jit(solution)/shard_map/ppermute | solution.py:307
  29.2 22.5 %collective-permute-start.9 = (bf16[512,512]{1,0:T(8,128)(2,1)}, bf16[512,512]{1,0:T(8,128)(2,1)S(1)}, u32[]{:S(2)}, u32[]{:S(2)}) collective-permute-start(bf16[512,512]{1,0:T(8,128)(2,1)} %copy-done.13), channel_id=1, source_target_pairs={{4,0},{8,4},{12,8},{14,12},{10,14},{6,10},{2,6},{0,2},{5,1},{9,5},... | collective-permute-start | bytes 1572872 | tf_op jit(solution)/shard_map/ppermute | solution.py:307
  51.8 27.0 %collective-permute-start.12 = (bf16[272,2048]{1,0:T(8,128)(2,1)S(1)}, bf16[272,2048]{1,0:T(8,128)(2,1)S(1)}, u32[]{:S(2)}, u32[]{:S(2)}) collective-permute-start(bf16[272,2048]{1,0:T(8,128)(2,1)S(1)} %copy-done.20), channel_id=1, source_target_pairs={{0,16},{16,0},{1,17},{17,1},{2,18},{18,2},{3,19},{19,3},{4,20},{20... | collective-permute-start | bytes 3342344 | tf_op jit(solution)/shard_map/ppermute | solution.py:359
  53.5 15.0 %collective-permute-start.10 = (bf16[512,512]{1,0:T(8,128)(2,1)}, bf16[512,512]{1,0:T(8,128)(2,1)S(1)}, u32[]{:S(2)}, u32[]{:S(2)}) collective-permute-start(bf16[512,512]{1,0:T(8,128)(2,1)} %collective-permute-done.3.refs_6_.refs_12_), channel_id=1, source_target_pairs={{0,4},{4,8},{8,12},{12,14},{14,10},{10,6},{6,2},{2,0},{1,5},{5,9},... | collective-permute-start | bytes 1572872 | tf_op jit(solution)/shard_map/ppermute | solution.py:307
  55.0 15.0 %collective-permute-start.11 = (bf16[512,512]{1,0:T(8,128)(2,1)}, bf16[512,512]{1,0:T(8,128)(2,1)S(1)}, u32[]{:S(2)}, u32[]{:S(2)}) collective-permute-start(bf16[512,512]{1,0:T(8,128)(2,1)} %collective-permute-done.4.refs_7_.refs_13_), channel_id=1, source_target_pairs={{4,0},{8,4},{12,8},{14,12},{10,14},{6,10},{2,6},{0,2},{5,1},{9,5},... | collective-permute-start | bytes 1572872 | tf_op jit(solution)/shard_map/ppermute | solution.py:307
  55.5 23.4 %collective-permute-start.14 = (bf16[512,512]{1,0:T(8,128)(2,1)S(1)}, bf16[512,512]{1,0:T(8,128)(2,1)S(1)}, u32[]{:S(2)}, u32[]{:S(2)}) collective-permute-start(bf16[512,512]{1,0:T(8,128)(2,1)S(1)} %collective-permute-done.8.refs_4_.refs_10_), channel_id=1, source_target_pairs={{0,4},{4,8},{8,12},{12,14},{14,10},{10,6},{6,2},{2,0},{1,5},{5,9},... | collective-permute-start | bytes 1572872 | tf_op jit(solution)/shard_map/ppermute | solution.py:307
  57.1 23.1 %collective-permute-start.15 = (bf16[512,512]{1,0:T(8,128)(2,1)S(1)}, bf16[512,512]{1,0:T(8,128)(2,1)S(1)}, u32[]{:S(2)}, u32[]{:S(2)}) collective-permute-start(bf16[512,512]{1,0:T(8,128)(2,1)S(1)} %collective-permute-done.9.refs_5_.refs_11_), channel_id=1, source_target_pairs={{4,0},{8,4},{12,8},{14,12},{10,14},{6,10},{2,6},{0,2},{5,1},{9,5},... | collective-permute-start | bytes 1572872 | tf_op jit(solution)/shard_map/ppermute | solution.py:307
  80.2 6.0 %collective-permute-start.16 = (bf16[272,2048]{1,0:T(8,128)(2,1)S(1)}, bf16[272,2048]{1,0:T(8,128)(2,1)S(1)}, u32[]{:S(2)}, u32[]{:S(2)}) collective-permute-start(bf16[272,2048]{1,0:T(8,128)(2,1)S(1)} %collective-permute-done.12.refs_5_), channel_id=1, source_target_pairs={{0,1},{1,0},{2,3},{3,2},{4,5},{5,4},{6,7},{7,6},{8,9},{9,8},{10,11... | collective-permute-start | bytes 3342344 | tf_op jit(solution)/shard_map/ppermute | solution.py:376
  80.8 8.5 %collective-permute-start.21 = (bf16[256,512]{1,0:T(8,128)(2,1)S(1)}, bf16[256,512]{1,0:T(8,128)(2,1)S(1)}, u32[]{:S(2)}, u32[]{:S(2)}) collective-permute-start(bf16[256,512]{1,0:T(8,128)(2,1)S(1)} %slice.48), channel_id=1, source_target_pairs={{0,4},{4,8},{8,12},{12,14},{14,10},{10,6},{6,2},{2,0},{1,5},{5,9},... | collective-permute-start | bytes 786440 | tf_op jit(solution)/shard_map/ppermute | solution.py:307
  82.4 8.2 %collective-permute-start.22 = (bf16[256,512]{1,0:T(8,128)(2,1)S(1)}, bf16[256,512]{1,0:T(8,128)(2,1)S(1)}, u32[]{:S(2)}, u32[]{:S(2)}) collective-permute-start(bf16[256,512]{1,0:T(8,128)(2,1)S(1)} %slice.49), channel_id=1, source_target_pairs={{4,0},{8,4},{12,8},{14,12},{10,14},{6,10},{2,6},{0,2},{5,1},{9,5},... | collective-permute-start | bytes 786440 | tf_op jit(solution)/shard_map/ppermute | solution.py:307
  86.2 14.3 %collective-permute-start.17 = (bf16[512,512]{1,0:T(8,128)(2,1)S(1)}, bf16[512,512]{1,0:T(8,128)(2,1)S(1)}, u32[]{:S(2)}, u32[]{:S(2)}) collective-permute-start(bf16[512,512]{1,0:T(8,128)(2,1)S(1)} %collective-permute-done.14.refs_3_.refs_12_), channel_id=1, source_target_pairs={{0,4},{4,8},{8,12},{12,14},{14,10},{10,6},{6,2},{2,0},{1,5},{5,9},... | collective-permute-start | bytes 1572872 | tf_op jit(solution)/shard_map/ppermute | solution.py:307
  87.9 14.0 %collective-permute-start.18 = (bf16[512,512]{1,0:T(8,128)(2,1)S(1)}, bf16[512,512]{1,0:T(8,128)(2,1)S(1)}, u32[]{:S(2)}, u32[]{:S(2)}) collective-permute-start(bf16[512,512]{1,0:T(8,128)(2,1)S(1)} %collective-permute-done.15.refs_4_.refs_13_), channel_id=1, source_target_pairs={{4,0},{8,4},{12,8},{14,12},{10,14},{6,10},{2,6},{0,2},{5,1},{9,5},... | collective-permute-start | bytes 1572872 | tf_op jit(solution)/shard_map/ppermute | solution.py:307
  95.4 22.9 %collective-permute-start.26 = (f16[640,512]{1,0:T(8,128)(2,1)S(1)}, f16[640,512]{1,0:T(8,128)(2,1)S(1)}, u32[]{:S(2)}, u32[]{:S(2)}) collective-permute-start(f16[640,512]{1,0:T(8,128)(2,1)S(1)} %fusion.1), channel_id=1, source_target_pairs={{0,16},{16,0},{1,17},{17,1},{2,18},{18,2},{3,19},{19,3},{4,20},{20... | collective-permute-start | bytes 1966088 | tf_op jit(solution)/shard_map/ppermute | solution.py:387
  101.9 12.7 %collective-permute-start.23 = (bf16[256,512]{1,0:T(8,128)(2,1)S(1)}, bf16[256,512]{1,0:T(8,128)(2,1)S(1)}, u32[]{:S(2)}, u32[]{:S(2)}) collective-permute-start(bf16[256,512]{1,0:T(8,128)(2,1)S(1)} %slice.41), channel_id=1, source_target_pairs={{0,4},{4,8},{8,12},{12,14},{14,10},{10,6},{6,2},{2,0},{1,5},{5,9},... | collective-permute-start | bytes 786440 | tf_op jit(solution)/shard_map/ppermute | solution.py:307
  103.5 11.1 %collective-permute-start.24 = (bf16[256,512]{1,0:T(8,128)(2,1)S(1)}, bf16[256,512]{1,0:T(8,128)(2,1)S(1)}, u32[]{:S(2)}, u32[]{:S(2)}) collective-permute-start(bf16[256,512]{1,0:T(8,128)(2,1)S(1)} %slice.42), channel_id=1, source_target_pairs={{4,0},{8,4},{12,8},{14,12},{10,14},{6,10},{2,6},{0,2},{5,1},{9,5},... | collective-permute-start | bytes 786440 | tf_op jit(solution)/shard_map/ppermute | solution.py:307
  120.9 16.6 %collective-permute-start.27 = (f16[640,512]{1,0:T(8,128)(2,1)}, f16[640,512]{1,0:T(8,128)(2,1)}, u32[]{:S(2)}, u32[]{:S(2)}) collective-permute-start(f16[640,512]{1,0:T(8,128)(2,1)} %fusion), channel_id=1, source_target_pairs={{0,16},{16,0},{1,17},{17,1},{2,18},{18,2},{3,19},{19,3},{4,20},{20... | collective-permute-start | bytes 1966088 | tf_op jit(solution)/shard_map/ppermute | solution.py:400
  123.4 12.8 %all-to-all-start = ((bf16[8,3,5120]{2,1,0:T(4,128)(2,1)}), bf16[8,3,5120]{2,1,0:T(4,128)(2,1)}, u32[]{:S(2)}, u32[]{:S(2)}) async-start(bf16[8,3,5120]{2,1,0:T(4,128)(2,1)} %bitcast.38), calls=%async_computation | async-start | bytes 655360 | tf_op jit(solution)/shard_map/all_to_all | solution.py:407
  (42 other events, 193.3 us)

commit v12 on v11

--- a/solution.py
+++ b/solution.py
@@ -13,6 +13,7 @@
 CHUNKS = 2
 MOST_SHARDS = 8
 VMEM_BYTES = 20 << 20
+FIRST_VMEM_BYTES = 60 << 20
 MERGED = 4
 RAISE = 16.0
 
@@ -135,7 +136,7 @@
             ],
             out_specs=[pl.BlockSpec((half // 2, chunk), lambda i, s: (i, 0))] * CHUNKS,
         ),
-        compiler_params=pltpu.CompilerParams(vmem_limit_bytes=VMEM_BYTES),
+        compiler_params=pltpu.CompilerParams(vmem_limit_bytes=FIRST_VMEM_BYTES),
         cost_estimate=pl.CostEstimate(
             flops=0, bytes_accessed=8 * half * width * kinds, transcendentals=0
         ),
@@ -182,8 +183,8 @@
     out_ref[...] = source_ref[first : first + out_ref.shape[0], :]
 
 
-def pick_columns(source, side, half, first, end):
-    rows, blocks = source.shape[0], source.shape[1] // (2 * half)
+def pick_columns(source, side, half, first, end, vmem_bytes=VMEM_BYTES):
+    rows, blocks = source.shape[0] if first else end, source.shape[1] // (2 * half)
     return pl.pallas_call(
         functools.partial(pick_kernel, first),
         out_shape=jax.ShapeDtypeStruct((end - first, blocks * half), source.dtype),
@@ -193,7 +194,7 @@
             in_specs=[pl.BlockSpec((rows, half), lambda j, s: (0, 2 * j + s[0]))],
             out_specs=pl.BlockSpec((end - first, half), lambda j, s: (0, j)),
         ),
-        compiler_params=pltpu.CompilerParams(vmem_limit_bytes=VMEM_BYTES),
+        compiler_params=pltpu.CompilerParams(vmem_limit_bytes=vmem_bytes),
         cost_estimate=pl.CostEstimate(
             flops=0, bytes_accessed=4 * (end - first) * blocks * half, transcendentals=0
         ),
@@ -293,6 +294,10 @@
     owners = lax.dynamic_index_in_dim(jnp.array(shard_order, jnp.int32), row_index, 1, keepdims=False)
     places = ((owners // half_rows) ^ core) * half_rows + owners % half_rows
 
+    cuts = (0, tokens // 4, tokens // 8 * 5, tokens)
+    sent = [pick_columns(passages, 1 - side, half, cuts[0], cuts[1], FIRST_VMEM_BYTES)]
+    kv_weight, sent[0], passages = fence(kv_weight, sent[0], passages)
+    got = [lax.ppermute(sent[0], "groups", partners)]
     own = own_half(kv_weight, side)
 
     ring, ends = [[(piece, piece)] for piece in own], [None, None]
@@ -322,21 +327,19 @@
         tokens_total = (total[:tokens] * RAISE).astype(jnp.float16)
         return tokens_total, total[tokens + new_padded :], total[tokens : tokens + count]
 
-    cuts = (0, 3 * tokens // 20, 23 * tokens // 40, tokens)
-    sent = [pick_columns(passages, 1 - side, half, cuts[0], cuts[1])]
-    (passages_later, new_hidden) = fence_with(0, passages, new_hidden)
-    got = [lax.ppermute(sent[0], "groups", partners)]
+    passages, new_hidden = fence_with(0, passages, new_hidden)
     step(0)
-    passages = passages_later
     sent += [pick_columns(passages, 1 - side, half, *cuts[i : i + 2]) for i in (1, 2)]
     kept = pick_columns(passages, side, half, 0, tokens)
     new_rows = jnp.swapaxes(new_hidden, 0, 1).reshape(count, half_model)
     new_rows = jnp.pad(new_rows, ((0, new_padded - count), (0, 0)))
     new_sent = pick_columns(new_rows, 1 - side, half, 0, new_padded)
     new_kept = pick_columns(new_rows, side, half, 0, new_padded)
-    got[0], sent, kept, new_sent, new_kept, lengths, destinations = fence_with(
-        0, got[0], sent, kept, new_sent, new_kept, lengths, destinations
-    )
+    new_got = lax.ppermute(new_sent, "groups", partners)
+    got[0], sent, kept, new_got, new_kept, lengths, destinations = fence_with(
+        0, got[0], sent, kept, new_got, new_kept, lengths, destinations
+    )
+    new_kept = jnp.concatenate([new_kept, new_got], 0)
 
     got.append(lax.ppermute(sent[1], "groups", partners))
     step(0)
@@ -365,22 +368,22 @@
         (ring[1][-1],) = fence_with(0, ring[1][-1])
         step(0)
         step(1)
-    held[0] = project(0, own_hidden, held[0], first, row_count - 1)
-    held.append(project(1, own_hidden, None, 0, early - 2))
+    held[0] = project(0, own_hidden, held[0], first, early)
     ends[0] = halved(ring[0][-1])
-    got[2], new_sent, held, places, ring[1][-1], ends[0] = fence_with(
-        0, got[2], new_sent, held, places, ring[1][-1], ends[0]
+    got[2], new_kept, held, places, ring[1][-1], ends[0] = fence_with(
+        0, got[2], new_kept, held, places, ring[1][-1], ends[0]
     )
 
     step(0)
     got_other.append(lax.ppermute(got[2], "tensor", cores))
-    new_kept = jnp.concatenate([new_kept, lax.ppermute(new_sent, "groups", partners)], 0)
     new_other = lax.ppermute(new_kept, "tensor", cores)
     (got_other[2],) = fence_with(1, got_other[2])
     step(1)
     away_hidden = list(zip(got, got_other)) + [(new_kept, new_other)]
+    held.append(project(1, own_hidden, None, 0, early))
+    places, held = fence(places, held)
     away = project(0, away_hidden, None, 0, row_count)
-    away, places, held = fence(homeward(away), places, held)
+    away, places = fence(homeward(away), places)
     (places,) = fence_with(1, places)
     ends[1] = halved(ring[1][-1])
     step(1)
@@ -391,8 +394,7 @@
     new_own.append(away[2])
     new_away.append(away[1])
     new_back = lax.ppermute(jnp.concatenate(new_away, 1), "groups", partners)
-    held[0] = project(0, own_hidden, held[0], row_count - 1, row_count)
-    held[1] = project(1, own_hidden, held[1], early - 2, early)
+    held[0] = project(0, own_hidden, held[0], early, row_count)
     queries = jnp.swapaxes(queries, 0, 1).reshape(count, -1)
     held, queries, places, away, new_back, homed[0] = fence(
         held, queries, places, away, new_back, homed[0]

time: 157 us -> 161 us (1.025)
  other arithmetic: 6.32 us -> 12.1 us
  starting transfers between devices: 33.7 us -> 30.4 us
  local copies, waits for them, and re-layouts: 18.3 us -> 21.1 us
  waiting for transfers between devices: 49.5 us -> 47.4 us
    ppermute x8, waiting for transfers between devices: 21.1 us -> 17.2 us  [step(): lax.ppermute(pair[0], 'rows', onward)]
    ppermute x1, waiting for transfers between devices: 2.92 us -> 6.78 us  [body(): got.append(lax.ppermute(sent[2], 'groups', partners))]
    ppermute x1, waiting for transfers between devices: 3.84 us -> 0.01 us  [body(): got = [lax.ppermute(sent[0], 'groups', partners)]]
    pallas_call x9 -> x7, Pallas kernels: 26.9 us -> 23.7 us  [products(): pl.pallas_call(functools.partial(product_kernel, depths, len(hidden), bas...]
    ppermute x8, starting transfers between devices: 14.4 us -> 11.6 us  [step(): lax.ppermute(pair[0], 'rows', onward)]
    pallas_call x6, Pallas kernels: 2.2 us -> 5.03 us  [pick_columns(): pl.pallas_call(functools.partial(pick_kernel, first), out_shape=jax.Shape...]
    pallas_call x1, Pallas kernels: 2.33 us -> 4.09 us  [own_half(): pl.pallas_call(own_kernel, out_shape=[jax.ShapeDtypeStruct((half, chunk),...]
    ppermute x8, starting transfers between devices: 3.21 us -> 4.95 us  [step(): lax.ppermute(pair[1], 'rows', back)]
  transfers between devices with their start and end apart: 29 -> 29, of which waited for: 16 -> 16; matrix products, arithmetic and copies ran while one was open for 5% -> 11% of each run, Pallas kernels for 19% -> 19%
where the time goes in v12:
time: 161 us; the launch traced here: 160 us
  waiting for transfers between devices  47.4 us (29%)
  Pallas kernels  35.9 us (22%)
  starting transfers between devices  30.4 us (19%)
  local copies, waits for them, and re-layouts  21.1 us (13%)
  blocking collectives  13 us (8%)
  other arithmetic  12.1 us (8%)
    pallas_call x7, Pallas kernels, products(): pl.pallas_call(functools.partial(product_kernel, depths, len(hidden), bas...  23.7 us
    ppermute x8, waiting for transfers between devices, step(): lax.ppermute(pair[0], 'rows', onward)  17.2 us
    unnamed x66, local copies, waits for them, and re-layouts  13.8 us
    all_to_all x1, blocking collectives, body(): lax.all_to_all(attended, 'rows', split_axis=0, concat_axis=0, tiled=True)  13 us
    ppermute x8, starting transfers between devices, step(): lax.ppermute(pair[0], 'rows', onward)  11.6 us
    ppermute x8, waiting for transfers between devices, step(): lax.ppermute(pair[1], 'rows', back)  8.64 us
    ppermute x1, waiting for transfers between devices, body(): got.append(lax.ppermute(sent[1], 'groups', partners))  7.65 us
    ppermute x1, waiting for transfers between devices, body(): got.append(lax.ppermute(sent[2], 'groups', partners))  6.78 us
  transfers between devices with their start and end apart: 29, of which 16 were waited for; matrix products, arithmetic and copies ran while one was open for 11% of the time, Pallas kernels for 19%

profile of v12, /device:TPU:0, one launch (start us, length us, event | category | flops | bytes accessed | tf_op | source)
XLA Modules:
  0.0 160.3 jit_solution(9196932307763081234)
XLA Ops:
  0.0 3.2 %pick_columns.6 = bf16[160,2048]{1,0:T(8,128)(2,1)} custom-call(s32[1]{0:T(128)} %bitcast.1.side_ref, bf16[640,4096]{1,0:T(8,128)(2,1)} %source_ref.4), custom_call_target="tpu_custom_call" | custom-call | bytes 1310720 | tf_op jit(solution)/shard_map/pick_columns/pallas_call | solution.py:188
  3.2 2.9 %collective-permute-start.2 = (bf16[160,2048]{1,0:T(8,128)(2,1)}, bf16[160,2048]{1,0:T(8,128)(2,1)S(1)}, u32[]{:S(2)}, u32[]{:S(2)}) collective-permute-start(bf16[160,2048]{1,0:T(8,128)(2,1)} %pick_columns.6), channel_id=1, source_target_pairs={{0,16},{16,0},{1,17},{17,1},{2,18},{18,2},{3,19},{19,3},{4,20},{20... | collective-permute-start | bytes 1966088 | tf_op jit(solution)/shard_map/ppermute | solution.py:300
  6.2 4.1 %own_half.1 = (bf16[512,512]{1,0:T(8,128)(2,1)}, bf16[512,512]{1,0:T(8,128)(2,1)}) custom-call(s32[1]{0:T(128)} %bitcast.side_ref, bf16[1024,2,512]{2,1,0:T(2,128)(2,1)} %weight_ref), custom_call_target="tpu_custom_call" | custom-call | bytes 4194304 | tf_op jit(solution)/shard_map/own_half/pallas_call | solution.py:128
  12.7 2.5 %copy-done = bf16[640,4096]{1,0:T(8,128)(2,1)S(1)} copy-done((bf16[640,4096]{1,0:T(8,128)(2,1)S(1)}, bf16[640,4096]{1,0:T(8,128)(2,1)}, u32[]{:S(2)}) %copy-start) | copy-done | bytes 5242904
  15.8 1.8 %copy-done.1 = bf16[640,4096]{1,0:T(8,128)(2,1)S(1)} copy-done((bf16[640,4096]{1,0:T(8,128)(2,1)S(1)}, bf16[640,4096]{1,0:T(8,128)(2,1)}, u32[]{:S(2)}) %copy-start.1) | copy-done | bytes 5242904
  20.5 3.4 %collective-permute-done.3 = bf16[32,2048]{1,0:T(8,128)(2,1)S(1)} collective-permute-done((bf16[32,2048]{1,0:T(8,128)(2,1)S(1)}, bf16[32,2048]{1,0:T(8,128)(2,1)S(1)}, u32[]{:S(2)}, u32[]{:S(2)}) %collective-permute-start.3) | collective-permute-done | bytes 131104 | tf_op jit(solution)/shard_map/ppermute | solution.py:338
  42.0 1.9 %multiply_cosine_fusion = (f32[640,64]{1,0:T(8,128)S(1)}, f32[640,64]{1,0:T(8,128)S(1)}) fusion(f32[64]{0:T(128)} %multiply_exponential_fusion, f32[640]{0:T(1024)S(1)} %subtract_convert_fusion), kind=kLoop, calls=%fused_computation.7 | loop fusion | flops 40960 | bytes 330496 | tf_op jit(solution)/shard_map/cos | solution.py:25
  47.8 3.9 %products.7.refs_7_ = f32[640,512]{1,0:T(8,128)S(1)} custom-call(s32[8]{0:T(128)S(1)} %fusion.3.refs_0_, bf16[640,2048]{1,0:T(8,128)(2,1)S(1)} %pick_columns.9.refs_1_, bf16[640,2048]{1,0:T(8,128)(2,1)} %collective-permute-done.7.refs_2_, bf16[512,512]{1,0:T(8,128)(2,1)S(1)} %copy-done.14, bf16[512,512]{1,0:T(8,128)(2,1)S(1)} %copy-done.16, ...), custom_call_target="tpu_custom_call" | custom-call | flops 1677721600 | bytes 7208960 | tf_op jit(solution)/shard_map/products/pallas_call | solution.py:240
  51.7 7.7 %collective-permute-done.6.refs_3_ = bf16[240,2048]{1,0:T(8,128)(2,1)S(1)} collective-permute-done((bf16[240,2048]{1,0:T(8,128)(2,1)}, bf16[240,2048]{1,0:T(8,128)(2,1)S(1)}, u32[]{:S(2)}, u32[]{:S(2)}) %collective-permute-start.6) | collective-permute-done | bytes 983072 | tf_op jit(solution)/shard_map/ppermute | solution.py:344
  64.3 10.9 %collective-permute-done.11.refs_14_.refs_3_ = bf16[512,512]{1,0:T(8,128)(2,1)S(1)} collective-permute-done((bf16[512,512]{1,0:T(8,128)(2,1)}, bf16[512,512]{1,0:T(8,128)(2,1)S(1)}, u32[]{:S(2)}, u32[]{:S(2)}) %collective-permute-start.11) | collective-permute-done | bytes 524320 | tf_op jit(solution)/shard_map/ppermute | solution.py:312
  76.8 6.8 %collective-permute-done.13.refs_5_ = bf16[240,2048]{1,0:T(8,128)(2,1)S(1)} collective-permute-done((bf16[240,2048]{1,0:T(8,128)(2,1)S(1)}, bf16[240,2048]{1,0:T(8,128)(2,1)S(1)}, u32[]{:S(2)}, u32[]{:S(2)}) %collective-permute-start.13) | collective-permute-done | bytes 983072 | tf_op jit(solution)/shard_map/ppermute | solution.py:362
  83.6 2.0 %collective-permute-done.15.refs_6_.refs_12_ = bf16[512,512]{1,0:T(8,128)(2,1)S(1)} collective-permute-done((bf16[512,512]{1,0:T(8,128)(2,1)S(1)}, bf16[512,512]{1,0:T(8,128)(2,1)S(1)}, u32[]{:S(2)}, u32[]{:S(2)}) %collective-permute-start.15) | collective-permute-done | bytes 524320 | tf_op jit(solution)/shard_map/ppermute | solution.py:312
  91.5 3.7 %products.8.refs_7_ = f32[640,512]{1,0:T(8,128)S(1)} custom-call(s32[8]{0:T(128)S(1)} %fusion.3.refs_0_, bf16[640,2048]{1,0:T(8,128)(2,1)S(1)} %pick_columns.9.refs_1_, bf16[640,2048]{1,0:T(8,128)(2,1)} %collective-permute-done.7.refs_2_, bf16[512,512]{1,0:T(8,128)(2,1)S(1)} %copy-done.13, bf16[512,512]{1,0:T(8,128)(2,1)S(1)} %collective-permute-done.9.refs_4_.refs_10_, ...), custom_call_target="tpu_custom_call" | custom-call | flops 1677721600 | bytes 7208960 | tf_op jit(solution)/shard_map/products/pallas_call | solution.py:240
  98.2 4.6 %products.9 = f32[704,512]{1,0:T(8,128)S(1)} custom-call(s32[8]{0:T(128)S(1)} %fusion.3.refs_0_, bf16[160,2048]{1,0:T(8,128)(2,1)S(1)} %collective-permute-done.2.refs_1_, bf16[160,2048]{1,0:T(8,128)(2,1)} %collective-permute-done.8.refs_2_, bf16[240,2048]{1,0:T(8,128)(2,1)S(1)} %collective-permute-done.6.refs_3_, ...), custom_call_target="tpu_custom_call" | custom-call | flops 2952790016 | bytes 11403264 | tf_op jit(solution)/shard_map/products/pallas_call | solution.py:240
  104.4 2.5 %collective-permute-done.18.refs_14_.refs_3_ = bf16[512,512]{1,0:T(8,128)(2,1)S(1)} collective-permute-done((bf16[512,512]{1,0:T(8,128)(2,1)S(1)}, bf16[512,512]{1,0:T(8,128)(2,1)S(1)}, u32[]{:S(2)}, u32[]{:S(2)}) %collective-permute-start.18) | collective-permute-done | bytes 524320 | tf_op jit(solution)/shard_map/ppermute | solution.py:312
  108.2 1.6 %collective-permute-start.23 = (bf16[256,512]{1,0:T(8,128)(2,1)S(1)}, bf16[256,512]{1,0:T(8,128)(2,1)S(1)}, u32[]{:S(2)}, u32[]{:S(2)}) collective-permute-start(bf16[256,512]{1,0:T(8,128)(2,1)S(1)} %slice.41), channel_id=1, source_target_pairs={{0,4},{4,8},{8,12},{12,14},{14,10},{10,6},{6,2},{2,0},{1,5},{5,9},... | collective-permute-start | bytes 786440 | tf_op jit(solution)/shard_map/ppermute | solution.py:312
  110.5 2.9 %products.10.refs_0_ = f32[640,512]{1,0:T(8,128)S(1)} custom-call(s32[8]{0:T(128)S(1)} %fusion.3.refs_0_, bf16[640,2048]{1,0:T(8,128)(2,1)S(1)} %pick_columns.9.refs_1_, bf16[640,2048]{1,0:T(8,128)(2,1)} %collective-permute-done.7.refs_2_, bf16[512,512]{1,0:T(8,128)(2,1)S(1)} %collective-permute-done.11.refs_14_.refs_3_, ...), custom_call_target="tpu_custom_call" | custom-call | flops 1006632960 | bytes 4849664 | tf_op jit(solution)/shard_map/products/pallas_call | solution.py:240
  114.6 3.9 %products.11.refs_11_ = f32[704,512]{1,0:T(8,128)S(1)} custom-call(s32[8]{0:T(128)S(1)} %fusion.3.refs_0_, bf16[160,2048]{1,0:T(8,128)(2,1)S(1)} %collective-permute-done.2.refs_1_, bf16[160,2048]{1,0:T(8,128)(2,1)} %collective-permute-done.8.refs_2_, bf16[240,2048]{1,0:T(8,128)(2,1)S(1)} %collective-permute-done.6.refs_3_, ...), custom_call_target="tpu_custom_call" | custom-call | flops 2583691264 | bytes 10158080 | tf_op jit(solution)/shard_map/products/pallas_call | solution.py:240
  118.5 1.7 %products.12 = f32[704,512]{1,0:T(8,128)S(1)} custom-call(s32[8]{0:T(128)S(1)} %fusion.3.refs_0_, bf16[160,2048]{1,0:T(8,128)(2,1)S(1)} %collective-permute-done.2.refs_1_, bf16[160,2048]{1,0:T(8,128)(2,1)} %collective-permute-done.8.refs_2_, bf16[240,2048]{1,0:T(8,128)(2,1)S(1)} %collective-permute-done.6.refs_3_, ...), custom_call_target="tpu_custom_call" | custom-call | flops 369098752 | bytes 2686976 | tf_op jit(solution)/shard_map/products/pallas_call | solution.py:240
  122.8 2.6 %collective-permute-done.25.refs_1_ = f32[32,1024]{1,0:T(8,128)S(1)} collective-permute-done((f32[32,1024]{1,0:T(8,128)S(1)}, f32[32,1024]{1,0:T(8,128)S(1)}, u32[]{:S(2)}, u32[]{:S(2)}) %collective-permute-start.25) | collective-permute-done | bytes 131104 | tf_op jit(solution)/shard_map/ppermute | solution.py:396
  127.8 4.1 %all-to-all-start = ((bf16[8,3,5120]{2,1,0:T(4,128)(2,1)}), bf16[8,3,5120]{2,1,0:T(4,128)(2,1)}, u32[]{:S(2)}, u32[]{:S(2)}) async-start(bf16[8,3,5120]{2,1,0:T(4,128)(2,1)} %bitcast.38), calls=%async_computation | async-start | bytes 655360 | tf_op jit(solution)/shard_map/all_to_all | solution.py:409
  135.3 3.0 %products.13.refs_1_ = f32[640,512]{1,0:T(8,128)S(1)} custom-call(s32[8]{0:T(128)S(1)} %fusion.3.refs_0_, bf16[640,2048]{1,0:T(8,128)(2,1)S(1)} %pick_columns.9.refs_1_, bf16[640,2048]{1,0:T(8,128)(2,1)} %collective-permute-done.7.refs_2_, bf16[512,512]{1,0:T(8,128)(2,1)S(1)} %copy-done.10, bf16[512,512]{1,0:T(8,128)(2,1)S(1)} %copy-done.12, ...), custom_call_target="tpu_custom_call" | custom-call | flops 1006632960 | bytes 4849664 | tf_op jit(solution)/shard_map/products/pallas_call | solution.py:240
  143.4 2.9 %rotate_attend.1 = bf16[24,4096]{1,0:T(8,128)(2,1)S(1)} custom-call(f32[640,512]{1,0:T(8,128)S(1)} %copy-done.6, f32[640,512]{1,0:T(8,128)S(1)} %copy-done.8, f32[640,512]{1,0:T(8,128)S(1)} %convert_multiply_fusion.1.refs_2_, f32[640,512]{1,0:T(8,128)S(1)} %convert_multiply_fusion.refs_3_, f32[640,128]{1,0:T(8,128)S(1)} %copy-done.19, ...), custom_call_target="tpu_custom_call" | custom-call | flops 251658240 | bytes 5636096 | tf_op jit(solution)/shard_map/rotate_attend/pallas_call | solution.py:101
  146.5 13.0 %all_to_all.10 = bf16[8,3,4096]{2,1,0:T(4,128)(2,1)S(1)} all-to-all(bf16[8,3,4096]{2,1,0:T(4,128)(2,1)S(1)} %bitcast.39), channel_id=1, replica_groups=mesh['groups'=2,'rows'=8,'tensor'=2] {'rows'}, dimensions={0} | all-to-all | bytes 393216 | tf_op jit(solution)/shard_map/all_to_all | solution.py:417
  (173 shorter events, 62.2 us)
Async XLA Ops:
  3.2 21.9 %collective-permute-start.2 = (bf16[160,2048]{1,0:T(8,128)(2,1)}, bf16[160,2048]{1,0:T(8,128)(2,1)S(1)}, u32[]{:S(2)}, u32[]{:S(2)}) collective-permute-start(bf16[160,2048]{1,0:T(8,128)(2,1)} %pick_columns.6), channel_id=1, source_target_pairs={{0,16},{16,0},{1,17},{17,1},{2,18},{18,2},{3,19},{19,3},{4,20},{20... | collective-permute-start | bytes 1966088 | tf_op jit(solution)/shard_map/ppermute | solution.py:300
  10.3 13.7 %collective-permute-start = (bf16[512,512]{1,0:T(8,128)(2,1)}, bf16[512,512]{1,0:T(8,128)(2,1)S(1)}, u32[]{:S(2)}, u32[]{:S(2)}) collective-permute-start(bf16[512,512]{1,0:T(8,128)(2,1)} %get-tuple-element.78.refs_3_.refs_9_), channel_id=1, source_target_pairs={{0,4},{4,8},{8,12},{12,14},{14,10},{10,6},{6,2},{2,0},{1,5},{5,9},... | collective-permute-start | bytes 1572872 | tf_op jit(solution)/shard_map/ppermute | solution.py:312
  11.8 13.3 %collective-permute-start.1 = (bf16[512,512]{1,0:T(8,128)(2,1)}, bf16[512,512]{1,0:T(8,128)(2,1)S(1)}, u32[]{:S(2)}, u32[]{:S(2)}) collective-permute-start(bf16[512,512]{1,0:T(8,128)(2,1)} %get-tuple-element.78.refs_3_.refs_9_), channel_id=1, source_target_pairs={{4,0},{8,4},{12,8},{14,12},{10,14},{6,10},{2,6},{0,2},{5,1},{9,5},... | collective-permute-start | bytes 1572872 | tf_op jit(solution)/shard_map/ppermute | solution.py:312
  12.5 11.4 %collective-permute-start.3 = (bf16[32,2048]{1,0:T(8,128)(2,1)S(1)}, bf16[32,2048]{1,0:T(8,128)(2,1)S(1)}, u32[]{:S(2)}, u32[]{:S(2)}) collective-permute-start(bf16[32,2048]{1,0:T(8,128)(2,1)S(1)} %pick_columns.10), channel_id=1, source_target_pairs={{0,16},{16,0},{1,17},{17,1},{2,18},{18,2},{3,19},{19,3},{4,20},{20... | collective-permute-start | bytes 393224 | tf_op jit(solution)/shard_map/ppermute | solution.py:338
  25.9 13.9 %collective-permute-start.7 = (bf16[640,2048]{1,0:T(8,128)(2,1)S(1)}, bf16[640,2048]{1,0:T(8,128)(2,1)}, u32[]{:S(2)}, u32[]{:S(2)}) collective-permute-start(bf16[640,2048]{1,0:T(8,128)(2,1)S(1)} %pick_columns.9.refs_1_), channel_id=1, source_target_pairs={{0,1},{1,0},{2,3},{3,2},{4,5},{5,4},{6,7},{7,6},{8,9},{9,8},{10,11... | collective-permute-start | bytes 7864328 | tf_op jit(solution)/shard_map/ppermute | solution.py:346
  30.6 9.3 %collective-permute-start.8 = (bf16[160,2048]{1,0:T(8,128)(2,1)S(1)}, bf16[160,2048]{1,0:T(8,128)(2,1)}, u32[]{:S(2)}, u32[]{:S(2)}) collective-permute-start(bf16[160,2048]{1,0:T(8,128)(2,1)S(1)} %collective-permute-done.2.refs_1_), channel_id=1, source_target_pairs={{0,1},{1,0},{2,3},{3,2},{4,5},{5,4},{6,7},{7,6},{8,9},{9,8},{10,11... | collective-permute-start | bytes 1966088 | tf_op jit(solution)/shard_map/ppermute | solution.py:347
  31.1 15.1 %collective-permute-start.4 = (bf16[512,512]{1,0:T(8,128)(2,1)}, bf16[512,512]{1,0:T(8,128)(2,1)}, u32[]{:S(2)}, u32[]{:S(2)}) collective-permute-start(bf16[512,512]{1,0:T(8,128)(2,1)} %copy-done.15), channel_id=1, source_target_pairs={{0,4},{4,8},{8,12},{12,14},{14,10},{10,6},{6,2},{2,0},{1,5},{5,9},... | collective-permute-start | bytes 1572872 | tf_op jit(solution)/shard_map/ppermute | solution.py:312
  32.7 15.1 %collective-permute-start.5 = (bf16[512,512]{1,0:T(8,128)(2,1)}, bf16[512,512]{1,0:T(8,128)(2,1)}, u32[]{:S(2)}, u32[]{:S(2)}) collective-permute-start(bf16[512,512]{1,0:T(8,128)(2,1)} %copy-done.17), channel_id=1, source_target_pairs={{4,0},{8,4},{12,8},{14,12},{10,14},{6,10},{2,6},{0,2},{5,1},{9,5},... | collective-permute-start | bytes 1572872 | tf_op jit(solution)/shard_map/ppermute | solution.py:312
  36.0 23.4 %collective-permute-start.6 = (bf16[240,2048]{1,0:T(8,128)(2,1)}, bf16[240,2048]{1,0:T(8,128)(2,1)S(1)}, u32[]{:S(2)}, u32[]{:S(2)}) collective-permute-start(bf16[240,2048]{1,0:T(8,128)(2,1)} %copy-done.24), channel_id=1, source_target_pairs={{0,16},{16,0},{1,17},{17,1},{2,18},{18,2},{3,19},{19,3},{4,20},{20... | collective-permute-start | bytes 2949128 | tf_op jit(solution)/shard_map/ppermute | solution.py:344
  39.9 19.5 %collective-permute-start.10 = (bf16[512,512]{1,0:T(8,128)(2,1)}, bf16[512,512]{1,0:T(8,128)(2,1)S(1)}, u32[]{:S(2)}, u32[]{:S(2)}) collective-permute-start(bf16[512,512]{1,0:T(8,128)(2,1)} %get-tuple-element.92.refs_3_.refs_9_), channel_id=1, source_target_pairs={{4,0},{8,4},{12,8},{14,12},{10,14},{6,10},{2,6},{0,2},{5,1},{9,5},... | collective-permute-start | bytes 1572872 | tf_op jit(solution)/shard_map/ppermute | solution.py:312
  41.5 17.9 %collective-permute-start.9 = (bf16[512,512]{1,0:T(8,128)(2,1)}, bf16[512,512]{1,0:T(8,128)(2,1)S(1)}, u32[]{:S(2)}, u32[]{:S(2)}) collective-permute-start(bf16[512,512]{1,0:T(8,128)(2,1)} %get-tuple-element.92.refs_3_.refs_9_), channel_id=1, source_target_pairs={{0,4},{4,8},{8,12},{12,14},{14,10},{10,6},{6,2},{2,0},{1,5},{5,9},... | collective-permute-start | bytes 1572872 | tf_op jit(solution)/shard_map/ppermute | solution.py:312
  59.4 24.2 %collective-permute-start.13 = (bf16[240,2048]{1,0:T(8,128)(2,1)S(1)}, bf16[240,2048]{1,0:T(8,128)(2,1)S(1)}, u32[]{:S(2)}, u32[]{:S(2)}) collective-permute-start(bf16[240,2048]{1,0:T(8,128)(2,1)S(1)} %copy-done.23), channel_id=1, source_target_pairs={{0,16},{16,0},{1,17},{17,1},{2,18},{18,2},{3,19},{19,3},{4,20},{20... | collective-permute-start | bytes 2949128 | tf_op jit(solution)/shard_map/ppermute | solution.py:362
  60.2 15.0 %collective-permute-start.11 = (bf16[512,512]{1,0:T(8,128)(2,1)}, bf16[512,512]{1,0:T(8,128)(2,1)S(1)}, u32[]{:S(2)}, u32[]{:S(2)}) collective-permute-start(bf16[512,512]{1,0:T(8,128)(2,1)} %collective-permute-done.4.refs_6_.refs_12_), channel_id=1, source_target_pairs={{0,4},{4,8},{8,12},{12,14},{14,10},{10,6},{6,2},{2,0},{1,5},{5,9},... | collective-permute-start | bytes 1572872 | tf_op jit(solution)/shard_map/ppermute | solution.py:312
  61.8 15.0 %collective-permute-start.12 = (bf16[512,512]{1,0:T(8,128)(2,1)}, bf16[512,512]{1,0:T(8,128)(2,1)S(1)}, u32[]{:S(2)}, u32[]{:S(2)}) collective-permute-start(bf16[512,512]{1,0:T(8,128)(2,1)} %collective-permute-done.5.refs_7_.refs_13_), channel_id=1, source_target_pairs={{4,0},{8,4},{12,8},{14,12},{10,14},{6,10},{2,6},{0,2},{5,1},{9,5},... | collective-permute-start | bytes 1572872 | tf_op jit(solution)/shard_map/ppermute | solution.py:312
  62.2 23.4 %collective-permute-start.15 = (bf16[512,512]{1,0:T(8,128)(2,1)S(1)}, bf16[512,512]{1,0:T(8,128)(2,1)S(1)}, u32[]{:S(2)}, u32[]{:S(2)}) collective-permute-start(bf16[512,512]{1,0:T(8,128)(2,1)S(1)} %collective-permute-done.9.refs_4_.refs_10_), channel_id=1, source_target_pairs={{0,4},{4,8},{8,12},{12,14},{14,10},{10,6},{6,2},{2,0},{1,5},{5,9},... | collective-permute-start | bytes 1572872 | tf_op jit(solution)/shard_map/ppermute | solution.py:312
  63.8 23.1 %collective-permute-start.16 = (bf16[512,512]{1,0:T(8,128)(2,1)S(1)}, bf16[512,512]{1,0:T(8,128)(2,1)S(1)}, u32[]{:S(2)}, u32[]{:S(2)}) collective-permute-start(bf16[512,512]{1,0:T(8,128)(2,1)S(1)} %collective-permute-done.10.refs_5_.refs_11_), channel_id=1, source_target_pairs={{4,0},{8,4},{12,8},{14,12},{10,14},{6,10},{2,6},{0,2},{5,1},{9,5},... | collective-permute-start | bytes 1572872 | tf_op jit(solution)/shard_map/ppermute | solution.py:312
  86.9 9.3 %collective-permute-start.20 = (bf16[64,2048]{1,0:T(8,128)(2,1)S(1)}, bf16[64,2048]{1,0:T(8,128)(2,1)S(1)}, u32[]{:S(2)}, u32[]{:S(2)}) collective-permute-start(bf16[64,2048]{1,0:T(8,128)(2,1)S(1)} %pad_maximum_fusion.1.refs_7_), channel_id=1, source_target_pairs={{0,1},{1,0},{2,3},{3,2},{4,5},{5,4},{6,7},{7,6},{8,9},{9,8},{10,11... | collective-permute-start | bytes 786440 | tf_op jit(solution)/shard_map/ppermute | solution.py:379
  89.0 9.2 %collective-permute-start.22 = (bf16[256,512]{1,0:T(8,128)(2,1)S(1)}, bf16[256,512]{1,0:T(8,128)(2,1)S(1)}, u32[]{:S(2)}, u32[]{:S(2)}) collective-permute-start(bf16[256,512]{1,0:T(8,128)(2,1)S(1)} %slice.49), channel_id=1, source_target_pairs={{4,0},{8,4},{12,8},{14,12},{10,14},{6,10},{2,6},{0,2},{5,1},{9,5},... | collective-permute-start | bytes 786440 | tf_op jit(solution)/shard_map/ppermute | solution.py:312
  89.5 17.4 %collective-permute-start.18 = (bf16[512,512]{1,0:T(8,128)(2,1)S(1)}, bf16[512,512]{1,0:T(8,128)(2,1)S(1)}, u32[]{:S(2)}, u32[]{:S(2)}) collective-permute-start(bf16[512,512]{1,0:T(8,128)(2,1)S(1)} %collective-permute-done.15.refs_6_.refs_12_), channel_id=1, source_target_pairs={{0,4},{4,8},{8,12},{12,14},{14,10},{10,6},{6,2},{2,0},{1,5},{5,9},... | collective-permute-start | bytes 1572872 | tf_op jit(solution)/shard_map/ppermute | solution.py:312
  91.1 17.1 %collective-permute-start.19 = (bf16[512,512]{1,0:T(8,128)(2,1)S(1)}, bf16[512,512]{1,0:T(8,128)(2,1)S(1)}, u32[]{:S(2)}, u32[]{:S(2)}) collective-permute-start(bf16[512,512]{1,0:T(8,128)(2,1)S(1)} %collective-permute-done.16.refs_7_.refs_13_), channel_id=1, source_target_pairs={{4,0},{8,4},{12,8},{14,12},{10,14},{6,10},{2,6},{0,2},{5,1},{9,5},... | collective-permute-start | bytes 1572872 | tf_op jit(solution)/shard_map/ppermute | solution.py:312
  103.0 19.7 %collective-permute-start.26 = (f16[640,512]{1,0:T(8,128)(2,1)S(1)}, f16[640,512]{1,0:T(8,128)(2,1)S(1)}, u32[]{:S(2)}, u32[]{:S(2)}) collective-permute-start(f16[640,512]{1,0:T(8,128)(2,1)S(1)} %fusion.1), channel_id=1, source_target_pairs={{0,16},{16,0},{1,17},{17,1},{2,18},{18,2},{3,19},{19,3},{4,20},{20... | collective-permute-start | bytes 1966088 | tf_op jit(solution)/shard_map/ppermute | solution.py:390
  108.2 10.3 %collective-permute-start.23 = (bf16[256,512]{1,0:T(8,128)(2,1)S(1)}, bf16[256,512]{1,0:T(8,128)(2,1)S(1)}, u32[]{:S(2)}, u32[]{:S(2)}) collective-permute-start(bf16[256,512]{1,0:T(8,128)(2,1)S(1)} %slice.41), channel_id=1, source_target_pairs={{0,4},{4,8},{8,12},{12,14},{14,10},{10,6},{6,2},{2,0},{1,5},{5,9},... | collective-permute-start | bytes 786440 | tf_op jit(solution)/shard_map/ppermute | solution.py:312
  125.4 16.4 %collective-permute-start.27 = (f16[640,512]{1,0:T(8,128)(2,1)}, f16[640,512]{1,0:T(8,128)(2,1)}, u32[]{:S(2)}, u32[]{:S(2)}) collective-permute-start(f16[640,512]{1,0:T(8,128)(2,1)} %fusion), channel_id=1, source_target_pairs={{0,16},{16,0},{1,17},{17,1},{2,18},{18,2},{3,19},{19,3},{4,20},{20... | collective-permute-start | bytes 1966088 | tf_op jit(solution)/shard_map/ppermute | solution.py:402
  127.8 12.8 %all-to-all-start = ((bf16[8,3,5120]{2,1,0:T(4,128)(2,1)}), bf16[8,3,5120]{2,1,0:T(4,128)(2,1)}, u32[]{:S(2)}, u32[]{:S(2)}) async-start(bf16[8,3,5120]{2,1,0:T(4,128)(2,1)} %bitcast.38), calls=%async_computation | async-start | bytes 655360 | tf_op jit(solution)/shard_map/all_to_all | solution.py:409
  (39 other events, 232.5 us)

commit v13 on v10

--- a/solution.py
+++ b/solution.py
@@ -201,14 +201,15 @@
     )(side.reshape(1), source)
 
 
-def product_kernel(depths, parts, base, has_total, *refs):
+def product_kernel(depths, parts, base, has_total, outs, *refs):
     place_ref, refs = refs[0], refs[1:]
     hidden, refs = refs[: 2 * parts], refs[2 * parts :]
-    weights, out_ref = refs[: sum(len(pieces) for pieces in depths)], refs[-1]
+    refs, out_refs = refs[:-outs], refs[-outs:]
+    weights = refs[: sum(len(pieces) for pieces in depths)]
     half = sum(depths[0])
     blocks = hidden[0].shape[1] // half
 
-    total, used = refs[-2][...] if has_total else None, 0
+    total, used = refs[-1][...] if has_total else None, 0
     for p, pieces in enumerate(depths):
         place = place_ref[base + p]
         here = place < blocks
@@ -223,10 +224,13 @@
         used += len(pieces)
         term = jnp.dot(rows, piece, preferred_element_type=jnp.float32)
         total = term if total is None else total + term
-    out_ref[...] = total
-
-
-def products(total, hidden, weights, places, base):
+    at = 0
+    for out_ref in out_refs:
+        out_ref[...] = total[at : at + out_ref.shape[0], :]
+        at += out_ref.shape[0]
+
+
+def products(total, hidden, weights, places, base, cut=None):
     shards = len(weights)
     flat = [w for shard in weights for w in shard]
     depths = tuple(tuple(w.shape[0] for w in shard) for shard in weights)
@@ -238,11 +242,13 @@
     vmem = pl.BlockSpec(memory_space=pltpu.VMEM)
     return pl.pallas_call(
         functools.partial(
-            product_kernel, depths, len(hidden), base, total is not None
-        ),
-        out_shape=jax.ShapeDtypeStruct((rows, width), jnp.float32),
+            product_kernel, depths, len(hidden), base, total is not None, 2 if cut else 1
+        ),
+        out_shape=jax.ShapeDtypeStruct((rows, width), jnp.float32)
+        if cut is None
+        else [jax.ShapeDtypeStruct((n, width), jnp.float32) for n in (cut, rows - cut)],
         in_specs=[pl.BlockSpec(memory_space=pltpu.SMEM)] + [vmem] * (len(operands) - 1),
-        out_specs=vmem,
+        out_specs=vmem if cut is None else [vmem, vmem],
         compiler_params=pltpu.CompilerParams(vmem_limit_bytes=VMEM_BYTES),
         cost_estimate=pl.CostEstimate(
             flops=2 * rows * half * width * shards,
@@ -310,20 +316,20 @@
         ring[c][-1], others = fence(ring[c][-1], others)
         return others
 
-    def project(c, hidden, total, begin, end):
+    def project(c, hidden, total, begin, end, cut=None):
         weights = [(own[c],)] + [(w,) for pair in ring[c][1:half_rows] for w in pair]
         weights += ring[c][half_rows:]
         for at in range(begin, end, MOST_SHARDS):
             some = weights[at : min(at + MOST_SHARDS, end)]
-            total = products(total, hidden, some, places, at)
+            total = products(total, hidden, some, places, at, cut if at + len(some) == end else None)
         return total
 
     def homeward(total):
-        tokens_total = (total[:tokens] * RAISE).astype(jnp.float16)
-        return tokens_total, total[tokens + new_padded :], total[tokens : tokens + count]
+        total, new = total
+        return (total * RAISE).astype(jnp.float16), new[new_padded:], new[:count]
 
     cuts = (0, 3 * tokens // 20, 23 * tokens // 40, tokens)
-    sent = [pick_columns(passages, 1 - side, half, cuts[0], cuts[1])]
+    sent = [pick_columns(passages[: cuts[1]], 1 - side, half, cuts[0], cuts[1])]
     (passages_later, new_hidden) = fence_with(0, passages, new_hidden)
     got = [lax.ppermute(sent[0], "groups", partners)]
     step(0)
@@ -362,7 +368,7 @@
         (ring[1][-1],) = fence_with(0, ring[1][-1])
         step(0)
         step(1)
-    held = [project(0, own_hidden, None, 0, early)]
+    held = [project(0, own_hidden, None, 0, early), project(1, own_hidden, None, 0, early - 2)]
     ends[0] = halved(ring[0][-1])
     got[2], new_sent, held, places, ring[1][-1], ends[0] = fence_with(
         0, got[2], new_sent, held, places, ring[1][-1], ends[0]
@@ -375,17 +381,15 @@
     (got_other[2],) = fence_with(1, got_other[2])
     step(1)
     away_hidden = list(zip(got, got_other)) + [(new_kept, new_other)]
-    held.append(project(1, own_hidden, None, 0, early))
-    places, held = fence(places, held)
-    away = project(0, away_hidden, None, 0, row_count)
-    away, places = fence(homeward(away), places)
+    away = project(0, away_hidden, None, 0, row_count, tokens)
+    away, places, held = fence(homeward(away), places, held)
     (places,) = fence_with(1, places)
     ends[1] = halved(ring[1][-1])
     step(1)
     homed = [lax.ppermute(away[0], "groups", partners)]
     new_own, new_away = [away[2]], [away[1]]
     away = project(1, away_hidden, None, 0, row_count - 1)
-    away = homeward(project(1, away_hidden, away, row_count - 1, row_count))
+    away = homeward(project(1, away_hidden, away, row_count - 1, row_count, tokens))
     new_own.append(away[2])
     new_away.append(away[1])
     new_back = lax.ppermute(jnp.concatenate(new_away, 1), "groups", partners)
@@ -398,7 +402,7 @@
     angles, new_angles, key_info, query_info = tables
     moved = pack(new_own, new_back, new_angles, queries)
     moved, places = fence(moved, places)
-    held[1] = project(1, own_hidden, held[1], early, row_count)
+    held[1] = project(1, own_hidden, held[1], early - 2, row_count)
     moved = moved.reshape(steps, requests, -1)
     moved = jnp.swapaxes(moved, 0, 1)
     moved = lax.all_to_all(moved, "rows", split_axis=0, concat_axis=0, tiled=True)

time: 152 us -> 168 us (1.11)
  local copies, waits for them, and re-layouts: 18.3 us -> 30.4 us
  other arithmetic: 6.32 us -> 12.4 us
  waiting for transfers between devices: 52.5 us -> 48.7 us
  starting transfers between devices: 30.9 us -> 29.2 us
    unnamed x73 -> x83, local copies, waits for them, and re-layouts: 14.5 us -> 20.7 us
    ppermute x1, waiting for transfers between devices: 10 us -> 5.86 us  [body(): got.append(lax.ppermute(sent[2], 'groups', partners))]
    ppermute x8, waiting for transfers between devices: 17.6 us -> 20.5 us  [step(): lax.ppermute(pair[0], 'rows', onward)]
    ppermute x8, waiting for transfers between devices: 5.95 us -> 8.69 us  [step(): lax.ppermute(pair[1], 'rows', back)]
    slice x5, local copies, waits for them, and re-layouts: 0.02 us -> 2.44 us  [the longest x4 1.26 us: homeward(): return ((total * RAISE).astype(jnp.float16), new[new_padded:], new[:count])]
    ppermute x1, waiting for transfers between devices: 3.85 us -> 1.44 us  [body(): got = [lax.ppermute(sent[0], 'groups', partners)]]
  transfers between devices with their start and end apart: 29 -> 29, of which waited for: 16 -> 19; matrix products, arithmetic and copies ran while one was open for 5% -> 12% of each run, Pallas kernels for 16% -> 16%
where the time goes in v13:
time: 168 us; the launch traced here: 167 us
  waiting for transfers between devices  48.7 us (29%)
  Pallas kernels  31.3 us (19%)
  local copies, waits for them, and re-layouts  30.4 us (18%)
  starting transfers between devices  29.2 us (17%)
  blocking collectives  13.9 us (8%)
  other arithmetic  12.4 us (7%)
    pallas_call x7, Pallas kernels, products(): pl.pallas_call(functools.partial(product_kernel, depths, len(hidden), bas...  23.8 us
    unnamed x83, local copies, waits for them, and re-layouts  20.7 us
    ppermute x8, waiting for transfers between devices, step(): lax.ppermute(pair[0], 'rows', onward)  20.5 us
    all_to_all x1, blocking collectives, body(): lax.all_to_all(attended, 'rows', split_axis=0, concat_axis=0, tiled=True)  13.9 us
    ppermute x8, starting transfers between devices, step(): lax.ppermute(pair[0], 'rows', onward)  13.2 us
    ppermute x8, waiting for transfers between devices, step(): lax.ppermute(pair[1], 'rows', back)  8.69 us
    ppermute x1, waiting for transfers between devices, body(): got.append(lax.ppermute(sent[1], 'groups', partners))  7.05 us
    ppermute x1, waiting for transfers between devices, body(): got.append(lax.ppermute(sent[2], 'groups', partners))  5.86 us
  transfers between devices with their start and end apart: 29, of which 19 were waited for; matrix products, arithmetic and copies ran while one was open for 12% of the time, Pallas kernels for 16%

profile of v13, /device:TPU:0, one launch (start us, length us, event | category | flops | bytes accessed | tf_op | source)
XLA Modules:
  0.0 166.6 jit_solution(12127568999222559035)
XLA Ops:
  1.6 2.4 %own_half.1 = (bf16[512,512]{1,0:T(8,128)(2,1)}, bf16[512,512]{1,0:T(8,128)(2,1)S(1)}) custom-call(s32[1]{0:T(128)} %bitcast.side_ref, bf16[1024,2,512]{2,1,0:T(2,128)(2,1)S(1)} %copy-done.11), custom_call_target="tpu_custom_call" | custom-call | bytes 4194304 | tf_op jit(solution)/shard_map/own_half/pallas_call | solution.py:127
  4.0 3.0 %collective-permute-start = (bf16[512,512]{1,0:T(8,128)(2,1)}, bf16[512,512]{1,0:T(8,128)(2,1)}, u32[]{:S(2)}, u32[]{:S(2)}) collective-permute-start(bf16[512,512]{1,0:T(8,128)(2,1)} %get-tuple-element.76.refs_3_.refs_9_), channel_id=1, source_target_pairs={{0,4},{4,8},{8,12},{12,14},{14,10},{10,6},{6,2},{2,0},{1,5},{5,9},... | collective-permute-start | bytes 1572872 | tf_op jit(solution)/shard_map/ppermute | solution.py:313
  8.5 2.0 %collective-permute-start.2 = (bf16[96,2048]{1,0:T(8,128)(2,1)S(1)}, bf16[96,2048]{1,0:T(8,128)(2,1)S(1)}, u32[]{:S(2)}, u32[]{:S(2)}) collective-permute-start(bf16[96,2048]{1,0:T(8,128)(2,1)S(1)} %pick_columns.6), channel_id=1, source_target_pairs={{0,16},{16,0},{1,17},{17,1},{2,18},{18,2},{3,19},{19,3},{4,20},{20... | collective-permute-start | bytes 1179656 | tf_op jit(solution)/shard_map/ppermute | solution.py:334
  10.5 2.5 %copy-done = bf16[640,4096]{1,0:T(8,128)(2,1)S(1)} copy-done((bf16[640,4096]{1,0:T(8,128)(2,1)S(1)}, bf16[640,4096]{1,0:T(8,128)(2,1)}, u32[]{:S(2)}) %copy-start) | copy-done | bytes 5242904
  35.1 1.6 collective-permute-start.8
  37.9 1.8 %multiply_cosine_fusion = (f32[640,64]{1,0:T(8,128)S(1)}, f32[640,64]{1,0:T(8,128)S(1)}) fusion(f32[64]{0:T(128)} %multiply_exponential_fusion, f32[640]{0:T(1024)S(1)} %subtract_convert_fusion), kind=kLoop, calls=%fused_computation.5 | loop fusion | flops 40960 | bytes 330496 | tf_op jit(solution)/shard_map/cos | solution.py:24
  40.6 6.1 %collective-permute-done.3.refs_6_.refs_12_ = bf16[512,512]{1,0:T(8,128)(2,1)S(1)} collective-permute-done((bf16[512,512]{1,0:T(8,128)(2,1)}, bf16[512,512]{1,0:T(8,128)(2,1)S(1)}, u32[]{:S(2)}, u32[]{:S(2)}) %collective-permute-start.3) | collective-permute-done | bytes 524320 | tf_op jit(solution)/shard_map/ppermute | solution.py:313
  48.3 7.0 %collective-permute-done.5.refs_3_ = bf16[272,2048]{1,0:T(8,128)(2,1)S(1)} collective-permute-done((bf16[272,2048]{1,0:T(8,128)(2,1)}, bf16[272,2048]{1,0:T(8,128)(2,1)S(1)}, u32[]{:S(2)}, u32[]{:S(2)}) %collective-permute-start.5) | collective-permute-done | bytes 1114144 | tf_op jit(solution)/shard_map/ppermute | solution.py:347
  62.8 4.0 %products.7.refs_7_ = f32[640,512]{1,0:T(8,128)S(1)} custom-call(s32[8]{0:T(128)S(1)} %fusion.1.refs_0_, bf16[640,2048]{1,0:T(8,128)(2,1)S(1)} %pick_columns.9.refs_1_, bf16[640,2048]{1,0:T(8,128)(2,1)} %collective-permute-done.6.refs_2_, bf16[512,512]{1,0:T(8,128)(2,1)} %get-tuple-element.76.refs_3_.refs_9_, ...), custom_call_target="tpu_custom_call" | custom-call | flops 1677721600 | bytes 7208960 | tf_op jit(solution)/shard_map/products/pallas_call | solution.py:243
  66.8 6.6 %collective-permute-done.10.refs_14_.refs_3_ = bf16[512,512]{1,0:T(8,128)(2,1)S(1)} collective-permute-done((bf16[512,512]{1,0:T(8,128)(2,1)S(1)}, bf16[512,512]{1,0:T(8,128)(2,1)S(1)}, u32[]{:S(2)}, u32[]{:S(2)}) %collective-permute-start.10) | collective-permute-done | bytes 524320 | tf_op jit(solution)/shard_map/ppermute | solution.py:313
  75.0 3.0 %products.8.refs_9_ = f32[640,512]{1,0:T(8,128)S(1)} custom-call(s32[8]{0:T(128)S(1)} %fusion.1.refs_0_, bf16[640,2048]{1,0:T(8,128)(2,1)S(1)} %pick_columns.9.refs_1_, bf16[640,2048]{1,0:T(8,128)(2,1)} %collective-permute-done.6.refs_2_, bf16[512,512]{1,0:T(8,128)(2,1)S(1)} %get-tuple-element.88.refs_3_.refs_9_, ...), custom_call_target="tpu_custom_call" | custom-call | flops 1006632960 | bytes 4849664 | tf_op jit(solution)/shard_map/products/pallas_call | solution.py:243
  79.1 5.9 %collective-permute-done.12.refs_5_ = bf16[272,2048]{1,0:T(8,128)(2,1)S(1)} collective-permute-done((bf16[272,2048]{1,0:T(8,128)(2,1)S(1)}, bf16[272,2048]{1,0:T(8,128)(2,1)S(1)}, u32[]{:S(2)}, u32[]{:S(2)}) %collective-permute-start.12) | collective-permute-done | bytes 1114144 | tf_op jit(solution)/shard_map/ppermute | solution.py:362
  88.8 2.3 %collective-permute-done.19 = bf16[32,2048]{1,0:T(8,128)(2,1)S(1)} collective-permute-done((bf16[32,2048]{1,0:T(8,128)(2,1)S(1)}, bf16[32,2048]{1,0:T(8,128)(2,1)S(1)}, u32[]{:S(2)}, u32[]{:S(2)}) %collective-permute-start.19) | collective-permute-done | bytes 131104 | tf_op jit(solution)/shard_map/ppermute | solution.py:379
  93.3 2.6 %collective-permute-done.21.refs_16_.refs_5_ = bf16[256,512]{1,0:T(8,128)(2,1)S(1)} collective-permute-done((bf16[256,512]{1,0:T(8,128)(2,1)S(1)}, bf16[256,512]{1,0:T(8,128)(2,1)S(1)}, u32[]{:S(2)}, u32[]{:S(2)}) %collective-permute-start.21) | collective-permute-done | bytes 262176 | tf_op jit(solution)/shard_map/ppermute | solution.py:313
  97.1 4.6 %products.9 = (f32[640,512]{1,0:T(8,128)S(1)}, f32[64,512]{1,0:T(8,128)S(1)}) custom-call(s32[8]{0:T(128)S(1)} %fusion.1.refs_0_, bf16[96,2048]{1,0:T(8,128)(2,1)S(1)} %collective-permute-done.2.refs_1_, bf16[96,2048]{1,0:T(8,128)(2,1)} %collective-permute-done.7.refs_2_, bf16[272,2048]{1,0:T(8,128)(2,1)S(1)} %collective-permute-done.5.refs_3_, ...), custom_call_target="tpu_custom_call" | custom-call | flops 2952790016 | bytes 11403264 | tf_op jit(solution)/shard_map/products/pallas_call | solution.py:243
  102.6 3.7 %collective-permute-done.17.refs_14_.refs_5_ = bf16[512,512]{1,0:T(8,128)(2,1)S(1)} collective-permute-done((bf16[512,512]{1,0:T(8,128)(2,1)S(1)}, bf16[512,512]{1,0:T(8,128)(2,1)S(1)}, u32[]{:S(2)}, u32[]{:S(2)}) %collective-permute-start.17) | collective-permute-done | bytes 524320 | tf_op jit(solution)/shard_map/ppermute | solution.py:313
  110.0 2.9 %products.10.refs_0_ = f32[640,512]{1,0:T(8,128)S(1)} custom-call(s32[8]{0:T(128)S(1)} %fusion.1.refs_0_, bf16[640,2048]{1,0:T(8,128)(2,1)S(1)} %pick_columns.9.refs_1_, bf16[640,2048]{1,0:T(8,128)(2,1)} %collective-permute-done.6.refs_2_, bf16[512,512]{1,0:T(8,128)(2,1)S(1)} %collective-permute-done.10.refs_14_.refs_3_, ...), custom_call_target="tpu_custom_call" | custom-call | flops 1006632960 | bytes 4849664 | tf_op jit(solution)/shard_map/products/pallas_call | solution.py:243
  114.0 3.8 %products.11.refs_11_ = f32[704,512]{1,0:T(8,128)S(1)} custom-call(s32[8]{0:T(128)S(1)} %fusion.1.refs_0_, bf16[96,2048]{1,0:T(8,128)(2,1)S(1)} %collective-permute-done.2.refs_1_, bf16[96,2048]{1,0:T(8,128)(2,1)} %collective-permute-done.7.refs_2_, bf16[272,2048]{1,0:T(8,128)(2,1)S(1)} %collective-permute-done.5.refs_3_, ...), custom_call_target="tpu_custom_call" | custom-call | flops 2583691264 | bytes 10158080 | tf_op jit(solution)/shard_map/products/pallas_call | solution.py:243
  117.8 1.7 %products.12 = (f32[640,512]{1,0:T(8,128)S(1)}, f32[64,512]{1,0:T(8,128)S(1)}) custom-call(s32[8]{0:T(128)S(1)} %fusion.1.refs_0_, bf16[96,2048]{1,0:T(8,128)(2,1)S(1)} %collective-permute-done.2.refs_1_, bf16[96,2048]{1,0:T(8,128)(2,1)} %collective-permute-done.7.refs_2_, bf16[272,2048]{1,0:T(8,128)(2,1)S(1)} %collective-permute-done.5.refs_3_, ...), custom_call_target="tpu_custom_call" | custom-call | flops 369098752 | bytes 2686976 | tf_op jit(solution)/shard_map/products/pallas_call | solution.py:243
  122.0 2.7 %collective-permute-done.25.refs_1_ = f32[32,1024]{1,0:T(8,128)S(1)} collective-permute-done((f32[32,1024]{1,0:T(8,128)S(1)}, f32[32,1024]{1,0:T(8,128)S(1)}, u32[]{:S(2)}, u32[]{:S(2)}) %collective-permute-start.25) | collective-permute-done | bytes 131104 | tf_op jit(solution)/shard_map/ppermute | solution.py:395
  130.6 4.1 %all-to-all-start = ((bf16[8,3,5120]{2,1,0:T(4,128)(2,1)}), bf16[8,3,5120]{2,1,0:T(4,128)(2,1)}, u32[]{:S(2)}, u32[]{:S(2)}) async-start(bf16[8,3,5120]{2,1,0:T(4,128)(2,1)} %bitcast.38), calls=%async_computation | async-start | bytes 655360 | tf_op jit(solution)/shard_map/all_to_all | solution.py:408
  141.0 3.7 %products.13.refs_1_ = f32[640,512]{1,0:T(8,128)S(1)} custom-call(s32[8]{0:T(128)S(1)} %fusion.1.refs_0_, bf16[640,2048]{1,0:T(8,128)(2,1)S(1)} %pick_columns.9.refs_1_, bf16[640,2048]{1,0:T(8,128)(2,1)} %collective-permute-done.6.refs_2_, bf16[512,512]{1,0:T(8,128)(2,1)S(1)} %copy-done.13, bf16[512,512]{1,0:T(8,128)(2,1)S(1)} %copy-done.15, ...), custom_call_target="tpu_custom_call" | custom-call | flops 1677721600 | bytes 7208960 | tf_op jit(solution)/shard_map/products/pallas_call | solution.py:243
  148.8 2.9 %rotate_attend.1 = bf16[24,4096]{1,0:T(8,128)(2,1)S(1)} custom-call(f32[640,512]{1,0:T(8,128)S(1)} %copy-done.2, f32[640,512]{1,0:T(8,128)S(1)} %copy-done.6, f32[640,512]{1,0:T(8,128)S(1)} %convert_multiply_fusion.1.refs_2_, f32[640,512]{1,0:T(8,128)S(1)} %convert_multiply_fusion.refs_3_, f32[640,128]{1,0:T(8,128)S(1)} %copy-done.16, ...), custom_call_target="tpu_custom_call" | custom-call | flops 251658240 | bytes 5636096 | tf_op jit(solution)/shard_map/rotate_attend/pallas_call | solution.py:100
  151.9 13.9 %all_to_all.10 = bf16[8,3,4096]{2,1,0:T(4,128)(2,1)S(1)} all-to-all(bf16[8,3,4096]{2,1,0:T(4,128)(2,1)S(1)} %bitcast.39), channel_id=1, replica_groups=mesh['groups'=2,'rows'=8,'tensor'=2] {'rows'}, dimensions={0} | all-to-all | bytes 393216 | tf_op jit(solution)/shard_map/all_to_all | solution.py:416
  (190 shorter events, 71.0 us)
Async XLA Ops:
  4.0 15.2 %collective-permute-start = (bf16[512,512]{1,0:T(8,128)(2,1)}, bf16[512,512]{1,0:T(8,128)(2,1)}, u32[]{:S(2)}, u32[]{:S(2)}) collective-permute-start(bf16[512,512]{1,0:T(8,128)(2,1)} %get-tuple-element.76.refs_3_.refs_9_), channel_id=1, source_target_pairs={{0,4},{4,8},{8,12},{12,14},{14,10},{10,6},{6,2},{2,0},{1,5},{5,9},... | collective-permute-start | bytes 1572872 | tf_op jit(solution)/shard_map/ppermute | solution.py:313
  7.1 13.7 %collective-permute-start.1 = (bf16[512,512]{1,0:T(8,128)(2,1)}, bf16[512,512]{1,0:T(8,128)(2,1)}, u32[]{:S(2)}, u32[]{:S(2)}) collective-permute-start(bf16[512,512]{1,0:T(8,128)(2,1)} %get-tuple-element.76.refs_3_.refs_9_), channel_id=1, source_target_pairs={{4,0},{8,4},{12,8},{14,12},{10,14},{6,10},{2,6},{0,2},{5,1},{9,5},... | collective-permute-start | bytes 1572872 | tf_op jit(solution)/shard_map/ppermute | solution.py:313
  8.5 10.6 %collective-permute-start.2 = (bf16[96,2048]{1,0:T(8,128)(2,1)S(1)}, bf16[96,2048]{1,0:T(8,128)(2,1)S(1)}, u32[]{:S(2)}, u32[]{:S(2)}) collective-permute-start(bf16[96,2048]{1,0:T(8,128)(2,1)S(1)} %pick_columns.6), channel_id=1, source_target_pairs={{0,16},{16,0},{1,17},{17,1},{2,18},{18,2},{3,19},{19,3},{4,20},{20... | collective-permute-start | bytes 1179656 | tf_op jit(solution)/shard_map/ppermute | solution.py:334
  20.8 14.3 %collective-permute-start.6 = (bf16[640,2048]{1,0:T(8,128)(2,1)S(1)}, bf16[640,2048]{1,0:T(8,128)(2,1)}, u32[]{:S(2)}, u32[]{:S(2)}) collective-permute-start(bf16[640,2048]{1,0:T(8,128)(2,1)S(1)} %pick_columns.9.refs_1_), channel_id=1, source_target_pairs={{0,1},{1,0},{2,3},{3,2},{4,5},{5,4},{6,7},{7,6},{8,9},{9,8},{10,11... | collective-permute-start | bytes 7864328 | tf_op jit(solution)/shard_map/ppermute | solution.py:349
  25.3 9.8 %collective-permute-start.7 = (bf16[96,2048]{1,0:T(8,128)(2,1)S(1)}, bf16[96,2048]{1,0:T(8,128)(2,1)}, u32[]{:S(2)}, u32[]{:S(2)}) collective-permute-start(bf16[96,2048]{1,0:T(8,128)(2,1)S(1)} %collective-permute-done.2.refs_1_), channel_id=1, source_target_pairs={{0,1},{1,0},{2,3},{3,2},{4,5},{5,4},{6,7},{7,6},{8,9},{9,8},{10,11... | collective-permute-start | bytes 1179656 | tf_op jit(solution)/shard_map/ppermute | solution.py:350
  28.7 26.7 %collective-permute-start.5 = (bf16[272,2048]{1,0:T(8,128)(2,1)}, bf16[272,2048]{1,0:T(8,128)(2,1)S(1)}, u32[]{:S(2)}, u32[]{:S(2)}) collective-permute-start(bf16[272,2048]{1,0:T(8,128)(2,1)} %copy-done.19), channel_id=1, source_target_pairs={{0,16},{16,0},{1,17},{17,1},{2,18},{18,2},{3,19},{19,3},{4,20},{20... | collective-permute-start | bytes 3342344 | tf_op jit(solution)/shard_map/ppermute | solution.py:347
  31.7 15.0 %collective-permute-start.3 = (bf16[512,512]{1,0:T(8,128)(2,1)}, bf16[512,512]{1,0:T(8,128)(2,1)S(1)}, u32[]{:S(2)}, u32[]{:S(2)}) collective-permute-start(bf16[512,512]{1,0:T(8,128)(2,1)} %collective-permute-done.refs_4_.refs_10_), channel_id=1, source_target_pairs={{0,4},{4,8},{8,12},{12,14},{14,10},{10,6},{6,2},{2,0},{1,5},{5,9},... | collective-permute-start | bytes 1572872 | tf_op jit(solution)/shard_map/ppermute | solution.py:313
  33.3 15.1 %collective-permute-start.4 = (bf16[512,512]{1,0:T(8,128)(2,1)}, bf16[512,512]{1,0:T(8,128)(2,1)S(1)}, u32[]{:S(2)}, u32[]{:S(2)}) collective-permute-start(bf16[512,512]{1,0:T(8,128)(2,1)} %collective-permute-done.1.refs_5_.refs_11_), channel_id=1, source_target_pairs={{4,0},{8,4},{12,8},{14,12},{10,14},{6,10},{2,6},{0,2},{5,1},{9,5},... | collective-permute-start | bytes 1572872 | tf_op jit(solution)/shard_map/ppermute | solution.py:313
  35.1 21.6 %collective-permute-start.8 = (bf16[512,512]{1,0:T(8,128)(2,1)S(1)}, bf16[512,512]{1,0:T(8,128)(2,1)S(1)}, u32[]{:S(2)}, u32[]{:S(2)}) collective-permute-start(bf16[512,512]{1,0:T(8,128)(2,1)S(1)} %get-tuple-element.88.refs_3_.refs_9_), channel_id=1, source_target_pairs={{0,4},{4,8},{8,12},{12,14},{14,10},{10,6},{6,2},{2,0},{1,5},{5,9},... | collective-permute-start | bytes 1572872 | tf_op jit(solution)/shard_map/ppermute | solution.py:313
  36.7 21.2 %collective-permute-start.9 = (bf16[512,512]{1,0:T(8,128)(2,1)S(1)}, bf16[512,512]{1,0:T(8,128)(2,1)S(1)}, u32[]{:S(2)}, u32[]{:S(2)}) collective-permute-start(bf16[512,512]{1,0:T(8,128)(2,1)S(1)} %get-tuple-element.88.refs_3_.refs_9_), channel_id=1, source_target_pairs={{4,0},{8,4},{12,8},{14,12},{10,14},{6,10},{2,6},{0,2},{5,1},{9,5},... | collective-permute-start | bytes 1572872 | tf_op jit(solution)/shard_map/ppermute | solution.py:313
  58.0 27.0 %collective-permute-start.12 = (bf16[272,2048]{1,0:T(8,128)(2,1)S(1)}, bf16[272,2048]{1,0:T(8,128)(2,1)S(1)}, u32[]{:S(2)}, u32[]{:S(2)}) collective-permute-start(bf16[272,2048]{1,0:T(8,128)(2,1)S(1)} %copy-done.18), channel_id=1, source_target_pairs={{0,16},{16,0},{1,17},{17,1},{2,18},{18,2},{3,19},{19,3},{4,20},{20... | collective-permute-start | bytes 3342344 | tf_op jit(solution)/shard_map/ppermute | solution.py:362
  58.6 14.8 %collective-permute-start.10 = (bf16[512,512]{1,0:T(8,128)(2,1)S(1)}, bf16[512,512]{1,0:T(8,128)(2,1)S(1)}, u32[]{:S(2)}, u32[]{:S(2)}) collective-permute-start(bf16[512,512]{1,0:T(8,128)(2,1)S(1)} %collective-permute-done.3.refs_6_.refs_12_), channel_id=1, source_target_pairs={{0,4},{4,8},{8,12},{12,14},{14,10},{10,6},{6,2},{2,0},{1,5},{5,9},... | collective-permute-start | bytes 1572872 | tf_op jit(solution)/shard_map/ppermute | solution.py:313
  60.2 14.8 %collective-permute-start.11 = (bf16[512,512]{1,0:T(8,128)(2,1)S(1)}, bf16[512,512]{1,0:T(8,128)(2,1)S(1)}, u32[]{:S(2)}, u32[]{:S(2)}) collective-permute-start(bf16[512,512]{1,0:T(8,128)(2,1)S(1)} %collective-permute-done.4.refs_7_.refs_13_), channel_id=1, source_target_pairs={{4,0},{8,4},{12,8},{14,12},{10,14},{6,10},{2,6},{0,2},{5,1},{9,5},... | collective-permute-start | bytes 1572872 | tf_op jit(solution)/shard_map/ppermute | solution.py:313
  60.7 24.2 %collective-permute-start.14 = (bf16[512,512]{1,0:T(8,128)(2,1)S(1)}, bf16[512,512]{1,0:T(8,128)(2,1)S(1)}, u32[]{:S(2)}, u32[]{:S(2)}) collective-permute-start(bf16[512,512]{1,0:T(8,128)(2,1)S(1)} %collective-permute-done.8.refs_4_.refs_10_), channel_id=1, source_target_pairs={{0,4},{4,8},{8,12},{12,14},{14,10},{10,6},{6,2},{2,0},{1,5},{5,9},... | collective-permute-start | bytes 1572872 | tf_op jit(solution)/shard_map/ppermute | solution.py:313
  62.3 22.9 %collective-permute-start.15 = (bf16[512,512]{1,0:T(8,128)(2,1)S(1)}, bf16[512,512]{1,0:T(8,128)(2,1)S(1)}, u32[]{:S(2)}, u32[]{:S(2)}) collective-permute-start(bf16[512,512]{1,0:T(8,128)(2,1)S(1)} %collective-permute-done.9.refs_5_.refs_11_), channel_id=1, source_target_pairs={{4,0},{8,4},{12,8},{14,12},{10,14},{6,10},{2,6},{0,2},{5,1},{9,5},... | collective-permute-start | bytes 1572872 | tf_op jit(solution)/shard_map/ppermute | solution.py:313
  86.7 9.2 %collective-permute-start.21 = (bf16[256,512]{1,0:T(8,128)(2,1)S(1)}, bf16[256,512]{1,0:T(8,128)(2,1)S(1)}, u32[]{:S(2)}, u32[]{:S(2)}) collective-permute-start(bf16[256,512]{1,0:T(8,128)(2,1)S(1)} %slice.44), channel_id=1, source_target_pairs={{0,4},{4,8},{8,12},{12,14},{14,10},{10,6},{6,2},{2,0},{1,5},{5,9},... | collective-permute-start | bytes 786440 | tf_op jit(solution)/shard_map/ppermute | solution.py:313
  88.3 8.8 %collective-permute-start.22 = (bf16[256,512]{1,0:T(8,128)(2,1)S(1)}, bf16[256,512]{1,0:T(8,128)(2,1)S(1)}, u32[]{:S(2)}, u32[]{:S(2)}) collective-permute-start(bf16[256,512]{1,0:T(8,128)(2,1)S(1)} %slice.45), channel_id=1, source_target_pairs={{4,0},{8,4},{12,8},{14,12},{10,14},{6,10},{2,6},{0,2},{5,1},{9,5},... | collective-permute-start | bytes 786440 | tf_op jit(solution)/shard_map/ppermute | solution.py:313
  91.2 15.1 %collective-permute-start.17 = (bf16[512,512]{1,0:T(8,128)(2,1)S(1)}, bf16[512,512]{1,0:T(8,128)(2,1)S(1)}, u32[]{:S(2)}, u32[]{:S(2)}) collective-permute-start(bf16[512,512]{1,0:T(8,128)(2,1)S(1)} %collective-permute-done.14.refs_12_.refs_3_), channel_id=1, source_target_pairs={{0,4},{4,8},{8,12},{12,14},{14,10},{10,6},{6,2},{2,0},{1,5},{5,9},... | collective-permute-start | bytes 1572872 | tf_op jit(solution)/shard_map/ppermute | solution.py:313
  92.8 14.8 %collective-permute-start.18 = (bf16[512,512]{1,0:T(8,128)(2,1)S(1)}, bf16[512,512]{1,0:T(8,128)(2,1)S(1)}, u32[]{:S(2)}, u32[]{:S(2)}) collective-permute-start(bf16[512,512]{1,0:T(8,128)(2,1)S(1)} %collective-permute-done.15.refs_13_.refs_4_), channel_id=1, source_target_pairs={{4,0},{8,4},{12,8},{14,12},{10,14},{6,10},{2,6},{0,2},{5,1},{9,5},... | collective-permute-start | bytes 1572872 | tf_op jit(solution)/shard_map/ppermute | solution.py:313
  102.5 19.4 %collective-permute-start.26 = (f16[640,512]{1,0:T(8,128)(2,1)S(1)}, f16[640,512]{1,0:T(8,128)(2,1)S(1)}, u32[]{:S(2)}, u32[]{:S(2)}) collective-permute-start(f16[640,512]{1,0:T(8,128)(2,1)S(1)} %multiply_convert_fusion.1), channel_id=1, source_target_pairs={{0,16},{16,0},{1,17},{17,1},{2,18},{18,2},{3,19},{19,3},{4,20},{20... | collective-permute-start | bytes 1966088 | tf_op jit(solution)/shard_map/ppermute | solution.py:389
  107.6 10.2 %collective-permute-start.23 = (bf16[256,512]{1,0:T(8,128)(2,1)S(1)}, bf16[256,512]{1,0:T(8,128)(2,1)S(1)}, u32[]{:S(2)}, u32[]{:S(2)}) collective-permute-start(bf16[256,512]{1,0:T(8,128)(2,1)S(1)} %slice.38), channel_id=1, source_target_pairs={{0,4},{4,8},{8,12},{12,14},{14,10},{10,6},{6,2},{2,0},{1,5},{5,9},... | collective-permute-start | bytes 786440 | tf_op jit(solution)/shard_map/ppermute | solution.py:313
  108.3 9.5 %collective-permute-start.24 = (bf16[256,512]{1,0:T(8,128)(2,1)S(1)}, bf16[256,512]{1,0:T(8,128)(2,1)S(1)}, u32[]{:S(2)}, u32[]{:S(2)}) collective-permute-start(bf16[256,512]{1,0:T(8,128)(2,1)S(1)} %slice.39), channel_id=1, source_target_pairs={{4,0},{8,4},{12,8},{14,12},{10,14},{6,10},{2,6},{0,2},{5,1},{9,5},... | collective-permute-start | bytes 786440 | tf_op jit(solution)/shard_map/ppermute | solution.py:313
  125.3 21.9 %collective-permute-start.27 = (f16[640,512]{1,0:T(8,128)(2,1)}, f16[640,512]{1,0:T(8,128)(2,1)}, u32[]{:S(2)}, u32[]{:S(2)}) collective-permute-start(f16[640,512]{1,0:T(8,128)(2,1)} %multiply_convert_fusion), channel_id=1, source_target_pairs={{0,16},{16,0},{1,17},{17,1},{2,18},{18,2},{3,19},{19,3},{4,20},{20... | collective-permute-start | bytes 1966088 | tf_op jit(solution)/shard_map/ppermute | solution.py:401
  130.6 15.4 %all-to-all-start = ((bf16[8,3,5120]{2,1,0:T(4,128)(2,1)}), bf16[8,3,5120]{2,1,0:T(4,128)(2,1)}, u32[]{:S(2)}, u32[]{:S(2)}) async-start(bf16[8,3,5120]{2,1,0:T(4,128)(2,1)} %bitcast.38), calls=%async_computation | async-start | bytes 655360 | tf_op jit(solution)/shard_map/all_to_all | solution.py:408
  (46 other events, 285.7 us)

commit v14 on v10

--- a/solution.py
+++ b/solution.py
@@ -3,6 +3,7 @@
 
 import jax
 import jax.numpy as jnp
+import numpy as np
 from jax import lax
 from jax.experimental import pallas as pl
 from jax.experimental.pallas import tpu as pltpu
@@ -34,13 +35,13 @@
     token_position = token[:, 0] - jnp.sum(jnp.where(inside, starts[None, :], 0), axis=1)
     token_target = jnp.sum(jnp.where(inside, my_targets[None, :], 0), axis=1)
     received = jnp.sum(jnp.where(destinations == row_index, lengths, 0), axis=1)
-    step = jnp.repeat(jnp.arange(steps, dtype=jnp.int32), requests)
-    new_target = jnp.tile(jnp.arange(requests, dtype=jnp.int32), steps)
+    step = np.repeat(np.arange(steps, dtype=np.int32), requests)
+    new_target = np.tile(np.arange(requests, dtype=np.int32), steps)
     new_position = jnp.tile(received, steps) + step
-    spare = jnp.zeros((padded - requests * steps,), jnp.int32)
-    target = jnp.concatenate([token_target, new_target, spare - 1])
-    seen_from = jnp.concatenate([jnp.zeros_like(token_target), step, spare])
-    query_info = jnp.stack([new_target, step], 1)
+    spare = np.zeros((padded - requests * steps,), np.int32)
+    target = jnp.concatenate([token_target, np.concatenate([new_target, spare - 1])])
+    seen_from = jnp.asarray(np.concatenate([np.zeros((tokens,), np.int32), step, spare]))
+    query_info = jnp.asarray(np.stack([new_target, step], 1))
     return token_position, new_position, jnp.stack([target, seen_from], 0), query_info
 
 
@@ -112,32 +113,29 @@
     )(*operands)
 
 
-def own_kernel(side_ref, weight_ref, *out_refs):
-    chunk = out_refs[0].shape[1] // 2
+def own_kernel(side_ref, weight_ref, out_ref):
+    chunk = weight_ref.shape[2]
     for kind in range(2):
-        columns = weight_ref[:, kind, :]
-        for c, out_ref in enumerate(out_refs):
-            out_ref[:, kind * chunk : (kind + 1) * chunk] = columns[:, c * chunk : (c + 1) * chunk]
-
-
-def own_half(weight, side):
+        out_ref[:, kind * chunk : (kind + 1) * chunk] = weight_ref[:, kind, :]
+
+
+def own_half(weight, side, c):
     depth, kinds, width = weight.shape
-    half = depth // 2
-    chunk = kinds * width // CHUNKS
+    half, chunk = depth // 2, width // CHUNKS
     return pl.pallas_call(
         own_kernel,
-        out_shape=[jax.ShapeDtypeStruct((half, chunk), weight.dtype)] * CHUNKS,
+        out_shape=jax.ShapeDtypeStruct((half, kinds * chunk), weight.dtype),
         grid_spec=pltpu.PrefetchScalarGridSpec(
             num_scalar_prefetch=1,
             grid=(2,),
             in_specs=[
-                pl.BlockSpec((half // 2, kinds, width), lambda i, s: (2 * s[0] + i, 0, 0))
+                pl.BlockSpec((half // 2, kinds, chunk), lambda i, s: (2 * s[0] + i, 0, c))
             ],
-            out_specs=[pl.BlockSpec((half // 2, chunk), lambda i, s: (i, 0))] * CHUNKS,
+            out_specs=pl.BlockSpec((half // 2, kinds * chunk), lambda i, s: (i, 0)),
         ),
         compiler_params=pltpu.CompilerParams(vmem_limit_bytes=VMEM_BYTES),
         cost_estimate=pl.CostEstimate(
-            flops=0, bytes_accessed=8 * half * width * kinds, transcendentals=0
+            flops=0, bytes_accessed=8 * half * chunk * kinds, transcendentals=0
         ),
         name="own_half",
     )(side.reshape(1), weight)
@@ -293,9 +291,9 @@
     owners = lax.dynamic_index_in_dim(jnp.array(shard_order, jnp.int32), row_index, 1, keepdims=False)
     places = ((owners // half_rows) ^ core) * half_rows + owners % half_rows
 
-    own = own_half(kv_weight, side)
-
-    ring, ends = [[(piece, piece)] for piece in own], [None, None]
+    own = [own_half(kv_weight, side, 0)]
+
+    ring, ends = [[(own[0], own[0])]], [None, None]
 
     def halved(pair):
         return pair[0][: half // 2], pair[1][half // 2 :]
@@ -324,25 +322,29 @@
 
     cuts = (0, 3 * tokens // 20, 23 * tokens // 40, tokens)
     sent = [pick_columns(passages, 1 - side, half, cuts[0], cuts[1])]
-    (passages_later, new_hidden) = fence_with(0, passages, new_hidden)
+    passages_later, new_hidden, weight_later = fence_with(0, passages, new_hidden, kv_weight)
     got = [lax.ppermute(sent[0], "groups", partners)]
     step(0)
     passages = passages_later
+    own.append(own_half(weight_later, side, 1))
+    ring.append([(own[1], own[1])])
     sent += [pick_columns(passages, 1 - side, half, *cuts[i : i + 2]) for i in (1, 2)]
     kept = pick_columns(passages, side, half, 0, tokens)
     new_rows = jnp.swapaxes(new_hidden, 0, 1).reshape(count, half_model)
     new_rows = jnp.pad(new_rows, ((0, new_padded - count), (0, 0)))
     new_sent = pick_columns(new_rows, 1 - side, half, 0, new_padded)
     new_kept = pick_columns(new_rows, side, half, 0, new_padded)
-    got[0], sent, kept, new_sent, new_kept, lengths, destinations = fence_with(
-        0, got[0], sent, kept, new_sent, new_kept, lengths, destinations
+    got[0], sent, kept, new_sent, new_kept, ring[1][0] = fence_with(
+        0, got[0], sent, kept, new_sent, new_kept, ring[1][0]
     )
 
     got.append(lax.ppermute(sent[1], "groups", partners))
     step(0)
     kept_other = lax.ppermute(kept, "tensor", cores)
     got_other = [lax.ppermute(got[0], "tensor", cores)]
-    kept_other, got_other = fence_with(1, kept_other, got_other)
+    kept_other, got_other, lengths, destinations = fence_with(
+        1, kept_other, got_other, lengths, destinations
+    )
     step(1)
     position, new_position, key_info, query_info = token_tables(
         lengths, destinations, row_index, tokens, requests, steps, new_padded

time: 152 us -> 153 us (level)
  waiting for transfers between devices: 52.5 us -> 44.6 us
  Pallas kernels: 29.8 us -> 34.1 us
  other arithmetic: 6.32 us -> 10.6 us
    ppermute x8, waiting for transfers between devices: 17.6 us -> 10.4 us  [step(): lax.ppermute(pair[0], 'rows', onward)]
    pallas_call x7, Pallas kernels: 22.3 us -> 25.5 us  [products(): pl.pallas_call(functools.partial(product_kernel, depths, len(hidden), bas...]
    pallas_call x1 -> x2, Pallas kernels: 2.33 us -> 3.37 us  [own_half(): pl.pallas_call(own_kernel, out_shape=jax.ShapeDtypeStruct((half, kinds *...]
    unnamed x73 -> x69, local copies, waits for them, and re-layouts: 14.5 us -> 13.7 us
  transfers between devices with their start and end apart: 29 -> 29, of which waited for: 16 -> 17; matrix products, arithmetic and copies ran while one was open for 5% -> 8% of each run, Pallas kernels for 16% -> 19%
where the time goes in v14:
time: 153 us; the launch traced here: 152 us
  waiting for transfers between devices  44.6 us (29%)
  Pallas kernels  34.1 us (22%)
  starting transfers between devices  30.7 us (20%)
  local copies, waits for them, and re-layouts  18.2 us (12%)
  blocking collectives  12.9 us (8%)
  other arithmetic  10.6 us (7%)
    pallas_call x7, Pallas kernels, products(): pl.pallas_call(functools.partial(product_kernel, depths, len(hidden), bas...  25.5 us
    ppermute x8, starting transfers between devices, step(): lax.ppermute(pair[0], 'rows', onward)  14.2 us
    unnamed x69, local copies, waits for them, and re-layouts  13.7 us
    all_to_all x1, blocking collectives, body(): lax.all_to_all(attended, 'rows', split_axis=0, concat_axis=0, tiled=True)  12.9 us
    ppermute x8, waiting for transfers between devices, step(): lax.ppermute(pair[0], 'rows', onward)  10.4 us
    ppermute x1, waiting for transfers between devices, body(): got.append(lax.ppermute(sent[2], 'groups', partners))  9.79 us
    ppermute x1, waiting for transfers between devices, body(): got.append(lax.ppermute(sent[1], 'groups', partners))  8.54 us
    ppermute x8, waiting for transfers between devices, step(): lax.ppermute(pair[1], 'rows', back)  6.1 us
  transfers between devices with their start and end apart: 29, of which 17 were waited for; matrix products, arithmetic and copies ran while one was open for 8% of the time, Pallas kernels for 19%

profile of v14, /device:TPU:0, one launch (start us, length us, event | category | flops | bytes accessed | tf_op | source)
XLA Modules:
  0.0 151.8 jit_solution(4200051870929423009)
XLA Ops:
  1.6 2.0 %own_half.2.refs_3_.refs_9_ = bf16[512,512]{1,0:T(8,128)(2,1)} custom-call(s32[1]{0:T(128)} %bitcast.side_ref, bf16[1024,2,512]{2,1,0:T(2,128)(2,1)S(1)} %copy-done.2), custom_call_target="tpu_custom_call" | custom-call | bytes 2097152 | tf_op jit(solution)/shard_map/own_half/pallas_call | solution.py:125
  3.6 3.0 %collective-permute-start = (bf16[512,512]{1,0:T(8,128)(2,1)}, bf16[512,512]{1,0:T(8,128)(2,1)}, u32[]{:S(2)}, u32[]{:S(2)}) collective-permute-start(bf16[512,512]{1,0:T(8,128)(2,1)} %own_half.2.refs_3_.refs_9_), channel_id=1, source_target_pairs={{0,4},{4,8},{8,12},{12,14},{14,10},{10,6},{6,2},{2,0},{1,5},{5,9},... | collective-permute-start | bytes 1572872 | tf_op jit(solution)/shard_map/ppermute | solution.py:305
  6.7 2.5 %copy-done = bf16[640,4096]{1,0:T(8,128)(2,1)S(1)} copy-done((bf16[640,4096]{1,0:T(8,128)(2,1)S(1)}, bf16[640,4096]{1,0:T(8,128)(2,1)}, u32[]{:S(2)}) %copy-start) | copy-done | bytes 5242904
  9.5 2.0 %collective-permute-start.2 = (bf16[96,2048]{1,0:T(8,128)(2,1)S(1)}, bf16[96,2048]{1,0:T(8,128)(2,1)S(1)}, u32[]{:S(2)}, u32[]{:S(2)}) collective-permute-start(bf16[96,2048]{1,0:T(8,128)(2,1)S(1)} %pick_columns.6), channel_id=1, source_target_pairs={{0,16},{16,0},{1,17},{17,1},{2,18},{18,2},{3,19},{19,3},{4,20},{20... | collective-permute-start | bytes 1179656 | tf_op jit(solution)/shard_map/ppermute | solution.py:326
  17.7 2.5 %collective-permute-done.2.refs_1_ = bf16[96,2048]{1,0:T(8,128)(2,1)S(1)} collective-permute-done((bf16[96,2048]{1,0:T(8,128)(2,1)S(1)}, bf16[96,2048]{1,0:T(8,128)(2,1)S(1)}, u32[]{:S(2)}, u32[]{:S(2)}) %collective-permute-start.2) | collective-permute-done | bytes 393248 | tf_op jit(solution)/shard_map/ppermute | solution.py:326
  28.9 1.6 %collective-permute-start.8 = (bf16[512,512]{1,0:T(8,128)(2,1)S(1)}, bf16[512,512]{1,0:T(8,128)(2,1)S(1)}, u32[]{:S(2)}, u32[]{:S(2)}) collective-permute-start(bf16[512,512]{1,0:T(8,128)(2,1)S(1)} %own_half.3.refs_3_.refs_9_), channel_id=1, source_target_pairs={{0,4},{4,8},{8,12},{12,14},{14,10},{10,6},{6,2},{2,0},{1,5},{5,9},... | collective-permute-start | bytes 1572872 | tf_op jit(solution)/shard_map/ppermute | solution.py:305
  33.3 1.8 %multiply_cosine_fusion = (f32[640,64]{1,0:T(8,128)S(1)}, f32[640,64]{1,0:T(8,128)S(1)}) fusion(f32[64]{0:T(128)} %multiply_exponential_fusion, f32[640]{0:T(1024)S(1)} %subtract_convert_fusion), kind=kLoop, calls=%fused_computation.7 | loop fusion | flops 40960 | bytes 330496 | tf_op jit(solution)/shard_map/cos | solution.py:25
  36.0 2.8 %collective-permute-done.3.refs_6_.refs_12_ = bf16[512,512]{1,0:T(8,128)(2,1)} collective-permute-done((bf16[512,512]{1,0:T(8,128)(2,1)}, bf16[512,512]{1,0:T(8,128)(2,1)}, u32[]{:S(2)}, u32[]{:S(2)}) %collective-permute-start.3) | collective-permute-done | bytes 524320 | tf_op jit(solution)/shard_map/ppermute | solution.py:305
  40.4 8.5 %collective-permute-done.5.refs_3_ = bf16[272,2048]{1,0:T(8,128)(2,1)} collective-permute-done((bf16[272,2048]{1,0:T(8,128)(2,1)}, bf16[272,2048]{1,0:T(8,128)(2,1)}, u32[]{:S(2)}, u32[]{:S(2)}) %collective-permute-start.5) | collective-permute-done | bytes 1114144 | tf_op jit(solution)/shard_map/ppermute | solution.py:341
  55.0 4.3 %products.7.refs_7_ = f32[640,512]{1,0:T(8,128)S(1)} custom-call(s32[8]{0:T(128)S(1)} %fusion.3.refs_0_, bf16[640,2048]{1,0:T(8,128)(2,1)S(1)} %pick_columns.9.refs_1_, bf16[640,2048]{1,0:T(8,128)(2,1)} %collective-permute-done.6.refs_2_, bf16[512,512]{1,0:T(8,128)(2,1)} %own_half.2.refs_3_.refs_9_, bf16[512,512]{1,0:T(8,128)(2,1)} %collective-permute-done.refs_4_.refs_10_, ...), custom_call_target="tpu_custom_call" | custom-call | flops 1677721600 | bytes 7208960 | tf_op jit(solution)/shard_map/products/pallas_call | solution.py:237
  59.3 6.2 %collective-permute-done.10.refs_14_.refs_3_ = bf16[512,512]{1,0:T(8,128)(2,1)S(1)} collective-permute-done((bf16[512,512]{1,0:T(8,128)(2,1)}, bf16[512,512]{1,0:T(8,128)(2,1)S(1)}, u32[]{:S(2)}, u32[]{:S(2)}) %collective-permute-start.10) | collective-permute-done | bytes 524320 | tf_op jit(solution)/shard_map/ppermute | solution.py:305
  67.2 9.8 %collective-permute-done.12.refs_5_ = bf16[272,2048]{1,0:T(8,128)(2,1)S(1)} collective-permute-done((bf16[272,2048]{1,0:T(8,128)(2,1)S(1)}, bf16[272,2048]{1,0:T(8,128)(2,1)S(1)}, u32[]{:S(2)}, u32[]{:S(2)}) %collective-permute-start.12) | collective-permute-done | bytes 1114144 | tf_op jit(solution)/shard_map/ppermute | solution.py:358
  78.8 1.6 %collective-permute-start.21 = (bf16[256,512]{1,0:T(8,128)(2,1)S(1)}, bf16[256,512]{1,0:T(8,128)(2,1)S(1)}, u32[]{:S(2)}, u32[]{:S(2)}) collective-permute-start(bf16[256,512]{1,0:T(8,128)(2,1)S(1)} %slice.48), channel_id=1, source_target_pairs={{0,4},{4,8},{8,12},{12,14},{14,10},{10,6},{6,2},{2,0},{1,5},{5,9},... | collective-permute-start | bytes 786440 | tf_op jit(solution)/shard_map/ppermute | solution.py:305
  80.9 2.3 %collective-permute-done.19 = bf16[32,2048]{1,0:T(8,128)(2,1)S(1)} collective-permute-done((bf16[32,2048]{1,0:T(8,128)(2,1)S(1)}, bf16[32,2048]{1,0:T(8,128)(2,1)S(1)}, u32[]{:S(2)}, u32[]{:S(2)}) %collective-permute-start.19) | collective-permute-done | bytes 131104 | tf_op jit(solution)/shard_map/ppermute | solution.py:375
  85.4 3.6 %products.8.refs_7_ = f32[640,512]{1,0:T(8,128)S(1)} custom-call(s32[8]{0:T(128)S(1)} %fusion.3.refs_0_, bf16[640,2048]{1,0:T(8,128)(2,1)S(1)} %pick_columns.9.refs_1_, bf16[640,2048]{1,0:T(8,128)(2,1)} %collective-permute-done.6.refs_2_, bf16[512,512]{1,0:T(8,128)(2,1)S(1)} %own_half.3.refs_3_.refs_9_, ...), custom_call_target="tpu_custom_call" | custom-call | flops 1677721600 | bytes 7208960 | tf_op jit(solution)/shard_map/products/pallas_call | solution.py:237
  90.2 5.3 %products.9 = f32[704,512]{1,0:T(8,128)S(1)} custom-call(s32[8]{0:T(128)S(1)} %fusion.3.refs_0_, bf16[96,2048]{1,0:T(8,128)(2,1)S(1)} %collective-permute-done.2.refs_1_, bf16[96,2048]{1,0:T(8,128)(2,1)} %collective-permute-done.7.refs_2_, bf16[272,2048]{1,0:T(8,128)(2,1)} %collective-permute-done.5.refs_3_, ...), custom_call_target="tpu_custom_call" | custom-call | flops 2952790016 | bytes 11403264 | tf_op jit(solution)/shard_map/products/pallas_call | solution.py:237
  102.2 3.0 %products.10.refs_0_ = f32[640,512]{1,0:T(8,128)S(1)} custom-call(s32[8]{0:T(128)S(1)} %fusion.3.refs_0_, bf16[640,2048]{1,0:T(8,128)(2,1)S(1)} %pick_columns.9.refs_1_, bf16[640,2048]{1,0:T(8,128)(2,1)} %collective-permute-done.6.refs_2_, bf16[512,512]{1,0:T(8,128)(2,1)S(1)} %collective-permute-done.10.refs_14_.refs_3_, ...), custom_call_target="tpu_custom_call" | custom-call | flops 1006632960 | bytes 4849664 | tf_op jit(solution)/shard_map/products/pallas_call | solution.py:237
  106.3 4.2 %products.11.refs_11_ = f32[704,512]{1,0:T(8,128)S(1)} custom-call(s32[8]{0:T(128)S(1)} %fusion.3.refs_0_, bf16[96,2048]{1,0:T(8,128)(2,1)S(1)} %collective-permute-done.2.refs_1_, bf16[96,2048]{1,0:T(8,128)(2,1)} %collective-permute-done.7.refs_2_, bf16[272,2048]{1,0:T(8,128)(2,1)} %collective-permute-done.5.refs_3_, ...), custom_call_target="tpu_custom_call" | custom-call | flops 2583691264 | bytes 10158080 | tf_op jit(solution)/shard_map/products/pallas_call | solution.py:237
  110.5 2.1 %products.12 = f32[704,512]{1,0:T(8,128)S(1)} custom-call(s32[8]{0:T(128)S(1)} %fusion.3.refs_0_, bf16[96,2048]{1,0:T(8,128)(2,1)S(1)} %collective-permute-done.2.refs_1_, bf16[96,2048]{1,0:T(8,128)(2,1)} %collective-permute-done.7.refs_2_, bf16[272,2048]{1,0:T(8,128)(2,1)} %collective-permute-done.5.refs_3_, ...), custom_call_target="tpu_custom_call" | custom-call | flops 369098752 | bytes 2686976 | tf_op jit(solution)/shard_map/products/pallas_call | solution.py:237
  114.4 3.3 %collective-permute-done.25.refs_1_ = f32[32,1024]{1,0:T(8,128)S(1)} collective-permute-done((f32[32,1024]{1,0:T(8,128)S(1)}, f32[32,1024]{1,0:T(8,128)S(1)}, u32[]{:S(2)}, u32[]{:S(2)}) %collective-permute-start.25) | collective-permute-done | bytes 131104 | tf_op jit(solution)/shard_map/ppermute | solution.py:393
  119.5 4.1 %all-to-all-start = ((bf16[8,3,5120]{2,1,0:T(4,128)(2,1)}), bf16[8,3,5120]{2,1,0:T(4,128)(2,1)}, u32[]{:S(2)}, u32[]{:S(2)}) async-start(bf16[8,3,5120]{2,1,0:T(4,128)(2,1)} %bitcast.38), calls=%async_computation | async-start | bytes 655360 | tf_op jit(solution)/shard_map/all_to_all | solution.py:406
  126.9 3.0 %products.13.refs_1_ = f32[640,512]{1,0:T(8,128)S(1)} custom-call(s32[8]{0:T(128)S(1)} %fusion.3.refs_0_, bf16[640,2048]{1,0:T(8,128)(2,1)S(1)} %pick_columns.9.refs_1_, bf16[640,2048]{1,0:T(8,128)(2,1)} %collective-permute-done.6.refs_2_, bf16[512,512]{1,0:T(8,128)(2,1)S(1)} %copy-done.12, bf16[512,512]{1,0:T(8,128)(2,1)S(1)} %copy-done.14, ...), custom_call_target="tpu_custom_call" | custom-call | flops 1006632960 | bytes 4849664 | tf_op jit(solution)/shard_map/products/pallas_call | solution.py:237
  135.0 2.9 %rotate_attend.1 = bf16[24,4096]{1,0:T(8,128)(2,1)S(1)} custom-call(f32[640,512]{1,0:T(8,128)S(1)} %copy-done.8, f32[640,512]{1,0:T(8,128)S(1)} %copy-done.10, f32[640,512]{1,0:T(8,128)S(1)} %convert_multiply_fusion.1.refs_2_, f32[640,512]{1,0:T(8,128)S(1)} %convert_multiply_fusion.refs_3_, f32[640,128]{1,0:T(8,128)S(1)} %copy-done.15, ...), custom_call_target="tpu_custom_call" | custom-call | flops 251658240 | bytes 5636096 | tf_op jit(solution)/shard_map/rotate_attend/pallas_call | solution.py:101
  138.1 12.9 %all_to_all.10 = bf16[8,3,4096]{2,1,0:T(4,128)(2,1)S(1)} all-to-all(bf16[8,3,4096]{2,1,0:T(4,128)(2,1)S(1)} %bitcast.39), channel_id=1, replica_groups=mesh['groups'=2,'rows'=8,'tensor'=2] {'rows'}, dimensions={0} | all-to-all | bytes 393216 | tf_op jit(solution)/shard_map/all_to_all | solution.py:414
  (161 shorter events, 55.8 us)
Async XLA Ops:
  3.6 16.5 %collective-permute-start = (bf16[512,512]{1,0:T(8,128)(2,1)}, bf16[512,512]{1,0:T(8,128)(2,1)}, u32[]{:S(2)}, u32[]{:S(2)}) collective-permute-start(bf16[512,512]{1,0:T(8,128)(2,1)} %own_half.2.refs_3_.refs_9_), channel_id=1, source_target_pairs={{0,4},{4,8},{8,12},{12,14},{14,10},{10,6},{6,2},{2,0},{1,5},{5,9},... | collective-permute-start | bytes 1572872 | tf_op jit(solution)/shard_map/ppermute | solution.py:305
  6.7 13.7 %collective-permute-start.1 = (bf16[512,512]{1,0:T(8,128)(2,1)}, bf16[512,512]{1,0:T(8,128)(2,1)}, u32[]{:S(2)}, u32[]{:S(2)}) collective-permute-start(bf16[512,512]{1,0:T(8,128)(2,1)} %own_half.2.refs_3_.refs_9_), channel_id=1, source_target_pairs={{4,0},{8,4},{12,8},{14,12},{10,14},{6,10},{2,6},{0,2},{5,1},{9,5},... | collective-permute-start | bytes 1572872 | tf_op jit(solution)/shard_map/ppermute | solution.py:305
  9.5 10.6 %collective-permute-start.2 = (bf16[96,2048]{1,0:T(8,128)(2,1)S(1)}, bf16[96,2048]{1,0:T(8,128)(2,1)S(1)}, u32[]{:S(2)}, u32[]{:S(2)}) collective-permute-start(bf16[96,2048]{1,0:T(8,128)(2,1)S(1)} %pick_columns.6), channel_id=1, source_target_pairs={{0,16},{16,0},{1,17},{17,1},{2,18},{18,2},{3,19},{19,3},{4,20},{20... | collective-permute-start | bytes 1179656 | tf_op jit(solution)/shard_map/ppermute | solution.py:326
  22.1 26.9 %collective-permute-start.5 = (bf16[272,2048]{1,0:T(8,128)(2,1)}, bf16[272,2048]{1,0:T(8,128)(2,1)}, u32[]{:S(2)}, u32[]{:S(2)}) collective-permute-start(bf16[272,2048]{1,0:T(8,128)(2,1)} %copy-done.18), channel_id=1, source_target_pairs={{0,16},{16,0},{1,17},{17,1},{2,18},{18,2},{3,19},{19,3},{4,20},{20... | collective-permute-start | bytes 3342344 | tf_op jit(solution)/shard_map/ppermute | solution.py:341
  23.7 15.1 %collective-permute-start.3 = (bf16[512,512]{1,0:T(8,128)(2,1)}, bf16[512,512]{1,0:T(8,128)(2,1)}, u32[]{:S(2)}, u32[]{:S(2)}) collective-permute-start(bf16[512,512]{1,0:T(8,128)(2,1)} %collective-permute-done.refs_4_.refs_10_), channel_id=1, source_target_pairs={{0,4},{4,8},{8,12},{12,14},{14,10},{10,6},{6,2},{2,0},{1,5},{5,9},... | collective-permute-start | bytes 1572872 | tf_op jit(solution)/shard_map/ppermute | solution.py:305
  25.2 15.2 %collective-permute-start.4 = (bf16[512,512]{1,0:T(8,128)(2,1)}, bf16[512,512]{1,0:T(8,128)(2,1)}, u32[]{:S(2)}, u32[]{:S(2)}) collective-permute-start(bf16[512,512]{1,0:T(8,128)(2,1)} %collective-permute-done.1.refs_5_.refs_11_), channel_id=1, source_target_pairs={{4,0},{8,4},{12,8},{14,12},{10,14},{6,10},{2,6},{0,2},{5,1},{9,5},... | collective-permute-start | bytes 1572872 | tf_op jit(solution)/shard_map/ppermute | solution.py:305
  28.9 20.1 %collective-permute-start.8 = (bf16[512,512]{1,0:T(8,128)(2,1)S(1)}, bf16[512,512]{1,0:T(8,128)(2,1)S(1)}, u32[]{:S(2)}, u32[]{:S(2)}) collective-permute-start(bf16[512,512]{1,0:T(8,128)(2,1)S(1)} %own_half.3.refs_3_.refs_9_), channel_id=1, source_target_pairs={{0,4},{4,8},{8,12},{12,14},{14,10},{10,6},{6,2},{2,0},{1,5},{5,9},... | collective-permute-start | bytes 1572872 | tf_op jit(solution)/shard_map/ppermute | solution.py:305
  30.5 19.5 %collective-permute-start.9 = (bf16[512,512]{1,0:T(8,128)(2,1)S(1)}, bf16[512,512]{1,0:T(8,128)(2,1)S(1)}, u32[]{:S(2)}, u32[]{:S(2)}) collective-permute-start(bf16[512,512]{1,0:T(8,128)(2,1)S(1)} %own_half.3.refs_3_.refs_9_), channel_id=1, source_target_pairs={{4,0},{8,4},{12,8},{14,12},{10,14},{6,10},{2,6},{0,2},{5,1},{9,5},... | collective-permute-start | bytes 1572872 | tf_op jit(solution)/shard_map/ppermute | solution.py:305
  50.0 27.0 %collective-permute-start.12 = (bf16[272,2048]{1,0:T(8,128)(2,1)S(1)}, bf16[272,2048]{1,0:T(8,128)(2,1)S(1)}, u32[]{:S(2)}, u32[]{:S(2)}) collective-permute-start(bf16[272,2048]{1,0:T(8,128)(2,1)S(1)} %copy-done.17), channel_id=1, source_target_pairs={{0,16},{16,0},{1,17},{17,1},{2,18},{18,2},{3,19},{19,3},{4,20},{20... | collective-permute-start | bytes 3342344 | tf_op jit(solution)/shard_map/ppermute | solution.py:358
  50.6 15.0 %collective-permute-start.10 = (bf16[512,512]{1,0:T(8,128)(2,1)}, bf16[512,512]{1,0:T(8,128)(2,1)S(1)}, u32[]{:S(2)}, u32[]{:S(2)}) collective-permute-start(bf16[512,512]{1,0:T(8,128)(2,1)} %collective-permute-done.3.refs_6_.refs_12_), channel_id=1, source_target_pairs={{0,4},{4,8},{8,12},{12,14},{14,10},{10,6},{6,2},{2,0},{1,5},{5,9},... | collective-permute-start | bytes 1572872 | tf_op jit(solution)/shard_map/ppermute | solution.py:305
  52.2 15.0 %collective-permute-start.11 = (bf16[512,512]{1,0:T(8,128)(2,1)}, bf16[512,512]{1,0:T(8,128)(2,1)S(1)}, u32[]{:S(2)}, u32[]{:S(2)}) collective-permute-start(bf16[512,512]{1,0:T(8,128)(2,1)} %collective-permute-done.4.refs_7_.refs_13_), channel_id=1, source_target_pairs={{4,0},{8,4},{12,8},{14,12},{10,14},{6,10},{2,6},{0,2},{5,1},{9,5},... | collective-permute-start | bytes 1572872 | tf_op jit(solution)/shard_map/ppermute | solution.py:305
  53.0 24.0 %collective-permute-start.14 = (bf16[512,512]{1,0:T(8,128)(2,1)S(1)}, bf16[512,512]{1,0:T(8,128)(2,1)S(1)}, u32[]{:S(2)}, u32[]{:S(2)}) collective-permute-start(bf16[512,512]{1,0:T(8,128)(2,1)S(1)} %collective-permute-done.8.refs_4_.refs_10_), channel_id=1, source_target_pairs={{0,4},{4,8},{8,12},{12,14},{14,10},{10,6},{6,2},{2,0},{1,5},{5,9},... | collective-permute-start | bytes 1572872 | tf_op jit(solution)/shard_map/ppermute | solution.py:305
  54.5 22.8 %collective-permute-start.15 = (bf16[512,512]{1,0:T(8,128)(2,1)S(1)}, bf16[512,512]{1,0:T(8,128)(2,1)S(1)}, u32[]{:S(2)}, u32[]{:S(2)}) collective-permute-start(bf16[512,512]{1,0:T(8,128)(2,1)S(1)} %collective-permute-done.9.refs_5_.refs_11_), channel_id=1, source_target_pairs={{4,0},{8,4},{12,8},{14,12},{10,14},{6,10},{2,6},{0,2},{5,1},{9,5},... | collective-permute-start | bytes 1572872 | tf_op jit(solution)/shard_map/ppermute | solution.py:305
  77.3 6.0 %collective-permute-start.16 = (bf16[272,2048]{1,0:T(8,128)(2,1)S(1)}, bf16[272,2048]{1,0:T(8,128)(2,1)S(1)}, u32[]{:S(2)}, u32[]{:S(2)}) collective-permute-start(bf16[272,2048]{1,0:T(8,128)(2,1)S(1)} %collective-permute-done.12.refs_5_), channel_id=1, source_target_pairs={{0,1},{1,0},{2,3},{3,2},{4,5},{5,4},{6,7},{7,6},{8,9},{9,8},{10,11... | collective-permute-start | bytes 3342344 | tf_op jit(solution)/shard_map/ppermute | solution.py:374
  78.8 11.3 %collective-permute-start.21 = (bf16[256,512]{1,0:T(8,128)(2,1)S(1)}, bf16[256,512]{1,0:T(8,128)(2,1)S(1)}, u32[]{:S(2)}, u32[]{:S(2)}) collective-permute-start(bf16[256,512]{1,0:T(8,128)(2,1)S(1)} %slice.48), channel_id=1, source_target_pairs={{0,4},{4,8},{8,12},{12,14},{14,10},{10,6},{6,2},{2,0},{1,5},{5,9},... | collective-permute-start | bytes 786440 | tf_op jit(solution)/shard_map/ppermute | solution.py:305
  80.5 9.7 %collective-permute-start.22 = (bf16[256,512]{1,0:T(8,128)(2,1)S(1)}, bf16[256,512]{1,0:T(8,128)(2,1)S(1)}, u32[]{:S(2)}, u32[]{:S(2)}) collective-permute-start(bf16[256,512]{1,0:T(8,128)(2,1)S(1)} %slice.49), channel_id=1, source_target_pairs={{4,0},{8,4},{12,8},{14,12},{10,14},{6,10},{2,6},{0,2},{5,1},{9,5},... | collective-permute-start | bytes 786440 | tf_op jit(solution)/shard_map/ppermute | solution.py:305
  83.3 6.9 %collective-permute-start.20 = (bf16[64,2048]{1,0:T(8,128)(2,1)S(1)}, bf16[64,2048]{1,0:T(8,128)(2,1)S(1)}, u32[]{:S(2)}, u32[]{:S(2)}) collective-permute-start(bf16[64,2048]{1,0:T(8,128)(2,1)S(1)} %constant_dynamic-update-slice_fusion.refs_7_), channel_id=1, source_target_pairs={{0,1},{1,0},{2,3},{3,2},{4,5},{5,4},{6,7},{7,6},{8,9},{9,8},{10,11... | collective-permute-start | bytes 786440 | tf_op jit(solution)/shard_map/ppermute | solution.py:376
  83.3 15.2 %collective-permute-start.17 = (bf16[512,512]{1,0:T(8,128)(2,1)S(1)}, bf16[512,512]{1,0:T(8,128)(2,1)S(1)}, u32[]{:S(2)}, u32[]{:S(2)}) collective-permute-start(bf16[512,512]{1,0:T(8,128)(2,1)S(1)} %collective-permute-done.14.refs_6_.refs_12_), channel_id=1, source_target_pairs={{0,4},{4,8},{8,12},{12,14},{14,10},{10,6},{6,2},{2,0},{1,5},{5,9},... | collective-permute-start | bytes 1572872 | tf_op jit(solution)/shard_map/ppermute | solution.py:305
  85.0 14.9 %collective-permute-start.18 = (bf16[512,512]{1,0:T(8,128)(2,1)S(1)}, bf16[512,512]{1,0:T(8,128)(2,1)S(1)}, u32[]{:S(2)}, u32[]{:S(2)}) collective-permute-start(bf16[512,512]{1,0:T(8,128)(2,1)S(1)} %collective-permute-done.15.refs_7_.refs_13_), channel_id=1, source_target_pairs={{4,0},{8,4},{12,8},{14,12},{10,14},{6,10},{2,6},{0,2},{5,1},{9,5},... | collective-permute-start | bytes 1572872 | tf_op jit(solution)/shard_map/ppermute | solution.py:305
  95.7 18.7 %collective-permute-start.26 = (f16[640,512]{1,0:T(8,128)(2,1)S(1)}, f16[640,512]{1,0:T(8,128)(2,1)S(1)}, u32[]{:S(2)}, u32[]{:S(2)}) collective-permute-start(f16[640,512]{1,0:T(8,128)(2,1)S(1)} %fusion.1), channel_id=1, source_target_pairs={{0,16},{16,0},{1,17},{17,1},{2,18},{18,2},{3,19},{19,3},{4,20},{20... | collective-permute-start | bytes 1966088 | tf_op jit(solution)/shard_map/ppermute | solution.py:387
  99.9 10.6 %collective-permute-start.23 = (bf16[256,512]{1,0:T(8,128)(2,1)S(1)}, bf16[256,512]{1,0:T(8,128)(2,1)S(1)}, u32[]{:S(2)}, u32[]{:S(2)}) collective-permute-start(bf16[256,512]{1,0:T(8,128)(2,1)S(1)} %slice.41), channel_id=1, source_target_pairs={{0,4},{4,8},{8,12},{12,14},{14,10},{10,6},{6,2},{2,0},{1,5},{5,9},... | collective-permute-start | bytes 786440 | tf_op jit(solution)/shard_map/ppermute | solution.py:305
  101.5 9.0 %collective-permute-start.24 = (bf16[256,512]{1,0:T(8,128)(2,1)S(1)}, bf16[256,512]{1,0:T(8,128)(2,1)S(1)}, u32[]{:S(2)}, u32[]{:S(2)}) collective-permute-start(bf16[256,512]{1,0:T(8,128)(2,1)S(1)} %slice.42), channel_id=1, source_target_pairs={{4,0},{8,4},{12,8},{14,12},{10,14},{6,10},{2,6},{0,2},{5,1},{9,5},... | collective-permute-start | bytes 786440 | tf_op jit(solution)/shard_map/ppermute | solution.py:305
  117.8 15.7 %collective-permute-start.27 = (f16[640,512]{1,0:T(8,128)(2,1)}, f16[640,512]{1,0:T(8,128)(2,1)}, u32[]{:S(2)}, u32[]{:S(2)}) collective-permute-start(f16[640,512]{1,0:T(8,128)(2,1)} %fusion), channel_id=1, source_target_pairs={{0,16},{16,0},{1,17},{17,1},{2,18},{18,2},{3,19},{19,3},{4,20},{20... | collective-permute-start | bytes 1966088 | tf_op jit(solution)/shard_map/ppermute | solution.py:399
  119.5 12.8 %all-to-all-start = ((bf16[8,3,5120]{2,1,0:T(4,128)(2,1)}), bf16[8,3,5120]{2,1,0:T(4,128)(2,1)}, u32[]{:S(2)}, u32[]{:S(2)}) async-start(bf16[8,3,5120]{2,1,0:T(4,128)(2,1)} %bitcast.38), calls=%async_computation | async-start | bytes 655360 | tf_op jit(solution)/shard_map/all_to_all | solution.py:406
  (40 other events, 236.1 us)

commit v15 on v14

--- a/solution.py
+++ b/solution.py
@@ -49,24 +49,25 @@
     return [first * cosine - second * sine, second * cosine + first * sine]
 
 
-def finish_kernel(chunks, group, *refs):
-    held, homed, refs = refs[:chunks], refs[chunks : 2 * chunks], refs[2 * chunks :]
-    angle_ref, keys_ref, rows_ref, new_ref, query_ref, out_ref = refs
+def finish_kernel(c, group, held_ref, homed_ref, angle_ref, keys_ref, rows_ref, new_ref, query_ref, *refs):
+    out_ref = refs[-1]
+    if c > 0:
+        out_ref[:, : refs[0].shape[1]] = refs[0][...]
     cosine, sine = angle_ref[:, :HALF], angle_ref[:, HALF:]
     allowed = (keys_ref[0:1, :] == rows_ref[:, 0:1]) & (keys_ref[1:2, :] <= rows_ref[:, 1:2])
     allowed = jnp.concatenate([allowed.astype(jnp.float32)] * group, 0) > 0.5
     queries = query_ref[...].astype(jnp.float32)
     count = queries.shape[0]
-    width = held[0].shape[1]
+    width = held_ref.shape[1]
     heads = width // (2 * HD)
-    for h in range(chunks * heads):
-        c, local = h // heads, h % heads
+    for local in range(heads):
+        h = c * heads + local
         key_at = slice(local * HD, (local + 1) * HD)
         value_at = slice((heads + local) * HD, (heads + local + 1) * HD)
         new_at = c * width
-        both = held[c][:, key_at] + homed[c][:, key_at]
+        both = held_ref[:, key_at] + homed_ref[:, key_at]
         keys = jnp.concatenate(rotate(both[:, :HALF], both[:, HALF:], cosine, sine), -1)
-        values = held[c][:, value_at] + homed[c][:, value_at]
+        values = held_ref[:, value_at] + homed_ref[:, value_at]
         keys, values = (
             jnp.concatenate(
                 [cached.astype(jnp.bfloat16), new_ref[:, new_at + at.start : new_at + at.stop]], 0
@@ -91,22 +92,24 @@
             ].astype(jnp.bfloat16)
 
 
-def finish(held, homed, angles, key_info, query_info, new_pairs, queries):
-    rows, width = held[0].shape
-    heads = len(held) * width // (2 * HD)
-    group = queries.shape[1] // (heads * HD)
+def finish(c, done, held, homed, angles, key_info, query_info, new_pairs, queries):
+    rows, width = held.shape
+    heads = width // (2 * HD)
+    group = queries.shape[1] // (CHUNKS * heads * HD)
     count = queries.shape[0]
     vmem = pl.BlockSpec(memory_space=pltpu.VMEM)
-    operands = [*held, *homed, angles, key_info, query_info, new_pairs, queries]
+    operands = [held, homed, angles, key_info, query_info, new_pairs, queries]
+    if done is not None:
+        operands.append(done)
     return pl.pallas_call(
-        functools.partial(finish_kernel, len(held), group),
-        out_shape=jax.ShapeDtypeStruct(queries.shape, jnp.bfloat16),
+        functools.partial(finish_kernel, c, group),
+        out_shape=jax.ShapeDtypeStruct((count, (c + 1) * heads * group * HD), jnp.bfloat16),
         in_specs=[vmem] * len(operands),
         out_specs=vmem,
         compiler_params=pltpu.CompilerParams(vmem_limit_bytes=VMEM_BYTES),
         cost_estimate=pl.CostEstimate(
             flops=4 * heads * group * count * rows * HD,
-            bytes_accessed=8 * len(held) * rows * width + 4 * queries.size,
+            bytes_accessed=8 * rows * width + 4 * queries.size,
             transcendentals=heads * group * count * rows,
         ),
         name="rotate_attend",
@@ -393,14 +396,12 @@
     new_back = lax.ppermute(jnp.concatenate(new_away, 1), "groups", partners)
     held[0] = project(0, own_hidden, held[0], early, row_count)
     queries = jnp.swapaxes(queries, 0, 1).reshape(count, -1)
-    held, queries, places, away, new_back, homed[0] = fence(
-        held, queries, places, away, new_back, homed[0]
-    )
+    places, away = fence(places, away)
+    held[1] = project(1, own_hidden, held[1], early, row_count)
+    held, queries, away, new_back, homed[0] = fence(held, queries, away, new_back, homed[0])
     homed.append(lax.ppermute(away[0], "groups", partners))
     angles, new_angles, key_info, query_info = tables
     moved = pack(new_own, new_back, new_angles, queries)
-    moved, places = fence(moved, places)
-    held[1] = project(1, own_hidden, held[1], early, row_count)
     moved = moved.reshape(steps, requests, -1)
     moved = jnp.swapaxes(moved, 0, 1)
     moved = lax.all_to_all(moved, "rows", split_axis=0, concat_axis=0, tiled=True)
@@ -409,7 +410,11 @@
     query_rows, new_pairs = moved[:, :heads_width], moved[:, heads_width:]
     new_pairs = jnp.pad(new_pairs, ((0, new_padded - count), (0, 0)))
     homed = [total.astype(jnp.float32) * (1.0 / RAISE) for total in homed]
-    attended = finish(held, homed, angles, key_info, query_info, new_pairs, query_rows)
+    attended = None
+    for c in range(CHUNKS):
+        attended = finish(
+            c, attended, held[c], homed[c], angles, key_info, query_info, new_pairs, query_rows
+        )
     attended = jnp.swapaxes(attended.reshape(steps, requests, -1), 0, 1)
     return lax.all_to_all(attended, "rows", split_axis=0, concat_axis=0, tiled=True)
 

time: 153 us -> 151 us (0.987)
  local copies, waits for them, and re-layouts: 18.2 us -> 11.6 us
  waiting for transfers between devices: 44.6 us -> 49.1 us
    all_to_all x1, waiting for transfers between devices: 1.05 us -> 7.38 us  [body(): lax.all_to_all(moved, 'rows', split_axis=0, concat_axis=0, tiled=True)]
    unnamed x69 -> x47, local copies, waits for them, and re-layouts: 13.7 us -> 8.28 us
    ppermute x1, waiting for transfers between devices: 3.34 us -> 0.01 us  [body(): new_back = lax.ppermute(jnp.concatenate(new_away, 1), 'groups', partners)]
    pallas_call x1 -> x2, Pallas kernels: 2.89 us -> 3.19 us  [finish(): pl.pallas_call(functools.partial(finish_kernel, c, group), out_shape=jax....]
  transfers between devices with their start and end apart: 29 -> 29, of which waited for: 17 -> 17; matrix products, arithmetic and copies ran while one was open for 8% -> 9% of each run, Pallas kernels for 19% -> 21%
where the time goes in v15:
time: 151 us; the launch traced here: 150 us
  waiting for transfers between devices  49.1 us (33%)
  Pallas kernels  34.7 us (23%)
  starting transfers between devices  30.7 us (20%)
  other arithmetic  11.9 us (8%)
  local copies, waits for them, and re-layouts  11.6 us (8%)
  blocking collectives  11.6 us (8%)
    pallas_call x7, Pallas kernels, products(): pl.pallas_call(functools.partial(product_kernel, depths, len(hidden), bas...  25.8 us
    ppermute x8, starting transfers between devices, step(): lax.ppermute(pair[0], 'rows', onward)  14.2 us
    all_to_all x1, blocking collectives, body(): lax.all_to_all(attended, 'rows', split_axis=0, concat_axis=0, tiled=True)  11.6 us
    ppermute x8, waiting for transfers between devices, step(): lax.ppermute(pair[0], 'rows', onward)  11.6 us
    ppermute x1, waiting for transfers between devices, body(): got.append(lax.ppermute(sent[2], 'groups', partners))  9.79 us
    ppermute x1, waiting for transfers between devices, body(): got.append(lax.ppermute(sent[1], 'groups', partners))  8.54 us
    unnamed x47, local copies, waits for them, and re-layouts  8.28 us
    all_to_all x1, waiting for transfers between devices, body(): lax.all_to_all(moved, 'rows', split_axis=0, concat_axis=0, tiled=True)  7.38 us
  transfers between devices with their start and end apart: 29, of which 17 were waited for; matrix products, arithmetic and copies ran while one was open for 9% of the time, Pallas kernels for 21%

profile of v15, /device:TPU:0, one launch (start us, length us, event | category | flops | bytes accessed | tf_op | source)
XLA Modules:
  0.0 150.2 jit_solution(723387194943516310)
XLA Ops:
  1.6 2.0 %own_half.2.refs_3_.refs_9_ = bf16[512,512]{1,0:T(8,128)(2,1)} custom-call(s32[1]{0:T(128)} %bitcast.side_ref, bf16[1024,2,512]{2,1,0:T(2,128)(2,1)S(1)} %copy-done.2), custom_call_target="tpu_custom_call" | custom-call | bytes 2097152 | tf_op jit(solution)/shard_map/own_half/pallas_call | solution.py:128
  3.6 3.0 %collective-permute-start = (bf16[512,512]{1,0:T(8,128)(2,1)}, bf16[512,512]{1,0:T(8,128)(2,1)}, u32[]{:S(2)}, u32[]{:S(2)}) collective-permute-start(bf16[512,512]{1,0:T(8,128)(2,1)} %own_half.2.refs_3_.refs_9_), channel_id=1, source_target_pairs={{0,4},{4,8},{8,12},{12,14},{14,10},{10,6},{6,2},{2,0},{1,5},{5,9},... | collective-permute-start | bytes 1572872 | tf_op jit(solution)/shard_map/ppermute | solution.py:308
  6.6 2.5 %copy-done = bf16[640,4096]{1,0:T(8,128)(2,1)S(1)} copy-done((bf16[640,4096]{1,0:T(8,128)(2,1)S(1)}, bf16[640,4096]{1,0:T(8,128)(2,1)}, u32[]{:S(2)}) %copy-start) | copy-done | bytes 5242904
  9.5 2.0 %collective-permute-start.2 = (bf16[96,2048]{1,0:T(8,128)(2,1)S(1)}, bf16[96,2048]{1,0:T(8,128)(2,1)S(1)}, u32[]{:S(2)}, u32[]{:S(2)}) collective-permute-start(bf16[96,2048]{1,0:T(8,128)(2,1)S(1)} %pick_columns.6), channel_id=1, source_target_pairs={{0,16},{16,0},{1,17},{17,1},{2,18},{18,2},{3,19},{19,3},{4,20},{20... | collective-permute-start | bytes 1179656 | tf_op jit(solution)/shard_map/ppermute | solution.py:329
  17.7 2.4 %collective-permute-done.2.refs_1_ = bf16[96,2048]{1,0:T(8,128)(2,1)S(1)} collective-permute-done((bf16[96,2048]{1,0:T(8,128)(2,1)S(1)}, bf16[96,2048]{1,0:T(8,128)(2,1)S(1)}, u32[]{:S(2)}, u32[]{:S(2)}) %collective-permute-start.2) | collective-permute-done | bytes 393248 | tf_op jit(solution)/shard_map/ppermute | solution.py:329
  28.7 1.6 %collective-permute-start.8 = (bf16[512,512]{1,0:T(8,128)(2,1)S(1)}, bf16[512,512]{1,0:T(8,128)(2,1)S(1)}, u32[]{:S(2)}, u32[]{:S(2)}) collective-permute-start(bf16[512,512]{1,0:T(8,128)(2,1)S(1)} %own_half.3.refs_3_.refs_9_), channel_id=1, source_target_pairs={{0,4},{4,8},{8,12},{12,14},{14,10},{10,6},{6,2},{2,0},{1,5},{5,9},... | collective-permute-start | bytes 1572872 | tf_op jit(solution)/shard_map/ppermute | solution.py:308
  33.1 1.9 %multiply_cosine_fusion = (f32[640,64]{1,0:T(8,128)S(1)}, f32[640,64]{1,0:T(8,128)S(1)}) fusion(f32[64]{0:T(128)} %multiply_exponential_fusion, f32[640]{0:T(1024)S(1)} %subtract_convert_fusion), kind=kLoop, calls=%fused_computation.7 | loop fusion | flops 40960 | bytes 330496 | tf_op jit(solution)/shard_map/cos | solution.py:25
  35.9 2.9 %collective-permute-done.3.refs_6_.refs_12_ = bf16[512,512]{1,0:T(8,128)(2,1)} collective-permute-done((bf16[512,512]{1,0:T(8,128)(2,1)}, bf16[512,512]{1,0:T(8,128)(2,1)}, u32[]{:S(2)}, u32[]{:S(2)}) %collective-permute-start.3) | collective-permute-done | bytes 524320 | tf_op jit(solution)/shard_map/ppermute | solution.py:308
  40.5 8.5 %collective-permute-done.5.refs_3_ = bf16[272,2048]{1,0:T(8,128)(2,1)} collective-permute-done((bf16[272,2048]{1,0:T(8,128)(2,1)}, bf16[272,2048]{1,0:T(8,128)(2,1)}, u32[]{:S(2)}, u32[]{:S(2)}) %collective-permute-start.5) | collective-permute-done | bytes 1114144 | tf_op jit(solution)/shard_map/ppermute | solution.py:344
  55.0 4.3 %products.7.refs_7_ = f32[640,512]{1,0:T(8,128)S(1)} custom-call(s32[8]{0:T(128)S(1)} %fusion.3.refs_0_, bf16[640,2048]{1,0:T(8,128)(2,1)S(1)} %pick_columns.9.refs_1_, bf16[640,2048]{1,0:T(8,128)(2,1)} %collective-permute-done.6.refs_2_, bf16[512,512]{1,0:T(8,128)(2,1)} %own_half.2.refs_3_.refs_9_, bf16[512,512]{1,0:T(8,128)(2,1)} %collective-permute-done.refs_4_.refs_10_, ...), custom_call_target="tpu_custom_call" | custom-call | flops 1677721600 | bytes 7208960 | tf_op jit(solution)/shard_map/products/pallas_call | solution.py:240
  59.4 6.2 %collective-permute-done.10.refs_14_.refs_3_ = bf16[512,512]{1,0:T(8,128)(2,1)S(1)} collective-permute-done((bf16[512,512]{1,0:T(8,128)(2,1)}, bf16[512,512]{1,0:T(8,128)(2,1)S(1)}, u32[]{:S(2)}, u32[]{:S(2)}) %collective-permute-start.10) | collective-permute-done | bytes 524320 | tf_op jit(solution)/shard_map/ppermute | solution.py:308
  67.2 9.8 %collective-permute-done.12.refs_5_ = bf16[272,2048]{1,0:T(8,128)(2,1)S(1)} collective-permute-done((bf16[272,2048]{1,0:T(8,128)(2,1)S(1)}, bf16[272,2048]{1,0:T(8,128)(2,1)S(1)}, u32[]{:S(2)}, u32[]{:S(2)}) %collective-permute-start.12) | collective-permute-done | bytes 1114144 | tf_op jit(solution)/shard_map/ppermute | solution.py:361
  78.9 1.6 %collective-permute-start.21 = (bf16[256,512]{1,0:T(8,128)(2,1)S(1)}, bf16[256,512]{1,0:T(8,128)(2,1)S(1)}, u32[]{:S(2)}, u32[]{:S(2)}) collective-permute-start(bf16[256,512]{1,0:T(8,128)(2,1)S(1)} %slice.48), channel_id=1, source_target_pairs={{0,4},{4,8},{8,12},{12,14},{14,10},{10,6},{6,2},{2,0},{1,5},{5,9},... | collective-permute-start | bytes 786440 | tf_op jit(solution)/shard_map/ppermute | solution.py:308
  81.0 2.3 %collective-permute-done.19 = bf16[32,2048]{1,0:T(8,128)(2,1)S(1)} collective-permute-done((bf16[32,2048]{1,0:T(8,128)(2,1)S(1)}, bf16[32,2048]{1,0:T(8,128)(2,1)S(1)}, u32[]{:S(2)}, u32[]{:S(2)}) %collective-permute-start.19) | collective-permute-done | bytes 131104 | tf_op jit(solution)/shard_map/ppermute | solution.py:378
  85.5 3.6 %products.8.refs_7_ = f32[640,512]{1,0:T(8,128)S(1)} custom-call(s32[8]{0:T(128)S(1)} %fusion.3.refs_0_, bf16[640,2048]{1,0:T(8,128)(2,1)S(1)} %pick_columns.9.refs_1_, bf16[640,2048]{1,0:T(8,128)(2,1)} %collective-permute-done.6.refs_2_, bf16[512,512]{1,0:T(8,128)(2,1)S(1)} %own_half.3.refs_3_.refs_9_, ...), custom_call_target="tpu_custom_call" | custom-call | flops 1677721600 | bytes 7208960 | tf_op jit(solution)/shard_map/products/pallas_call | solution.py:240
  89.5 5.3 %products.9 = f32[704,512]{1,0:T(8,128)S(1)} custom-call(s32[8]{0:T(128)S(1)} %fusion.3.refs_0_, bf16[96,2048]{1,0:T(8,128)(2,1)S(1)} %collective-permute-done.2.refs_1_, bf16[96,2048]{1,0:T(8,128)(2,1)} %collective-permute-done.7.refs_2_, bf16[272,2048]{1,0:T(8,128)(2,1)} %collective-permute-done.5.refs_3_, ...), custom_call_target="tpu_custom_call" | custom-call | flops 2952790016 | bytes 11403264 | tf_op jit(solution)/shard_map/products/pallas_call | solution.py:240
  96.2 2.4 %collective-permute-done.17.refs_14_.refs_3_ = bf16[512,512]{1,0:T(8,128)(2,1)S(1)} collective-permute-done((bf16[512,512]{1,0:T(8,128)(2,1)S(1)}, bf16[512,512]{1,0:T(8,128)(2,1)S(1)}, u32[]{:S(2)}, u32[]{:S(2)}) %collective-permute-start.17) | collective-permute-done | bytes 524320 | tf_op jit(solution)/shard_map/ppermute | solution.py:308
  102.3 4.2 %products.11.refs_11_ = f32[704,512]{1,0:T(8,128)S(1)} custom-call(s32[8]{0:T(128)S(1)} %fusion.3.refs_0_, bf16[96,2048]{1,0:T(8,128)(2,1)S(1)} %collective-permute-done.2.refs_1_, bf16[96,2048]{1,0:T(8,128)(2,1)} %collective-permute-done.7.refs_2_, bf16[272,2048]{1,0:T(8,128)(2,1)} %collective-permute-done.5.refs_3_, ...), custom_call_target="tpu_custom_call" | custom-call | flops 2583691264 | bytes 10158080 | tf_op jit(solution)/shard_map/products/pallas_call | solution.py:240
  106.5 3.0 %products.10.held_ref = f32[640,512]{1,0:T(8,128)S(1)} custom-call(s32[8]{0:T(128)S(1)} %fusion.3.refs_0_, bf16[640,2048]{1,0:T(8,128)(2,1)S(1)} %pick_columns.9.refs_1_, bf16[640,2048]{1,0:T(8,128)(2,1)} %collective-permute-done.6.refs_2_, bf16[512,512]{1,0:T(8,128)(2,1)S(1)} %collective-permute-done.10.refs_14_.refs_3_, ...), custom_call_target="tpu_custom_call" | custom-call | flops 1006632960 | bytes 4849664 | tf_op jit(solution)/shard_map/products/pallas_call | solution.py:240
  109.5 2.4 %products.12 = f32[704,512]{1,0:T(8,128)S(1)} custom-call(s32[8]{0:T(128)S(1)} %fusion.3.refs_0_, bf16[96,2048]{1,0:T(8,128)(2,1)S(1)} %collective-permute-done.2.refs_1_, bf16[96,2048]{1,0:T(8,128)(2,1)} %collective-permute-done.7.refs_2_, bf16[272,2048]{1,0:T(8,128)(2,1)} %collective-permute-done.5.refs_3_, ...), custom_call_target="tpu_custom_call" | custom-call | flops 369098752 | bytes 2686976 | tf_op jit(solution)/shard_map/products/pallas_call | solution.py:240
  113.6 3.0 %products.13.held_ref = f32[640,512]{1,0:T(8,128)S(1)} custom-call(s32[8]{0:T(128)S(1)} %fusion.3.refs_0_, bf16[640,2048]{1,0:T(8,128)(2,1)S(1)} %pick_columns.9.refs_1_, bf16[640,2048]{1,0:T(8,128)(2,1)} %collective-permute-done.6.refs_2_, bf16[512,512]{1,0:T(8,128)(2,1)S(1)} %collective-permute-done.17.refs_14_.refs_3_, ...), custom_call_target="tpu_custom_call" | custom-call | flops 1006632960 | bytes 4849664 | tf_op jit(solution)/shard_map/products/pallas_call | solution.py:240
  120.3 3.5 %all-to-all-start = ((bf16[8,3,5120]{2,1,0:T(4,128)(2,1)}), bf16[8,3,5120]{2,1,0:T(4,128)(2,1)S(1)}, u32[]{:S(2)}, u32[]{:S(2)}) async-start(bf16[8,3,5120]{2,1,0:T(4,128)(2,1)} %bitcast.32), calls=%async_computation | async-start | bytes 655360 | tf_op jit(solution)/shard_map/all_to_all | solution.py:407
  125.3 7.4 %all-to-all-done = bf16[8,3,5120]{2,1,0:T(4,128)(2,1)S(1)} async-done(((bf16[8,3,5120]{2,1,0:T(4,128)(2,1)}), bf16[8,3,5120]{2,1,0:T(4,128)(2,1)S(1)}, u32[]{:S(2)}, u32[]{:S(2)}) %all-to-all-start) | async-done | bytes 245792 | tf_op jit(solution)/shard_map/all_to_all | solution.py:407
  137.7 11.6 %all_to_all.10 = bf16[8,3,4096]{2,1,0:T(4,128)(2,1)S(1)} all-to-all(bf16[8,3,4096]{2,1,0:T(4,128)(2,1)S(1)} %bitcast.39), channel_id=1, replica_groups=mesh['groups'=2,'rows'=8,'tensor'=2] {'rows'}, dimensions={0} | all-to-all | bytes 393216 | tf_op jit(solution)/shard_map/all_to_all | solution.py:419
  (140 shorter events, 52.1 us)
Async XLA Ops:
  3.6 16.5 %collective-permute-start = (bf16[512,512]{1,0:T(8,128)(2,1)}, bf16[512,512]{1,0:T(8,128)(2,1)}, u32[]{:S(2)}, u32[]{:S(2)}) collective-permute-start(bf16[512,512]{1,0:T(8,128)(2,1)} %own_half.2.refs_3_.refs_9_), channel_id=1, source_target_pairs={{0,4},{4,8},{8,12},{12,14},{14,10},{10,6},{6,2},{2,0},{1,5},{5,9},... | collective-permute-start | bytes 1572872 | tf_op jit(solution)/shard_map/ppermute | solution.py:308
  6.6 13.7 %collective-permute-start.1 = (bf16[512,512]{1,0:T(8,128)(2,1)}, bf16[512,512]{1,0:T(8,128)(2,1)}, u32[]{:S(2)}, u32[]{:S(2)}) collective-permute-start(bf16[512,512]{1,0:T(8,128)(2,1)} %own_half.2.refs_3_.refs_9_), channel_id=1, source_target_pairs={{4,0},{8,4},{12,8},{14,12},{10,14},{6,10},{2,6},{0,2},{5,1},{9,5},... | collective-permute-start | bytes 1572872 | tf_op jit(solution)/shard_map/ppermute | solution.py:308
  9.5 10.6 %collective-permute-start.2 = (bf16[96,2048]{1,0:T(8,128)(2,1)S(1)}, bf16[96,2048]{1,0:T(8,128)(2,1)S(1)}, u32[]{:S(2)}, u32[]{:S(2)}) collective-permute-start(bf16[96,2048]{1,0:T(8,128)(2,1)S(1)} %pick_columns.6), channel_id=1, source_target_pairs={{0,16},{16,0},{1,17},{17,1},{2,18},{18,2},{3,19},{19,3},{4,20},{20... | collective-permute-start | bytes 1179656 | tf_op jit(solution)/shard_map/ppermute | solution.py:329
  22.1 26.9 %collective-permute-start.5 = (bf16[272,2048]{1,0:T(8,128)(2,1)}, bf16[272,2048]{1,0:T(8,128)(2,1)}, u32[]{:S(2)}, u32[]{:S(2)}) collective-permute-start(bf16[272,2048]{1,0:T(8,128)(2,1)} %copy-done.12), channel_id=1, source_target_pairs={{0,16},{16,0},{1,17},{17,1},{2,18},{18,2},{3,19},{19,3},{4,20},{20... | collective-permute-start | bytes 3342344 | tf_op jit(solution)/shard_map/ppermute | solution.py:344
  23.7 15.1 %collective-permute-start.3 = (bf16[512,512]{1,0:T(8,128)(2,1)}, bf16[512,512]{1,0:T(8,128)(2,1)}, u32[]{:S(2)}, u32[]{:S(2)}) collective-permute-start(bf16[512,512]{1,0:T(8,128)(2,1)} %collective-permute-done.refs_4_.refs_10_), channel_id=1, source_target_pairs={{0,4},{4,8},{8,12},{12,14},{14,10},{10,6},{6,2},{2,0},{1,5},{5,9},... | collective-permute-start | bytes 1572872 | tf_op jit(solution)/shard_map/ppermute | solution.py:308
  25.3 15.2 %collective-permute-start.4 = (bf16[512,512]{1,0:T(8,128)(2,1)}, bf16[512,512]{1,0:T(8,128)(2,1)}, u32[]{:S(2)}, u32[]{:S(2)}) collective-permute-start(bf16[512,512]{1,0:T(8,128)(2,1)} %collective-permute-done.1.refs_5_.refs_11_), channel_id=1, source_target_pairs={{4,0},{8,4},{12,8},{14,12},{10,14},{6,10},{2,6},{0,2},{5,1},{9,5},... | collective-permute-start | bytes 1572872 | tf_op jit(solution)/shard_map/ppermute | solution.py:308
  28.7 20.3 %collective-permute-start.8 = (bf16[512,512]{1,0:T(8,128)(2,1)S(1)}, bf16[512,512]{1,0:T(8,128)(2,1)S(1)}, u32[]{:S(2)}, u32[]{:S(2)}) collective-permute-start(bf16[512,512]{1,0:T(8,128)(2,1)S(1)} %own_half.3.refs_3_.refs_9_), channel_id=1, source_target_pairs={{0,4},{4,8},{8,12},{12,14},{14,10},{10,6},{6,2},{2,0},{1,5},{5,9},... | collective-permute-start | bytes 1572872 | tf_op jit(solution)/shard_map/ppermute | solution.py:308
  30.3 19.7 %collective-permute-start.9 = (bf16[512,512]{1,0:T(8,128)(2,1)S(1)}, bf16[512,512]{1,0:T(8,128)(2,1)S(1)}, u32[]{:S(2)}, u32[]{:S(2)}) collective-permute-start(bf16[512,512]{1,0:T(8,128)(2,1)S(1)} %own_half.3.refs_3_.refs_9_), channel_id=1, source_target_pairs={{4,0},{8,4},{12,8},{14,12},{10,14},{6,10},{2,6},{0,2},{5,1},{9,5},... | collective-permute-start | bytes 1572872 | tf_op jit(solution)/shard_map/ppermute | solution.py:308
  50.0 27.0 %collective-permute-start.12 = (bf16[272,2048]{1,0:T(8,128)(2,1)S(1)}, bf16[272,2048]{1,0:T(8,128)(2,1)S(1)}, u32[]{:S(2)}, u32[]{:S(2)}) collective-permute-start(bf16[272,2048]{1,0:T(8,128)(2,1)S(1)} %copy-done.11), channel_id=1, source_target_pairs={{0,16},{16,0},{1,17},{17,1},{2,18},{18,2},{3,19},{19,3},{4,20},{20... | collective-permute-start | bytes 3342344 | tf_op jit(solution)/shard_map/ppermute | solution.py:361
  50.6 15.0 %collective-permute-start.10 = (bf16[512,512]{1,0:T(8,128)(2,1)}, bf16[512,512]{1,0:T(8,128)(2,1)S(1)}, u32[]{:S(2)}, u32[]{:S(2)}) collective-permute-start(bf16[512,512]{1,0:T(8,128)(2,1)} %collective-permute-done.3.refs_6_.refs_12_), channel_id=1, source_target_pairs={{0,4},{4,8},{8,12},{12,14},{14,10},{10,6},{6,2},{2,0},{1,5},{5,9},... | collective-permute-start | bytes 1572872 | tf_op jit(solution)/shard_map/ppermute | solution.py:308
  52.2 15.0 %collective-permute-start.11 = (bf16[512,512]{1,0:T(8,128)(2,1)}, bf16[512,512]{1,0:T(8,128)(2,1)S(1)}, u32[]{:S(2)}, u32[]{:S(2)}) collective-permute-start(bf16[512,512]{1,0:T(8,128)(2,1)} %collective-permute-done.4.refs_7_.refs_13_), channel_id=1, source_target_pairs={{4,0},{8,4},{12,8},{14,12},{10,14},{6,10},{2,6},{0,2},{5,1},{9,5},... | collective-permute-start | bytes 1572872 | tf_op jit(solution)/shard_map/ppermute | solution.py:308
  53.0 24.0 %collective-permute-start.14 = (bf16[512,512]{1,0:T(8,128)(2,1)S(1)}, bf16[512,512]{1,0:T(8,128)(2,1)S(1)}, u32[]{:S(2)}, u32[]{:S(2)}) collective-permute-start(bf16[512,512]{1,0:T(8,128)(2,1)S(1)} %collective-permute-done.8.refs_4_.refs_10_), channel_id=1, source_target_pairs={{0,4},{4,8},{8,12},{12,14},{14,10},{10,6},{6,2},{2,0},{1,5},{5,9},... | collective-permute-start | bytes 1572872 | tf_op jit(solution)/shard_map/ppermute | solution.py:308
  54.6 22.8 %collective-permute-start.15 = (bf16[512,512]{1,0:T(8,128)(2,1)S(1)}, bf16[512,512]{1,0:T(8,128)(2,1)S(1)}, u32[]{:S(2)}, u32[]{:S(2)}) collective-permute-start(bf16[512,512]{1,0:T(8,128)(2,1)S(1)} %collective-permute-done.9.refs_5_.refs_11_), channel_id=1, source_target_pairs={{4,0},{8,4},{12,8},{14,12},{10,14},{6,10},{2,6},{0,2},{5,1},{9,5},... | collective-permute-start | bytes 1572872 | tf_op jit(solution)/shard_map/ppermute | solution.py:308
  77.4 6.0 %collective-permute-start.16 = (bf16[272,2048]{1,0:T(8,128)(2,1)S(1)}, bf16[272,2048]{1,0:T(8,128)(2,1)S(1)}, u32[]{:S(2)}, u32[]{:S(2)}) collective-permute-start(bf16[272,2048]{1,0:T(8,128)(2,1)S(1)} %collective-permute-done.12.refs_5_), channel_id=1, source_target_pairs={{0,1},{1,0},{2,3},{3,2},{4,5},{5,4},{6,7},{7,6},{8,9},{9,8},{10,11... | collective-permute-start | bytes 3342344 | tf_op jit(solution)/shard_map/ppermute | solution.py:377
  78.9 10.2 %collective-permute-start.21 = (bf16[256,512]{1,0:T(8,128)(2,1)S(1)}, bf16[256,512]{1,0:T(8,128)(2,1)S(1)}, u32[]{:S(2)}, u32[]{:S(2)}) collective-permute-start(bf16[256,512]{1,0:T(8,128)(2,1)S(1)} %slice.48), channel_id=1, source_target_pairs={{0,4},{4,8},{8,12},{12,14},{14,10},{10,6},{6,2},{2,0},{1,5},{5,9},... | collective-permute-start | bytes 786440 | tf_op jit(solution)/shard_map/ppermute | solution.py:308
  80.5 9.0 %collective-permute-start.22 = (bf16[256,512]{1,0:T(8,128)(2,1)S(1)}, bf16[256,512]{1,0:T(8,128)(2,1)S(1)}, u32[]{:S(2)}, u32[]{:S(2)}) collective-permute-start(bf16[256,512]{1,0:T(8,128)(2,1)S(1)} %slice.49), channel_id=1, source_target_pairs={{4,0},{8,4},{12,8},{14,12},{10,14},{6,10},{2,6},{0,2},{5,1},{9,5},... | collective-permute-start | bytes 786440 | tf_op jit(solution)/shard_map/ppermute | solution.py:308
  83.3 6.2 %collective-permute-start.20 = (bf16[64,2048]{1,0:T(8,128)(2,1)S(1)}, bf16[64,2048]{1,0:T(8,128)(2,1)S(1)}, u32[]{:S(2)}, u32[]{:S(2)}) collective-permute-start(bf16[64,2048]{1,0:T(8,128)(2,1)S(1)} %constant_dynamic-update-slice_fusion.refs_7_), channel_id=1, source_target_pairs={{0,1},{1,0},{2,3},{3,2},{4,5},{5,4},{6,7},{7,6},{8,9},{9,8},{10,11... | collective-permute-start | bytes 786440 | tf_op jit(solution)/shard_map/ppermute | solution.py:379
  83.4 15.2 %collective-permute-start.17 = (bf16[512,512]{1,0:T(8,128)(2,1)S(1)}, bf16[512,512]{1,0:T(8,128)(2,1)S(1)}, u32[]{:S(2)}, u32[]{:S(2)}) collective-permute-start(bf16[512,512]{1,0:T(8,128)(2,1)S(1)} %collective-permute-done.14.refs_6_.refs_12_), channel_id=1, source_target_pairs={{0,4},{4,8},{8,12},{12,14},{14,10},{10,6},{6,2},{2,0},{1,5},{5,9},... | collective-permute-start | bytes 1572872 | tf_op jit(solution)/shard_map/ppermute | solution.py:308
  85.0 14.9 %collective-permute-start.18 = (bf16[512,512]{1,0:T(8,128)(2,1)S(1)}, bf16[512,512]{1,0:T(8,128)(2,1)S(1)}, u32[]{:S(2)}, u32[]{:S(2)}) collective-permute-start(bf16[512,512]{1,0:T(8,128)(2,1)S(1)} %collective-permute-done.15.refs_7_.refs_13_), channel_id=1, source_target_pairs={{4,0},{8,4},{12,8},{14,12},{10,14},{6,10},{2,6},{0,2},{5,1},{9,5},... | collective-permute-start | bytes 1572872 | tf_op jit(solution)/shard_map/ppermute | solution.py:308
  95.0 22.7 %collective-permute-start.26 = (f16[640,512]{1,0:T(8,128)(2,1)S(1)}, f16[640,512]{1,0:T(8,128)(2,1)S(1)}, u32[]{:S(2)}, u32[]{:S(2)}) collective-permute-start(f16[640,512]{1,0:T(8,128)(2,1)S(1)} %fusion.1), channel_id=1, source_target_pairs={{0,16},{16,0},{1,17},{17,1},{2,18},{18,2},{3,19},{19,3},{4,20},{20... | collective-permute-start | bytes 1966088 | tf_op jit(solution)/shard_map/ppermute | solution.py:390
  99.9 9.5 %collective-permute-start.23 = (bf16[256,512]{1,0:T(8,128)(2,1)S(1)}, bf16[256,512]{1,0:T(8,128)(2,1)S(1)}, u32[]{:S(2)}, u32[]{:S(2)}) collective-permute-start(bf16[256,512]{1,0:T(8,128)(2,1)S(1)} %slice.41), channel_id=1, source_target_pairs={{0,4},{4,8},{8,12},{12,14},{14,10},{10,6},{6,2},{2,0},{1,5},{5,9},... | collective-permute-start | bytes 786440 | tf_op jit(solution)/shard_map/ppermute | solution.py:308
  101.5 7.9 %collective-permute-start.24 = (bf16[256,512]{1,0:T(8,128)(2,1)S(1)}, bf16[256,512]{1,0:T(8,128)(2,1)S(1)}, u32[]{:S(2)}, u32[]{:S(2)}) collective-permute-start(bf16[256,512]{1,0:T(8,128)(2,1)S(1)} %slice.42), channel_id=1, source_target_pairs={{4,0},{8,4},{12,8},{14,12},{10,14},{6,10},{2,6},{0,2},{5,1},{9,5},... | collective-permute-start | bytes 786440 | tf_op jit(solution)/shard_map/ppermute | solution.py:308
  117.7 16.7 %collective-permute-start.27 = (f16[640,512]{1,0:T(8,128)(2,1)}, f16[640,512]{1,0:T(8,128)(2,1)}, u32[]{:S(2)}, u32[]{:S(2)}) collective-permute-start(f16[640,512]{1,0:T(8,128)(2,1)} %fusion), channel_id=1, source_target_pairs={{0,16},{16,0},{1,17},{17,1},{2,18},{18,2},{3,19},{19,3},{4,20},{20... | collective-permute-start | bytes 1966088 | tf_op jit(solution)/shard_map/ppermute | solution.py:402
  120.3 12.3 %all-to-all-start = ((bf16[8,3,5120]{2,1,0:T(4,128)(2,1)}), bf16[8,3,5120]{2,1,0:T(4,128)(2,1)S(1)}, u32[]{:S(2)}, u32[]{:S(2)}) async-start(bf16[8,3,5120]{2,1,0:T(4,128)(2,1)} %bitcast.32), calls=%async_computation | async-start | bytes 655360 | tf_op jit(solution)/shard_map/all_to_all | solution.py:407
  (29 other events, 215.0 us)

commit v16 on v15

--- a/solution.py
+++ b/solution.py
@@ -145,38 +145,39 @@
 
 
 def pack_kernel(chunks, own_ref, *refs):
-    owns, (got_ref, angle_ref, query_ref, out_ref) = (own_ref, *refs[: chunks - 1]), refs[chunks - 1 :]
+    owns, refs = (own_ref, *refs[: chunks - 1]), refs[chunks - 1 :]
+    gots, (angle_ref, query_ref, out_ref) = refs[:chunks], refs[chunks:]
     cosine, sine = angle_ref[:, :HALF], angle_ref[:, HALF:]
-    count, base = query_ref.shape
+    base = query_ref.shape[1]
     width = owns[0].shape[1]
     half = width // 2
     out_ref[:, :base] = query_ref[...]
     for c in range(chunks):
         for h in range(half // HD):
             at = h * HD
-            both = owns[c][:, at : at + HD] + got_ref[:count, c * width + at : c * width + at + HD]
+            both = owns[c][:, at : at + HD] + gots[c][:, at : at + HD]
             both = jnp.concatenate(rotate(both[:, :HALF], both[:, HALF:], cosine, sine), -1)
             at += base + c * width
             out_ref[:, at : at + HD] = both.astype(jnp.bfloat16)
-        values = owns[c][:, half:] + got_ref[:count, c * width + half : (c + 1) * width]
+        values = owns[c][:, half:] + gots[c][:, half:]
         at = base + c * width + half
         out_ref[:, at : at + half] = values.astype(jnp.bfloat16)
 
 
-def pack(owns, got, angles, queries):
+def pack(owns, gots, angles, queries):
     vmem = pl.BlockSpec(memory_space=pltpu.VMEM)
-    width = queries.shape[1] + got.shape[1]
+    width = queries.shape[1] + sum(got.shape[1] for got in gots)
     return pl.pallas_call(
         functools.partial(pack_kernel, len(owns)),
         out_shape=jax.ShapeDtypeStruct((queries.shape[0], width), jnp.bfloat16),
-        in_specs=[vmem] * (len(owns) + 3),
+        in_specs=[vmem] * (2 * len(owns) + 2),
         out_specs=vmem,
         compiler_params=pltpu.CompilerParams(vmem_limit_bytes=VMEM_BYTES),
         cost_estimate=pl.CostEstimate(
-            flops=0, bytes_accessed=4 * queries.size + 10 * got.size, transcendentals=0
+            flops=0, bytes_accessed=4 * queries.size + 20 * gots[0].size, transcendentals=0
         ),
         name="pack_new",
-    )(*owns, got, angles, queries)
+    )(*owns, *gots, angles, queries)
 
 
 def pick_kernel(first, side_ref, source_ref, out_ref):
@@ -321,7 +322,8 @@
 
     def homeward(total):
         tokens_total = (total[:tokens] * RAISE).astype(jnp.float16)
-        return tokens_total, total[tokens + new_padded :], total[tokens : tokens + count]
+        at = tokens + new_padded
+        return tokens_total, total[at : at + count], total[tokens : tokens + count]
 
     cuts = (0, 3 * tokens // 20, 23 * tokens // 40, tokens)
     sent = [pick_columns(passages, 1 - side, half, cuts[0], cuts[1])]
@@ -388,12 +390,11 @@
     ends[1] = halved(ring[1][-1])
     step(1)
     homed = [lax.ppermute(away[0], "groups", partners)]
-    new_own, new_away = [away[2]], [away[1]]
+    new_own, new_back = [away[2]], [lax.ppermute(away[1], "groups", partners)]
     away = project(1, away_hidden, None, 0, row_count - 1)
     away = homeward(project(1, away_hidden, away, row_count - 1, row_count))
     new_own.append(away[2])
-    new_away.append(away[1])
-    new_back = lax.ppermute(jnp.concatenate(new_away, 1), "groups", partners)
+    new_back.append(lax.ppermute(away[1], "groups", partners))
     held[0] = project(0, own_hidden, held[0], early, row_count)
     queries = jnp.swapaxes(queries, 0, 1).reshape(count, -1)
     places, away = fence(places, away)

time: 151 us -> 151 us (level)
    unnamed x47 -> x45, local copies, waits for them, and re-layouts: 8.28 us -> 9.28 us
  transfers between devices with their start and end apart: 29 -> 30, of which waited for: 17 -> 17; matrix products, arithmetic and copies ran while one was open for 9% -> 8% of each run, Pallas kernels for 21% -> 20%
where the time goes in v16:
time: 151 us
  waiting for transfers between devices  48.3 us (32%)
  Pallas kernels  34.3 us (23%)
  starting transfers between devices  31.6 us (21%)
  local copies, waits for them, and re-layouts  12.6 us (8%)
  other arithmetic  11.8 us (8%)
  blocking collectives  11.6 us (8%)
    pallas_call x7, Pallas kernels, products(): pl.pallas_call(functools.partial(product_kernel, depths, len(hidden), bas...  25.4 us
    ppermute x8, starting transfers between devices, step(): lax.ppermute(pair[0], 'rows', onward)  14.2 us
    all_to_all x1, blocking collectives, body(): lax.all_to_all(attended, 'rows', split_axis=0, concat_axis=0, tiled=True)  11.6 us
    ppermute x8, waiting for transfers between devices, step(): lax.ppermute(pair[0], 'rows', onward)  10.7 us
    ppermute x1, waiting for transfers between devices, body(): got.append(lax.ppermute(sent[2], 'groups', partners))  9.79 us
    unnamed x45, local copies, waits for them, and re-layouts  9.28 us
    ppermute x1, waiting for transfers between devices, body(): got.append(lax.ppermute(sent[1], 'groups', partners))  8.54 us
    all_to_all x1, waiting for transfers between devices, body(): lax.all_to_all(moved, 'rows', split_axis=0, concat_axis=0, tiled=True)  7.37 us
  transfers between devices with their start and end apart: 30, of which 17 were waited for; matrix products, arithmetic and copies ran while one was open for 8% of the time, Pallas kernels for 20%

profile of v16, /device:TPU:0, one launch (start us, length us, event | category | flops | bytes accessed | tf_op | source)
XLA Modules:
  0.0 150.7 jit_solution(15097005112178962419)
XLA Ops:
  1.6 2.0 %own_half.2.refs_3_.refs_9_ = bf16[512,512]{1,0:T(8,128)(2,1)} custom-call(s32[1]{0:T(128)} %bitcast.side_ref, bf16[1024,2,512]{2,1,0:T(2,128)(2,1)S(1)} %copy-done.2), custom_call_target="tpu_custom_call" | custom-call | bytes 2097152 | tf_op jit(solution)/shard_map/own_half/pallas_call | solution.py:128
  3.6 3.0 %collective-permute-start = (bf16[512,512]{1,0:T(8,128)(2,1)}, bf16[512,512]{1,0:T(8,128)(2,1)}, u32[]{:S(2)}, u32[]{:S(2)}) collective-permute-start(bf16[512,512]{1,0:T(8,128)(2,1)} %own_half.2.refs_3_.refs_9_), channel_id=1, source_target_pairs={{0,4},{4,8},{8,12},{12,14},{14,10},{10,6},{6,2},{2,0},{1,5},{5,9},... | collective-permute-start | bytes 1572872 | tf_op jit(solution)/shard_map/ppermute | solution.py:309
  6.6 2.5 %copy-done = bf16[640,4096]{1,0:T(8,128)(2,1)S(1)} copy-done((bf16[640,4096]{1,0:T(8,128)(2,1)S(1)}, bf16[640,4096]{1,0:T(8,128)(2,1)}, u32[]{:S(2)}) %copy-start) | copy-done | bytes 5242904
  9.5 2.0 %collective-permute-start.2 = (bf16[96,2048]{1,0:T(8,128)(2,1)S(1)}, bf16[96,2048]{1,0:T(8,128)(2,1)S(1)}, u32[]{:S(2)}, u32[]{:S(2)}) collective-permute-start(bf16[96,2048]{1,0:T(8,128)(2,1)S(1)} %pick_columns.6), channel_id=1, source_target_pairs={{0,16},{16,0},{1,17},{17,1},{2,18},{18,2},{3,19},{19,3},{4,20},{20... | collective-permute-start | bytes 1179656 | tf_op jit(solution)/shard_map/ppermute | solution.py:331
  17.6 2.5 %collective-permute-done.2.refs_1_ = bf16[96,2048]{1,0:T(8,128)(2,1)S(1)} collective-permute-done((bf16[96,2048]{1,0:T(8,128)(2,1)S(1)}, bf16[96,2048]{1,0:T(8,128)(2,1)S(1)}, u32[]{:S(2)}, u32[]{:S(2)}) %collective-permute-start.2) | collective-permute-done | bytes 393248 | tf_op jit(solution)/shard_map/ppermute | solution.py:331
  28.8 1.6 %collective-permute-start.8 = (bf16[512,512]{1,0:T(8,128)(2,1)S(1)}, bf16[512,512]{1,0:T(8,128)(2,1)S(1)}, u32[]{:S(2)}, u32[]{:S(2)}) collective-permute-start(bf16[512,512]{1,0:T(8,128)(2,1)S(1)} %own_half.3.refs_3_.refs_9_), channel_id=1, source_target_pairs={{0,4},{4,8},{8,12},{12,14},{14,10},{10,6},{6,2},{2,0},{1,5},{5,9},... | collective-permute-start | bytes 1572872 | tf_op jit(solution)/shard_map/ppermute | solution.py:309
  33.1 1.8 %multiply_cosine_fusion = (f32[640,64]{1,0:T(8,128)S(1)}, f32[640,64]{1,0:T(8,128)S(1)}) fusion(f32[64]{0:T(128)} %multiply_exponential_fusion, f32[640]{0:T(1024)S(1)} %subtract_convert_fusion), kind=kLoop, calls=%fused_computation.7 | loop fusion | flops 40960 | bytes 330496 | tf_op jit(solution)/shard_map/cos | solution.py:25
  35.8 2.9 %collective-permute-done.3.refs_6_.refs_12_ = bf16[512,512]{1,0:T(8,128)(2,1)} collective-permute-done((bf16[512,512]{1,0:T(8,128)(2,1)}, bf16[512,512]{1,0:T(8,128)(2,1)}, u32[]{:S(2)}, u32[]{:S(2)}) %collective-permute-start.3) | collective-permute-done | bytes 524320 | tf_op jit(solution)/shard_map/ppermute | solution.py:309
  40.4 8.5 %collective-permute-done.5.refs_3_ = bf16[272,2048]{1,0:T(8,128)(2,1)} collective-permute-done((bf16[272,2048]{1,0:T(8,128)(2,1)}, bf16[272,2048]{1,0:T(8,128)(2,1)}, u32[]{:S(2)}, u32[]{:S(2)}) %collective-permute-start.5) | collective-permute-done | bytes 1114144 | tf_op jit(solution)/shard_map/ppermute | solution.py:346
  55.0 4.3 %products.7.refs_7_ = f32[640,512]{1,0:T(8,128)S(1)} custom-call(s32[8]{0:T(128)S(1)} %fusion.3.refs_0_, bf16[640,2048]{1,0:T(8,128)(2,1)S(1)} %pick_columns.9.refs_1_, bf16[640,2048]{1,0:T(8,128)(2,1)} %collective-permute-done.6.refs_2_, bf16[512,512]{1,0:T(8,128)(2,1)} %own_half.2.refs_3_.refs_9_, bf16[512,512]{1,0:T(8,128)(2,1)} %collective-permute-done.refs_4_.refs_10_, ...), custom_call_target="tpu_custom_call" | custom-call | flops 1677721600 | bytes 7208960 | tf_op jit(solution)/shard_map/products/pallas_call | solution.py:241
  59.3 6.2 %collective-permute-done.10.refs_14_.refs_3_ = bf16[512,512]{1,0:T(8,128)(2,1)S(1)} collective-permute-done((bf16[512,512]{1,0:T(8,128)(2,1)}, bf16[512,512]{1,0:T(8,128)(2,1)S(1)}, u32[]{:S(2)}, u32[]{:S(2)}) %collective-permute-start.10) | collective-permute-done | bytes 524320 | tf_op jit(solution)/shard_map/ppermute | solution.py:309
  67.2 9.8 %collective-permute-done.12.refs_5_ = bf16[272,2048]{1,0:T(8,128)(2,1)S(1)} collective-permute-done((bf16[272,2048]{1,0:T(8,128)(2,1)S(1)}, bf16[272,2048]{1,0:T(8,128)(2,1)S(1)}, u32[]{:S(2)}, u32[]{:S(2)}) %collective-permute-start.12) | collective-permute-done | bytes 1114144 | tf_op jit(solution)/shard_map/ppermute | solution.py:363
  78.8 1.6 %collective-permute-start.21 = (bf16[256,512]{1,0:T(8,128)(2,1)S(1)}, bf16[256,512]{1,0:T(8,128)(2,1)S(1)}, u32[]{:S(2)}, u32[]{:S(2)}) collective-permute-start(bf16[256,512]{1,0:T(8,128)(2,1)S(1)} %slice.48), channel_id=1, source_target_pairs={{0,4},{4,8},{8,12},{12,14},{14,10},{10,6},{6,2},{2,0},{1,5},{5,9},... | collective-permute-start | bytes 786440 | tf_op jit(solution)/shard_map/ppermute | solution.py:309
  80.9 2.3 %collective-permute-done.19 = bf16[32,2048]{1,0:T(8,128)(2,1)S(1)} collective-permute-done((bf16[32,2048]{1,0:T(8,128)(2,1)S(1)}, bf16[32,2048]{1,0:T(8,128)(2,1)S(1)}, u32[]{:S(2)}, u32[]{:S(2)}) %collective-permute-start.19) | collective-permute-done | bytes 131104 | tf_op jit(solution)/shard_map/ppermute | solution.py:380
  83.3 1.6 %collective-permute-start.17 = (bf16[512,512]{1,0:T(8,128)(2,1)S(1)}, bf16[512,512]{1,0:T(8,128)(2,1)S(1)}, u32[]{:S(2)}, u32[]{:S(2)}) collective-permute-start(bf16[512,512]{1,0:T(8,128)(2,1)S(1)} %collective-permute-done.14.refs_6_.refs_12_), channel_id=1, source_target_pairs={{0,4},{4,8},{8,12},{12,14},{14,10},{10,6},{6,2},{2,0},{1,5},{5,9},... | collective-permute-start | bytes 1572872 | tf_op jit(solution)/shard_map/ppermute | solution.py:309
  85.4 3.6 %products.8.refs_7_ = f32[640,512]{1,0:T(8,128)S(1)} custom-call(s32[8]{0:T(128)S(1)} %fusion.3.refs_0_, bf16[640,2048]{1,0:T(8,128)(2,1)S(1)} %pick_columns.9.refs_1_, bf16[640,2048]{1,0:T(8,128)(2,1)} %collective-permute-done.6.refs_2_, bf16[512,512]{1,0:T(8,128)(2,1)S(1)} %own_half.3.refs_3_.refs_9_, ...), custom_call_target="tpu_custom_call" | custom-call | flops 1677721600 | bytes 7208960 | tf_op jit(solution)/shard_map/products/pallas_call | solution.py:241
  89.4 5.3 %products.9 = f32[704,512]{1,0:T(8,128)S(1)} custom-call(s32[8]{0:T(128)S(1)} %fusion.3.refs_0_, bf16[96,2048]{1,0:T(8,128)(2,1)S(1)} %collective-permute-done.2.refs_1_, bf16[96,2048]{1,0:T(8,128)(2,1)} %collective-permute-done.7.refs_2_, bf16[272,2048]{1,0:T(8,128)(2,1)} %collective-permute-done.5.refs_3_, ...), custom_call_target="tpu_custom_call" | custom-call | flops 2952790016 | bytes 11403264 | tf_op jit(solution)/shard_map/products/pallas_call | solution.py:241
  102.2 4.2 %products.11.refs_11_ = f32[704,512]{1,0:T(8,128)S(1)} custom-call(s32[8]{0:T(128)S(1)} %fusion.3.refs_0_, bf16[96,2048]{1,0:T(8,128)(2,1)S(1)} %collective-permute-done.2.refs_1_, bf16[96,2048]{1,0:T(8,128)(2,1)} %collective-permute-done.7.refs_2_, bf16[272,2048]{1,0:T(8,128)(2,1)} %collective-permute-done.5.refs_3_, ...), custom_call_target="tpu_custom_call" | custom-call | flops 2583691264 | bytes 10158080 | tf_op jit(solution)/shard_map/products/pallas_call | solution.py:241
  106.4 3.0 %products.10.held_ref = f32[640,512]{1,0:T(8,128)S(1)} custom-call(s32[8]{0:T(128)S(1)} %fusion.3.refs_0_, bf16[640,2048]{1,0:T(8,128)(2,1)S(1)} %pick_columns.9.refs_1_, bf16[640,2048]{1,0:T(8,128)(2,1)} %collective-permute-done.6.refs_2_, bf16[512,512]{1,0:T(8,128)(2,1)S(1)} %collective-permute-done.10.refs_14_.refs_3_, ...), custom_call_target="tpu_custom_call" | custom-call | flops 1006632960 | bytes 4849664 | tf_op jit(solution)/shard_map/products/pallas_call | solution.py:241
  110.4 1.9 %products.12 = f32[704,512]{1,0:T(8,128)S(1)} custom-call(s32[8]{0:T(128)S(1)} %fusion.3.refs_0_, bf16[96,2048]{1,0:T(8,128)(2,1)S(1)} %collective-permute-done.2.refs_1_, bf16[96,2048]{1,0:T(8,128)(2,1)} %collective-permute-done.7.refs_2_, bf16[272,2048]{1,0:T(8,128)(2,1)} %collective-permute-done.5.refs_3_, ...), custom_call_target="tpu_custom_call" | custom-call | flops 369098752 | bytes 2686976 | tf_op jit(solution)/shard_map/products/pallas_call | solution.py:241
  114.1 3.0 %products.13.held_ref = f32[640,512]{1,0:T(8,128)S(1)} custom-call(s32[8]{0:T(128)S(1)} %fusion.3.refs_0_, bf16[640,2048]{1,0:T(8,128)(2,1)S(1)} %pick_columns.9.refs_1_, bf16[640,2048]{1,0:T(8,128)(2,1)} %collective-permute-done.6.refs_2_, bf16[512,512]{1,0:T(8,128)(2,1)S(1)} %collective-permute-done.17.refs_14_.refs_3_, ...), custom_call_target="tpu_custom_call" | custom-call | flops 1006632960 | bytes 4849664 | tf_op jit(solution)/shard_map/products/pallas_call | solution.py:241
  120.8 3.5 %all-to-all-start = ((bf16[8,3,5120]{2,1,0:T(4,128)(2,1)}), bf16[8,3,5120]{2,1,0:T(4,128)(2,1)S(1)}, u32[]{:S(2)}, u32[]{:S(2)}) async-start(bf16[8,3,5120]{2,1,0:T(4,128)(2,1)} %bitcast.32), calls=%async_computation | async-start | bytes 655360 | tf_op jit(solution)/shard_map/all_to_all | solution.py:408
  125.7 7.4 %all-to-all-done = bf16[8,3,5120]{2,1,0:T(4,128)(2,1)S(1)} async-done(((bf16[8,3,5120]{2,1,0:T(4,128)(2,1)}), bf16[8,3,5120]{2,1,0:T(4,128)(2,1)S(1)}, u32[]{:S(2)}, u32[]{:S(2)}) %all-to-all-start) | async-done | bytes 245792 | tf_op jit(solution)/shard_map/all_to_all | solution.py:408
  138.2 11.6 %all_to_all.10 = bf16[8,3,4096]{2,1,0:T(4,128)(2,1)S(1)} all-to-all(bf16[8,3,4096]{2,1,0:T(4,128)(2,1)S(1)} %bitcast.39), channel_id=1, replica_groups=mesh['groups'=2,'rows'=8,'tensor'=2] {'rows'}, dimensions={0} | all-to-all | bytes 393216 | tf_op jit(solution)/shard_map/all_to_all | solution.py:420
  (136 shorter events, 53.9 us)
Async XLA Ops:
  3.6 16.5 %collective-permute-start = (bf16[512,512]{1,0:T(8,128)(2,1)}, bf16[512,512]{1,0:T(8,128)(2,1)}, u32[]{:S(2)}, u32[]{:S(2)}) collective-permute-start(bf16[512,512]{1,0:T(8,128)(2,1)} %own_half.2.refs_3_.refs_9_), channel_id=1, source_target_pairs={{0,4},{4,8},{8,12},{12,14},{14,10},{10,6},{6,2},{2,0},{1,5},{5,9},... | collective-permute-start | bytes 1572872 | tf_op jit(solution)/shard_map/ppermute | solution.py:309
  6.6 13.7 %collective-permute-start.1 = (bf16[512,512]{1,0:T(8,128)(2,1)}, bf16[512,512]{1,0:T(8,128)(2,1)}, u32[]{:S(2)}, u32[]{:S(2)}) collective-permute-start(bf16[512,512]{1,0:T(8,128)(2,1)} %own_half.2.refs_3_.refs_9_), channel_id=1, source_target_pairs={{4,0},{8,4},{12,8},{14,12},{10,14},{6,10},{2,6},{0,2},{5,1},{9,5},... | collective-permute-start | bytes 1572872 | tf_op jit(solution)/shard_map/ppermute | solution.py:309
  9.5 10.6 %collective-permute-start.2 = (bf16[96,2048]{1,0:T(8,128)(2,1)S(1)}, bf16[96,2048]{1,0:T(8,128)(2,1)S(1)}, u32[]{:S(2)}, u32[]{:S(2)}) collective-permute-start(bf16[96,2048]{1,0:T(8,128)(2,1)S(1)} %pick_columns.6), channel_id=1, source_target_pairs={{0,16},{16,0},{1,17},{17,1},{2,18},{18,2},{3,19},{19,3},{4,20},{20... | collective-permute-start | bytes 1179656 | tf_op jit(solution)/shard_map/ppermute | solution.py:331
  22.1 26.9 %collective-permute-start.5 = (bf16[272,2048]{1,0:T(8,128)(2,1)}, bf16[272,2048]{1,0:T(8,128)(2,1)}, u32[]{:S(2)}, u32[]{:S(2)}) collective-permute-start(bf16[272,2048]{1,0:T(8,128)(2,1)} %copy-done.11), channel_id=1, source_target_pairs={{0,16},{16,0},{1,17},{17,1},{2,18},{18,2},{3,19},{19,3},{4,20},{20... | collective-permute-start | bytes 3342344 | tf_op jit(solution)/shard_map/ppermute | solution.py:346
  23.6 15.1 %collective-permute-start.3 = (bf16[512,512]{1,0:T(8,128)(2,1)}, bf16[512,512]{1,0:T(8,128)(2,1)}, u32[]{:S(2)}, u32[]{:S(2)}) collective-permute-start(bf16[512,512]{1,0:T(8,128)(2,1)} %collective-permute-done.refs_4_.refs_10_), channel_id=1, source_target_pairs={{0,4},{4,8},{8,12},{12,14},{14,10},{10,6},{6,2},{2,0},{1,5},{5,9},... | collective-permute-start | bytes 1572872 | tf_op jit(solution)/shard_map/ppermute | solution.py:309
  25.2 15.2 %collective-permute-start.4 = (bf16[512,512]{1,0:T(8,128)(2,1)}, bf16[512,512]{1,0:T(8,128)(2,1)}, u32[]{:S(2)}, u32[]{:S(2)}) collective-permute-start(bf16[512,512]{1,0:T(8,128)(2,1)} %collective-permute-done.1.refs_5_.refs_11_), channel_id=1, source_target_pairs={{4,0},{8,4},{12,8},{14,12},{10,14},{6,10},{2,6},{0,2},{5,1},{9,5},... | collective-permute-start | bytes 1572872 | tf_op jit(solution)/shard_map/ppermute | solution.py:309
  28.8 20.2 %collective-permute-start.8 = (bf16[512,512]{1,0:T(8,128)(2,1)S(1)}, bf16[512,512]{1,0:T(8,128)(2,1)S(1)}, u32[]{:S(2)}, u32[]{:S(2)}) collective-permute-start(bf16[512,512]{1,0:T(8,128)(2,1)S(1)} %own_half.3.refs_3_.refs_9_), channel_id=1, source_target_pairs={{0,4},{4,8},{8,12},{12,14},{14,10},{10,6},{6,2},{2,0},{1,5},{5,9},... | collective-permute-start | bytes 1572872 | tf_op jit(solution)/shard_map/ppermute | solution.py:309
  30.4 19.6 %collective-permute-start.9 = (bf16[512,512]{1,0:T(8,128)(2,1)S(1)}, bf16[512,512]{1,0:T(8,128)(2,1)S(1)}, u32[]{:S(2)}, u32[]{:S(2)}) collective-permute-start(bf16[512,512]{1,0:T(8,128)(2,1)S(1)} %own_half.3.refs_3_.refs_9_), channel_id=1, source_target_pairs={{4,0},{8,4},{12,8},{14,12},{10,14},{6,10},{2,6},{0,2},{5,1},{9,5},... | collective-permute-start | bytes 1572872 | tf_op jit(solution)/shard_map/ppermute | solution.py:309
  50.0 27.0 %collective-permute-start.12 = (bf16[272,2048]{1,0:T(8,128)(2,1)S(1)}, bf16[272,2048]{1,0:T(8,128)(2,1)S(1)}, u32[]{:S(2)}, u32[]{:S(2)}) collective-permute-start(bf16[272,2048]{1,0:T(8,128)(2,1)S(1)} %copy-done.10), channel_id=1, source_target_pairs={{0,16},{16,0},{1,17},{17,1},{2,18},{18,2},{3,19},{19,3},{4,20},{20... | collective-permute-start | bytes 3342344 | tf_op jit(solution)/shard_map/ppermute | solution.py:363
  50.6 15.0 %collective-permute-start.10 = (bf16[512,512]{1,0:T(8,128)(2,1)}, bf16[512,512]{1,0:T(8,128)(2,1)S(1)}, u32[]{:S(2)}, u32[]{:S(2)}) collective-permute-start(bf16[512,512]{1,0:T(8,128)(2,1)} %collective-permute-done.3.refs_6_.refs_12_), channel_id=1, source_target_pairs={{0,4},{4,8},{8,12},{12,14},{14,10},{10,6},{6,2},{2,0},{1,5},{5,9},... | collective-permute-start | bytes 1572872 | tf_op jit(solution)/shard_map/ppermute | solution.py:309
  52.1 15.0 %collective-permute-start.11 = (bf16[512,512]{1,0:T(8,128)(2,1)}, bf16[512,512]{1,0:T(8,128)(2,1)S(1)}, u32[]{:S(2)}, u32[]{:S(2)}) collective-permute-start(bf16[512,512]{1,0:T(8,128)(2,1)} %collective-permute-done.4.refs_7_.refs_13_), channel_id=1, source_target_pairs={{4,0},{8,4},{12,8},{14,12},{10,14},{6,10},{2,6},{0,2},{5,1},{9,5},... | collective-permute-start | bytes 1572872 | tf_op jit(solution)/shard_map/ppermute | solution.py:309
  52.9 24.0 %collective-permute-start.14 = (bf16[512,512]{1,0:T(8,128)(2,1)S(1)}, bf16[512,512]{1,0:T(8,128)(2,1)S(1)}, u32[]{:S(2)}, u32[]{:S(2)}) collective-permute-start(bf16[512,512]{1,0:T(8,128)(2,1)S(1)} %collective-permute-done.8.refs_4_.refs_10_), channel_id=1, source_target_pairs={{0,4},{4,8},{8,12},{12,14},{14,10},{10,6},{6,2},{2,0},{1,5},{5,9},... | collective-permute-start | bytes 1572872 | tf_op jit(solution)/shard_map/ppermute | solution.py:309
  54.5 22.8 %collective-permute-start.15 = (bf16[512,512]{1,0:T(8,128)(2,1)S(1)}, bf16[512,512]{1,0:T(8,128)(2,1)S(1)}, u32[]{:S(2)}, u32[]{:S(2)}) collective-permute-start(bf16[512,512]{1,0:T(8,128)(2,1)S(1)} %collective-permute-done.9.refs_5_.refs_11_), channel_id=1, source_target_pairs={{4,0},{8,4},{12,8},{14,12},{10,14},{6,10},{2,6},{0,2},{5,1},{9,5},... | collective-permute-start | bytes 1572872 | tf_op jit(solution)/shard_map/ppermute | solution.py:309
  78.8 10.2 %collective-permute-start.21 = (bf16[256,512]{1,0:T(8,128)(2,1)S(1)}, bf16[256,512]{1,0:T(8,128)(2,1)S(1)}, u32[]{:S(2)}, u32[]{:S(2)}) collective-permute-start(bf16[256,512]{1,0:T(8,128)(2,1)S(1)} %slice.48), channel_id=1, source_target_pairs={{0,4},{4,8},{8,12},{12,14},{14,10},{10,6},{6,2},{2,0},{1,5},{5,9},... | collective-permute-start | bytes 786440 | tf_op jit(solution)/shard_map/ppermute | solution.py:309
  80.4 9.0 %collective-permute-start.22 = (bf16[256,512]{1,0:T(8,128)(2,1)S(1)}, bf16[256,512]{1,0:T(8,128)(2,1)S(1)}, u32[]{:S(2)}, u32[]{:S(2)}) collective-permute-start(bf16[256,512]{1,0:T(8,128)(2,1)S(1)} %slice.49), channel_id=1, source_target_pairs={{4,0},{8,4},{12,8},{14,12},{10,14},{6,10},{2,6},{0,2},{5,1},{9,5},... | collective-permute-start | bytes 786440 | tf_op jit(solution)/shard_map/ppermute | solution.py:309
  83.2 6.2 %collective-permute-start.20 = (bf16[64,2048]{1,0:T(8,128)(2,1)S(1)}, bf16[64,2048]{1,0:T(8,128)(2,1)S(1)}, u32[]{:S(2)}, u32[]{:S(2)}) collective-permute-start(bf16[64,2048]{1,0:T(8,128)(2,1)S(1)} %constant_dynamic-update-slice_fusion.refs_7_), channel_id=1, source_target_pairs={{0,1},{1,0},{2,3},{3,2},{4,5},{5,4},{6,7},{7,6},{8,9},{9,8},{10,11... | collective-permute-start | bytes 786440 | tf_op jit(solution)/shard_map/ppermute | solution.py:381
  83.3 15.2 %collective-permute-start.17 = (bf16[512,512]{1,0:T(8,128)(2,1)S(1)}, bf16[512,512]{1,0:T(8,128)(2,1)S(1)}, u32[]{:S(2)}, u32[]{:S(2)}) collective-permute-start(bf16[512,512]{1,0:T(8,128)(2,1)S(1)} %collective-permute-done.14.refs_6_.refs_12_), channel_id=1, source_target_pairs={{0,4},{4,8},{8,12},{12,14},{14,10},{10,6},{6,2},{2,0},{1,5},{5,9},... | collective-permute-start | bytes 1572872 | tf_op jit(solution)/shard_map/ppermute | solution.py:309
  85.0 14.9 %collective-permute-start.18 = (bf16[512,512]{1,0:T(8,128)(2,1)S(1)}, bf16[512,512]{1,0:T(8,128)(2,1)S(1)}, u32[]{:S(2)}, u32[]{:S(2)}) collective-permute-start(bf16[512,512]{1,0:T(8,128)(2,1)S(1)} %collective-permute-done.15.refs_7_.refs_13_), channel_id=1, source_target_pairs={{4,0},{8,4},{12,8},{14,12},{10,14},{6,10},{2,6},{0,2},{5,1},{9,5},... | collective-permute-start | bytes 1572872 | tf_op jit(solution)/shard_map/ppermute | solution.py:309
  94.9 23.3 %collective-permute-start.27 = (f16[640,512]{1,0:T(8,128)(2,1)S(1)}, f16[640,512]{1,0:T(8,128)(2,1)S(1)}, u32[]{:S(2)}, u32[]{:S(2)}) collective-permute-start(f16[640,512]{1,0:T(8,128)(2,1)S(1)} %fusion.1), channel_id=1, source_target_pairs={{0,16},{16,0},{1,17},{17,1},{2,18},{18,2},{3,19},{19,3},{4,20},{20... | collective-permute-start | bytes 1966088 | tf_op jit(solution)/shard_map/ppermute | solution.py:392
  96.1 22.1 %collective-permute-start.25 = (f32[24,512]{1,0:T(8,128)S(1)}, f32[24,512]{1,0:T(8,128)S(1)}, u32[]{:S(2)}, u32[]{:S(2)}) collective-permute-start(f32[24,512]{1,0:T(8,128)S(1)} %get-tuple-element.123), channel_id=1, source_target_pairs={{0,16},{16,0},{1,17},{17,1},{2,18},{18,2},{3,19},{19,3},{4,20},{20... | collective-permute-start | bytes 147464 | tf_op jit(solution)/shard_map/ppermute | solution.py:393
  99.9 10.5 %collective-permute-start.23 = (bf16[256,512]{1,0:T(8,128)(2,1)S(1)}, bf16[256,512]{1,0:T(8,128)(2,1)S(1)}, u32[]{:S(2)}, u32[]{:S(2)}) collective-permute-start(bf16[256,512]{1,0:T(8,128)(2,1)S(1)} %slice.41), channel_id=1, source_target_pairs={{0,4},{4,8},{8,12},{12,14},{14,10},{10,6},{6,2},{2,0},{1,5},{5,9},... | collective-permute-start | bytes 786440 | tf_op jit(solution)/shard_map/ppermute | solution.py:309
  101.5 8.9 %collective-permute-start.24 = (bf16[256,512]{1,0:T(8,128)(2,1)S(1)}, bf16[256,512]{1,0:T(8,128)(2,1)S(1)}, u32[]{:S(2)}, u32[]{:S(2)}) collective-permute-start(bf16[256,512]{1,0:T(8,128)(2,1)S(1)} %slice.42), channel_id=1, source_target_pairs={{4,0},{8,4},{12,8},{14,12},{10,14},{6,10},{2,6},{0,2},{5,1},{9,5},... | collective-permute-start | bytes 786440 | tf_op jit(solution)/shard_map/ppermute | solution.py:309
  118.2 16.7 %collective-permute-start.28 = (f16[640,512]{1,0:T(8,128)(2,1)}, f16[640,512]{1,0:T(8,128)(2,1)}, u32[]{:S(2)}, u32[]{:S(2)}) collective-permute-start(f16[640,512]{1,0:T(8,128)(2,1)} %fusion), channel_id=1, source_target_pairs={{0,16},{16,0},{1,17},{17,1},{2,18},{18,2},{3,19},{19,3},{4,20},{20... | collective-permute-start | bytes 1966088 | tf_op jit(solution)/shard_map/ppermute | solution.py:403
  120.8 12.3 %all-to-all-start = ((bf16[8,3,5120]{2,1,0:T(4,128)(2,1)}), bf16[8,3,5120]{2,1,0:T(4,128)(2,1)S(1)}, u32[]{:S(2)}, u32[]{:S(2)}) async-start(bf16[8,3,5120]{2,1,0:T(4,128)(2,1)} %bitcast.32), calls=%async_computation | async-start | bytes 655360 | tf_op jit(solution)/shard_map/all_to_all | solution.py:408
  (28 other events, 212.0 us)

commit v17 on v16

--- a/solution.py
+++ b/solution.py
@@ -397,12 +397,14 @@
     new_back.append(lax.ppermute(away[1], "groups", partners))
     held[0] = project(0, own_hidden, held[0], early, row_count)
     queries = jnp.swapaxes(queries, 0, 1).reshape(count, -1)
-    places, away = fence(places, away)
-    held[1] = project(1, own_hidden, held[1], early, row_count)
-    held, queries, away, new_back, homed[0] = fence(held, queries, away, new_back, homed[0])
+    held, queries, places, away, new_back, homed[0] = fence(
+        held, queries, places, away, new_back, homed[0]
+    )
     homed.append(lax.ppermute(away[0], "groups", partners))
     angles, new_angles, key_info, query_info = tables
     moved = pack(new_own, new_back, new_angles, queries)
+    moved, places = fence(moved, places)
+    held[1] = project(1, own_hidden, held[1], early, row_count)
     moved = moved.reshape(steps, requests, -1)
     moved = jnp.swapaxes(moved, 0, 1)
     moved = lax.all_to_all(moved, "rows", split_axis=0, concat_axis=0, tiled=True)

time: 151 us -> 153 us (1.013)
  local copies, waits for them, and re-layouts: 12.6 us -> 19.2 us
  waiting for transfers between devices: 48.3 us -> 42.4 us
  blocking collectives: 11.6 us -> 13.8 us
    all_to_all x1, waiting for transfers between devices: 7.37 us -> 0.1 us  [body(): lax.all_to_all(moved, 'rows', split_axis=0, concat_axis=0, tiled=True)]
    unnamed x45 -> x67, local copies, waits for them, and re-layouts: 9.28 us -> 14.7 us
    ppermute x1, waiting for transfers between devices: 0.01 us -> 2.48 us  [body(): new_back.append(lax.ppermute(away[1], 'groups', partners))]
    all_to_all x1, blocking collectives: 11.6 us -> 13.8 us  [body(): lax.all_to_all(attended, 'rows', split_axis=0, concat_axis=0, tiled=True)]
where the time goes in v17:
time: 153 us; the launch traced here: 152 us
  waiting for transfers between devices  42.4 us (28%)
  Pallas kernels  34.5 us (23%)
  starting transfers between devices  31.3 us (20%)
  local copies, waits for them, and re-layouts  19.2 us (13%)
  blocking collectives  13.8 us (9%)
  other arithmetic  10.5 us (7%)
    pallas_call x7, Pallas kernels, products(): pl.pallas_call(functools.partial(product_kernel, depths, len(hidden), bas...  25.5 us
    unnamed x67, local copies, waits for them, and re-layouts  14.7 us
    ppermute x8, starting transfers between devices, step(): lax.ppermute(pair[0], 'rows', onward)  14.2 us
    all_to_all x1, blocking collectives, body(): lax.all_to_all(attended, 'rows', split_axis=0, concat_axis=0, tiled=True)  13.8 us
    ppermute x8, waiting for transfers between devices, step(): lax.ppermute(pair[0], 'rows', onward)  10 us
    ppermute x1, waiting for transfers between devices, body(): got.append(lax.ppermute(sent[2], 'groups', partners))  9.79 us
    ppermute x1, waiting for transfers between devices, body(): got.append(lax.ppermute(sent[1], 'groups', partners))  8.54 us
    ppermute x8, waiting for transfers between devices, step(): lax.ppermute(pair[1], 'rows', back)  6.1 us
  transfers between devices with their start and end apart: 30, of which 17 were waited for; matrix products, arithmetic and copies ran while one was open for 8% of the time, Pallas kernels for 20%

profile of v17, /device:TPU:0, one launch (start us, length us, event | category | flops | bytes accessed | tf_op | source)
XLA Modules:
  0.0 152.2 jit_solution(10220761212691113939)
XLA Ops:
  1.6 2.0 %own_half.2.refs_3_.refs_9_ = bf16[512,512]{1,0:T(8,128)(2,1)} custom-call(s32[1]{0:T(128)} %bitcast.side_ref, bf16[1024,2,512]{2,1,0:T(2,128)(2,1)S(1)} %copy-done.2), custom_call_target="tpu_custom_call" | custom-call | bytes 2097152 | tf_op jit(solution)/shard_map/own_half/pallas_call | solution.py:128
  3.6 3.0 %collective-permute-start = (bf16[512,512]{1,0:T(8,128)(2,1)}, bf16[512,512]{1,0:T(8,128)(2,1)}, u32[]{:S(2)}, u32[]{:S(2)}) collective-permute-start(bf16[512,512]{1,0:T(8,128)(2,1)} %own_half.2.refs_3_.refs_9_), channel_id=1, source_target_pairs={{0,4},{4,8},{8,12},{12,14},{14,10},{10,6},{6,2},{2,0},{1,5},{5,9},... | collective-permute-start | bytes 1572872 | tf_op jit(solution)/shard_map/ppermute | solution.py:309
  6.7 2.5 %copy-done = bf16[640,4096]{1,0:T(8,128)(2,1)S(1)} copy-done((bf16[640,4096]{1,0:T(8,128)(2,1)S(1)}, bf16[640,4096]{1,0:T(8,128)(2,1)}, u32[]{:S(2)}) %copy-start) | copy-done | bytes 5242904
  9.5 2.0 %collective-permute-start.2 = (bf16[96,2048]{1,0:T(8,128)(2,1)S(1)}, bf16[96,2048]{1,0:T(8,128)(2,1)S(1)}, u32[]{:S(2)}, u32[]{:S(2)}) collective-permute-start(bf16[96,2048]{1,0:T(8,128)(2,1)S(1)} %pick_columns.6), channel_id=1, source_target_pairs={{0,16},{16,0},{1,17},{17,1},{2,18},{18,2},{3,19},{19,3},{4,20},{20... | collective-permute-start | bytes 1179656 | tf_op jit(solution)/shard_map/ppermute | solution.py:331
  17.7 2.5 %collective-permute-done.2.refs_1_ = bf16[96,2048]{1,0:T(8,128)(2,1)S(1)} collective-permute-done((bf16[96,2048]{1,0:T(8,128)(2,1)S(1)}, bf16[96,2048]{1,0:T(8,128)(2,1)S(1)}, u32[]{:S(2)}, u32[]{:S(2)}) %collective-permute-start.2) | collective-permute-done | bytes 393248 | tf_op jit(solution)/shard_map/ppermute | solution.py:331
  28.8 1.6 %collective-permute-start.8 = (bf16[512,512]{1,0:T(8,128)(2,1)S(1)}, bf16[512,512]{1,0:T(8,128)(2,1)S(1)}, u32[]{:S(2)}, u32[]{:S(2)}) collective-permute-start(bf16[512,512]{1,0:T(8,128)(2,1)S(1)} %own_half.3.refs_3_.refs_9_), channel_id=1, source_target_pairs={{0,4},{4,8},{8,12},{12,14},{14,10},{10,6},{6,2},{2,0},{1,5},{5,9},... | collective-permute-start | bytes 1572872 | tf_op jit(solution)/shard_map/ppermute | solution.py:309
  33.2 1.8 %multiply_cosine_fusion = (f32[640,64]{1,0:T(8,128)S(1)}, f32[640,64]{1,0:T(8,128)S(1)}) fusion(f32[64]{0:T(128)} %multiply_exponential_fusion, f32[640]{0:T(1024)S(1)} %subtract_convert_fusion), kind=kLoop, calls=%fused_computation.7 | loop fusion | flops 40960 | bytes 330496 | tf_op jit(solution)/shard_map/cos | solution.py:25
  35.9 2.9 %collective-permute-done.3.refs_6_.refs_12_ = bf16[512,512]{1,0:T(8,128)(2,1)} collective-permute-done((bf16[512,512]{1,0:T(8,128)(2,1)}, bf16[512,512]{1,0:T(8,128)(2,1)}, u32[]{:S(2)}, u32[]{:S(2)}) %collective-permute-start.3) | collective-permute-done | bytes 524320 | tf_op jit(solution)/shard_map/ppermute | solution.py:309
  40.4 8.5 %collective-permute-done.5.refs_3_ = bf16[272,2048]{1,0:T(8,128)(2,1)} collective-permute-done((bf16[272,2048]{1,0:T(8,128)(2,1)}, bf16[272,2048]{1,0:T(8,128)(2,1)}, u32[]{:S(2)}, u32[]{:S(2)}) %collective-permute-start.5) | collective-permute-done | bytes 1114144 | tf_op jit(solution)/shard_map/ppermute | solution.py:346
  55.0 4.4 %products.7.refs_7_ = f32[640,512]{1,0:T(8,128)S(1)} custom-call(s32[8]{0:T(128)S(1)} %fusion.3.refs_0_, bf16[640,2048]{1,0:T(8,128)(2,1)S(1)} %pick_columns.9.refs_1_, bf16[640,2048]{1,0:T(8,128)(2,1)} %collective-permute-done.6.refs_2_, bf16[512,512]{1,0:T(8,128)(2,1)} %own_half.2.refs_3_.refs_9_, bf16[512,512]{1,0:T(8,128)(2,1)} %collective-permute-done.refs_4_.refs_10_, ...), custom_call_target="tpu_custom_call" | custom-call | flops 1677721600 | bytes 7208960 | tf_op jit(solution)/shard_map/products/pallas_call | solution.py:241
  59.3 6.2 %collective-permute-done.10.refs_14_.refs_3_ = bf16[512,512]{1,0:T(8,128)(2,1)S(1)} collective-permute-done((bf16[512,512]{1,0:T(8,128)(2,1)}, bf16[512,512]{1,0:T(8,128)(2,1)S(1)}, u32[]{:S(2)}, u32[]{:S(2)}) %collective-permute-start.10) | collective-permute-done | bytes 524320 | tf_op jit(solution)/shard_map/ppermute | solution.py:309
  67.2 9.8 %collective-permute-done.12.refs_5_ = bf16[272,2048]{1,0:T(8,128)(2,1)S(1)} collective-permute-done((bf16[272,2048]{1,0:T(8,128)(2,1)S(1)}, bf16[272,2048]{1,0:T(8,128)(2,1)S(1)}, u32[]{:S(2)}, u32[]{:S(2)}) %collective-permute-start.12) | collective-permute-done | bytes 1114144 | tf_op jit(solution)/shard_map/ppermute | solution.py:363
  78.8 1.6 %collective-permute-start.19 = (bf16[256,512]{1,0:T(8,128)(2,1)S(1)}, bf16[256,512]{1,0:T(8,128)(2,1)S(1)}, u32[]{:S(2)}, u32[]{:S(2)}) collective-permute-start(bf16[256,512]{1,0:T(8,128)(2,1)S(1)} %slice.48), channel_id=1, source_target_pairs={{0,4},{4,8},{8,12},{12,14},{14,10},{10,6},{6,2},{2,0},{1,5},{5,9},... | collective-permute-start | bytes 786440 | tf_op jit(solution)/shard_map/ppermute | solution.py:309
  80.9 2.3 %collective-permute-done.17 = bf16[32,2048]{1,0:T(8,128)(2,1)S(1)} collective-permute-done((bf16[32,2048]{1,0:T(8,128)(2,1)S(1)}, bf16[32,2048]{1,0:T(8,128)(2,1)S(1)}, u32[]{:S(2)}, u32[]{:S(2)}) %collective-permute-start.17) | collective-permute-done | bytes 131104 | tf_op jit(solution)/shard_map/ppermute | solution.py:380
  85.4 3.6 %products.8.refs_7_ = f32[640,512]{1,0:T(8,128)S(1)} custom-call(s32[8]{0:T(128)S(1)} %fusion.3.refs_0_, bf16[640,2048]{1,0:T(8,128)(2,1)S(1)} %pick_columns.9.refs_1_, bf16[640,2048]{1,0:T(8,128)(2,1)} %collective-permute-done.6.refs_2_, bf16[512,512]{1,0:T(8,128)(2,1)S(1)} %own_half.3.refs_3_.refs_9_, ...), custom_call_target="tpu_custom_call" | custom-call | flops 1677721600 | bytes 7208960 | tf_op jit(solution)/shard_map/products/pallas_call | solution.py:241
  90.1 5.3 %products.9 = f32[704,512]{1,0:T(8,128)S(1)} custom-call(s32[8]{0:T(128)S(1)} %fusion.3.refs_0_, bf16[96,2048]{1,0:T(8,128)(2,1)S(1)} %collective-permute-done.2.refs_1_, bf16[96,2048]{1,0:T(8,128)(2,1)} %collective-permute-done.7.refs_2_, bf16[272,2048]{1,0:T(8,128)(2,1)} %collective-permute-done.5.refs_3_, ...), custom_call_target="tpu_custom_call" | custom-call | flops 2952790016 | bytes 11403264 | tf_op jit(solution)/shard_map/products/pallas_call | solution.py:241
  102.2 4.2 %products.10.refs_11_ = f32[704,512]{1,0:T(8,128)S(1)} custom-call(s32[8]{0:T(128)S(1)} %fusion.3.refs_0_, bf16[96,2048]{1,0:T(8,128)(2,1)S(1)} %collective-permute-done.2.refs_1_, bf16[96,2048]{1,0:T(8,128)(2,1)} %collective-permute-done.7.refs_2_, bf16[272,2048]{1,0:T(8,128)(2,1)} %collective-permute-done.5.refs_3_, ...), custom_call_target="tpu_custom_call" | custom-call | flops 2583691264 | bytes 10158080 | tf_op jit(solution)/shard_map/products/pallas_call | solution.py:241
  106.4 2.9 %products.12.held_ref = f32[640,512]{1,0:T(8,128)S(1)} custom-call(s32[8]{0:T(128)S(1)} %fusion.3.refs_0_, bf16[640,2048]{1,0:T(8,128)(2,1)S(1)} %pick_columns.9.refs_1_, bf16[640,2048]{1,0:T(8,128)(2,1)} %collective-permute-done.6.refs_2_, bf16[512,512]{1,0:T(8,128)(2,1)S(1)} %collective-permute-done.10.refs_14_.refs_3_, ...), custom_call_target="tpu_custom_call" | custom-call | flops 1006632960 | bytes 4849664 | tf_op jit(solution)/shard_map/products/pallas_call | solution.py:241
  110.5 2.1 %products.11 = f32[704,512]{1,0:T(8,128)S(1)} custom-call(s32[8]{0:T(128)S(1)} %fusion.3.refs_0_, bf16[96,2048]{1,0:T(8,128)(2,1)S(1)} %collective-permute-done.2.refs_1_, bf16[96,2048]{1,0:T(8,128)(2,1)} %collective-permute-done.7.refs_2_, bf16[272,2048]{1,0:T(8,128)(2,1)} %collective-permute-done.5.refs_3_, ...), custom_call_target="tpu_custom_call" | custom-call | flops 369098752 | bytes 2686976 | tf_op jit(solution)/shard_map/products/pallas_call | solution.py:241
  114.4 2.5 %collective-permute-done.26.refs_2_ = f32[24,512]{1,0:T(8,128)S(1)} collective-permute-done((f32[24,512]{1,0:T(8,128)S(1)}, f32[24,512]{1,0:T(8,128)S(1)}, u32[]{:S(2)}, u32[]{:S(2)}) %collective-permute-start.26) | collective-permute-done | bytes 49184 | tf_op jit(solution)/shard_map/ppermute | solution.py:397
  118.5 4.1 %all-to-all-start = ((bf16[8,3,5120]{2,1,0:T(4,128)(2,1)}), bf16[8,3,5120]{2,1,0:T(4,128)(2,1)}, u32[]{:S(2)}, u32[]{:S(2)}) async-start(bf16[8,3,5120]{2,1,0:T(4,128)(2,1)} %bitcast.32), calls=%async_computation | async-start | bytes 655360 | tf_op jit(solution)/shard_map/all_to_all | solution.py:410
  126.9 3.0 %products.13.held_ref = f32[640,512]{1,0:T(8,128)S(1)} custom-call(s32[8]{0:T(128)S(1)} %fusion.3.refs_0_, bf16[640,2048]{1,0:T(8,128)(2,1)S(1)} %pick_columns.9.refs_1_, bf16[640,2048]{1,0:T(8,128)(2,1)} %collective-permute-done.6.refs_2_, bf16[512,512]{1,0:T(8,128)(2,1)S(1)} %copy-done.11, bf16[512,512]{1,0:T(8,128)(2,1)S(1)} %copy-done.13, ...), custom_call_target="tpu_custom_call" | custom-call | flops 1006632960 | bytes 4849664 | tf_op jit(solution)/shard_map/products/pallas_call | solution.py:241
  132.6 1.6 %rotate_attend.2.refs_0_ = bf16[24,2048]{1,0:T(8,128)(2,1)S(1)} custom-call(f32[640,512]{1,0:T(8,128)S(1)} %copy-done.7, f32[640,512]{1,0:T(8,128)S(1)} %convert_multiply_fusion.homed_ref, f32[640,128]{1,0:T(8,128)S(1)} %copy-done.14, s32[2,672]{1,0:T(2,128)S(1)} %pad_add_fusion.keys_ref, s32[24,2]{1,0:T(8,128)S(1)} %copy-done.27, ...), custom_call_target="tpu_custom_call" | custom-call | flops 125829120 | bytes 3014656 | tf_op jit(solution)/shard_map/rotate_attend/pallas_call | solution.py:104
  137.5 13.8 %all_to_all.10 = bf16[8,3,4096]{2,1,0:T(4,128)(2,1)S(1)} all-to-all(bf16[8,3,4096]{2,1,0:T(4,128)(2,1)S(1)} %bitcast.38), channel_id=1, replica_groups=mesh['groups'=2,'rows'=8,'tensor'=2] {'rows'}, dimensions={0} | all-to-all | bytes 393216 | tf_op jit(solution)/shard_map/all_to_all | solution.py:422
  (158 shorter events, 57.3 us)
Async XLA Ops:
  3.6 16.5 %collective-permute-start = (bf16[512,512]{1,0:T(8,128)(2,1)}, bf16[512,512]{1,0:T(8,128)(2,1)}, u32[]{:S(2)}, u32[]{:S(2)}) collective-permute-start(bf16[512,512]{1,0:T(8,128)(2,1)} %own_half.2.refs_3_.refs_9_), channel_id=1, source_target_pairs={{0,4},{4,8},{8,12},{12,14},{14,10},{10,6},{6,2},{2,0},{1,5},{5,9},... | collective-permute-start | bytes 1572872 | tf_op jit(solution)/shard_map/ppermute | solution.py:309
  6.7 13.7 %collective-permute-start.1 = (bf16[512,512]{1,0:T(8,128)(2,1)}, bf16[512,512]{1,0:T(8,128)(2,1)}, u32[]{:S(2)}, u32[]{:S(2)}) collective-permute-start(bf16[512,512]{1,0:T(8,128)(2,1)} %own_half.2.refs_3_.refs_9_), channel_id=1, source_target_pairs={{4,0},{8,4},{12,8},{14,12},{10,14},{6,10},{2,6},{0,2},{5,1},{9,5},... | collective-permute-start | bytes 1572872 | tf_op jit(solution)/shard_map/ppermute | solution.py:309
  9.5 10.6 %collective-permute-start.2 = (bf16[96,2048]{1,0:T(8,128)(2,1)S(1)}, bf16[96,2048]{1,0:T(8,128)(2,1)S(1)}, u32[]{:S(2)}, u32[]{:S(2)}) collective-permute-start(bf16[96,2048]{1,0:T(8,128)(2,1)S(1)} %pick_columns.6), channel_id=1, source_target_pairs={{0,16},{16,0},{1,17},{17,1},{2,18},{18,2},{3,19},{19,3},{4,20},{20... | collective-permute-start | bytes 1179656 | tf_op jit(solution)/shard_map/ppermute | solution.py:331
  22.1 26.9 %collective-permute-start.5 = (bf16[272,2048]{1,0:T(8,128)(2,1)}, bf16[272,2048]{1,0:T(8,128)(2,1)}, u32[]{:S(2)}, u32[]{:S(2)}) collective-permute-start(bf16[272,2048]{1,0:T(8,128)(2,1)} %copy-done.17), channel_id=1, source_target_pairs={{0,16},{16,0},{1,17},{17,1},{2,18},{18,2},{3,19},{19,3},{4,20},{20... | collective-permute-start | bytes 3342344 | tf_op jit(solution)/shard_map/ppermute | solution.py:346
  23.7 15.1 %collective-permute-start.3 = (bf16[512,512]{1,0:T(8,128)(2,1)}, bf16[512,512]{1,0:T(8,128)(2,1)}, u32[]{:S(2)}, u32[]{:S(2)}) collective-permute-start(bf16[512,512]{1,0:T(8,128)(2,1)} %collective-permute-done.refs_4_.refs_10_), channel_id=1, source_target_pairs={{0,4},{4,8},{8,12},{12,14},{14,10},{10,6},{6,2},{2,0},{1,5},{5,9},... | collective-permute-start | bytes 1572872 | tf_op jit(solution)/shard_map/ppermute | solution.py:309
  25.2 15.2 %collective-permute-start.4 = (bf16[512,512]{1,0:T(8,128)(2,1)}, bf16[512,512]{1,0:T(8,128)(2,1)}, u32[]{:S(2)}, u32[]{:S(2)}) collective-permute-start(bf16[512,512]{1,0:T(8,128)(2,1)} %collective-permute-done.1.refs_5_.refs_11_), channel_id=1, source_target_pairs={{4,0},{8,4},{12,8},{14,12},{10,14},{6,10},{2,6},{0,2},{5,1},{9,5},... | collective-permute-start | bytes 1572872 | tf_op jit(solution)/shard_map/ppermute | solution.py:309
  28.8 20.2 %collective-permute-start.8 = (bf16[512,512]{1,0:T(8,128)(2,1)S(1)}, bf16[512,512]{1,0:T(8,128)(2,1)S(1)}, u32[]{:S(2)}, u32[]{:S(2)}) collective-permute-start(bf16[512,512]{1,0:T(8,128)(2,1)S(1)} %own_half.3.refs_3_.refs_9_), channel_id=1, source_target_pairs={{0,4},{4,8},{8,12},{12,14},{14,10},{10,6},{6,2},{2,0},{1,5},{5,9},... | collective-permute-start | bytes 1572872 | tf_op jit(solution)/shard_map/ppermute | solution.py:309
  30.4 19.6 %collective-permute-start.9 = (bf16[512,512]{1,0:T(8,128)(2,1)S(1)}, bf16[512,512]{1,0:T(8,128)(2,1)S(1)}, u32[]{:S(2)}, u32[]{:S(2)}) collective-permute-start(bf16[512,512]{1,0:T(8,128)(2,1)S(1)} %own_half.3.refs_3_.refs_9_), channel_id=1, source_target_pairs={{4,0},{8,4},{12,8},{14,12},{10,14},{6,10},{2,6},{0,2},{5,1},{9,5},... | collective-permute-start | bytes 1572872 | tf_op jit(solution)/shard_map/ppermute | solution.py:309
  50.0 27.0 %collective-permute-start.12 = (bf16[272,2048]{1,0:T(8,128)(2,1)S(1)}, bf16[272,2048]{1,0:T(8,128)(2,1)S(1)}, u32[]{:S(2)}, u32[]{:S(2)}) collective-permute-start(bf16[272,2048]{1,0:T(8,128)(2,1)S(1)} %copy-done.16), channel_id=1, source_target_pairs={{0,16},{16,0},{1,17},{17,1},{2,18},{18,2},{3,19},{19,3},{4,20},{20... | collective-permute-start | bytes 3342344 | tf_op jit(solution)/shard_map/ppermute | solution.py:363
  50.6 15.0 %collective-permute-start.10 = (bf16[512,512]{1,0:T(8,128)(2,1)}, bf16[512,512]{1,0:T(8,128)(2,1)S(1)}, u32[]{:S(2)}, u32[]{:S(2)}) collective-permute-start(bf16[512,512]{1,0:T(8,128)(2,1)} %collective-permute-done.3.refs_6_.refs_12_), channel_id=1, source_target_pairs={{0,4},{4,8},{8,12},{12,14},{14,10},{10,6},{6,2},{2,0},{1,5},{5,9},... | collective-permute-start | bytes 1572872 | tf_op jit(solution)/shard_map/ppermute | solution.py:309
  52.2 15.0 %collective-permute-start.11 = (bf16[512,512]{1,0:T(8,128)(2,1)}, bf16[512,512]{1,0:T(8,128)(2,1)S(1)}, u32[]{:S(2)}, u32[]{:S(2)}) collective-permute-start(bf16[512,512]{1,0:T(8,128)(2,1)} %collective-permute-done.4.refs_7_.refs_13_), channel_id=1, source_target_pairs={{4,0},{8,4},{12,8},{14,12},{10,14},{6,10},{2,6},{0,2},{5,1},{9,5},... | collective-permute-start | bytes 1572872 | tf_op jit(solution)/shard_map/ppermute | solution.py:309
  53.0 24.0 %collective-permute-start.14 = (bf16[512,512]{1,0:T(8,128)(2,1)S(1)}, bf16[512,512]{1,0:T(8,128)(2,1)S(1)}, u32[]{:S(2)}, u32[]{:S(2)}) collective-permute-start(bf16[512,512]{1,0:T(8,128)(2,1)S(1)} %collective-permute-done.8.refs_4_.refs_10_), channel_id=1, source_target_pairs={{0,4},{4,8},{8,12},{12,14},{14,10},{10,6},{6,2},{2,0},{1,5},{5,9},... | collective-permute-start | bytes 1572872 | tf_op jit(solution)/shard_map/ppermute | solution.py:309
  54.5 22.8 %collective-permute-start.15 = (bf16[512,512]{1,0:T(8,128)(2,1)S(1)}, bf16[512,512]{1,0:T(8,128)(2,1)S(1)}, u32[]{:S(2)}, u32[]{:S(2)}) collective-permute-start(bf16[512,512]{1,0:T(8,128)(2,1)S(1)} %collective-permute-done.9.refs_5_.refs_11_), channel_id=1, source_target_pairs={{4,0},{8,4},{12,8},{14,12},{10,14},{6,10},{2,6},{0,2},{5,1},{9,5},... | collective-permute-start | bytes 1572872 | tf_op jit(solution)/shard_map/ppermute | solution.py:309
  78.8 11.3 %collective-permute-start.19 = (bf16[256,512]{1,0:T(8,128)(2,1)S(1)}, bf16[256,512]{1,0:T(8,128)(2,1)S(1)}, u32[]{:S(2)}, u32[]{:S(2)}) collective-permute-start(bf16[256,512]{1,0:T(8,128)(2,1)S(1)} %slice.48), channel_id=1, source_target_pairs={{0,4},{4,8},{8,12},{12,14},{14,10},{10,6},{6,2},{2,0},{1,5},{5,9},... | collective-permute-start | bytes 786440 | tf_op jit(solution)/shard_map/ppermute | solution.py:309
  80.5 9.7 %collective-permute-start.20 = (bf16[256,512]{1,0:T(8,128)(2,1)S(1)}, bf16[256,512]{1,0:T(8,128)(2,1)S(1)}, u32[]{:S(2)}, u32[]{:S(2)}) collective-permute-start(bf16[256,512]{1,0:T(8,128)(2,1)S(1)} %slice.49), channel_id=1, source_target_pairs={{4,0},{8,4},{12,8},{14,12},{10,14},{6,10},{2,6},{0,2},{5,1},{9,5},... | collective-permute-start | bytes 786440 | tf_op jit(solution)/shard_map/ppermute | solution.py:309
  83.3 6.9 %collective-permute-start.18 = (bf16[64,2048]{1,0:T(8,128)(2,1)S(1)}, bf16[64,2048]{1,0:T(8,128)(2,1)S(1)}, u32[]{:S(2)}, u32[]{:S(2)}) collective-permute-start(bf16[64,2048]{1,0:T(8,128)(2,1)S(1)} %constant_dynamic-update-slice_fusion.refs_7_), channel_id=1, source_target_pairs={{0,1},{1,0},{2,3},{3,2},{4,5},{5,4},{6,7},{7,6},{8,9},{9,8},{10,11... | collective-permute-start | bytes 786440 | tf_op jit(solution)/shard_map/ppermute | solution.py:381
  83.3 15.2 %collective-permute-start.21 = (bf16[512,512]{1,0:T(8,128)(2,1)S(1)}, bf16[512,512]{1,0:T(8,128)(2,1)S(1)}, u32[]{:S(2)}, u32[]{:S(2)}) collective-permute-start(bf16[512,512]{1,0:T(8,128)(2,1)S(1)} %collective-permute-done.14.refs_6_.refs_12_), channel_id=1, source_target_pairs={{0,4},{4,8},{8,12},{12,14},{14,10},{10,6},{6,2},{2,0},{1,5},{5,9},... | collective-permute-start | bytes 1572872 | tf_op jit(solution)/shard_map/ppermute | solution.py:309
  85.0 14.9 %collective-permute-start.22 = (bf16[512,512]{1,0:T(8,128)(2,1)S(1)}, bf16[512,512]{1,0:T(8,128)(2,1)S(1)}, u32[]{:S(2)}, u32[]{:S(2)}) collective-permute-start(bf16[512,512]{1,0:T(8,128)(2,1)S(1)} %collective-permute-done.15.refs_7_.refs_13_), channel_id=1, source_target_pairs={{4,0},{8,4},{12,8},{14,12},{10,14},{6,10},{2,6},{0,2},{5,1},{9,5},... | collective-permute-start | bytes 1572872 | tf_op jit(solution)/shard_map/ppermute | solution.py:309
  95.6 18.7 %collective-permute-start.27 = (f16[640,512]{1,0:T(8,128)(2,1)S(1)}, f16[640,512]{1,0:T(8,128)(2,1)S(1)}, u32[]{:S(2)}, u32[]{:S(2)}) collective-permute-start(f16[640,512]{1,0:T(8,128)(2,1)S(1)} %fusion.1), channel_id=1, source_target_pairs={{0,16},{16,0},{1,17},{17,1},{2,18},{18,2},{3,19},{19,3},{4,20},{20... | collective-permute-start | bytes 1966088 | tf_op jit(solution)/shard_map/ppermute | solution.py:392
  97.2 17.1 %collective-permute-start.25 = (f32[24,512]{1,0:T(8,128)S(1)}, f32[24,512]{1,0:T(8,128)S(1)}, u32[]{:S(2)}, u32[]{:S(2)}) collective-permute-start(f32[24,512]{1,0:T(8,128)S(1)} %get-tuple-element.123), channel_id=1, source_target_pairs={{0,16},{16,0},{1,17},{17,1},{2,18},{18,2},{3,19},{19,3},{4,20},{20... | collective-permute-start | bytes 147464 | tf_op jit(solution)/shard_map/ppermute | solution.py:393
  99.9 10.6 %collective-permute-start.23 = (bf16[256,512]{1,0:T(8,128)(2,1)S(1)}, bf16[256,512]{1,0:T(8,128)(2,1)S(1)}, u32[]{:S(2)}, u32[]{:S(2)}) collective-permute-start(bf16[256,512]{1,0:T(8,128)(2,1)S(1)} %slice.41), channel_id=1, source_target_pairs={{0,4},{4,8},{8,12},{12,14},{14,10},{10,6},{6,2},{2,0},{1,5},{5,9},... | collective-permute-start | bytes 786440 | tf_op jit(solution)/shard_map/ppermute | solution.py:309
  101.5 9.0 %collective-permute-start.24 = (bf16[256,512]{1,0:T(8,128)(2,1)S(1)}, bf16[256,512]{1,0:T(8,128)(2,1)S(1)}, u32[]{:S(2)}, u32[]{:S(2)}) collective-permute-start(bf16[256,512]{1,0:T(8,128)(2,1)S(1)} %slice.42), channel_id=1, source_target_pairs={{4,0},{8,4},{12,8},{14,12},{10,14},{6,10},{2,6},{0,2},{5,1},{9,5},... | collective-permute-start | bytes 786440 | tf_op jit(solution)/shard_map/ppermute | solution.py:309
  116.8 17.4 %collective-permute-start.28 = (f16[640,512]{1,0:T(8,128)(2,1)}, f16[640,512]{1,0:T(8,128)(2,1)}, u32[]{:S(2)}, u32[]{:S(2)}) collective-permute-start(f16[640,512]{1,0:T(8,128)(2,1)} %fusion), channel_id=1, source_target_pairs={{0,16},{16,0},{1,17},{17,1},{2,18},{18,2},{3,19},{19,3},{4,20},{20... | collective-permute-start | bytes 1966088 | tf_op jit(solution)/shard_map/ppermute | solution.py:403
  118.5 12.8 %all-to-all-start = ((bf16[8,3,5120]{2,1,0:T(4,128)(2,1)}), bf16[8,3,5120]{2,1,0:T(4,128)(2,1)}, u32[]{:S(2)}, u32[]{:S(2)}) async-start(bf16[8,3,5120]{2,1,0:T(4,128)(2,1)} %bitcast.32), calls=%async_computation | async-start | bytes 655360 | tf_op jit(solution)/shard_map/all_to_all | solution.py:410
  (39 other events, 225.3 us)
